TPU v7x, 32 devices: a whole 2x2x4 slice. The times are simulated.
32 devices in a mesh: gx: 4 (over y, core), gz: 4 (over z), ta: 2 (over x).
Axes of the slice: x: 2, y: 2, z: 4, core: 2. Of those that a mesh axis runs over, the one named last changes fastest.
Arguments:
- residual: bfloat16 [16, 2, 12, 8192], P(None, None, None, ('gx', 'gz', 'ta')), may hold values from -6 to 6
- null_vectors: bfloat16 [2, 24, 12, 8192], P(None, None, None, ('gx', 'gz', 'ta')), may hold values from -0.29882812 to 0.29882812
- clover_inverse: bfloat16 [2, 2, 6, 6, 8192], P(None, None, None, None, ('gx', 'gz', 'ta')), may hold values from -2.390625 to 2.390625
- coarse_op: float32 [32, 9, 2, 2304], P(('gx', 'gz', 'ta')), may hold values from -0.15 to 2.5
- vector_count: int32 [32], P(('gx', 'gz', 'ta')), may hold values from 12 to 24
Outputs:
- correction: bfloat16 [16, 2, 12, 8192], P(None, None, None, ('gx', 'gz', 'ta'))
All inputs are finite; a program needn't handle non-finite values.
Results may differ from a plain program's by a relative error of at most 0.0029.
Values sent between devices are 32-bit elements; how exact they have to be, the bound alone decides.
No kernel may reach another device: no remote copies, remote signals or barrier semaphores. Data moves between devices by JAX's collectives and lax.ppermute only.
A program may use at most 64 MiB of HBM per device.

v0:
```python
import jax
import jax.numpy as jnp
from jax import lax
from jax.sharding import PartitionSpec as P

ITERS = 5


omega_step = 0.5
exact = lax.Precision.HIGHEST


def shifted(block, axis, distance):
    devices = range(lax.axis_size(axis))
    route = [((i - distance) % len(devices), i) for i in devices]
    return lax.ppermute(block, axis, route)


def with_halo(cells, sides, width):
    for axis, dim in sides:
        count = lax.axis_size(axis)
        head = lax.slice_in_dim(cells, 0, width, axis=dim)
        tail = lax.slice_in_dim(cells, cells.shape[dim] - width, cells.shape[dim], axis=dim)
        cells = jnp.concatenate(
            [
                lax.ppermute(tail, axis, [(i, (i + 1) % count) for i in range(count)]),
                cells,
                lax.ppermute(head, axis, [((i + 1) % count, i) for i in range(count)]),
            ],
            axis=dim,
        )
    return cells


def complex_mul(matrix, vector):

    def product(left, right):
        return jnp.einsum("bij,bjr->bir", left, right, precision=exact)

    real_part = product(matrix[:, 0], vector[:, 0]) - product(matrix[:, 1], vector[:, 1])
    imag_part = product(matrix[:, 0], vector[:, 1]) + product(matrix[:, 1], vector[:, 0])
    return jnp.stack([real_part, imag_part], 1)


def plane_neighbours(vector, plane_y):
    position = lax.axis_index("gx")
    plane_col = position % plane_y
    along_row = {}
    for offset in [-plane_y, plane_y]:
        along_row[offset] = shifted(vector, "gx", offset)
    senders = {
        -1: jnp.where(plane_col == 0, along_row[plane_y], vector),
        1: jnp.where(plane_col == plane_y - 1, along_row[-plane_y], vector),
    }
    along_col = {}
    for offset in [-1, 1]:
        along_col[offset] = shifted(senders[offset], "gx", offset)
    return [along_row[-plane_y], along_row[plane_y], along_col[-1], along_col[1]]


def coarse_apply(operator, vector, plane_y):
    in_plane = plane_neighbours(vector, plane_y)
    padded = with_halo(vector[None], (("gz", 0), ("ta", 1)), 1)
    moved = [vector] + in_plane + [padded[2, 1:-1], padded[0, 1:-1], padded[1, 2:], padded[1, :-2]]
    summed = jnp.zeros(vector.shape, jnp.float32)
    for link_id in range(9):
        summed = summed + complex_mul(operator[:, link_id], moved[link_id])
    return summed


def body(residual, null_vectors, clover_inverse, coarse_op, vector_count):
    rhs_count = residual.shape[0]
    vec_total = null_vectors.shape[1]
    time_blocks = coarse_op.shape[0]
    local_sites = residual.shape[3]
    block_sites = local_sites // time_blocks
    coarse_dim = 2 * vec_total
    plane_y = min(8, lax.axis_size("gx") // 2)
    in_use = (lax.iota(jnp.int32, vec_total)[None, :] < vector_count[:, None]).astype(jnp.float32)
    in_use = in_use[:, None, None, :, None]
    fine_rows = residual.reshape(rhs_count, 2, 2, 6, time_blocks, block_sites)
    vectors = null_vectors.reshape(2, vec_total, 2, 6, time_blocks, block_sites)

    def contract(left, right):
        return jnp.einsum("kxcbw,rxcbw->bxkr", left, right, preferred_element_type=jnp.float32)

    real_part = contract(vectors[0], fine_rows[:, 0]) + contract(vectors[1], fine_rows[:, 1])
    imag_part = contract(vectors[0], fine_rows[:, 1]) - contract(vectors[1], fine_rows[:, 0])
    restricted = (jnp.stack([real_part, imag_part], 1) * in_use).reshape(
        time_blocks, 2, coarse_dim, rhs_count
    )
    operator = coarse_op.reshape(time_blocks, 9, 2, coarse_dim, coarse_dim)
    coarse = omega_step * restricted
    for sweep_id in range(ITERS - 1):
        coarse = coarse + omega_step * (restricted - coarse_apply(operator, coarse, plane_y))
    coarse_rounded = (coarse.reshape(time_blocks, 2, 2, vec_total, rhs_count) * in_use).astype(
        jnp.bfloat16
    )

    def spread_out(left, right):
        return jnp.einsum("kxcbw,bxkr->rxcbw", left, right, preferred_element_type=jnp.float32)

    def local_apply(left, right):
        return jnp.einsum("xabs,rxbs->rxas", left, right, preferred_element_type=jnp.float32)

    lift_real = spread_out(vectors[0], coarse_rounded[:, 0]) - spread_out(
        vectors[1], coarse_rounded[:, 1]
    )
    lift_imag = spread_out(vectors[0], coarse_rounded[:, 1]) + spread_out(
        vectors[1], coarse_rounded[:, 0]
    )
    flat_rows = residual.reshape(rhs_count, 2, 2, 6, local_sites)
    local_real = local_apply(clover_inverse[0], flat_rows[:, 0]) - local_apply(
        clover_inverse[1], flat_rows[:, 1]
    )
    local_imag = local_apply(clover_inverse[0], flat_rows[:, 1]) + local_apply(
        clover_inverse[1], flat_rows[:, 0]
    )
    result = jnp.stack(
        [
            local_real + lift_real.reshape(rhs_count, 2, 6, local_sites),
            local_imag + lift_imag.reshape(rhs_count, 2, 6, local_sites),
        ],
        1,
    )
    return result.reshape(rhs_count, 2, 12, local_sites).astype(jnp.bfloat16)


def solution(mesh):
    in_specs = (
        P(None, None, None, ("gx", "gz", "ta")),
        P(None, None, None, ("gx", "gz", "ta")),
        P(None, None, None, None, ("gx", "gz", "ta")),
        P(("gx", "gz", "ta"), None, None, None),
        P(("gx", "gz", "ta")),
    )
    out_specs = P(None, None, None, ("gx", "gz", "ta"))
    return jax.shard_map(body, mesh=mesh, in_specs=in_specs, out_specs=out_specs, check_vma=False)
```

profile of v0, /device:TPU:0, one launch (start us, length us, event | category | flops | bytes accessed | tf_op | source)
XLA Modules:
  0.0 119.8 jit_solution(14644347394657016805)
XLA Ops:
  6.0 3.0 %collective-permute-start.4 = (f32[1,1,2,48,16]{3,4,2,1,0:T(8,128)}, f32[1,1,2,48,16]{3,4,2,1,0:T(8,128)}, u32[]{:S(2)}, u32[]{:S(2)}) collective-permute-start(f32[1,1,2,48,16]{3,4,2,1,0:T(8,128)} %broadcast_multiply_fusion), channel_id=1, source_target_pairs={{0,2},{2,4},{4,6},{6,0},{1,3},{3,5},{5,7},{7,1},{8,10},{10,12},{12... | collective-permute-start | bytes 18440 | tf_op jit(solution)/shard_map/ppermute | solution.py:26
  9.0 2.0 %collective-permute-start.3 = (f32[1,1,2,48,16]{3,4,2,1,0:T(8,128)}, f32[1,1,2,48,16]{3,4,2,1,0:T(8,128)}, u32[]{:S(2)}, u32[]{:S(2)}) collective-permute-start(f32[1,1,2,48,16]{3,4,2,1,0:T(8,128)} %broadcast_multiply_fusion), channel_id=1, source_target_pairs={{2,0},{4,2},{6,4},{0,6},{3,1},{5,3},{7,5},{1,7},{10,8},{12,10},{14... | collective-permute-start | bytes 18440 | tf_op jit(solution)/shard_map/ppermute | solution.py:28
  11.8 1.8 %collective-permute-start = (f32[1,2,48,16]{2,3,1,0:T(8,128)}, f32[1,2,48,16]{2,3,1,0:T(8,128)}, u32[]{:S(2)}, u32[]{:S(2)}) collective-permute-start(f32[1,2,48,16]{2,3,1,0:T(8,128)} %broadcast_multiply_fusion.1), channel_id=1, source_target_pairs={{16,0},{24,8},{0,16},{8,24},{17,1},{25,9},{1,17},{9,25},{18,2},{26... | collective-permute-start | bytes 18440 | tf_op jit(solution)/shard_map/ppermute | solution.py:16
  14.0 1.5 %fusion.140 = f32[16,48]{1,0:T(8,128)} fusion(f32[1,2,48,48]{3,2,1,0:T(8,128)S(1)} %get-tuple-element.13, f32[1,2,48,16]{2,3,1,0:T(8,128)} %broadcast_multiply_fusion.1), kind=kOutput, calls=%fused_computation.274 | convolution fusion | flops 442368 | bytes 35840 | tf_op jit(solution)/shard_map/bij,bjr->bir/dot_general | solution.py:38
  15.4 1.4 %fusion.141 = f32[16,48]{1,0:T(8,128)} fusion(f32[1,2,48,48]{3,2,1,0:T(8,128)S(1)} %get-tuple-element.13, f32[1,2,48,16]{2,3,1,0:T(8,128)} %broadcast_multiply_fusion.1), kind=kOutput, calls=%fused_computation.275 | convolution fusion | flops 442368 | bytes 35840 | tf_op jit(solution)/shard_map/bij,bjr->bir/dot_general | solution.py:38
  19.4 1.5 %copy.197 = bf16[16,1,2,6,256]{0,3,4,2,1:T(8,128)(2,1)S(1)} copy(bf16[16,1,2,6,256]{4,0,3,2,1:T(8,128)(2,1)} %get-tuple-element.17) | data formatting | bytes 196608
  20.9 2.3 %copy.196 = bf16[1,2,6,6,256]{3,2,4,1,0:T(8,128)(2,1)} copy(bf16[1,2,6,6,256]{4,1,3,2,0:T(2,128)(2,1)} %get-tuple-element.19) | data formatting | bytes 73728
  23.1 3.3 %fusion.30 = f32[2,256,16,6]{2,3,1,0:T(8,128)} fusion(bf16[16,1,2,6,256]{0,3,4,2,1:T(8,128)(2,1)S(1)} %copy.197, bf16[1,2,6,6,256]{3,2,4,1,0:T(8,128)(2,1)} %copy.196), kind=kOutput, calls=%fused_computation.108 | convolution fusion | flops 589824 | bytes 331776 | tf_op jit(solution)/shard_map/xabs,rxbs->rxas/dot_general | solution.py:104
  26.4 2.0 %fusion.34 = f32[2,256,16,6]{2,3,1,0:T(8,128)} fusion(bf16[1,2,6,6,256]{3,2,4,1,0:T(8,128)(2,1)S(1)} %copy-done, bf16[16,1,2,6,256]{0,3,4,2,1:T(8,128)(2,1)S(1)} %copy.195), kind=kOutput, calls=%fused_computation.112 | convolution fusion | flops 589824 | bytes 331776 | tf_op jit(solution)/shard_map/xabs,rxbs->rxas/dot_general | solution.py:104
  28.5 2.0 %fusion.26 = f32[2,256,16,6]{2,3,1,0:T(8,128)} fusion(bf16[1,2,6,6,256]{3,2,4,1,0:T(8,128)(2,1)S(1)} %copy.198, bf16[16,1,2,6,256]{0,3,4,2,1:T(8,128)(2,1)S(1)} %copy.195), kind=kOutput, calls=%fused_computation.104 | convolution fusion | flops 589824 | bytes 331776 | tf_op jit(solution)/shard_map/xabs,rxbs->rxas/dot_general | solution.py:104
  30.5 2.1 %fusion.28 = f32[2,256,16,6]{2,3,1,0:T(8,128)} fusion(bf16[1,2,6,6,256]{3,2,4,1,0:T(8,128)(2,1)S(1)} %copy.198, bf16[16,1,2,6,256]{0,3,4,2,1:T(8,128)(2,1)S(1)} %copy.197), kind=kOutput, calls=%fused_computation.106 | convolution fusion | flops 589824 | bytes 331776 | tf_op jit(solution)/shard_map/xabs,rxbs->rxas/dot_general | solution.py:104
  36.4 2.0 %copy.186 = f32[2,256,16,6]{1,2,3,0:T(8,128)S(1)} copy(f32[2,256,16,6]{2,3,1,0:T(8,128)} %fusion.30) | data formatting | bytes 393216 | tf_op jit(solution)/shard_map/xabs,rxbs->rxas/dot_general | solution.py:104
  39.0 2.2 %copy.187 = f32[2,256,16,6]{1,2,3,0:T(8,128)S(1)} copy(f32[2,256,16,6]{2,3,1,0:T(8,128)} %fusion.26) | data formatting | bytes 393216 | tf_op jit(solution)/shard_map/xabs,rxbs->rxas/dot_general | solution.py:104
  42.5 1.5 %collective-permute-start.6 = (f32[3,1,2,48,16]{3,4,2,1,0:T(8,128)S(1)}, f32[3,1,2,48,16]{3,4,2,1,0:T(8,128)S(1)}, u32[]{:S(2)}, u32[]{:S(2)}) collective-permute-start(f32[3,1,2,48,16]{3,4,2,1,0:T(8,128)S(1)} %pad_maximum_fusion.1), channel_id=1, source_target_pairs={{0,1},{1,0},{2,3},{3,2},{4,5},{5,4},{6,7},{7,6},{8,9},{9,8},{10,11... | collective-permute-start | bytes 55304 | tf_op jit(solution)/shard_map/ppermute | solution.py:26
  48.7 1.7 %collective-permute-start.1 = (f32[1,2,48,16]{2,3,1,0:T(8,128)S(1)}, f32[1,2,48,16]{2,3,1,0:T(8,128)S(1)}, u32[]{:S(2)}, u32[]{:S(2)}) collective-permute-start(f32[1,2,48,16]{2,3,1,0:T(8,128)S(1)} %get-tuple-element.21), channel_id=1, source_target_pairs={{8,0},{16,8},{24,16},{0,24},{9,1},{17,9},{25,17},{1,25},{10,2},{18... | collective-permute-start | bytes 18440 | tf_op jit(solution)/shard_map/ppermute | solution.py:16
  64.9 3.8 %collective-permute-start.10 = (f32[1,1,2,48,16]{3,4,2,1,0:T(8,128)S(1)}, f32[1,1,2,48,16]{3,4,2,1,0:T(8,128)S(1)}, u32[]{:S(2)}, u32[]{:S(2)}) collective-permute-start(f32[1,1,2,48,16]{3,4,2,1,0:T(8,128)S(1)} %fusion.93), channel_id=1, source_target_pairs={{2,0},{4,2},{6,4},{0,6},{3,1},{5,3},{7,5},{1,7},{10,8},{12,10},{14... | collective-permute-start | bytes 18440 | tf_op jit(solution)/shard_map/ppermute | solution.py:28
  71.1 1.6 %collective-permute-start.13 = (f32[3,1,2,48,16]{3,4,2,1,0:T(8,128)S(1)}, f32[3,1,2,48,16]{3,4,2,1,0:T(8,128)S(1)}, u32[]{:S(2)}, u32[]{:S(2)}) collective-permute-start(f32[3,1,2,48,16]{3,4,2,1,0:T(8,128)S(1)} %pad_maximum_fusion.2), channel_id=1, source_target_pairs={{0,1},{1,0},{2,3},{3,2},{4,5},{5,4},{6,7},{7,6},{8,9},{9,8},{10,11... | collective-permute-start | bytes 55304 | tf_op jit(solution)/shard_map/ppermute | solution.py:26
  75.9 2.0 %collective-permute-start.8 = (f32[1,2,48,16]{2,3,1,0:T(8,128)S(1)}, f32[1,2,48,16]{2,3,1,0:T(8,128)S(1)}, u32[]{:S(2)}, u32[]{:S(2)}) collective-permute-start(f32[1,2,48,16]{2,3,1,0:T(8,128)S(1)} %get-tuple-element.27), channel_id=1, source_target_pairs={{8,0},{16,8},{24,16},{0,24},{9,1},{17,9},{25,17},{1,25},{10,2},{18... | collective-permute-start | bytes 18440 | tf_op jit(solution)/shard_map/ppermute | solution.py:16
  82.5 3.8 %collective-permute-start.17 = (f32[1,1,2,48,16]{3,4,2,1,0:T(8,128)S(1)}, f32[1,1,2,48,16]{3,4,2,1,0:T(8,128)S(1)}, u32[]{:S(2)}, u32[]{:S(2)}) collective-permute-start(f32[1,1,2,48,16]{3,4,2,1,0:T(8,128)S(1)} %fusion.113), channel_id=1, source_target_pairs={{2,0},{4,2},{6,4},{0,6},{3,1},{5,3},{7,5},{1,7},{10,8},{12,10},{14... | collective-permute-start | bytes 18440 | tf_op jit(solution)/shard_map/ppermute | solution.py:28
  89.0 1.6 %collective-permute-start.20 = (f32[3,1,2,48,16]{3,4,2,1,0:T(8,128)S(1)}, f32[3,1,2,48,16]{3,4,2,1,0:T(8,128)S(1)}, u32[]{:S(2)}, u32[]{:S(2)}) collective-permute-start(f32[3,1,2,48,16]{3,4,2,1,0:T(8,128)S(1)} %pad_maximum_fusion.3), channel_id=1, source_target_pairs={{0,1},{1,0},{2,3},{3,2},{4,5},{5,4},{6,7},{7,6},{8,9},{9,8},{10,11... | collective-permute-start | bytes 55304 | tf_op jit(solution)/shard_map/ppermute | solution.py:26
  93.8 1.8 %collective-permute-start.15 = (f32[1,2,48,16]{2,3,1,0:T(8,128)S(1)}, f32[1,2,48,16]{2,3,1,0:T(8,128)S(1)}, u32[]{:S(2)}, u32[]{:S(2)}) collective-permute-start(f32[1,2,48,16]{2,3,1,0:T(8,128)S(1)} %get-tuple-element.25), channel_id=1, source_target_pairs={{8,0},{16,8},{24,16},{0,24},{9,1},{17,9},{25,17},{1,25},{10,2},{18... | collective-permute-start | bytes 18440 | tf_op jit(solution)/shard_map/ppermute | solution.py:16
  101.3 3.8 %collective-permute-start.24 = (f32[1,1,2,48,16]{3,4,2,1,0:T(8,128)S(1)}, f32[1,1,2,48,16]{3,4,2,1,0:T(8,128)S(1)}, u32[]{:S(2)}, u32[]{:S(2)}) collective-permute-start(f32[1,1,2,48,16]{3,4,2,1,0:T(8,128)S(1)} %fusion.133), channel_id=1, source_target_pairs={{2,0},{4,2},{6,4},{0,6},{3,1},{5,3},{7,5},{1,7},{10,8},{12,10},{14... | collective-permute-start | bytes 18440 | tf_op jit(solution)/shard_map/ppermute | solution.py:28
  107.5 1.6 %collective-permute-start.27 = (f32[3,1,2,48,16]{3,4,2,1,0:T(8,128)S(1)}, f32[3,1,2,48,16]{3,4,2,1,0:T(8,128)S(1)}, u32[]{:S(2)}, u32[]{:S(2)}) collective-permute-start(f32[3,1,2,48,16]{3,4,2,1,0:T(8,128)S(1)} %pad_maximum_fusion.4), channel_id=1, source_target_pairs={{0,1},{1,0},{2,3},{3,2},{4,5},{5,4},{6,7},{7,6},{8,9},{9,8},{10,11... | collective-permute-start | bytes 55304 | tf_op jit(solution)/shard_map/ppermute | solution.py:26
  111.4 1.7 %collective-permute-start.22 = (f32[1,2,48,16]{2,3,1,0:T(8,128)S(1)}, f32[1,2,48,16]{2,3,1,0:T(8,128)S(1)}, u32[]{:S(2)}, u32[]{:S(2)}) collective-permute-start(f32[1,2,48,16]{2,3,1,0:T(8,128)S(1)} %get-tuple-element.23), channel_id=1, source_target_pairs={{8,0},{16,8},{24,16},{0,24},{9,1},{17,9},{25,17},{1,25},{10,2},{18... | collective-permute-start | bytes 18440 | tf_op jit(solution)/shard_map/ppermute | solution.py:16
  (447 shorter events, 66.1 us)
Async XLA Ops:
  6.0 35.8 %collective-permute-start.4 = (f32[1,1,2,48,16]{3,4,2,1,0:T(8,128)}, f32[1,1,2,48,16]{3,4,2,1,0:T(8,128)}, u32[]{:S(2)}, u32[]{:S(2)}) collective-permute-start(f32[1,1,2,48,16]{3,4,2,1,0:T(8,128)} %broadcast_multiply_fusion), channel_id=1, source_target_pairs={{0,2},{2,4},{4,6},{6,0},{1,3},{3,5},{5,7},{7,1},{8,10},{10,12},{12... | collective-permute-start | bytes 18440 | tf_op jit(solution)/shard_map/ppermute | solution.py:26
  9.0 32.7 %collective-permute-start.3 = (f32[1,1,2,48,16]{3,4,2,1,0:T(8,128)}, f32[1,1,2,48,16]{3,4,2,1,0:T(8,128)}, u32[]{:S(2)}, u32[]{:S(2)}) collective-permute-start(f32[1,1,2,48,16]{3,4,2,1,0:T(8,128)} %broadcast_multiply_fusion), channel_id=1, source_target_pairs={{2,0},{4,2},{6,4},{0,6},{3,1},{5,3},{7,5},{1,7},{10,8},{12,10},{14... | collective-permute-start | bytes 18440 | tf_op jit(solution)/shard_map/ppermute | solution.py:28
  11.8 36.1 %collective-permute-start = (f32[1,2,48,16]{2,3,1,0:T(8,128)}, f32[1,2,48,16]{2,3,1,0:T(8,128)}, u32[]{:S(2)}, u32[]{:S(2)}) collective-permute-start(f32[1,2,48,16]{2,3,1,0:T(8,128)} %broadcast_multiply_fusion.1), channel_id=1, source_target_pairs={{16,0},{24,8},{0,16},{8,24},{17,1},{25,9},{1,17},{9,25},{18,2},{26... | collective-permute-start | bytes 18440 | tf_op jit(solution)/shard_map/ppermute | solution.py:16
  42.5 20.6 %collective-permute-start.6 = (f32[3,1,2,48,16]{3,4,2,1,0:T(8,128)S(1)}, f32[3,1,2,48,16]{3,4,2,1,0:T(8,128)S(1)}, u32[]{:S(2)}, u32[]{:S(2)}) collective-permute-start(f32[3,1,2,48,16]{3,4,2,1,0:T(8,128)S(1)} %pad_maximum_fusion.1), channel_id=1, source_target_pairs={{0,1},{1,0},{2,3},{3,2},{4,5},{5,4},{6,7},{7,6},{8,9},{9,8},{10,11... | collective-permute-start | bytes 55304 | tf_op jit(solution)/shard_map/ppermute | solution.py:26
  44.0 19.4 %collective-permute-start.5 = (f32[3,1,2,48,16]{3,4,2,1,0:T(8,128)S(1)}, f32[3,1,2,48,16]{3,4,2,1,0:T(8,128)S(1)}, u32[]{:S(2)}, u32[]{:S(2)}) collective-permute-start(f32[3,1,2,48,16]{3,4,2,1,0:T(8,128)S(1)} %pad_maximum_fusion.1), channel_id=1, source_target_pairs={{1,0},{0,1},{3,2},{2,3},{5,4},{4,5},{7,6},{6,7},{9,8},{8,9},{11,10... | collective-permute-start | bytes 55304 | tf_op jit(solution)/shard_map/ppermute | solution.py:28
  48.7 12.7 %collective-permute-start.2 = (f32[1,2,48,16]{2,3,1,0:T(8,128)S(1)}, f32[1,2,48,16]{2,3,1,0:T(8,128)S(1)}, u32[]{:S(2)}, u32[]{:S(2)}) collective-permute-start(f32[1,2,48,16]{2,3,1,0:T(8,128)S(1)} %get-tuple-element.20), channel_id=1, source_target_pairs={{24,0},{0,8},{8,16},{16,24},{25,1},{1,9},{9,17},{17,25},{26,2},{2,... | collective-permute-start | bytes 18440 | tf_op jit(solution)/shard_map/ppermute | solution.py:16
  48.7 13.0 %collective-permute-start.1 = (f32[1,2,48,16]{2,3,1,0:T(8,128)S(1)}, f32[1,2,48,16]{2,3,1,0:T(8,128)S(1)}, u32[]{:S(2)}, u32[]{:S(2)}) collective-permute-start(f32[1,2,48,16]{2,3,1,0:T(8,128)S(1)} %get-tuple-element.21), channel_id=1, source_target_pairs={{8,0},{16,8},{24,16},{0,24},{9,1},{17,9},{25,17},{1,25},{10,2},{18... | collective-permute-start | bytes 18440 | tf_op jit(solution)/shard_map/ppermute | solution.py:16
  64.8 5.6 %collective-permute-start.11 = (f32[1,1,2,48,16]{3,4,2,1,0:T(8,128)S(1)}, f32[1,1,2,48,16]{3,4,2,1,0:T(8,128)S(1)}, u32[]{:S(2)}, u32[]{:S(2)}) collective-permute-start(f32[1,1,2,48,16]{3,4,2,1,0:T(8,128)S(1)} %fusion.93), channel_id=1, source_target_pairs={{0,2},{2,4},{4,6},{6,0},{1,3},{3,5},{5,7},{7,1},{8,10},{10,12},{12... | collective-permute-start | bytes 18440 | tf_op jit(solution)/shard_map/ppermute | solution.py:26
  64.9 5.8 %collective-permute-start.10 = (f32[1,1,2,48,16]{3,4,2,1,0:T(8,128)S(1)}, f32[1,1,2,48,16]{3,4,2,1,0:T(8,128)S(1)}, u32[]{:S(2)}, u32[]{:S(2)}) collective-permute-start(f32[1,1,2,48,16]{3,4,2,1,0:T(8,128)S(1)} %fusion.93), channel_id=1, source_target_pairs={{2,0},{4,2},{6,4},{0,6},{3,1},{5,3},{7,5},{1,7},{10,8},{12,10},{14... | collective-permute-start | bytes 18440 | tf_op jit(solution)/shard_map/ppermute | solution.py:28
  68.7 5.1 %collective-permute-start.7 = (f32[1,2,48,16]{2,3,1,0:T(8,128)S(1)}, f32[1,2,48,16]{2,3,1,0:T(8,128)S(1)}, u32[]{:S(2)}, u32[]{:S(2)}) collective-permute-start(f32[1,2,48,16]{2,3,1,0:T(8,128)S(1)} %fusion.83), channel_id=1, source_target_pairs={{16,0},{24,8},{0,16},{8,24},{17,1},{25,9},{1,17},{9,25},{18,2},{26... | collective-permute-start | bytes 18440 | tf_op jit(solution)/shard_map/ppermute | solution.py:16
  71.1 9.6 %collective-permute-start.13 = (f32[3,1,2,48,16]{3,4,2,1,0:T(8,128)S(1)}, f32[3,1,2,48,16]{3,4,2,1,0:T(8,128)S(1)}, u32[]{:S(2)}, u32[]{:S(2)}) collective-permute-start(f32[3,1,2,48,16]{3,4,2,1,0:T(8,128)S(1)} %pad_maximum_fusion.2), channel_id=1, source_target_pairs={{0,1},{1,0},{2,3},{3,2},{4,5},{5,4},{6,7},{7,6},{8,9},{9,8},{10,11... | collective-permute-start | bytes 55304 | tf_op jit(solution)/shard_map/ppermute | solution.py:26
  72.6 8.3 %collective-permute-start.12 = (f32[3,1,2,48,16]{3,4,2,1,0:T(8,128)S(1)}, f32[3,1,2,48,16]{3,4,2,1,0:T(8,128)S(1)}, u32[]{:S(2)}, u32[]{:S(2)}) collective-permute-start(f32[3,1,2,48,16]{3,4,2,1,0:T(8,128)S(1)} %pad_maximum_fusion.2), channel_id=1, source_target_pairs={{1,0},{0,1},{3,2},{2,3},{5,4},{4,5},{7,6},{6,7},{9,8},{8,9},{11,10... | collective-permute-start | bytes 55304 | tf_op jit(solution)/shard_map/ppermute | solution.py:28
  73.9 4.0 %collective-permute-start.9 = (f32[1,2,48,16]{2,3,1,0:T(8,128)S(1)}, f32[1,2,48,16]{2,3,1,0:T(8,128)S(1)}, u32[]{:S(2)}, u32[]{:S(2)}) collective-permute-start(f32[1,2,48,16]{2,3,1,0:T(8,128)S(1)} %get-tuple-element.26), channel_id=1, source_target_pairs={{24,0},{0,8},{8,16},{16,24},{25,1},{1,9},{9,17},{17,25},{26,2},{2,... | collective-permute-start | bytes 18440 | tf_op jit(solution)/shard_map/ppermute | solution.py:16
  82.4 5.9 %collective-permute-start.18 = (f32[1,1,2,48,16]{3,4,2,1,0:T(8,128)S(1)}, f32[1,1,2,48,16]{3,4,2,1,0:T(8,128)S(1)}, u32[]{:S(2)}, u32[]{:S(2)}) collective-permute-start(f32[1,1,2,48,16]{3,4,2,1,0:T(8,128)S(1)} %fusion.113), channel_id=1, source_target_pairs={{0,2},{2,4},{4,6},{6,0},{1,3},{3,5},{5,7},{7,1},{8,10},{10,12},{12... | collective-permute-start | bytes 18440 | tf_op jit(solution)/shard_map/ppermute | solution.py:26
  82.5 6.1 %collective-permute-start.17 = (f32[1,1,2,48,16]{3,4,2,1,0:T(8,128)S(1)}, f32[1,1,2,48,16]{3,4,2,1,0:T(8,128)S(1)}, u32[]{:S(2)}, u32[]{:S(2)}) collective-permute-start(f32[1,1,2,48,16]{3,4,2,1,0:T(8,128)S(1)} %fusion.113), channel_id=1, source_target_pairs={{2,0},{4,2},{6,4},{0,6},{3,1},{5,3},{7,5},{1,7},{10,8},{12,10},{14... | collective-permute-start | bytes 18440 | tf_op jit(solution)/shard_map/ppermute | solution.py:28
  86.3 5.4 %collective-permute-start.14 = (f32[1,2,48,16]{2,3,1,0:T(8,128)S(1)}, f32[1,2,48,16]{2,3,1,0:T(8,128)S(1)}, u32[]{:S(2)}, u32[]{:S(2)}) collective-permute-start(f32[1,2,48,16]{2,3,1,0:T(8,128)S(1)} %fusion.103), channel_id=1, source_target_pairs={{16,0},{24,8},{0,16},{8,24},{17,1},{25,9},{1,17},{9,25},{18,2},{26... | collective-permute-start | bytes 18440 | tf_op jit(solution)/shard_map/ppermute | solution.py:16
  89.0 9.4 %collective-permute-start.20 = (f32[3,1,2,48,16]{3,4,2,1,0:T(8,128)S(1)}, f32[3,1,2,48,16]{3,4,2,1,0:T(8,128)S(1)}, u32[]{:S(2)}, u32[]{:S(2)}) collective-permute-start(f32[3,1,2,48,16]{3,4,2,1,0:T(8,128)S(1)} %pad_maximum_fusion.3), channel_id=1, source_target_pairs={{0,1},{1,0},{2,3},{3,2},{4,5},{5,4},{6,7},{7,6},{8,9},{9,8},{10,11... | collective-permute-start | bytes 55304 | tf_op jit(solution)/shard_map/ppermute | solution.py:26
  90.5 8.2 %collective-permute-start.19 = (f32[3,1,2,48,16]{3,4,2,1,0:T(8,128)S(1)}, f32[3,1,2,48,16]{3,4,2,1,0:T(8,128)S(1)}, u32[]{:S(2)}, u32[]{:S(2)}) collective-permute-start(f32[3,1,2,48,16]{3,4,2,1,0:T(8,128)S(1)} %pad_maximum_fusion.3), channel_id=1, source_target_pairs={{1,0},{0,1},{3,2},{2,3},{5,4},{4,5},{7,6},{6,7},{9,8},{8,9},{11,10... | collective-permute-start | bytes 55304 | tf_op jit(solution)/shard_map/ppermute | solution.py:28
  91.8 3.8 %collective-permute-start.16 = (f32[1,2,48,16]{2,3,1,0:T(8,128)S(1)}, f32[1,2,48,16]{2,3,1,0:T(8,128)S(1)}, u32[]{:S(2)}, u32[]{:S(2)}) collective-permute-start(f32[1,2,48,16]{2,3,1,0:T(8,128)S(1)} %get-tuple-element.24), channel_id=1, source_target_pairs={{24,0},{0,8},{8,16},{16,24},{25,1},{1,9},{9,17},{17,25},{26,2},{2,... | collective-permute-start | bytes 18440 | tf_op jit(solution)/shard_map/ppermute | solution.py:16
  100.1 9.5 %collective-permute-start.21 = (f32[1,2,48,16]{2,3,1,0:T(8,128)S(1)}, f32[1,2,48,16]{2,3,1,0:T(8,128)S(1)}, u32[]{:S(2)}, u32[]{:S(2)}) collective-permute-start(f32[1,2,48,16]{2,3,1,0:T(8,128)S(1)} %fusion.123), channel_id=1, source_target_pairs={{16,0},{24,8},{0,16},{8,24},{17,1},{25,9},{1,17},{9,25},{18,2},{26... | collective-permute-start | bytes 18440 | tf_op jit(solution)/shard_map/ppermute | solution.py:16
  101.2 5.6 %collective-permute-start.25 = (f32[1,1,2,48,16]{3,4,2,1,0:T(8,128)S(1)}, f32[1,1,2,48,16]{3,4,2,1,0:T(8,128)S(1)}, u32[]{:S(2)}, u32[]{:S(2)}) collective-permute-start(f32[1,1,2,48,16]{3,4,2,1,0:T(8,128)S(1)} %fusion.133), channel_id=1, source_target_pairs={{0,2},{2,4},{4,6},{6,0},{1,3},{3,5},{5,7},{7,1},{8,10},{10,12},{12... | collective-permute-start | bytes 18440 | tf_op jit(solution)/shard_map/ppermute | solution.py:26
  101.3 5.9 %collective-permute-start.24 = (f32[1,1,2,48,16]{3,4,2,1,0:T(8,128)S(1)}, f32[1,1,2,48,16]{3,4,2,1,0:T(8,128)S(1)}, u32[]{:S(2)}, u32[]{:S(2)}) collective-permute-start(f32[1,1,2,48,16]{3,4,2,1,0:T(8,128)S(1)} %fusion.133), channel_id=1, source_target_pairs={{2,0},{4,2},{6,4},{0,6},{3,1},{5,3},{7,5},{1,7},{10,8},{12,10},{14... | collective-permute-start | bytes 18440 | tf_op jit(solution)/shard_map/ppermute | solution.py:28
  107.5 8.7 %collective-permute-start.27 = (f32[3,1,2,48,16]{3,4,2,1,0:T(8,128)S(1)}, f32[3,1,2,48,16]{3,4,2,1,0:T(8,128)S(1)}, u32[]{:S(2)}, u32[]{:S(2)}) collective-permute-start(f32[3,1,2,48,16]{3,4,2,1,0:T(8,128)S(1)} %pad_maximum_fusion.4), channel_id=1, source_target_pairs={{0,1},{1,0},{2,3},{3,2},{4,5},{5,4},{6,7},{7,6},{8,9},{9,8},{10,11... | collective-permute-start | bytes 55304 | tf_op jit(solution)/shard_map/ppermute | solution.py:26
  109.1 7.5 %collective-permute-start.26 = (f32[3,1,2,48,16]{3,4,2,1,0:T(8,128)S(1)}, f32[3,1,2,48,16]{3,4,2,1,0:T(8,128)S(1)}, u32[]{:S(2)}, u32[]{:S(2)}) collective-permute-start(f32[3,1,2,48,16]{3,4,2,1,0:T(8,128)S(1)} %pad_maximum_fusion.4), channel_id=1, source_target_pairs={{1,0},{0,1},{3,2},{2,3},{5,4},{4,5},{7,6},{6,7},{9,8},{8,9},{11,10... | collective-permute-start | bytes 55304 | tf_op jit(solution)/shard_map/ppermute | solution.py:28
  (36 other events, 392.8 us)
where the time goes:
time: 122 us; the launch traced here: 120 us
  matrix products  48 us (39%)
  starting transfers between devices  36.7 us (30%)
  local copies, waits for them, and re-layouts  24.9 us (20%)
  waiting for transfers between devices  4.44 us (4%)
  other arithmetic  4.11 us (3%)
  between operations  1.67 us (1%)
    dot_general x144, matrix products, product(): return jnp.einsum('bij,bjr->bir', left, right, precision=exact)  37.3 us
    ppermute x8, starting transfers between devices, with_halo(): lax.ppermute(head, axis, [((i + 1) % count, i) for i in range(count)])  15.6 us
    ppermute x12, starting transfers between devices, shifted(): return lax.ppermute(block, axis, route)  11.7 us
    dot_general x4, matrix products, local_apply(): jnp.einsum('xabs,rxbs->rxas', left, right, preferred_element_type=jnp.flo...  9.46 us
    ppermute x8, starting transfers between devices, with_halo(): lax.ppermute(tail, axis, [(i, (i + 1) % count) for i in range(count)])  9.36 us
    unnamed x69, local copies, waits for them, and re-layouts  7.87 us
    another operation x144, local copies, waits for them, and re-layouts, complex_mul(): return jnp.stack([real_part, imag_part], 1)  7.78 us
    dot_general x4, local copies, waits for them, and re-layouts, local_apply(): jnp.einsum('xabs,rxbs->rxas', left, right, preferred_element_type=jnp.flo...  5.23 us
  transfers between devices with their start and end apart: 28, of which 5 were waited for; matrix products, arithmetic and copies ran while one was open for 54% of the time, Pallas kernels for 0%

commit v1 on v0

v1 whole, which is shorter than its diff:
```python
import jax
import jax.numpy as jnp
from jax import lax
from jax.sharding import PartitionSpec as P

ITERS = 5


omega_step = 0.5
exact = lax.Precision.HIGHEST


def routes():
    total = lax.axis_size("gx")
    plane_y = min(8, total // 2)
    plane_x = total // plane_y
    links = []
    for step in (1, -1):
        links.append(
            ("gx", tuple(((g // plane_y + step) % plane_x) * plane_y + g % plane_y for g in range(total)))
        )
    for step in (1, -1):
        links.append(
            ("gx", tuple((g // plane_y) * plane_y + (g % plane_y + step) % plane_y for g in range(total)))
        )
    for axis in ("gz", "ta"):
        count = lax.axis_size(axis)
        for step in (1, -1):
            links.append((axis, tuple((i + step) % count for i in range(count))))
    return links


def fetch(block, link):
    axis, sources = link
    return lax.ppermute(block, axis, [(source, i) for i, source in enumerate(sources)])


def body(residual, null_vectors, clover_inverse, coarse_op, vector_count):
    rhs_count = residual.shape[0]
    vec_total = null_vectors.shape[1]
    coarse_dim = 2 * vec_total
    sites = residual.shape[3]
    in_use = (lax.iota(jnp.int32, vec_total)[None, :] < vector_count[:, None]).astype(jnp.float32)[0]
    used = jnp.tile(in_use, 4)

    fine_rows = residual.transpose(2, 1, 0, 3).reshape(2, 6, 2 * rhs_count, sites)
    vectors = null_vectors.transpose(2, 0, 1, 3).reshape(2, 6, 2 * vec_total, sites)
    product = jnp.einsum("xcrs,xcks->xrk", fine_rows, vectors, preferred_element_type=jnp.float32)
    product = product.reshape(2, 2, rhs_count, 2, vec_total)
    real_part = product[:, 0, :, 0] + product[:, 1, :, 1]
    imag_part = product[:, 1, :, 0] - product[:, 0, :, 1]
    restricted = jnp.stack([real_part, imag_part]).transpose(2, 0, 1, 3)
    half = omega_step * (restricted.reshape(rhs_count, 2 * coarse_dim) * used)

    operator = coarse_op.reshape(9, 2, coarse_dim, coarse_dim)
    grouped = {}
    for link_id, link in enumerate(routes()):
        grouped.setdefault(link, []).append(operator[link_id + 1])
    order = sorted(grouped, key=lambda link: ("gz", "ta", "gx").index(link[0]))

    def real_form(matrix):
        upper = jnp.concatenate([matrix[0], -matrix[1]], 1)
        lower = jnp.concatenate([matrix[1], matrix[0]], 1)
        return omega_step * jnp.concatenate([upper, lower], 0)

    own = jnp.eye(2 * coarse_dim, dtype=jnp.float32) - real_form(operator[0])
    around = jnp.concatenate([-real_form(sum(grouped[link])) for link in order], 1)

    def apply(vector, matrix):
        return lax.dot_general(vector, matrix, (((1,), (1,)), ((), ())), precision=exact)

    coarse = half
    for sweep_id in range(ITERS - 1):
        moved = [fetch(coarse, link) for link in order]
        kept = half + apply(coarse, own)
        coarse = kept + apply(jnp.concatenate(moved, 1), around)

    rounded = (coarse * used).reshape(rhs_count, 2, 2, vec_total)
    real_rows = jnp.stack([rounded[:, 0], -rounded[:, 1]], 1)
    imag_rows = jnp.stack([rounded[:, 1], rounded[:, 0]], 1)
    weights = jnp.stack([real_rows, imag_rows]).transpose(3, 0, 1, 2, 4)
    weights = weights.reshape(2, 2 * rhs_count, 2 * vec_total).astype(jnp.bfloat16)
    lift = jnp.einsum("xrk,xcks->xcrs", weights, vectors, preferred_element_type=jnp.float32)

    rows = residual.reshape(rhs_count, 2, 2, 6, sites).astype(jnp.float32)
    clover = clover_inverse.astype(jnp.float32)

    def local_apply(left, right):
        return sum(left[:, :, b][None] * right[:, :, b][:, :, None] for b in range(6))

    local_real = local_apply(clover[0], rows[:, 0]) - local_apply(clover[1], rows[:, 1])
    local_imag = local_apply(clover[0], rows[:, 1]) + local_apply(clover[1], rows[:, 0])
    lift = lift.reshape(2, 6, 2, rhs_count, sites).transpose(3, 2, 0, 1, 4)
    result = jnp.stack([local_real, local_imag], 1) + lift
    return result.reshape(rhs_count, 2, 12, sites).astype(jnp.bfloat16)


def solution(mesh):
    in_specs = (
        P(None, None, None, ("gx", "gz", "ta")),
        P(None, None, None, ("gx", "gz", "ta")),
        P(None, None, None, None, ("gx", "gz", "ta")),
        P(("gx", "gz", "ta"), None, None, None),
        P(("gx", "gz", "ta")),
    )
    out_specs = P(None, None, None, ("gx", "gz", "ta"))
    return jax.shard_map(body, mesh=mesh, in_specs=in_specs, out_specs=out_specs, check_vma=False)
```

time: 122 us -> 44.4 us (0.36); the launches traced: 120 us -> 44.2 us
  matrix products: 48 us -> 2.22 us
  local copies, waits for them, and re-layouts: 24.9 us -> 5.8 us
  starting transfers between devices: 36.7 us -> 22.2 us
  waiting for transfers between devices: 4.44 us -> 11.6 us
  other arithmetic: 4.11 us -> 1.2 us
    dot_general x156 -> x10, matrix products: 48 us -> 2.22 us  [the longest x8 1.84 us: apply(): lax.dot_general(vector, matrix, (((1,), (1,)), ((), ())), precision=exact)]
    ppermute x28 -> x20, starting transfers between devices: 36.7 us -> 22.2 us  [fetch(): lax.ppermute(block, axis, [(source, i) for i, source in enumerate(sources)])]
    another operation x149 -> x1, local copies, waits for them, and re-layouts: 8.98 us -> 0.01 us  [body(): used = jnp.tile(in_use, 4)]
    ppermute x28 -> x20, waiting for transfers between devices: 4.44 us -> 11.6 us  [fetch(): lax.ppermute(block, axis, [(source, i) for i, source in enumerate(sources)])]
    unnamed x69 -> x8, local copies, waits for them, and re-layouts: 7.87 us -> 2.6 us
    dot_general x4 -> x0, local copies, waits for them, and re-layouts: 5.23 us -> none  [local_apply(): jnp.einsum('xabs,rxbs->rxas', left, right, preferred_element_type=jnp.flo...]
    slice x3 -> x4, local copies, waits for them, and re-layouts: 2.32 us -> 0.3 us  [the longest x3 0.29 us: real_form(): upper = jnp.concatenate([matrix[0], -matrix[1]], 1)]
    mul x3 -> x1, other arithmetic: 1.83 us -> 0.01 us  [body(): half = omega_step * (restricted.reshape(rhs_count, 2 * coarse_dim) * used)]
  transfers between devices with their start and end apart: 28 -> 20, of which waited for: 5 -> 5; matrix products, arithmetic and copies ran while one was open for 54% -> 8% of each run, Pallas kernels for 0% -> 0%
where the time goes in v1:
time: 44.4 us; the launch traced here: 44.2 us
  starting transfers between devices  22.2 us (50%)
  waiting for transfers between devices  11.6 us (26%)
  local copies, waits for them, and re-layouts  5.8 us (13%)
  matrix products  2.22 us (5%)
  other arithmetic  1.2 us (3%)
  between operations  1.17 us (3%)
    ppermute x20, starting transfers between devices, fetch(): lax.ppermute(block, axis, [(source, i) for i, source in enumerate(sources)])  22.2 us
    ppermute x20, waiting for transfers between devices, fetch(): lax.ppermute(block, axis, [(source, i) for i, source in enumerate(sources)])  11.6 us
    unnamed x8, local copies, waits for them, and re-layouts  2.6 us
    dot_general x8, matrix products, apply(): lax.dot_general(vector, matrix, (((1,), (1,)), ((), ())), precision=exact)  1.84 us
  transfers between devices with their start and end apart: 20, of which 5 were waited for; matrix products, arithmetic and copies ran while one was open for 8% of the time, Pallas kernels for 0%

profile of v1, /device:TPU:0, one launch (start us, length us, event | category | flops | bytes accessed | tf_op | source)
XLA Modules:
  0.0 44.2 jit_solution(15578544917076687391)
XLA Ops:
  0.0 1.0 %copy.49 = bf16[2,24,12,256]{3,1,0,2:T(8,128)(2,1)S(1)} copy(bf16[2,24,12,256]{3,1,2,0:T(8,128)(2,1)} %param.6) | data formatting | bytes 589824 | tf_op args[1]
  2.4 5.1 %collective-permute-start = (f32[16,96]{1,0:T(8,128)S(1)}, f32[16,96]{1,0:T(8,128)S(1)}, u32[]{:S(2)}, u32[]{:S(2)}) collective-permute-start(f32[16,96]{1,0:T(8,128)S(1)} %multiply_multiply_fusion), channel_id=1, source_target_pairs={{2,0},{4,2},{6,4},{0,6},{3,1},{5,3},{7,5},{1,7},{10,8},{12,10},{14... | collective-permute-start | bytes 18440 | tf_op jit(solution)/shard_map/ppermute | solution.py:35
  7.4 1.5 %collective-permute-start.2 = (f32[16,96]{1,0:T(8,128)S(1)}, f32[16,96]{1,0:T(8,128)S(1)}, u32[]{:S(2)}, u32[]{:S(2)}) collective-permute-start(f32[16,96]{1,0:T(8,128)S(1)} %multiply_multiply_fusion), channel_id=1, source_target_pairs={{1,0},{0,1},{3,2},{2,3},{5,4},{4,5},{7,6},{6,7},{9,8},{8,9},{11,10... | collective-permute-start | bytes 18440 | tf_op jit(solution)/shard_map/ppermute | solution.py:35
  8.9 1.5 %collective-permute-start.3 = (f32[16,96]{1,0:T(8,128)S(1)}, f32[16,96]{1,0:T(8,128)S(1)}, u32[]{:S(2)}, u32[]{:S(2)}) collective-permute-start(f32[16,96]{1,0:T(8,128)S(1)} %multiply_multiply_fusion), channel_id=1, source_target_pairs={{16,0},{24,8},{0,16},{8,24},{17,1},{25,9},{1,17},{9,25},{18,2},{26... | collective-permute-start | bytes 18440 | tf_op jit(solution)/shard_map/ppermute | solution.py:35
  10.6 0.8 %copy-done.2 = bf16[2,2,6,6,256]{4,1,3,2,0:T(2,128)(2,1)S(1)} copy-done((bf16[2,2,6,6,256]{4,1,3,2,0:T(2,128)(2,1)S(1)}, bf16[2,2,6,6,256]{4,1,3,2,0:T(2,128)(2,1)}, u32[]{:S(2)}) %copy-start.2) | copy-done | bytes 73752
  12.1 0.7 %copy-done.1 = f32[1,9,2,2304]{3,2,1,0:T(2,128)S(1)} copy-done((f32[1,9,2,2304]{3,2,1,0:T(2,128)S(1)}, f32[1,9,2,2304]{3,2,1,0:T(2,128)}, u32[]{:S(2)}) %copy-start.1) | copy-done | bytes 165912
  14.3 0.2 convolution_add_fusion
  15.3 3.9 %collective-permute-start.5 = (f32[16,96]{1,0:T(8,128)S(1)}, f32[16,96]{1,0:T(8,128)S(1)}, u32[]{:S(2)}, u32[]{:S(2)}) collective-permute-start(f32[16,96]{1,0:T(8,128)S(1)} %convolution_add_fusion.7), channel_id=1, source_target_pairs={{2,0},{4,2},{6,4},{0,6},{3,1},{5,3},{7,5},{1,7},{10,8},{12,10},{14... | collective-permute-start | bytes 18440 | tf_op jit(solution)/shard_map/ppermute | solution.py:35
  19.1 0.5 %collective-permute-start.7 = (f32[16,96]{1,0:T(8,128)S(1)}, f32[16,96]{1,0:T(8,128)S(1)}, u32[]{:S(2)}, u32[]{:S(2)}) collective-permute-start(f32[16,96]{1,0:T(8,128)S(1)} %convolution_add_fusion.7), channel_id=1, source_target_pairs={{1,0},{0,1},{3,2},{2,3},{5,4},{4,5},{7,6},{6,7},{9,8},{8,9},{11,10... | collective-permute-start | bytes 18440 | tf_op jit(solution)/shard_map/ppermute | solution.py:35
  19.7 0.5 %collective-permute-start.8 = (f32[16,96]{1,0:T(8,128)S(1)}, f32[16,96]{1,0:T(8,128)S(1)}, u32[]{:S(2)}, u32[]{:S(2)}) collective-permute-start(f32[16,96]{1,0:T(8,128)S(1)} %convolution_add_fusion.7), channel_id=1, source_target_pairs={{16,0},{24,8},{0,16},{8,24},{17,1},{25,9},{1,17},{9,25},{18,2},{26... | collective-permute-start | bytes 18440 | tf_op jit(solution)/shard_map/ppermute | solution.py:35
  20.2 0.2 convolution_add_fusion.6
  20.5 4.1 %collective-permute-done.6 = f32[16,96]{1,0:T(8,128)S(1)} collective-permute-done((f32[16,96]{1,0:T(8,128)S(1)}, f32[16,96]{1,0:T(8,128)S(1)}, u32[]{:S(2)}, u32[]{:S(2)}) %collective-permute-start.6) | collective-permute-done | bytes 6176 | tf_op jit(solution)/shard_map/ppermute | solution.py:35
  24.9 2.6 %collective-permute-start.10 = (f32[16,96]{1,0:T(8,128)S(1)}, f32[16,96]{1,0:T(8,128)S(1)}, u32[]{:S(2)}, u32[]{:S(2)}) collective-permute-start(f32[16,96]{1,0:T(8,128)S(1)} %convolution_add_fusion.5), channel_id=1, source_target_pairs={{2,0},{4,2},{6,4},{0,6},{3,1},{5,3},{7,5},{1,7},{10,8},{12,10},{14... | collective-permute-start | bytes 18440 | tf_op jit(solution)/shard_map/ppermute | solution.py:35
  27.5 1.5 %collective-permute-start.12 = (f32[16,96]{1,0:T(8,128)S(1)}, f32[16,96]{1,0:T(8,128)S(1)}, u32[]{:S(2)}, u32[]{:S(2)}) collective-permute-start(f32[16,96]{1,0:T(8,128)S(1)} %convolution_add_fusion.5), channel_id=1, source_target_pairs={{1,0},{0,1},{3,2},{2,3},{5,4},{4,5},{7,6},{6,7},{9,8},{8,9},{11,10... | collective-permute-start | bytes 18440 | tf_op jit(solution)/shard_map/ppermute | solution.py:35
  29.0 0.5 %collective-permute-start.13 = (f32[16,96]{1,0:T(8,128)S(1)}, f32[16,96]{1,0:T(8,128)S(1)}, u32[]{:S(2)}, u32[]{:S(2)}) collective-permute-start(f32[16,96]{1,0:T(8,128)S(1)} %convolution_add_fusion.5), channel_id=1, source_target_pairs={{16,0},{24,8},{0,16},{8,24},{17,1},{25,9},{1,17},{9,25},{18,2},{26... | collective-permute-start | bytes 18440 | tf_op jit(solution)/shard_map/ppermute | solution.py:35
  29.5 0.2 convolution_add_fusion.4
  29.8 3.2 %collective-permute-done.11 = f32[16,96]{1,0:T(8,128)S(1)} collective-permute-done((f32[16,96]{1,0:T(8,128)S(1)}, f32[16,96]{1,0:T(8,128)S(1)}, u32[]{:S(2)}, u32[]{:S(2)}) %collective-permute-start.11) | collective-permute-done | bytes 6176 | tf_op jit(solution)/shard_map/ppermute | solution.py:35
  33.3 3.6 %collective-permute-start.15 = (f32[16,96]{1,0:T(8,128)S(1)}, f32[16,96]{1,0:T(8,128)S(1)}, u32[]{:S(2)}, u32[]{:S(2)}) collective-permute-start(f32[16,96]{1,0:T(8,128)S(1)} %convolution_add_fusion.3), channel_id=1, source_target_pairs={{2,0},{4,2},{6,4},{0,6},{3,1},{5,3},{7,5},{1,7},{10,8},{12,10},{14... | collective-permute-start | bytes 18440 | tf_op jit(solution)/shard_map/ppermute | solution.py:35
  36.9 0.5 %collective-permute-start.17 = (f32[16,96]{1,0:T(8,128)S(1)}, f32[16,96]{1,0:T(8,128)S(1)}, u32[]{:S(2)}, u32[]{:S(2)}) collective-permute-start(f32[16,96]{1,0:T(8,128)S(1)} %convolution_add_fusion.3), channel_id=1, source_target_pairs={{1,0},{0,1},{3,2},{2,3},{5,4},{4,5},{7,6},{6,7},{9,8},{8,9},{11,10... | collective-permute-start | bytes 18440 | tf_op jit(solution)/shard_map/ppermute | solution.py:35
  37.4 0.5 %collective-permute-start.18 = (f32[16,96]{1,0:T(8,128)S(1)}, f32[16,96]{1,0:T(8,128)S(1)}, u32[]{:S(2)}, u32[]{:S(2)}) collective-permute-start(f32[16,96]{1,0:T(8,128)S(1)} %convolution_add_fusion.3), channel_id=1, source_target_pairs={{16,0},{24,8},{0,16},{8,24},{17,1},{25,9},{1,17},{9,25},{18,2},{26... | collective-permute-start | bytes 18440 | tf_op jit(solution)/shard_map/ppermute | solution.py:35
  37.9 0.2 convolution_add_fusion.2
  38.3 4.1 %collective-permute-done.16 = f32[16,96]{1,0:T(8,128)S(1)} collective-permute-done((f32[16,96]{1,0:T(8,128)S(1)}, f32[16,96]{1,0:T(8,128)S(1)}, u32[]{:S(2)}, u32[]{:S(2)}) %collective-permute-start.16) | collective-permute-done | bytes 6176 | tf_op jit(solution)/shard_map/ppermute | solution.py:35
  42.4 0.2 fusion
  43.4 0.8 %copy.54 = bf16[16,2,2,6,256]{4,1,3,2,0:T(2,128)(2,1)} copy(bf16[16,2,2,6,256]{4,0,1,3,2:T(8,128)(2,1)S(1)} %fusion.1) | data formatting | bytes 393216 | tf_op jit(solution)/shard_map/convert_element_type | solution.py:95
  (104 shorter events, 4.9 us)
Async XLA Ops:
  0.0 1.0 %copy-start = (bf16[16,2,12,256]{3,1,2,0:T(2,128)(2,1)S(1)}, bf16[16,2,12,256]{3,1,2,0:T(2,128)(2,1)}, u32[]{:S(2)}) copy-start(bf16[16,2,12,256]{3,1,2,0:T(2,128)(2,1)} %param.5) | copy-start | bytes 589828
  2.4 12.5 %collective-permute-start = (f32[16,96]{1,0:T(8,128)S(1)}, f32[16,96]{1,0:T(8,128)S(1)}, u32[]{:S(2)}, u32[]{:S(2)}) collective-permute-start(f32[16,96]{1,0:T(8,128)S(1)} %multiply_multiply_fusion), channel_id=1, source_target_pairs={{2,0},{4,2},{6,4},{0,6},{3,1},{5,3},{7,5},{1,7},{10,8},{12,10},{14... | collective-permute-start | bytes 18440 | tf_op jit(solution)/shard_map/ppermute | solution.py:35
  7.4 7.5 %collective-permute-start.1 = (f32[16,96]{1,0:T(8,128)S(1)}, f32[16,96]{1,0:T(8,128)S(1)}, u32[]{:S(2)}, u32[]{:S(2)}) collective-permute-start(f32[16,96]{1,0:T(8,128)S(1)} %multiply_multiply_fusion), channel_id=1, source_target_pairs={{6,0},{0,2},{2,4},{4,6},{7,1},{1,3},{3,5},{5,7},{14,8},{8,10},{10,... | collective-permute-start | bytes 18440 | tf_op jit(solution)/shard_map/ppermute | solution.py:35
  7.4 7.5 %collective-permute-start.2 = (f32[16,96]{1,0:T(8,128)S(1)}, f32[16,96]{1,0:T(8,128)S(1)}, u32[]{:S(2)}, u32[]{:S(2)}) collective-permute-start(f32[16,96]{1,0:T(8,128)S(1)} %multiply_multiply_fusion), channel_id=1, source_target_pairs={{1,0},{0,1},{3,2},{2,3},{5,4},{4,5},{7,6},{6,7},{9,8},{8,9},{11,10... | collective-permute-start | bytes 18440 | tf_op jit(solution)/shard_map/ppermute | solution.py:35
  8.9 6.0 %collective-permute-start.3 = (f32[16,96]{1,0:T(8,128)S(1)}, f32[16,96]{1,0:T(8,128)S(1)}, u32[]{:S(2)}, u32[]{:S(2)}) collective-permute-start(f32[16,96]{1,0:T(8,128)S(1)} %multiply_multiply_fusion), channel_id=1, source_target_pairs={{16,0},{24,8},{0,16},{8,24},{17,1},{25,9},{1,17},{9,25},{18,2},{26... | collective-permute-start | bytes 18440 | tf_op jit(solution)/shard_map/ppermute | solution.py:35
  10.5 4.5 %collective-permute-start.4 = (f32[16,96]{1,0:T(8,128)S(1)}, f32[16,96]{1,0:T(8,128)S(1)}, u32[]{:S(2)}, u32[]{:S(2)}) collective-permute-start(f32[16,96]{1,0:T(8,128)S(1)} %multiply_multiply_fusion), channel_id=1, source_target_pairs={{8,0},{0,8},{24,16},{16,24},{9,1},{1,9},{25,17},{17,25},{10,2},{2,... | collective-permute-start | bytes 18440 | tf_op jit(solution)/shard_map/ppermute | solution.py:35
  10.5 0.9 %copy-start.2 = (bf16[2,2,6,6,256]{4,1,3,2,0:T(2,128)(2,1)S(1)}, bf16[2,2,6,6,256]{4,1,3,2,0:T(2,128)(2,1)}, u32[]{:S(2)}) copy-start(bf16[2,2,6,6,256]{4,1,3,2,0:T(2,128)(2,1)} %param.7) | copy-start | bytes 221188
  11.9 0.9 %copy-start.1 = (f32[1,9,2,2304]{3,2,1,0:T(2,128)S(1)}, f32[1,9,2,2304]{3,2,1,0:T(2,128)}, u32[]{:S(2)}) copy-start(f32[1,9,2,2304]{3,2,1,0:T(2,128)} %param.8) | copy-start | bytes 497668
  15.3 5.2 %collective-permute-start.5 = (f32[16,96]{1,0:T(8,128)S(1)}, f32[16,96]{1,0:T(8,128)S(1)}, u32[]{:S(2)}, u32[]{:S(2)}) collective-permute-start(f32[16,96]{1,0:T(8,128)S(1)} %convolution_add_fusion.7), channel_id=1, source_target_pairs={{2,0},{4,2},{6,4},{0,6},{3,1},{5,3},{7,5},{1,7},{10,8},{12,10},{14... | collective-permute-start | bytes 18440 | tf_op jit(solution)/shard_map/ppermute | solution.py:35
  19.1 5.4 %collective-permute-start.6 = (f32[16,96]{1,0:T(8,128)S(1)}, f32[16,96]{1,0:T(8,128)S(1)}, u32[]{:S(2)}, u32[]{:S(2)}) collective-permute-start(f32[16,96]{1,0:T(8,128)S(1)} %convolution_add_fusion.7), channel_id=1, source_target_pairs={{6,0},{0,2},{2,4},{4,6},{7,1},{1,3},{3,5},{5,7},{14,8},{8,10},{10,... | collective-permute-start | bytes 18440 | tf_op jit(solution)/shard_map/ppermute | solution.py:35
  19.1 5.4 %collective-permute-start.7 = (f32[16,96]{1,0:T(8,128)S(1)}, f32[16,96]{1,0:T(8,128)S(1)}, u32[]{:S(2)}, u32[]{:S(2)}) collective-permute-start(f32[16,96]{1,0:T(8,128)S(1)} %convolution_add_fusion.7), channel_id=1, source_target_pairs={{1,0},{0,1},{3,2},{2,3},{5,4},{4,5},{7,6},{6,7},{9,8},{8,9},{11,10... | collective-permute-start | bytes 18440 | tf_op jit(solution)/shard_map/ppermute | solution.py:35
  19.7 4.9 %collective-permute-start.8 = (f32[16,96]{1,0:T(8,128)S(1)}, f32[16,96]{1,0:T(8,128)S(1)}, u32[]{:S(2)}, u32[]{:S(2)}) collective-permute-start(f32[16,96]{1,0:T(8,128)S(1)} %convolution_add_fusion.7), channel_id=1, source_target_pairs={{16,0},{24,8},{0,16},{8,24},{17,1},{25,9},{1,17},{9,25},{18,2},{26... | collective-permute-start | bytes 18440 | tf_op jit(solution)/shard_map/ppermute | solution.py:35
  20.2 4.4 %collective-permute-start.9 = (f32[16,96]{1,0:T(8,128)S(1)}, f32[16,96]{1,0:T(8,128)S(1)}, u32[]{:S(2)}, u32[]{:S(2)}) collective-permute-start(f32[16,96]{1,0:T(8,128)S(1)} %convolution_add_fusion.7), channel_id=1, source_target_pairs={{8,0},{0,8},{24,16},{16,24},{9,1},{1,9},{25,17},{17,25},{10,2},{2,... | collective-permute-start | bytes 18440 | tf_op jit(solution)/shard_map/ppermute | solution.py:35
  24.9 4.9 %collective-permute-start.10 = (f32[16,96]{1,0:T(8,128)S(1)}, f32[16,96]{1,0:T(8,128)S(1)}, u32[]{:S(2)}, u32[]{:S(2)}) collective-permute-start(f32[16,96]{1,0:T(8,128)S(1)} %convolution_add_fusion.5), channel_id=1, source_target_pairs={{2,0},{4,2},{6,4},{0,6},{3,1},{5,3},{7,5},{1,7},{10,8},{12,10},{14... | collective-permute-start | bytes 18440 | tf_op jit(solution)/shard_map/ppermute | solution.py:35
  27.5 5.4 %collective-permute-start.11 = (f32[16,96]{1,0:T(8,128)S(1)}, f32[16,96]{1,0:T(8,128)S(1)}, u32[]{:S(2)}, u32[]{:S(2)}) collective-permute-start(f32[16,96]{1,0:T(8,128)S(1)} %convolution_add_fusion.5), channel_id=1, source_target_pairs={{6,0},{0,2},{2,4},{4,6},{7,1},{1,3},{3,5},{5,7},{14,8},{8,10},{10,... | collective-permute-start | bytes 18440 | tf_op jit(solution)/shard_map/ppermute | solution.py:35
  27.5 5.4 %collective-permute-start.12 = (f32[16,96]{1,0:T(8,128)S(1)}, f32[16,96]{1,0:T(8,128)S(1)}, u32[]{:S(2)}, u32[]{:S(2)}) collective-permute-start(f32[16,96]{1,0:T(8,128)S(1)} %convolution_add_fusion.5), channel_id=1, source_target_pairs={{1,0},{0,1},{3,2},{2,3},{5,4},{4,5},{7,6},{6,7},{9,8},{8,9},{11,10... | collective-permute-start | bytes 18440 | tf_op jit(solution)/shard_map/ppermute | solution.py:35
  29.0 4.0 %collective-permute-start.13 = (f32[16,96]{1,0:T(8,128)S(1)}, f32[16,96]{1,0:T(8,128)S(1)}, u32[]{:S(2)}, u32[]{:S(2)}) collective-permute-start(f32[16,96]{1,0:T(8,128)S(1)} %convolution_add_fusion.5), channel_id=1, source_target_pairs={{16,0},{24,8},{0,16},{8,24},{17,1},{25,9},{1,17},{9,25},{18,2},{26... | collective-permute-start | bytes 18440 | tf_op jit(solution)/shard_map/ppermute | solution.py:35
  29.5 3.5 %collective-permute-start.14 = (f32[16,96]{1,0:T(8,128)S(1)}, f32[16,96]{1,0:T(8,128)S(1)}, u32[]{:S(2)}, u32[]{:S(2)}) collective-permute-start(f32[16,96]{1,0:T(8,128)S(1)} %convolution_add_fusion.5), channel_id=1, source_target_pairs={{8,0},{0,8},{24,16},{16,24},{9,1},{1,9},{25,17},{17,25},{10,2},{2,... | collective-permute-start | bytes 18440 | tf_op jit(solution)/shard_map/ppermute | solution.py:35
  33.3 4.9 %collective-permute-start.15 = (f32[16,96]{1,0:T(8,128)S(1)}, f32[16,96]{1,0:T(8,128)S(1)}, u32[]{:S(2)}, u32[]{:S(2)}) collective-permute-start(f32[16,96]{1,0:T(8,128)S(1)} %convolution_add_fusion.3), channel_id=1, source_target_pairs={{2,0},{4,2},{6,4},{0,6},{3,1},{5,3},{7,5},{1,7},{10,8},{12,10},{14... | collective-permute-start | bytes 18440 | tf_op jit(solution)/shard_map/ppermute | solution.py:35
  36.9 5.4 %collective-permute-start.16 = (f32[16,96]{1,0:T(8,128)S(1)}, f32[16,96]{1,0:T(8,128)S(1)}, u32[]{:S(2)}, u32[]{:S(2)}) collective-permute-start(f32[16,96]{1,0:T(8,128)S(1)} %convolution_add_fusion.3), channel_id=1, source_target_pairs={{6,0},{0,2},{2,4},{4,6},{7,1},{1,3},{3,5},{5,7},{14,8},{8,10},{10,... | collective-permute-start | bytes 18440 | tf_op jit(solution)/shard_map/ppermute | solution.py:35
  36.9 5.4 %collective-permute-start.17 = (f32[16,96]{1,0:T(8,128)S(1)}, f32[16,96]{1,0:T(8,128)S(1)}, u32[]{:S(2)}, u32[]{:S(2)}) collective-permute-start(f32[16,96]{1,0:T(8,128)S(1)} %convolution_add_fusion.3), channel_id=1, source_target_pairs={{1,0},{0,1},{3,2},{2,3},{5,4},{4,5},{7,6},{6,7},{9,8},{8,9},{11,10... | collective-permute-start | bytes 18440 | tf_op jit(solution)/shard_map/ppermute | solution.py:35
  37.4 4.9 %collective-permute-start.18 = (f32[16,96]{1,0:T(8,128)S(1)}, f32[16,96]{1,0:T(8,128)S(1)}, u32[]{:S(2)}, u32[]{:S(2)}) collective-permute-start(f32[16,96]{1,0:T(8,128)S(1)} %convolution_add_fusion.3), channel_id=1, source_target_pairs={{16,0},{24,8},{0,16},{8,24},{17,1},{25,9},{1,17},{9,25},{18,2},{26... | collective-permute-start | bytes 18440 | tf_op jit(solution)/shard_map/ppermute | solution.py:35
  37.9 4.4 %collective-permute-start.19 = (f32[16,96]{1,0:T(8,128)S(1)}, f32[16,96]{1,0:T(8,128)S(1)}, u32[]{:S(2)}, u32[]{:S(2)}) collective-permute-start(f32[16,96]{1,0:T(8,128)S(1)} %convolution_add_fusion.3), channel_id=1, source_target_pairs={{8,0},{0,8},{24,16},{16,24},{9,1},{1,9},{25,17},{17,25},{10,2},{2,... | collective-permute-start | bytes 18440 | tf_op jit(solution)/shard_map/ppermute | solution.py:35

commit v2 on v1

--- a/solution.py
+++ b/solution.py
@@ -14,19 +14,30 @@
     total = lax.axis_size("gx")
     plane_y = min(8, total // 2)
     plane_x = total // plane_y
+
+    def ring(count):
+        up = [(i + 1) % count for i in range(count)]
+        down = [(i - 1) % count for i in range(count)]
+        if count % 2:
+            return up, down, False
+        even = [(up if i % 2 == 0 else down)[i] for i in range(count)]
+        odd = [(down if i % 2 == 0 else up)[i] for i in range(count)]
+        return even, odd, True
+
     links = []
-    for step in (1, -1):
-        links.append(
-            ("gx", tuple(((g // plane_y + step) % plane_x) * plane_y + g % plane_y for g in range(total)))
-        )
-    for step in (1, -1):
-        links.append(
-            ("gx", tuple((g // plane_y) * plane_y + (g % plane_y + step) % plane_y for g in range(total)))
-        )
+    first, second, paired = ring(plane_x)
+    links.append(
+        [("gx", tuple(way[g // plane_y] * plane_y + g % plane_y for g in range(total))) for way in (first, second)]
+        + [paired, lax.axis_index("gx") // plane_y]
+    )
+    first, second, paired = ring(plane_y)
+    links.append(
+        [("gx", tuple((g // plane_y) * plane_y + way[g % plane_y] for g in range(total))) for way in (first, second)]
+        + [paired, lax.axis_index("gx") % plane_y]
+    )
     for axis in ("gz", "ta"):
-        count = lax.axis_size(axis)
-        for step in (1, -1):
-            links.append((axis, tuple((i + step) % count for i in range(count))))
+        first, second, paired = ring(lax.axis_size(axis))
+        links.append([(axis, tuple(first)), (axis, tuple(second)), paired, lax.axis_index(axis)])
     return links
 
 
@@ -54,9 +65,20 @@
 
     operator = coarse_op.reshape(9, 2, coarse_dim, coarse_dim)
     grouped = {}
-    for link_id, link in enumerate(routes()):
-        grouped.setdefault(link, []).append(operator[link_id + 1])
-    order = sorted(grouped, key=lambda link: ("gz", "ta", "gx").index(link[0]))
+    for way, (first, second, paired, place) in enumerate(routes()):
+        plus, minus = operator[2 * way + 1], operator[2 * way + 2]
+        if first == second:
+            grouped[first] = plus + minus
+        else:
+            swap = (place % 2 == 1) & paired
+            grouped[first] = jnp.where(swap, minus, plus)
+            grouped[second] = jnp.where(swap, plus, minus)
+
+    def reach(link):
+        axis, sources = link
+        return ("gz", "ta", "gx").index(axis), -max(abs(source - i) for i, source in enumerate(sources))
+
+    order = sorted(grouped, key=reach)
 
     def real_form(matrix):
         upper = jnp.concatenate([matrix[0], -matrix[1]], 1)
@@ -64,7 +86,7 @@
         return omega_step * jnp.concatenate([upper, lower], 0)
 
     own = jnp.eye(2 * coarse_dim, dtype=jnp.float32) - real_form(operator[0])
-    around = jnp.concatenate([-real_form(sum(grouped[link])) for link in order], 1)
+    around = jnp.concatenate([-real_form(grouped[link]) for link in order], 1)
 
     def apply(vector, matrix):
         return lax.dot_general(vector, matrix, (((1,), (1,)), ((), ())), precision=exact)

time: 44.4 us -> 38.9 us (0.88)
  waiting for transfers between devices: 11.6 us -> 8.74 us
  starting transfers between devices: 22.2 us -> 19.4 us
    ppermute x20, waiting for transfers between devices: 11.6 us -> 8.74 us  [fetch(): lax.ppermute(block, axis, [(source, i) for i, source in enumerate(sources)])]
    ppermute x20, starting transfers between devices: 22.2 us -> 19.4 us  [fetch(): lax.ppermute(block, axis, [(source, i) for i, source in enumerate(sources)])]
  transfers between devices with their start and end apart: 20 -> 20, of which waited for: 5 -> 9; matrix products, arithmetic and copies ran while one was open for 8% -> 9% of each run, Pallas kernels for 0% -> 0%
where the time goes in v2:
time: 38.9 us; the launch traced here: 38.7 us
  starting transfers between devices  19.4 us (50%)
  waiting for transfers between devices  8.74 us (22%)
  local copies, waits for them, and re-layouts  5.78 us (15%)
  matrix products  2.23 us (6%)
  other arithmetic  1.28 us (3%)
  between operations  1.18 us (3%)
    ppermute x20, starting transfers between devices, fetch(): lax.ppermute(block, axis, [(source, i) for i, source in enumerate(sources)])  19.4 us
    ppermute x20, waiting for transfers between devices, fetch(): lax.ppermute(block, axis, [(source, i) for i, source in enumerate(sources)])  8.74 us
    unnamed x8, local copies, waits for them, and re-layouts  2.59 us
    dot_general x8, matrix products, apply(): lax.dot_general(vector, matrix, (((1,), (1,)), ((), ())), precision=exact)  1.84 us
    squeeze x12, local copies, waits for them, and re-layouts, real_form(): upper = jnp.concatenate([matrix[0], -matrix[1]], 1)  0.89 us
    convert_element_type x1, local copies, waits for them, and re-layouts, body(): return result.reshape(rhs_count, 2, 12, sites).astype(jnp.bfloat16)  0.83 us
  transfers between devices with their start and end apart: 20, of which 9 were waited for; matrix products, arithmetic and copies ran while one was open for 9% of the time, Pallas kernels for 0%

profile of v2, /device:TPU:0, one launch (start us, length us, event | category | flops | bytes accessed | tf_op | source)
XLA Modules:
  0.0 38.7 jit_solution(10686504280659040500)
XLA Ops:
  0.0 1.0 %copy.49 = bf16[2,24,12,256]{3,1,0,2:T(8,128)(2,1)S(1)} copy(bf16[2,24,12,256]{3,1,2,0:T(8,128)(2,1)} %param.6) | data formatting | bytes 589824 | tf_op args[1]
  2.4 5.1 %collective-permute-start = (f32[16,96]{1,0:T(8,128)S(1)}, f32[16,96]{1,0:T(8,128)S(1)}, u32[]{:S(2)}, u32[]{:S(2)}) collective-permute-start(f32[16,96]{1,0:T(8,128)S(1)} %multiply_multiply_fusion), channel_id=1, source_target_pairs={{6,0},{4,2},{2,4},{0,6},{7,1},{5,3},{3,5},{1,7},{14,8},{12,10},{10... | collective-permute-start | bytes 18440 | tf_op jit(solution)/shard_map/ppermute | solution.py:46
  7.5 1.5 %collective-permute-start.2 = (f32[16,96]{1,0:T(8,128)S(1)}, f32[16,96]{1,0:T(8,128)S(1)}, u32[]{:S(2)}, u32[]{:S(2)}) collective-permute-start(f32[16,96]{1,0:T(8,128)S(1)} %multiply_multiply_fusion), channel_id=1, source_target_pairs={{1,0},{0,1},{3,2},{2,3},{5,4},{4,5},{7,6},{6,7},{9,8},{8,9},{11,10... | collective-permute-start | bytes 18440 | tf_op jit(solution)/shard_map/ppermute | solution.py:46
  8.9 1.5 %collective-permute-start.3 = (f32[16,96]{1,0:T(8,128)S(1)}, f32[16,96]{1,0:T(8,128)S(1)}, u32[]{:S(2)}, u32[]{:S(2)}) collective-permute-start(f32[16,96]{1,0:T(8,128)S(1)} %multiply_multiply_fusion), channel_id=1, source_target_pairs={{16,0},{24,8},{0,16},{8,24},{17,1},{25,9},{1,17},{9,25},{18,2},{26... | collective-permute-start | bytes 18440 | tf_op jit(solution)/shard_map/ppermute | solution.py:46
  10.6 0.8 %copy-done.2 = bf16[2,2,6,6,256]{4,1,3,2,0:T(2,128)(2,1)S(1)} copy-done((bf16[2,2,6,6,256]{4,1,3,2,0:T(2,128)(2,1)S(1)}, bf16[2,2,6,6,256]{4,1,3,2,0:T(2,128)(2,1)}, u32[]{:S(2)}) %copy-start.2) | copy-done | bytes 73752
  12.1 0.7 %copy-done.1 = f32[1,9,2,2304]{3,2,1,0:T(2,128)S(1)} copy-done((f32[1,9,2,2304]{3,2,1,0:T(2,128)S(1)}, f32[1,9,2,2304]{3,2,1,0:T(2,128)}, u32[]{:S(2)}) %copy-start.1) | copy-done | bytes 165912
  15.4 1.0 %collective-permute-start.5 = (f32[16,96]{1,0:T(8,128)S(1)}, f32[16,96]{1,0:T(8,128)S(1)}, u32[]{:S(2)}, u32[]{:S(2)}) collective-permute-start(f32[16,96]{1,0:T(8,128)S(1)} %convolution_add_fusion.7), channel_id=1, source_target_pairs={{6,0},{4,2},{2,4},{0,6},{7,1},{5,3},{3,5},{1,7},{14,8},{12,10},{10... | collective-permute-start | bytes 18440 | tf_op jit(solution)/shard_map/ppermute | solution.py:46
  16.3 1.2 %collective-permute-start.6 = (f32[16,96]{1,0:T(8,128)S(1)}, f32[16,96]{1,0:T(8,128)S(1)}, u32[]{:S(2)}, u32[]{:S(2)}) collective-permute-start(f32[16,96]{1,0:T(8,128)S(1)} %convolution_add_fusion.7), channel_id=1, source_target_pairs={{2,0},{0,2},{6,4},{4,6},{3,1},{1,3},{7,5},{5,7},{10,8},{8,10},{14,... | collective-permute-start | bytes 18440 | tf_op jit(solution)/shard_map/ppermute | solution.py:46
  17.5 0.5 %collective-permute-start.7 = (f32[16,96]{1,0:T(8,128)S(1)}, f32[16,96]{1,0:T(8,128)S(1)}, u32[]{:S(2)}, u32[]{:S(2)}) collective-permute-start(f32[16,96]{1,0:T(8,128)S(1)} %convolution_add_fusion.7), channel_id=1, source_target_pairs={{1,0},{0,1},{3,2},{2,3},{5,4},{4,5},{7,6},{6,7},{9,8},{8,9},{11,10... | collective-permute-start | bytes 18440 | tf_op jit(solution)/shard_map/ppermute | solution.py:46
  18.1 0.5 %collective-permute-start.8 = (f32[16,96]{1,0:T(8,128)S(1)}, f32[16,96]{1,0:T(8,128)S(1)}, u32[]{:S(2)}, u32[]{:S(2)}) collective-permute-start(f32[16,96]{1,0:T(8,128)S(1)} %convolution_add_fusion.7), channel_id=1, source_target_pairs={{16,0},{24,8},{0,16},{8,24},{17,1},{25,9},{1,17},{9,25},{18,2},{26... | collective-permute-start | bytes 18440 | tf_op jit(solution)/shard_map/ppermute | solution.py:46
  18.8 2.1 %collective-permute-done.5 = f32[16,96]{1,0:T(8,128)S(1)} collective-permute-done((f32[16,96]{1,0:T(8,128)S(1)}, f32[16,96]{1,0:T(8,128)S(1)}, u32[]{:S(2)}, u32[]{:S(2)}) %collective-permute-start.5) | collective-permute-done | bytes 6176 | tf_op jit(solution)/shard_map/ppermute | solution.py:46
  21.2 0.5 %collective-permute-done.8 = f32[16,96]{1,0:T(8,128)S(1)} collective-permute-done((f32[16,96]{1,0:T(8,128)S(1)}, f32[16,96]{1,0:T(8,128)S(1)}, u32[]{:S(2)}, u32[]{:S(2)}) %collective-permute-start.8) | collective-permute-done | bytes 6176 | tf_op jit(solution)/shard_map/ppermute | solution.py:46
  22.1 2.9 %collective-permute-start.10 = (f32[16,96]{1,0:T(8,128)S(1)}, f32[16,96]{1,0:T(8,128)S(1)}, u32[]{:S(2)}, u32[]{:S(2)}) collective-permute-start(f32[16,96]{1,0:T(8,128)S(1)} %convolution_add_fusion.5), channel_id=1, source_target_pairs={{6,0},{4,2},{2,4},{0,6},{7,1},{5,3},{3,5},{1,7},{14,8},{12,10},{10... | collective-permute-start | bytes 18440 | tf_op jit(solution)/shard_map/ppermute | solution.py:46
  25.0 1.5 %collective-permute-start.12 = (f32[16,96]{1,0:T(8,128)S(1)}, f32[16,96]{1,0:T(8,128)S(1)}, u32[]{:S(2)}, u32[]{:S(2)}) collective-permute-start(f32[16,96]{1,0:T(8,128)S(1)} %convolution_add_fusion.5), channel_id=1, source_target_pairs={{1,0},{0,1},{3,2},{2,3},{5,4},{4,5},{7,6},{6,7},{9,8},{8,9},{11,10... | collective-permute-start | bytes 18440 | tf_op jit(solution)/shard_map/ppermute | solution.py:46
  26.5 0.5 %collective-permute-start.13 = (f32[16,96]{1,0:T(8,128)S(1)}, f32[16,96]{1,0:T(8,128)S(1)}, u32[]{:S(2)}, u32[]{:S(2)}) collective-permute-start(f32[16,96]{1,0:T(8,128)S(1)} %convolution_add_fusion.5), channel_id=1, source_target_pairs={{16,0},{24,8},{0,16},{8,24},{17,1},{25,9},{1,17},{9,25},{18,2},{26... | collective-permute-start | bytes 18440 | tf_op jit(solution)/shard_map/ppermute | solution.py:46
  27.6 1.0 %collective-permute-done.11 = f32[16,96]{1,0:T(8,128)S(1)} collective-permute-done((f32[16,96]{1,0:T(8,128)S(1)}, f32[16,96]{1,0:T(8,128)S(1)}, u32[]{:S(2)}, u32[]{:S(2)}) %collective-permute-start.11) | collective-permute-done | bytes 6176 | tf_op jit(solution)/shard_map/ppermute | solution.py:46
  28.6 1.5 %collective-permute-done.13 = f32[16,96]{1,0:T(8,128)S(1)} collective-permute-done((f32[16,96]{1,0:T(8,128)S(1)}, f32[16,96]{1,0:T(8,128)S(1)}, u32[]{:S(2)}, u32[]{:S(2)}) %collective-permute-start.13) | collective-permute-done | bytes 6176 | tf_op jit(solution)/shard_map/ppermute | solution.py:46
  30.4 1.1 %collective-permute-start.15 = (f32[16,96]{1,0:T(8,128)S(1)}, f32[16,96]{1,0:T(8,128)S(1)}, u32[]{:S(2)}, u32[]{:S(2)}) collective-permute-start(f32[16,96]{1,0:T(8,128)S(1)} %convolution_add_fusion.3), channel_id=1, source_target_pairs={{6,0},{4,2},{2,4},{0,6},{7,1},{5,3},{3,5},{1,7},{14,8},{12,10},{10... | collective-permute-start | bytes 18440 | tf_op jit(solution)/shard_map/ppermute | solution.py:46
  31.5 1.1 %collective-permute-start.16 = (f32[16,96]{1,0:T(8,128)S(1)}, f32[16,96]{1,0:T(8,128)S(1)}, u32[]{:S(2)}, u32[]{:S(2)}) collective-permute-start(f32[16,96]{1,0:T(8,128)S(1)} %convolution_add_fusion.3), channel_id=1, source_target_pairs={{2,0},{0,2},{6,4},{4,6},{3,1},{1,3},{7,5},{5,7},{10,8},{8,10},{14,... | collective-permute-start | bytes 18440 | tf_op jit(solution)/shard_map/ppermute | solution.py:46
  32.6 0.5 %collective-permute-start.17 = (f32[16,96]{1,0:T(8,128)S(1)}, f32[16,96]{1,0:T(8,128)S(1)}, u32[]{:S(2)}, u32[]{:S(2)}) collective-permute-start(f32[16,96]{1,0:T(8,128)S(1)} %convolution_add_fusion.3), channel_id=1, source_target_pairs={{1,0},{0,1},{3,2},{2,3},{5,4},{4,5},{7,6},{6,7},{9,8},{8,9},{11,10... | collective-permute-start | bytes 18440 | tf_op jit(solution)/shard_map/ppermute | solution.py:46
  33.2 0.5 %collective-permute-start.18 = (f32[16,96]{1,0:T(8,128)S(1)}, f32[16,96]{1,0:T(8,128)S(1)}, u32[]{:S(2)}, u32[]{:S(2)}) collective-permute-start(f32[16,96]{1,0:T(8,128)S(1)} %convolution_add_fusion.3), channel_id=1, source_target_pairs={{16,0},{24,8},{0,16},{8,24},{17,1},{25,9},{1,17},{9,25},{18,2},{26... | collective-permute-start | bytes 18440 | tf_op jit(solution)/shard_map/ppermute | solution.py:46
  33.9 2.1 %collective-permute-done.15 = f32[16,96]{1,0:T(8,128)S(1)} collective-permute-done((f32[16,96]{1,0:T(8,128)S(1)}, f32[16,96]{1,0:T(8,128)S(1)}, u32[]{:S(2)}, u32[]{:S(2)}) %collective-permute-start.15) | collective-permute-done | bytes 6176 | tf_op jit(solution)/shard_map/ppermute | solution.py:46
  36.3 0.5 %collective-permute-done.18 = f32[16,96]{1,0:T(8,128)S(1)} collective-permute-done((f32[16,96]{1,0:T(8,128)S(1)}, f32[16,96]{1,0:T(8,128)S(1)}, u32[]{:S(2)}, u32[]{:S(2)}) %collective-permute-start.18) | collective-permute-done | bytes 6176 | tf_op jit(solution)/shard_map/ppermute | solution.py:46
  37.8 0.8 %copy.54 = bf16[16,2,2,6,256]{4,1,3,2,0:T(2,128)(2,1)} copy(bf16[16,2,2,6,256]{4,0,1,3,2:T(8,128)(2,1)S(1)} %fusion.1) | data formatting | bytes 393216 | tf_op jit(solution)/shard_map/convert_element_type | solution.py:117
  (106 shorter events, 6.9 us)
Async XLA Ops:
  0.0 1.0 %copy-start = (bf16[16,2,12,256]{3,1,2,0:T(2,128)(2,1)S(1)}, bf16[16,2,12,256]{3,1,2,0:T(2,128)(2,1)}, u32[]{:S(2)}) copy-start(bf16[16,2,12,256]{3,1,2,0:T(2,128)(2,1)} %param.5) | copy-start | bytes 589828
  2.4 12.6 %collective-permute-start = (f32[16,96]{1,0:T(8,128)S(1)}, f32[16,96]{1,0:T(8,128)S(1)}, u32[]{:S(2)}, u32[]{:S(2)}) collective-permute-start(f32[16,96]{1,0:T(8,128)S(1)} %multiply_multiply_fusion), channel_id=1, source_target_pairs={{6,0},{4,2},{2,4},{0,6},{7,1},{5,3},{3,5},{1,7},{14,8},{12,10},{10... | collective-permute-start | bytes 18440 | tf_op jit(solution)/shard_map/ppermute | solution.py:46
  7.5 7.6 %collective-permute-start.1 = (f32[16,96]{1,0:T(8,128)S(1)}, f32[16,96]{1,0:T(8,128)S(1)}, u32[]{:S(2)}, u32[]{:S(2)}) collective-permute-start(f32[16,96]{1,0:T(8,128)S(1)} %multiply_multiply_fusion), channel_id=1, source_target_pairs={{2,0},{0,2},{6,4},{4,6},{3,1},{1,3},{7,5},{5,7},{10,8},{8,10},{14,... | collective-permute-start | bytes 18440 | tf_op jit(solution)/shard_map/ppermute | solution.py:46
  7.5 7.6 %collective-permute-start.2 = (f32[16,96]{1,0:T(8,128)S(1)}, f32[16,96]{1,0:T(8,128)S(1)}, u32[]{:S(2)}, u32[]{:S(2)}) collective-permute-start(f32[16,96]{1,0:T(8,128)S(1)} %multiply_multiply_fusion), channel_id=1, source_target_pairs={{1,0},{0,1},{3,2},{2,3},{5,4},{4,5},{7,6},{6,7},{9,8},{8,9},{11,10... | collective-permute-start | bytes 18440 | tf_op jit(solution)/shard_map/ppermute | solution.py:46
  8.9 6.1 %collective-permute-start.3 = (f32[16,96]{1,0:T(8,128)S(1)}, f32[16,96]{1,0:T(8,128)S(1)}, u32[]{:S(2)}, u32[]{:S(2)}) collective-permute-start(f32[16,96]{1,0:T(8,128)S(1)} %multiply_multiply_fusion), channel_id=1, source_target_pairs={{16,0},{24,8},{0,16},{8,24},{17,1},{25,9},{1,17},{9,25},{18,2},{26... | collective-permute-start | bytes 18440 | tf_op jit(solution)/shard_map/ppermute | solution.py:46
  10.5 4.6 %collective-permute-start.4 = (f32[16,96]{1,0:T(8,128)S(1)}, f32[16,96]{1,0:T(8,128)S(1)}, u32[]{:S(2)}, u32[]{:S(2)}) collective-permute-start(f32[16,96]{1,0:T(8,128)S(1)} %multiply_multiply_fusion), channel_id=1, source_target_pairs={{8,0},{0,8},{24,16},{16,24},{9,1},{1,9},{25,17},{17,25},{10,2},{2,... | collective-permute-start | bytes 18440 | tf_op jit(solution)/shard_map/ppermute | solution.py:46
  10.5 0.9 %copy-start.2 = (bf16[2,2,6,6,256]{4,1,3,2,0:T(2,128)(2,1)S(1)}, bf16[2,2,6,6,256]{4,1,3,2,0:T(2,128)(2,1)}, u32[]{:S(2)}) copy-start(bf16[2,2,6,6,256]{4,1,3,2,0:T(2,128)(2,1)} %param.7) | copy-start | bytes 221188
  11.9 0.9 %copy-start.1 = (f32[1,9,2,2304]{3,2,1,0:T(2,128)S(1)}, f32[1,9,2,2304]{3,2,1,0:T(2,128)}, u32[]{:S(2)}) copy-start(f32[1,9,2,2304]{3,2,1,0:T(2,128)} %param.8) | copy-start | bytes 497668
  15.4 5.5 %collective-permute-start.5 = (f32[16,96]{1,0:T(8,128)S(1)}, f32[16,96]{1,0:T(8,128)S(1)}, u32[]{:S(2)}, u32[]{:S(2)}) collective-permute-start(f32[16,96]{1,0:T(8,128)S(1)} %convolution_add_fusion.7), channel_id=1, source_target_pairs={{6,0},{4,2},{2,4},{0,6},{7,1},{5,3},{3,5},{1,7},{14,8},{12,10},{10... | collective-permute-start | bytes 18440 | tf_op jit(solution)/shard_map/ppermute | solution.py:46
  16.3 4.6 %collective-permute-start.6 = (f32[16,96]{1,0:T(8,128)S(1)}, f32[16,96]{1,0:T(8,128)S(1)}, u32[]{:S(2)}, u32[]{:S(2)}) collective-permute-start(f32[16,96]{1,0:T(8,128)S(1)} %convolution_add_fusion.7), channel_id=1, source_target_pairs={{2,0},{0,2},{6,4},{4,6},{3,1},{1,3},{7,5},{5,7},{10,8},{8,10},{14,... | collective-permute-start | bytes 18440 | tf_op jit(solution)/shard_map/ppermute | solution.py:46
  17.5 3.7 %collective-permute-start.7 = (f32[16,96]{1,0:T(8,128)S(1)}, f32[16,96]{1,0:T(8,128)S(1)}, u32[]{:S(2)}, u32[]{:S(2)}) collective-permute-start(f32[16,96]{1,0:T(8,128)S(1)} %convolution_add_fusion.7), channel_id=1, source_target_pairs={{1,0},{0,1},{3,2},{2,3},{5,4},{4,5},{7,6},{6,7},{9,8},{8,9},{11,10... | collective-permute-start | bytes 18440 | tf_op jit(solution)/shard_map/ppermute | solution.py:46
  18.1 3.7 %collective-permute-start.8 = (f32[16,96]{1,0:T(8,128)S(1)}, f32[16,96]{1,0:T(8,128)S(1)}, u32[]{:S(2)}, u32[]{:S(2)}) collective-permute-start(f32[16,96]{1,0:T(8,128)S(1)} %convolution_add_fusion.7), channel_id=1, source_target_pairs={{16,0},{24,8},{0,16},{8,24},{17,1},{25,9},{1,17},{9,25},{18,2},{26... | collective-permute-start | bytes 18440 | tf_op jit(solution)/shard_map/ppermute | solution.py:46
  18.6 3.1 %collective-permute-start.9 = (f32[16,96]{1,0:T(8,128)S(1)}, f32[16,96]{1,0:T(8,128)S(1)}, u32[]{:S(2)}, u32[]{:S(2)}) collective-permute-start(f32[16,96]{1,0:T(8,128)S(1)} %convolution_add_fusion.7), channel_id=1, source_target_pairs={{8,0},{0,8},{24,16},{16,24},{9,1},{1,9},{25,17},{17,25},{10,2},{2,... | collective-permute-start | bytes 18440 | tf_op jit(solution)/shard_map/ppermute | solution.py:46
  22.1 5.5 %collective-permute-start.10 = (f32[16,96]{1,0:T(8,128)S(1)}, f32[16,96]{1,0:T(8,128)S(1)}, u32[]{:S(2)}, u32[]{:S(2)}) collective-permute-start(f32[16,96]{1,0:T(8,128)S(1)} %convolution_add_fusion.5), channel_id=1, source_target_pairs={{6,0},{4,2},{2,4},{0,6},{7,1},{5,3},{3,5},{1,7},{14,8},{12,10},{10... | collective-permute-start | bytes 18440 | tf_op jit(solution)/shard_map/ppermute | solution.py:46
  25.0 3.7 %collective-permute-start.11 = (f32[16,96]{1,0:T(8,128)S(1)}, f32[16,96]{1,0:T(8,128)S(1)}, u32[]{:S(2)}, u32[]{:S(2)}) collective-permute-start(f32[16,96]{1,0:T(8,128)S(1)} %convolution_add_fusion.5), channel_id=1, source_target_pairs={{2,0},{0,2},{6,4},{4,6},{3,1},{1,3},{7,5},{5,7},{10,8},{8,10},{14,... | collective-permute-start | bytes 18440 | tf_op jit(solution)/shard_map/ppermute | solution.py:46
  25.0 3.7 %collective-permute-start.12 = (f32[16,96]{1,0:T(8,128)S(1)}, f32[16,96]{1,0:T(8,128)S(1)}, u32[]{:S(2)}, u32[]{:S(2)}) collective-permute-start(f32[16,96]{1,0:T(8,128)S(1)} %convolution_add_fusion.5), channel_id=1, source_target_pairs={{1,0},{0,1},{3,2},{2,3},{5,4},{4,5},{7,6},{6,7},{9,8},{8,9},{11,10... | collective-permute-start | bytes 18440 | tf_op jit(solution)/shard_map/ppermute | solution.py:46
  26.5 3.7 %collective-permute-start.13 = (f32[16,96]{1,0:T(8,128)S(1)}, f32[16,96]{1,0:T(8,128)S(1)}, u32[]{:S(2)}, u32[]{:S(2)}) collective-permute-start(f32[16,96]{1,0:T(8,128)S(1)} %convolution_add_fusion.5), channel_id=1, source_target_pairs={{16,0},{24,8},{0,16},{8,24},{17,1},{25,9},{1,17},{9,25},{18,2},{26... | collective-permute-start | bytes 18440 | tf_op jit(solution)/shard_map/ppermute | solution.py:46
  27.0 3.1 %collective-permute-start.14 = (f32[16,96]{1,0:T(8,128)S(1)}, f32[16,96]{1,0:T(8,128)S(1)}, u32[]{:S(2)}, u32[]{:S(2)}) collective-permute-start(f32[16,96]{1,0:T(8,128)S(1)} %convolution_add_fusion.5), channel_id=1, source_target_pairs={{8,0},{0,8},{24,16},{16,24},{9,1},{1,9},{25,17},{17,25},{10,2},{2,... | collective-permute-start | bytes 18440 | tf_op jit(solution)/shard_map/ppermute | solution.py:46
  30.4 5.5 %collective-permute-start.15 = (f32[16,96]{1,0:T(8,128)S(1)}, f32[16,96]{1,0:T(8,128)S(1)}, u32[]{:S(2)}, u32[]{:S(2)}) collective-permute-start(f32[16,96]{1,0:T(8,128)S(1)} %convolution_add_fusion.3), channel_id=1, source_target_pairs={{6,0},{4,2},{2,4},{0,6},{7,1},{5,3},{3,5},{1,7},{14,8},{12,10},{10... | collective-permute-start | bytes 18440 | tf_op jit(solution)/shard_map/ppermute | solution.py:46
  31.5 4.5 %collective-permute-start.16 = (f32[16,96]{1,0:T(8,128)S(1)}, f32[16,96]{1,0:T(8,128)S(1)}, u32[]{:S(2)}, u32[]{:S(2)}) collective-permute-start(f32[16,96]{1,0:T(8,128)S(1)} %convolution_add_fusion.3), channel_id=1, source_target_pairs={{2,0},{0,2},{6,4},{4,6},{3,1},{1,3},{7,5},{5,7},{10,8},{8,10},{14,... | collective-permute-start | bytes 18440 | tf_op jit(solution)/shard_map/ppermute | solution.py:46
  32.6 3.7 %collective-permute-start.17 = (f32[16,96]{1,0:T(8,128)S(1)}, f32[16,96]{1,0:T(8,128)S(1)}, u32[]{:S(2)}, u32[]{:S(2)}) collective-permute-start(f32[16,96]{1,0:T(8,128)S(1)} %convolution_add_fusion.3), channel_id=1, source_target_pairs={{1,0},{0,1},{3,2},{2,3},{5,4},{4,5},{7,6},{6,7},{9,8},{8,9},{11,10... | collective-permute-start | bytes 18440 | tf_op jit(solution)/shard_map/ppermute | solution.py:46
  33.2 3.7 %collective-permute-start.18 = (f32[16,96]{1,0:T(8,128)S(1)}, f32[16,96]{1,0:T(8,128)S(1)}, u32[]{:S(2)}, u32[]{:S(2)}) collective-permute-start(f32[16,96]{1,0:T(8,128)S(1)} %convolution_add_fusion.3), channel_id=1, source_target_pairs={{16,0},{24,8},{0,16},{8,24},{17,1},{25,9},{1,17},{9,25},{18,2},{26... | collective-permute-start | bytes 18440 | tf_op jit(solution)/shard_map/ppermute | solution.py:46
  33.7 3.1 %collective-permute-start.19 = (f32[16,96]{1,0:T(8,128)S(1)}, f32[16,96]{1,0:T(8,128)S(1)}, u32[]{:S(2)}, u32[]{:S(2)}) collective-permute-start(f32[16,96]{1,0:T(8,128)S(1)} %convolution_add_fusion.3), channel_id=1, source_target_pairs={{8,0},{0,8},{24,16},{16,24},{9,1},{1,9},{25,17},{17,25},{10,2},{2,... | collective-permute-start | bytes 18440 | tf_op jit(solution)/shard_map/ppermute | solution.py:46

commit v3 on v2

--- a/solution.py
+++ b/solution.py
@@ -44,6 +44,21 @@
 def fetch(block, link):
     axis, sources = link
     return lax.ppermute(block, axis, [(source, i) for i, source in enumerate(sources)])
+
+
+def fetch_all(block, order):
+    axes = ("gx", "gz", "ta")
+    everything = lax.all_gather(block, axes)
+    moved = []
+    for axis, sources in order:
+        position = 0
+        for name in axes:
+            place = lax.axis_index(name)
+            if name == axis:
+                place = jnp.asarray(sources, jnp.int32)[place]
+            position = position * lax.axis_size(name) + place
+        moved.append(lax.dynamic_index_in_dim(everything, position, 0, keepdims=False))
+    return moved
 
 
 def body(residual, null_vectors, clover_inverse, coarse_op, vector_count):
@@ -93,7 +108,7 @@
 
     coarse = half
     for sweep_id in range(ITERS - 1):
-        moved = [fetch(coarse, link) for link in order]
+        moved = fetch_all(coarse, order)
         kept = half + apply(coarse, own)
         coarse = kept + apply(jnp.concatenate(moved, 1), around)
 

time: 38.9 us -> 288 us (7.40)
  blocking collectives: 0 us -> 268 us
  starting transfers between devices: 19.4 us -> 0 us
  waiting for transfers between devices: 8.74 us -> 0 us
  local copies, waits for them, and re-layouts: 5.78 us -> 11.7 us
  between operations: 1.18 us -> 4.51 us
    all_gather x0 -> x4, blocking collectives: none -> 268 us  [fetch_all(): everything = lax.all_gather(block, axes)]
    ppermute x20 -> x0, starting transfers between devices: 19.4 us -> none  [fetch(): lax.ppermute(block, axis, [(source, i) for i, source in enumerate(sources)])]
    ppermute x20 -> x0, waiting for transfers between devices: 8.74 us -> none  [fetch(): lax.ppermute(block, axis, [(source, i) for i, source in enumerate(sources)])]
  transfers between devices with their start and end apart: 20 -> 0, of which waited for: 9 -> 0; matrix products, arithmetic and copies ran while one was open for 9% -> 0% of each run, Pallas kernels for 0% -> 0%
where the time goes in v3:
time: 288 us
  blocking collectives  268 us (93%)
  local copies, waits for them, and re-layouts  11.7 us (4%)
  between operations  4.51 us (2%)
    all_gather x4, blocking collectives, fetch_all(): everything = lax.all_gather(block, axes)  268 us

profile of v3, /device:TPU:0, one launch (start us, length us, event | category | flops | bytes accessed | tf_op | source)
XLA Modules:
  0.0 287.5 jit_solution(11133158829758660622)
XLA Ops:
  0.0 1.0 copy.77
  1.1 0.8 copy-done.3
  2.6 0.7 copy-done.2
  5.0 0.5 copy-done.4
  5.5 0.7 fusion.22
  7.6 0.6 copy-done.7
  8.2 0.6 dynamic_slice.121
  9.5 0.6 copy-done.6
  10.1 0.6 dynamic_slice.125
  11.4 0.6 copy-done.5
  12.0 0.6 dynamic_slice.127
  13.3 0.9 copy-done
  15.5 71.2 %all_gather.22 = f32[32,16,96]{2,1,0:T(8,128)S(1)} all-gather(f32[1,16,96]{2,1,0:T(8,128)S(1)} %multiply_multiply_fusion), channel_id=1, replica_groups=mesh['gx'=4,'gz'=4,'ta'=2] {'gx','gz','ta'}, dimensions={0}, use_global_device_ids=true | all-gather | bytes 202752 | tf_op jit(solution)/shard_map/all_gather | solution.py:51
  87.4 0.2 fusion
  87.6 64.7 %all-gather = f32[512,96]{1,0:T(8,128)S(1)} all-gather(f32[16,96]{1,0:T(8,128)S(1)} %fusion), channel_id=2, replica_groups=mesh['gx'=4,'gz'=4,'ta'=2] {'gx','gz','ta'}, dimensions={0}, use_global_device_ids=true | all-gather | bytes 202752 | tf_op jit(solution)/shard_map/all_gather | solution.py:51
  152.5 0.2 convolution_add_fusion.6
  152.7 0.3 convolution_add_fusion.5
  153.0 67.0 %all-gather.1 = f32[512,96]{1,0:T(8,128)S(1)} all-gather(f32[16,96]{1,0:T(8,128)S(1)} %convolution_add_fusion.5), channel_id=3, replica_groups=mesh['gx'=4,'gz'=4,'ta'=2] {'gx','gz','ta'}, dimensions={0}, use_global_device_ids=true | all-gather | bytes 202752 | tf_op jit(solution)/shard_map/all_gather | solution.py:51
  220.1 0.2 convolution_add_fusion.4
  220.4 0.3 convolution_add_fusion.3
  220.6 64.7 %all-gather.2 = f32[512,96]{1,0:T(8,128)S(1)} all-gather(f32[16,96]{1,0:T(8,128)S(1)} %convolution_add_fusion.3), channel_id=4, replica_groups=mesh['gx'=4,'gz'=4,'ta'=2] {'gx','gz','ta'}, dimensions={0}, use_global_device_ids=true | all-gather | bytes 202752 | tf_op jit(solution)/shard_map/all_gather | solution.py:51
  285.5 0.2 convolution_add_fusion.2
  285.7 0.3 fusion.1
  286.7 0.8 copy.96
  (88 shorter events, 4.5 us)
Async XLA Ops:
  1.0 0.9 copy-start.3
  2.4 0.9 copy-start.2
  4.8 0.7 copy-start.4
  4.9 8.4 %copy-start.1 = (bf16[2,24,12,256]{3,1,2,0:T(8,128)(2,1)S(1)}, bf16[2,24,12,256]{3,1,2,0:T(8,128)(2,1)}, u32[]{:S(2)}) copy-start(bf16[2,24,12,256]{3,1,2,0:T(8,128)(2,1)} %param.26) | copy-start | bytes 884740
  7.5 0.7 copy-start.7
  9.4 0.7 copy-start.6
  11.3 0.7 copy-start.5
  13.3 0.9 copy-start

commit v4 on v3

--- a/solution.py
+++ b/solution.py
@@ -48,7 +48,10 @@
 
 def fetch_all(block, order):
     axes = ("gx", "gz", "ta")
-    everything = lax.all_gather(block, axes)
+    count = 1
+    for name in axes:
+        count *= lax.axis_size(name)
+    everything = lax.all_to_all(jnp.broadcast_to(block, (count,) + block.shape), axes, 0, 0)
     moved = []
     for axis, sources in order:
         position = 0

time: 288 us -> 70.6 us (0.25)
  blocking collectives: 268 us -> 0 us
  waiting for transfers between devices: 0 us -> 30.8 us
  starting transfers between devices: 0 us -> 18.3 us
    all_gather x4 -> x0, blocking collectives: 268 us -> none  [fetch_all(): everything = lax.all_gather(block, axes)]
    all_to_all x0 -> x4, waiting for transfers between devices: none -> 30.8 us  [fetch_all(): lax.all_to_all(jnp.broadcast_to(block, (count,) + block.shape), axes, 0, 0)]
    all_to_all x0 -> x4, starting transfers between devices: none -> 18.3 us  [fetch_all(): lax.all_to_all(jnp.broadcast_to(block, (count,) + block.shape), axes, 0, 0)]
    broadcast_in_dim x0 -> x4, local copies, waits for them, and re-layouts: none -> 2.99 us  [fetch_all(): jnp.broadcast_to(block, (count,) + block.shape)]
  transfers between devices with their start and end apart: 0 -> 4, of which waited for: 0 -> 3; matrix products, arithmetic and copies ran while one was open for 0% -> 8% of each run, Pallas kernels for 0% -> 0%
where the time goes in v4:
time: 70.6 us; the launch traced here: 70.1 us
  waiting for transfers between devices  30.8 us (44%)
  starting transfers between devices  18.3 us (26%)
  local copies, waits for them, and re-layouts  13 us (18%)
  between operations  4.52 us (6%)
  matrix products  2.28 us (3%)
  other arithmetic  1.23 us (2%)
    all_to_all x4, waiting for transfers between devices, fetch_all(): lax.all_to_all(jnp.broadcast_to(block, (count,) + block.shape), axes, 0, 0)  30.8 us
    all_to_all x4, starting transfers between devices, fetch_all(): lax.all_to_all(jnp.broadcast_to(block, (count,) + block.shape), axes, 0, 0)  18.3 us
    unnamed x16, local copies, waits for them, and re-layouts  4.39 us
    broadcast_in_dim x4, local copies, waits for them, and re-layouts, fetch_all(): jnp.broadcast_to(block, (count,) + block.shape)  2.99 us
    dynamic_slice x4, local copies, waits for them, and re-layouts, fetch_all(): place = jnp.asarray(sources, jnp.int32)[place]  2.39 us
    dot_general x8, matrix products, apply(): lax.dot_general(vector, matrix, (((1,), (1,)), ((), ())), precision=exact)  1.89 us
  transfers between devices with their start and end apart: 4, of which 3 were waited for; matrix products, arithmetic and copies ran while one was open for 8% of the time, Pallas kernels for 0%

profile of v4, /device:TPU:0, one launch (start us, length us, event | category | flops | bytes accessed | tf_op | source)
XLA Modules:
  0.0 70.1 jit_solution(8438904087178898366)
XLA Ops:
  0.0 1.0 %copy.69 = bf16[2,24,12,256]{3,1,0,2:T(8,128)(2,1)S(1)} copy(bf16[2,24,12,256]{3,1,2,0:T(8,128)(2,1)} %param.26) | data formatting | bytes 589824 | tf_op args[1]
  2.4 0.7 %broadcast_in_dim.14 = f32[32,16,96]{2,1,0:T(8,128)} broadcast(f32[16,96]{1,0:T(8,128)S(1)} %multiply_multiply_fusion), dimensions={1,2} | broadcast | bytes 202752 | tf_op jit(solution)/shard_map/broadcast_in_dim | solution.py:54
  3.1 7.3 %all-to-all-start = ((f32[32,16,96]{2,1,0:T(8,128)}), f32[32,16,96]{2,1,0:T(8,128)S(1)}, u32[]{:S(2)}, u32[]{:S(2)}) async-start(f32[32,16,96]{2,1,0:T(8,128)} %broadcast_in_dim.14), calls=%async_computation | async-start | bytes 524288 | tf_op jit(solution)/shard_map/all_to_all | solution.py:54
  11.4 0.7 %copy-done.2 = bf16[2,2,6,6,256]{4,1,3,2,0:T(2,128)(2,1)S(1)} copy-done((bf16[2,2,6,6,256]{4,1,3,2,0:T(2,128)(2,1)S(1)}, bf16[2,2,6,6,256]{4,1,3,2,0:T(2,128)(2,1)}, u32[]{:S(2)}) %copy-start.2) | copy-done | bytes 73752
  12.6 0.6 copy-done.3
  13.3 0.6 fusion.17
  14.6 0.6 copy-done.6
  15.3 0.6 dynamic_slice.127
  16.5 0.6 copy-done.5
  17.2 0.6 dynamic_slice.125
  19.1 0.6 copy-done.4
  19.7 0.6 dynamic_slice.121
  22.1 0.3 fusion
  22.4 0.8 %broadcast_in_dim.15 = f32[32,16,96]{2,1,0:T(8,128)} broadcast(f32[16,96]{1,0:T(8,128)S(1)} %fusion), dimensions={1,2} | broadcast | bytes 202752 | tf_op jit(solution)/shard_map/broadcast_in_dim | solution.py:54
  23.1 5.8 %all-to-all-start.1 = ((f32[32,16,96]{2,1,0:T(8,128)}), f32[32,16,96]{2,1,0:T(8,128)S(1)}, u32[]{:S(2)}, u32[]{:S(2)}) async-start(f32[32,16,96]{2,1,0:T(8,128)} %broadcast_in_dim.15), calls=%async_computation.1 | async-start | bytes 524288 | tf_op jit(solution)/shard_map/all_to_all | solution.py:54
  29.0 0.2 convolution_add_fusion.6
  29.2 10.4 %all-to-all-done.1 = f32[32,16,96]{2,1,0:T(8,128)S(1)} async-done(((f32[32,16,96]{2,1,0:T(8,128)}), f32[32,16,96]{2,1,0:T(8,128)S(1)}, u32[]{:S(2)}, u32[]{:S(2)}) %all-to-all-start.1) | async-done | bytes 196640 | tf_op jit(solution)/shard_map/all_to_all | solution.py:54
  39.9 0.8 %broadcast_in_dim.16 = f32[32,16,96]{2,1,0:T(8,128)} broadcast(f32[16,96]{1,0:T(8,128)S(1)} %convolution_add_fusion.5), dimensions={1,2} | broadcast | bytes 202752 | tf_op jit(solution)/shard_map/broadcast_in_dim | solution.py:54
  40.7 2.6 %all-to-all-start.2 = ((f32[32,16,96]{2,1,0:T(8,128)}), f32[32,16,96]{2,1,0:T(8,128)S(1)}, u32[]{:S(2)}, u32[]{:S(2)}) async-start(f32[32,16,96]{2,1,0:T(8,128)} %broadcast_in_dim.16), calls=%async_computation.2 | async-start | bytes 524288 | tf_op jit(solution)/shard_map/all_to_all | solution.py:54
  43.7 10.2 %all-to-all-done.2 = f32[32,16,96]{2,1,0:T(8,128)S(1)} async-done(((f32[32,16,96]{2,1,0:T(8,128)}), f32[32,16,96]{2,1,0:T(8,128)S(1)}, u32[]{:S(2)}, u32[]{:S(2)}) %all-to-all-start.2) | async-done | bytes 196640 | tf_op jit(solution)/shard_map/all_to_all | solution.py:54
  54.3 0.8 %broadcast_in_dim.17 = f32[32,16,96]{2,1,0:T(8,128)} broadcast(f32[16,96]{1,0:T(8,128)S(1)} %convolution_add_fusion.3), dimensions={1,2} | broadcast | bytes 202752 | tf_op jit(solution)/shard_map/broadcast_in_dim | solution.py:54
  55.0 2.6 %all-to-all-start.3 = ((f32[32,16,96]{2,1,0:T(8,128)}), f32[32,16,96]{2,1,0:T(8,128)S(1)}, u32[]{:S(2)}, u32[]{:S(2)}) async-start(f32[32,16,96]{2,1,0:T(8,128)} %broadcast_in_dim.17), calls=%async_computation.3 | async-start | bytes 524288 | tf_op jit(solution)/shard_map/all_to_all | solution.py:54
  58.0 10.2 %all-to-all-done.3 = f32[32,16,96]{2,1,0:T(8,128)S(1)} async-done(((f32[32,16,96]{2,1,0:T(8,128)}), f32[32,16,96]{2,1,0:T(8,128)S(1)}, u32[]{:S(2)}, u32[]{:S(2)}) %all-to-all-start.3) | async-done | bytes 196640 | tf_op jit(solution)/shard_map/all_to_all | solution.py:54
  69.3 0.8 %copy.74 = bf16[16,2,2,6,256]{4,1,3,2,0:T(2,128)(2,1)} copy(bf16[16,2,2,6,256]{4,0,1,3,2:T(8,128)(2,1)S(1)} %fusion.2) | data formatting | bytes 393216 | tf_op jit(solution)/shard_map/convert_element_type | solution.py:135
  (94 shorter events, 5.4 us)
Async XLA Ops:
  0.0 1.0 %copy-start = (bf16[16,2,12,256]{3,1,2,0:T(2,128)(2,1)S(1)}, bf16[16,2,12,256]{3,1,2,0:T(2,128)(2,1)}, u32[]{:S(2)}) copy-start(bf16[16,2,12,256]{3,1,2,0:T(2,128)(2,1)} %param.25) | copy-start | bytes 589828
  3.1 7.3 %copy-start.1 = (f32[1,9,2,2304]{3,2,1,0:T(2,128)S(1)}, f32[1,9,2,2304]{3,2,1,0:T(2,128)}, u32[]{:S(2)}) copy-start(f32[1,9,2,2304]{3,2,1,0:T(2,128)} %param.28) | copy-start | bytes 497668
  3.1 18.6 %all-to-all-start = ((f32[32,16,96]{2,1,0:T(8,128)}), f32[32,16,96]{2,1,0:T(8,128)S(1)}, u32[]{:S(2)}, u32[]{:S(2)}) async-start(f32[32,16,96]{2,1,0:T(8,128)} %broadcast_in_dim.14), calls=%async_computation | async-start | bytes 524288 | tf_op jit(solution)/shard_map/all_to_all | solution.py:54
  11.3 0.9 %copy-start.2 = (bf16[2,2,6,6,256]{4,1,3,2,0:T(2,128)(2,1)S(1)}, bf16[2,2,6,6,256]{4,1,3,2,0:T(2,128)(2,1)}, u32[]{:S(2)}) copy-start(bf16[2,2,6,6,256]{4,1,3,2,0:T(2,128)(2,1)} %param.27) | copy-start | bytes 221188
  12.6 0.7 copy-start.3
  14.6 0.7 copy-start.6
  16.5 0.7 copy-start.5
  19.0 0.7 copy-start.4
  23.1 16.5 %all-to-all-start.1 = ((f32[32,16,96]{2,1,0:T(8,128)}), f32[32,16,96]{2,1,0:T(8,128)S(1)}, u32[]{:S(2)}, u32[]{:S(2)}) async-start(f32[32,16,96]{2,1,0:T(8,128)} %broadcast_in_dim.15), calls=%async_computation.1 | async-start | bytes 524288 | tf_op jit(solution)/shard_map/all_to_all | solution.py:54
  40.7 13.2 %all-to-all-start.2 = ((f32[32,16,96]{2,1,0:T(8,128)}), f32[32,16,96]{2,1,0:T(8,128)S(1)}, u32[]{:S(2)}, u32[]{:S(2)}) async-start(f32[32,16,96]{2,1,0:T(8,128)} %broadcast_in_dim.16), calls=%async_computation.2 | async-start | bytes 524288 | tf_op jit(solution)/shard_map/all_to_all | solution.py:54
  55.0 13.2 %all-to-all-start.3 = ((f32[32,16,96]{2,1,0:T(8,128)}), f32[32,16,96]{2,1,0:T(8,128)S(1)}, u32[]{:S(2)}, u32[]{:S(2)}) async-start(f32[32,16,96]{2,1,0:T(8,128)} %broadcast_in_dim.17), calls=%async_computation.3 | async-start | bytes 524288 | tf_op jit(solution)/shard_map/all_to_all | solution.py:54

commit v5 on v2

--- a/solution.py
+++ b/solution.py
@@ -1,6 +1,8 @@
 import jax
 import jax.numpy as jnp
 from jax import lax
+from jax.experimental import pallas as pl
+from jax.experimental.pallas import tpu as pltpu
 from jax.sharding import PartitionSpec as P
 
 ITERS = 5
@@ -46,22 +48,117 @@
     return lax.ppermute(block, axis, [(source, i) for i, source in enumerate(sources)])
 
 
+def restrict_kernel(count_hbm, rows_hbm, vectors_hbm, out_ref, count_ref, rows_ref, vectors_ref, scratch, sems):
+    rhs, parts, _, sites = rows_ref.shape
+    vecs = vectors_ref.shape[2]
+    half = parts // 2
+    copies = []
+    for chi in range(2):
+        span = pl.ds(half * chi, half)
+        copies.append(
+            [
+                pltpu.make_async_copy(rows_hbm.at[:, span], rows_ref.at[:, span], sems.at[2 * chi]),
+                pltpu.make_async_copy(vectors_hbm.at[:, span], vectors_ref.at[:, span], sems.at[2 * chi + 1]),
+            ]
+        )
+    count_copy = pltpu.make_async_copy(count_hbm, count_ref, sems.at[4])
+    for copy in copies[0] + [count_copy] + copies[1]:
+        copy.start()
+    for chi in range(2):
+        for copy in copies[chi]:
+            copy.wait()
+        total = jnp.zeros((2 * rhs, 2 * vecs), jnp.float32)
+        for c in range(half * chi, half * chi + half):
+            rows = rows_ref[:, c].reshape(2 * rhs, sites)
+            vectors = jnp.concatenate([vectors_ref[0, c], vectors_ref[1, c]], 0)
+            total += lax.dot_general(
+                rows, vectors, (((1,), (1,)), ((), ())), preferred_element_type=jnp.float32
+            )
+        scratch[chi, :, : 2 * vecs] = total
+    count_copy.wait()
+    real, imag = [], []
+    for chi in range(2):
+        even = scratch[chi, pl.ds(0, rhs, stride=2), :]
+        odd = scratch[chi, pl.ds(1, rhs, stride=2), :]
+        real.append(even[:, :vecs] + odd[:, vecs : 2 * vecs])
+        imag.append(odd[:, :vecs] - even[:, vecs : 2 * vecs])
+    lane = lax.broadcasted_iota(jnp.int32, (rhs, vecs), 1)
+    keep = jnp.where(lane < count_ref[0], omega_step, 0.0)
+    out_ref[...] = jnp.concatenate([part * keep for part in real + imag], 1)
+
+
+def local_kernel(rows_ref, clover_ref, out_ref):
+    rhs, parts, _, sites = rows_ref.shape
+    half = parts // 2
+    row = lax.broadcasted_iota(jnp.int32, (2 * rhs, 2 * rhs), 0)
+    col = lax.broadcasted_iota(jnp.int32, (2 * rhs, 2 * rhs), 1)
+    turn = jnp.where((row % 2 == 0) & (col == row + 1), -1.0, 0.0)
+    turn = jnp.where((row % 2 == 1) & (col == row - 1), 1.0, turn).astype(jnp.bfloat16)
+    for chi in range(2):
+        for start in range(0, sites, 128):
+            lanes = slice(start, start + 128)
+            plain, turned = [], []
+            for b in range(half):
+                rows = rows_ref[:, half * chi + b, :, lanes].reshape(2 * rhs, 128)
+                plain.append(rows.astype(jnp.float32))
+                turned.append(jnp.dot(turn, rows, preferred_element_type=jnp.float32))
+            for a in range(half):
+                total = jnp.zeros((2 * rhs, 128), jnp.float32)
+                for b in range(half):
+                    real = clover_ref[0, a, b, :, lanes].astype(jnp.float32)[chi : chi + 1]
+                    imag = clover_ref[1, a, b, :, lanes].astype(jnp.float32)[chi : chi + 1]
+                    total += real * plain[b] + imag * turned[b]
+                out_ref[half * chi + a, :, lanes] = total
+
+
+def extend_kernel(count_ref, coarse_ref, vectors_ref, local_ref, out_ref, scratch):
+    rhs, parts, _, sites = out_ref.shape
+    vecs = vectors_ref.shape[2]
+    half = parts // 2
+    lane = lax.broadcasted_iota(jnp.int32, (rhs, vecs), 1)
+    keep = lane < count_ref[...]
+    pieces = [jnp.where(keep, coarse_ref[:, p * vecs : p * vecs + vecs], 0.0) for p in range(4)]
+    for chi in range(2):
+        real, imag = pieces[chi], pieces[2 + chi]
+        scratch[chi, pl.ds(0, rhs, stride=2), : 2 * vecs] = jnp.concatenate([real, -imag], 1)
+        scratch[chi, pl.ds(1, rhs, stride=2), : 2 * vecs] = jnp.concatenate([imag, real], 1)
+        weights = scratch[chi, :, : 2 * vecs].astype(jnp.bfloat16)
+        for c in range(half * chi, half * chi + half):
+            vectors = jnp.concatenate([vectors_ref[0, c], vectors_ref[1, c]], 0)
+            lift = jnp.dot(weights, vectors, preferred_element_type=jnp.float32)
+            total = (local_ref[c] + lift).astype(jnp.bfloat16)
+            out_ref[:, c] = total.reshape(rhs, 2, sites)
+
+
+in_hbm = pl.BlockSpec(memory_space=pltpu.HBM)
+in_vmem = pl.BlockSpec(memory_space=pltpu.VMEM)
+
+
 def body(residual, null_vectors, clover_inverse, coarse_op, vector_count):
     rhs_count = residual.shape[0]
     vec_total = null_vectors.shape[1]
     coarse_dim = 2 * vec_total
+    parts = residual.shape[2]
     sites = residual.shape[3]
-    in_use = (lax.iota(jnp.int32, vec_total)[None, :] < vector_count[:, None]).astype(jnp.float32)[0]
-    used = jnp.tile(in_use, 4)
-
-    fine_rows = residual.transpose(2, 1, 0, 3).reshape(2, 6, 2 * rhs_count, sites)
-    vectors = null_vectors.transpose(2, 0, 1, 3).reshape(2, 6, 2 * vec_total, sites)
-    product = jnp.einsum("xcrs,xcks->xrk", fine_rows, vectors, preferred_element_type=jnp.float32)
-    product = product.reshape(2, 2, rhs_count, 2, vec_total)
-    real_part = product[:, 0, :, 0] + product[:, 1, :, 1]
-    imag_part = product[:, 1, :, 0] - product[:, 0, :, 1]
-    restricted = jnp.stack([real_part, imag_part]).transpose(2, 0, 1, 3)
-    half = omega_step * (restricted.reshape(rhs_count, 2 * coarse_dim) * used)
+    count = vector_count.reshape(1, 1)
+    rows = residual.transpose(0, 2, 1, 3)
+    vectors = null_vectors.transpose(0, 2, 1, 3)
+    clover = clover_inverse.transpose(0, 2, 3, 1, 4)
+
+    half = pl.pallas_call(
+        restrict_kernel,
+        out_shape=jax.ShapeDtypeStruct((rhs_count, 2 * coarse_dim), jnp.float32),
+        in_specs=[in_hbm] * 3,
+        out_specs=in_vmem,
+        scratch_shapes=[
+            pltpu.SMEM((1,), jnp.int32),
+            pltpu.VMEM(rows.shape, rows.dtype),
+            pltpu.VMEM(vectors.shape, vectors.dtype),
+            pltpu.VMEM((2, 2 * rhs_count, 128), jnp.float32),
+            pltpu.SemaphoreType.DMA((5,)),
+        ],
+        cost_estimate=pl.CostEstimate(flops=10**7, bytes_accessed=5 * 10**5, transcendentals=0),
+    )(vector_count, rows, vectors)
 
     operator = coarse_op.reshape(9, 2, coarse_dim, coarse_dim)
     grouped = {}
@@ -95,26 +192,26 @@
     for sweep_id in range(ITERS - 1):
         moved = [fetch(coarse, link) for link in order]
         kept = half + apply(coarse, own)
+        if sweep_id == 1:
+            held_rows, held_clover, _ = lax.optimization_barrier((rows, clover, coarse))
+            local = pl.pallas_call(
+                local_kernel,
+                out_shape=jax.ShapeDtypeStruct((parts, 2 * rhs_count, sites), jnp.float32),
+                in_specs=[in_vmem] * 2,
+                out_specs=in_vmem,
+                cost_estimate=pl.CostEstimate(flops=10**7, bytes_accessed=10**6, transcendentals=0),
+            )(held_rows, held_clover)
         coarse = kept + apply(jnp.concatenate(moved, 1), around)
 
-    rounded = (coarse * used).reshape(rhs_count, 2, 2, vec_total)
-    real_rows = jnp.stack([rounded[:, 0], -rounded[:, 1]], 1)
-    imag_rows = jnp.stack([rounded[:, 1], rounded[:, 0]], 1)
-    weights = jnp.stack([real_rows, imag_rows]).transpose(3, 0, 1, 2, 4)
-    weights = weights.reshape(2, 2 * rhs_count, 2 * vec_total).astype(jnp.bfloat16)
-    lift = jnp.einsum("xrk,xcks->xcrs", weights, vectors, preferred_element_type=jnp.float32)
-
-    rows = residual.reshape(rhs_count, 2, 2, 6, sites).astype(jnp.float32)
-    clover = clover_inverse.astype(jnp.float32)
-
-    def local_apply(left, right):
-        return sum(left[:, :, b][None] * right[:, :, b][:, :, None] for b in range(6))
-
-    local_real = local_apply(clover[0], rows[:, 0]) - local_apply(clover[1], rows[:, 1])
-    local_imag = local_apply(clover[0], rows[:, 1]) + local_apply(clover[1], rows[:, 0])
-    lift = lift.reshape(2, 6, 2, rhs_count, sites).transpose(3, 2, 0, 1, 4)
-    result = jnp.stack([local_real, local_imag], 1) + lift
-    return result.reshape(rhs_count, 2, 12, sites).astype(jnp.bfloat16)
+    result = pl.pallas_call(
+        extend_kernel,
+        out_shape=jax.ShapeDtypeStruct((rhs_count, parts, 2, sites), jnp.bfloat16),
+        in_specs=[in_vmem] * 4,
+        out_specs=in_vmem,
+        scratch_shapes=[pltpu.VMEM((2, 2 * rhs_count, 128), jnp.float32)],
+        cost_estimate=pl.CostEstimate(flops=10**7, bytes_accessed=10**6, transcendentals=0),
+    )(count, coarse, vectors, local)
+    return result.transpose(0, 2, 1, 3)
 
 
 def solution(mesh):

time: 38.9 us -> 41.6 us (1.069)
  Pallas kernels: 0 us -> 6.65 us
  local copies, waits for them, and re-layouts: 5.78 us -> 2.25 us
  starting transfers between devices: 19.4 us -> 21 us
  waiting for transfers between devices: 8.74 us -> 7.6 us
  other arithmetic: 1.28 us -> 0.53 us
    pallas_call x0 -> x3, Pallas kernels: none -> 6.65 us  [the longest x1 2.34 us: body(): pl.pallas_call(local_kernel, out_shape=jax.ShapeDtypeStruct((parts, 2 * r...]
    unnamed x8 -> x4, local copies, waits for them, and re-layouts: 2.59 us -> 0.63 us
    ppermute x20, starting transfers between devices: 19.4 us -> 21 us  [fetch(): lax.ppermute(block, axis, [(source, i) for i, source in enumerate(sources)])]
    ppermute x20, waiting for transfers between devices: 8.74 us -> 7.6 us  [fetch(): lax.ppermute(block, axis, [(source, i) for i, source in enumerate(sources)])]
    convert_element_type x4 -> x0, local copies, waits for them, and re-layouts: 0.98 us -> none  [the longest x1 0.83 us: body(): return result.reshape(rhs_count, 2, 12, sites).astype(jnp.bfloat16)]
    dot_general x8, matrix products: 1.84 us -> 2.48 us  [apply(): lax.dot_general(vector, matrix, (((1,), (1,)), ((), ())), precision=exact)]
  transfers between devices with their start and end apart: 20 -> 20, of which waited for: 9 -> 8; matrix products, arithmetic and copies ran while one was open for 9% -> 7% of each run, Pallas kernels for 0% -> 6%
where the time goes in v5:
time: 41.6 us; the launch traced here: 41.4 us
  starting transfers between devices  21 us (50%)
  waiting for transfers between devices  7.6 us (18%)
  Pallas kernels  6.65 us (16%)
  matrix products  2.48 us (6%)
  local copies, waits for them, and re-layouts  2.25 us (5%)
  between operations  0.92 us (2%)
  other arithmetic  0.53 us (1%)
    ppermute x20, starting transfers between devices, fetch(): lax.ppermute(block, axis, [(source, i) for i, source in enumerate(sources)])  21 us
    ppermute x20, waiting for transfers between devices, fetch(): lax.ppermute(block, axis, [(source, i) for i, source in enumerate(sources)])  7.6 us
    dot_general x8, matrix products, apply(): lax.dot_general(vector, matrix, (((1,), (1,)), ((), ())), precision=exact)  2.48 us
    pallas_call x1, Pallas kernels, body(): pl.pallas_call(local_kernel, out_shape=jax.ShapeDtypeStruct((parts, 2 * r...  2.34 us
    pallas_call x1, Pallas kernels, body(): pl.pallas_call(restrict_kernel, out_shape=jax.ShapeDtypeStruct((rhs_count...  2.18 us
    pallas_call x1, Pallas kernels, body(): pl.pallas_call(extend_kernel, out_shape=jax.ShapeDtypeStruct((rhs_count,...  2.13 us
    squeeze x12, local copies, waits for them, and re-layouts, real_form(): upper = jnp.concatenate([matrix[0], -matrix[1]], 1)  0.89 us
  transfers between devices with their start and end apart: 20, of which 8 were waited for; matrix products, arithmetic and copies ran while one was open for 7% of the time, Pallas kernels for 6%

profile of v5, /device:TPU:0, one launch (start us, length us, event | category | flops | bytes accessed | tf_op | source)
XLA Modules:
  0.0 41.4 jit_solution(15899899358545036516)
XLA Ops:
  0.7 2.2 %shard_map.55 = f32[16,96]{1,0:T(8,128)} custom-call(s32[1]{0:T(128)} %copy.6.count_hbm, bf16[16,12,2,256]{3,2,1,0:T(2,128)(2,1)} %bitcast.20, bf16[2,12,24,256]{3,2,1,0:T(8,128)(2,1)} %bitcast.18), custom_call_target="tpu_custom_call" | custom-call | flops 10000000 | bytes 500000 | tf_op jit(solution)/shard_map/pallas_call | solution.py:148
  2.9 0.5 %collective-permute-start.4 = (f32[16,96]{1,0:T(8,128)}, f32[16,96]{1,0:T(8,128)S(1)}, u32[]{:S(2)}, u32[]{:S(2)}) collective-permute-start(f32[16,96]{1,0:T(8,128)} %shard_map.55), channel_id=1, source_target_pairs={{8,0},{0,8},{24,16},{16,24},{9,1},{1,9},{25,17},{17,25},{10,2},{2,... | collective-permute-start | bytes 18440 | tf_op jit(solution)/shard_map/ppermute | solution.py:48
  3.4 2.6 %collective-permute-start.3 = (f32[16,96]{1,0:T(8,128)}, f32[16,96]{1,0:T(8,128)S(1)}, u32[]{:S(2)}, u32[]{:S(2)}) collective-permute-start(f32[16,96]{1,0:T(8,128)} %shard_map.55), channel_id=1, source_target_pairs={{16,0},{24,8},{0,16},{8,24},{17,1},{25,9},{1,17},{9,25},{18,2},{26... | collective-permute-start | bytes 18440 | tf_op jit(solution)/shard_map/ppermute | solution.py:48
  6.0 1.5 %collective-permute-start.2 = (f32[16,96]{1,0:T(8,128)}, f32[16,96]{1,0:T(8,128)S(1)}, u32[]{:S(2)}, u32[]{:S(2)}) collective-permute-start(f32[16,96]{1,0:T(8,128)} %shard_map.55), channel_id=1, source_target_pairs={{1,0},{0,1},{3,2},{2,3},{5,4},{4,5},{7,6},{6,7},{9,8},{8,9},{11,10... | collective-permute-start | bytes 18440 | tf_op jit(solution)/shard_map/ppermute | solution.py:48
  7.5 1.6 %collective-permute-start.1 = (f32[16,96]{1,0:T(8,128)}, f32[16,96]{1,0:T(8,128)S(1)}, u32[]{:S(2)}, u32[]{:S(2)}) collective-permute-start(f32[16,96]{1,0:T(8,128)} %shard_map.55), channel_id=1, source_target_pairs={{2,0},{0,2},{6,4},{4,6},{3,1},{1,3},{7,5},{5,7},{10,8},{8,10},{14,... | collective-permute-start | bytes 18440 | tf_op jit(solution)/shard_map/ppermute | solution.py:48
  9.0 2.5 %collective-permute-start = (f32[16,96]{1,0:T(8,128)}, f32[16,96]{1,0:T(8,128)S(1)}, u32[]{:S(2)}, u32[]{:S(2)}) collective-permute-start(f32[16,96]{1,0:T(8,128)} %shard_map.55), channel_id=1, source_target_pairs={{6,0},{4,2},{2,4},{0,6},{7,1},{5,3},{3,5},{1,7},{14,8},{12,10},{10... | collective-permute-start | bytes 18440 | tf_op jit(solution)/shard_map/ppermute | solution.py:48
  12.8 0.6 %copy-done.1 = f32[16,96]{1,0:T(8,128)S(1)} copy-done((f32[16,96]{1,0:T(8,128)S(1)}, f32[16,96]{1,0:T(8,128)}, u32[]{:S(2)}) %copy-start.1) | copy-done | bytes 6168
  15.1 0.6 %collective-permute-start.8 = (f32[16,96]{1,0:T(8,128)S(1)}, f32[16,96]{1,0:T(8,128)S(1)}, u32[]{:S(2)}, u32[]{:S(2)}) collective-permute-start(f32[16,96]{1,0:T(8,128)S(1)} %convolution_add_fusion.7), channel_id=1, source_target_pairs={{16,0},{24,8},{0,16},{8,24},{17,1},{25,9},{1,17},{9,25},{18,2},{26... | collective-permute-start | bytes 18440 | tf_op jit(solution)/shard_map/ppermute | solution.py:48
  15.7 0.5 %collective-permute-start.7 = (f32[16,96]{1,0:T(8,128)S(1)}, f32[16,96]{1,0:T(8,128)S(1)}, u32[]{:S(2)}, u32[]{:S(2)}) collective-permute-start(f32[16,96]{1,0:T(8,128)S(1)} %convolution_add_fusion.7), channel_id=1, source_target_pairs={{1,0},{0,1},{3,2},{2,3},{5,4},{4,5},{7,6},{6,7},{9,8},{8,9},{11,10... | collective-permute-start | bytes 18440 | tf_op jit(solution)/shard_map/ppermute | solution.py:48
  16.5 2.1 %collective-permute-start.5 = (f32[16,96]{1,0:T(8,128)S(1)}, f32[16,96]{1,0:T(8,128)S(1)}, u32[]{:S(2)}, u32[]{:S(2)}) collective-permute-start(f32[16,96]{1,0:T(8,128)S(1)} %convolution_add_fusion.7), channel_id=1, source_target_pairs={{6,0},{4,2},{2,4},{0,6},{7,1},{5,3},{3,5},{1,7},{14,8},{12,10},{10... | collective-permute-start | bytes 18440 | tf_op jit(solution)/shard_map/ppermute | solution.py:48
  18.9 2.3 %shard_map.56.local_ref = f32[12,32,256]{2,1,0:T(8,128)} custom-call(bf16[16,12,2,256]{3,2,1,0:T(2,128)(2,1)} %bitcast.21, bf16[2,6,6,2,256]{4,3,2,1,0:T(2,128)(2,1)} %bitcast.22), custom_call_target="tpu_custom_call" | custom-call | flops 10000000 | bytes 1000000 | tf_op jit(solution)/shard_map/pallas_call | solution.py:197
  21.3 0.7 %collective-permute-done.5 = f32[16,96]{1,0:T(8,128)S(1)} collective-permute-done((f32[16,96]{1,0:T(8,128)S(1)}, f32[16,96]{1,0:T(8,128)S(1)}, u32[]{:S(2)}, u32[]{:S(2)}) %collective-permute-start.5) | collective-permute-done | bytes 6176 | tf_op jit(solution)/shard_map/ppermute | solution.py:48
  22.4 1.6 %collective-permute-start.13 = (f32[16,96]{1,0:T(8,128)S(1)}, f32[16,96]{1,0:T(8,128)S(1)}, u32[]{:S(2)}, u32[]{:S(2)}) collective-permute-start(f32[16,96]{1,0:T(8,128)S(1)} %convolution_add_fusion.5), channel_id=1, source_target_pairs={{16,0},{24,8},{0,16},{8,24},{17,1},{25,9},{1,17},{9,25},{18,2},{26... | collective-permute-start | bytes 18440 | tf_op jit(solution)/shard_map/ppermute | solution.py:48
  24.0 1.5 %collective-permute-start.12 = (f32[16,96]{1,0:T(8,128)S(1)}, f32[16,96]{1,0:T(8,128)S(1)}, u32[]{:S(2)}, u32[]{:S(2)}) collective-permute-start(f32[16,96]{1,0:T(8,128)S(1)} %convolution_add_fusion.5), channel_id=1, source_target_pairs={{1,0},{0,1},{3,2},{2,3},{5,4},{4,5},{7,6},{6,7},{9,8},{8,9},{11,10... | collective-permute-start | bytes 18440 | tf_op jit(solution)/shard_map/ppermute | solution.py:48
  25.9 1.9 %collective-permute-start.10 = (f32[16,96]{1,0:T(8,128)S(1)}, f32[16,96]{1,0:T(8,128)S(1)}, u32[]{:S(2)}, u32[]{:S(2)}) collective-permute-start(f32[16,96]{1,0:T(8,128)S(1)} %convolution_add_fusion.5), channel_id=1, source_target_pairs={{6,0},{4,2},{2,4},{0,6},{7,1},{5,3},{3,5},{1,7},{14,8},{12,10},{10... | collective-permute-start | bytes 18440 | tf_op jit(solution)/shard_map/ppermute | solution.py:48
  28.1 1.0 %collective-permute-done.11 = f32[16,96]{1,0:T(8,128)S(1)} collective-permute-done((f32[16,96]{1,0:T(8,128)S(1)}, f32[16,96]{1,0:T(8,128)S(1)}, u32[]{:S(2)}, u32[]{:S(2)}) %collective-permute-start.11) | collective-permute-done | bytes 6176 | tf_op jit(solution)/shard_map/ppermute | solution.py:48
  29.1 2.2 %collective-permute-done.10 = f32[16,96]{1,0:T(8,128)S(1)} collective-permute-done((f32[16,96]{1,0:T(8,128)S(1)}, f32[16,96]{1,0:T(8,128)S(1)}, u32[]{:S(2)}, u32[]{:S(2)}) %collective-permute-start.10) | collective-permute-done | bytes 6176 | tf_op jit(solution)/shard_map/ppermute | solution.py:48
  31.7 0.6 %collective-permute-start.18 = (f32[16,96]{1,0:T(8,128)S(1)}, f32[16,96]{1,0:T(8,128)S(1)}, u32[]{:S(2)}, u32[]{:S(2)}) collective-permute-start(f32[16,96]{1,0:T(8,128)S(1)} %convolution_add_fusion.3), channel_id=1, source_target_pairs={{16,0},{24,8},{0,16},{8,24},{17,1},{25,9},{1,17},{9,25},{18,2},{26... | collective-permute-start | bytes 18440 | tf_op jit(solution)/shard_map/ppermute | solution.py:48
  32.3 0.5 %collective-permute-start.17 = (f32[16,96]{1,0:T(8,128)S(1)}, f32[16,96]{1,0:T(8,128)S(1)}, u32[]{:S(2)}, u32[]{:S(2)}) collective-permute-start(f32[16,96]{1,0:T(8,128)S(1)} %convolution_add_fusion.3), channel_id=1, source_target_pairs={{1,0},{0,1},{3,2},{2,3},{5,4},{4,5},{7,6},{6,7},{9,8},{8,9},{11,10... | collective-permute-start | bytes 18440 | tf_op jit(solution)/shard_map/ppermute | solution.py:48
  32.9 1.9 %collective-permute-start.15 = (f32[16,96]{1,0:T(8,128)S(1)}, f32[16,96]{1,0:T(8,128)S(1)}, u32[]{:S(2)}, u32[]{:S(2)}) collective-permute-start(f32[16,96]{1,0:T(8,128)S(1)} %convolution_add_fusion.3), channel_id=1, source_target_pairs={{6,0},{4,2},{2,4},{0,6},{7,1},{5,3},{3,5},{1,7},{14,8},{12,10},{10... | collective-permute-start | bytes 18440 | tf_op jit(solution)/shard_map/ppermute | solution.py:48
  36.0 0.5 %collective-permute-done.16 = f32[16,96]{1,0:T(8,128)S(1)} collective-permute-done((f32[16,96]{1,0:T(8,128)S(1)}, f32[16,96]{1,0:T(8,128)S(1)}, u32[]{:S(2)}, u32[]{:S(2)}) %collective-permute-start.16) | collective-permute-done | bytes 6176 | tf_op jit(solution)/shard_map/ppermute | solution.py:48
  36.5 1.8 %collective-permute-done.15 = f32[16,96]{1,0:T(8,128)S(1)} collective-permute-done((f32[16,96]{1,0:T(8,128)S(1)}, f32[16,96]{1,0:T(8,128)S(1)}, u32[]{:S(2)}, u32[]{:S(2)}) %collective-permute-start.15) | collective-permute-done | bytes 6176 | tf_op jit(solution)/shard_map/ppermute | solution.py:48
  38.4 0.9 %convolution_add_fusion.1.coarse_ref = f32[16,96]{1,0:T(8,128)} fusion(f32[16,96]{1,0:T(8,128)S(1)} %convolution_add_fusion.2, f32[16,480]{1,0:T(8,128)S(1)} %concatenate.91, f32[96,480]{1,0:T(8,128)S(1)} %concatenate.88), kind=kOutput, calls=%fused_computation.1 | convolution fusion | flops 8848896 | bytes 227328 | tf_op jit(solution)/shard_map/dot_general | solution.py:189
  39.3 2.1 %shard_map.57 = bf16[16,12,2,256]{3,2,1,0:T(2,128)(2,1)} custom-call(s32[1,1]{1,0:T(1,128)} %bitcast.17.count_ref, f32[16,96]{1,0:T(8,128)} %convolution_add_fusion.1.coarse_ref, bf16[2,12,24,256]{3,2,1,0:T(8,128)(2,1)} %bitcast.19, f32[12,32,256]{2,1,0:T(8,128)} %shard_map.56.local_ref), custom_call_target="tpu_custom_call" | custom-call | flops 10000000 | bytes 1000000 | tf_op jit(solution)/shard_map/pallas_call | solution.py:206
  (64 shorter events, 6.1 us)
Async XLA Ops:
  0.7 10.9 %copy-start = (f32[1,9,2,2304]{3,2,1,0:T(2,128)S(1)}, f32[1,9,2,2304]{3,2,1,0:T(2,128)}, u32[]{:S(2)}) copy-start(f32[1,9,2,2304]{3,2,1,0:T(2,128)} %param.8) | copy-start | bytes 497668
  2.9 11.4 %collective-permute-start.4 = (f32[16,96]{1,0:T(8,128)}, f32[16,96]{1,0:T(8,128)S(1)}, u32[]{:S(2)}, u32[]{:S(2)}) collective-permute-start(f32[16,96]{1,0:T(8,128)} %shard_map.55), channel_id=1, source_target_pairs={{8,0},{0,8},{24,16},{16,24},{9,1},{1,9},{25,17},{17,25},{10,2},{2,... | collective-permute-start | bytes 18440 | tf_op jit(solution)/shard_map/ppermute | solution.py:48
  3.4 10.9 %collective-permute-start.3 = (f32[16,96]{1,0:T(8,128)}, f32[16,96]{1,0:T(8,128)S(1)}, u32[]{:S(2)}, u32[]{:S(2)}) collective-permute-start(f32[16,96]{1,0:T(8,128)} %shard_map.55), channel_id=1, source_target_pairs={{16,0},{24,8},{0,16},{8,24},{17,1},{25,9},{1,17},{9,25},{18,2},{26... | collective-permute-start | bytes 18440 | tf_op jit(solution)/shard_map/ppermute | solution.py:48
  6.0 8.4 %collective-permute-start.2 = (f32[16,96]{1,0:T(8,128)}, f32[16,96]{1,0:T(8,128)S(1)}, u32[]{:S(2)}, u32[]{:S(2)}) collective-permute-start(f32[16,96]{1,0:T(8,128)} %shard_map.55), channel_id=1, source_target_pairs={{1,0},{0,1},{3,2},{2,3},{5,4},{4,5},{7,6},{6,7},{9,8},{8,9},{11,10... | collective-permute-start | bytes 18440 | tf_op jit(solution)/shard_map/ppermute | solution.py:48
  7.5 6.9 %collective-permute-start.1 = (f32[16,96]{1,0:T(8,128)}, f32[16,96]{1,0:T(8,128)S(1)}, u32[]{:S(2)}, u32[]{:S(2)}) collective-permute-start(f32[16,96]{1,0:T(8,128)} %shard_map.55), channel_id=1, source_target_pairs={{2,0},{0,2},{6,4},{4,6},{3,1},{1,3},{7,5},{5,7},{10,8},{8,10},{14,... | collective-permute-start | bytes 18440 | tf_op jit(solution)/shard_map/ppermute | solution.py:48
  9.0 5.7 %collective-permute-start = (f32[16,96]{1,0:T(8,128)}, f32[16,96]{1,0:T(8,128)S(1)}, u32[]{:S(2)}, u32[]{:S(2)}) collective-permute-start(f32[16,96]{1,0:T(8,128)} %shard_map.55), channel_id=1, source_target_pairs={{6,0},{4,2},{2,4},{0,6},{7,1},{5,3},{3,5},{1,7},{14,8},{12,10},{10... | collective-permute-start | bytes 18440 | tf_op jit(solution)/shard_map/ppermute | solution.py:48
  12.8 0.7 %copy-start.1 = (f32[16,96]{1,0:T(8,128)S(1)}, f32[16,96]{1,0:T(8,128)}, u32[]{:S(2)}) copy-start(f32[16,96]{1,0:T(8,128)} %shard_map.55) | copy-start | bytes 18436
  15.0 6.2 %collective-permute-start.9 = (f32[16,96]{1,0:T(8,128)S(1)}, f32[16,96]{1,0:T(8,128)S(1)}, u32[]{:S(2)}, u32[]{:S(2)}) collective-permute-start(f32[16,96]{1,0:T(8,128)S(1)} %convolution_add_fusion.7), channel_id=1, source_target_pairs={{8,0},{0,8},{24,16},{16,24},{9,1},{1,9},{25,17},{17,25},{10,2},{2,... | collective-permute-start | bytes 18440 | tf_op jit(solution)/shard_map/ppermute | solution.py:48
  15.1 6.2 %collective-permute-start.8 = (f32[16,96]{1,0:T(8,128)S(1)}, f32[16,96]{1,0:T(8,128)S(1)}, u32[]{:S(2)}, u32[]{:S(2)}) collective-permute-start(f32[16,96]{1,0:T(8,128)S(1)} %convolution_add_fusion.7), channel_id=1, source_target_pairs={{16,0},{24,8},{0,16},{8,24},{17,1},{25,9},{1,17},{9,25},{18,2},{26... | collective-permute-start | bytes 18440 | tf_op jit(solution)/shard_map/ppermute | solution.py:48
  15.7 5.6 %collective-permute-start.7 = (f32[16,96]{1,0:T(8,128)S(1)}, f32[16,96]{1,0:T(8,128)S(1)}, u32[]{:S(2)}, u32[]{:S(2)}) collective-permute-start(f32[16,96]{1,0:T(8,128)S(1)} %convolution_add_fusion.7), channel_id=1, source_target_pairs={{1,0},{0,1},{3,2},{2,3},{5,4},{4,5},{7,6},{6,7},{9,8},{8,9},{11,10... | collective-permute-start | bytes 18440 | tf_op jit(solution)/shard_map/ppermute | solution.py:48
  16.2 5.1 %collective-permute-start.6 = (f32[16,96]{1,0:T(8,128)S(1)}, f32[16,96]{1,0:T(8,128)S(1)}, u32[]{:S(2)}, u32[]{:S(2)}) collective-permute-start(f32[16,96]{1,0:T(8,128)S(1)} %convolution_add_fusion.7), channel_id=1, source_target_pairs={{2,0},{0,2},{6,4},{4,6},{3,1},{1,3},{7,5},{5,7},{10,8},{8,10},{14,... | collective-permute-start | bytes 18440 | tf_op jit(solution)/shard_map/ppermute | solution.py:48
  16.5 5.4 %collective-permute-start.5 = (f32[16,96]{1,0:T(8,128)S(1)}, f32[16,96]{1,0:T(8,128)S(1)}, u32[]{:S(2)}, u32[]{:S(2)}) collective-permute-start(f32[16,96]{1,0:T(8,128)S(1)} %convolution_add_fusion.7), channel_id=1, source_target_pairs={{6,0},{4,2},{2,4},{0,6},{7,1},{5,3},{3,5},{1,7},{14,8},{12,10},{10... | collective-permute-start | bytes 18440 | tf_op jit(solution)/shard_map/ppermute | solution.py:48
  22.3 5.8 %collective-permute-start.14 = (f32[16,96]{1,0:T(8,128)S(1)}, f32[16,96]{1,0:T(8,128)S(1)}, u32[]{:S(2)}, u32[]{:S(2)}) collective-permute-start(f32[16,96]{1,0:T(8,128)S(1)} %convolution_add_fusion.5), channel_id=1, source_target_pairs={{8,0},{0,8},{24,16},{16,24},{9,1},{1,9},{25,17},{17,25},{10,2},{2,... | collective-permute-start | bytes 18440 | tf_op jit(solution)/shard_map/ppermute | solution.py:48
  22.4 5.7 %collective-permute-start.13 = (f32[16,96]{1,0:T(8,128)S(1)}, f32[16,96]{1,0:T(8,128)S(1)}, u32[]{:S(2)}, u32[]{:S(2)}) collective-permute-start(f32[16,96]{1,0:T(8,128)S(1)} %convolution_add_fusion.5), channel_id=1, source_target_pairs={{16,0},{24,8},{0,16},{8,24},{17,1},{25,9},{1,17},{9,25},{18,2},{26... | collective-permute-start | bytes 18440 | tf_op jit(solution)/shard_map/ppermute | solution.py:48
  24.0 4.2 %collective-permute-start.12 = (f32[16,96]{1,0:T(8,128)S(1)}, f32[16,96]{1,0:T(8,128)S(1)}, u32[]{:S(2)}, u32[]{:S(2)}) collective-permute-start(f32[16,96]{1,0:T(8,128)S(1)} %convolution_add_fusion.5), channel_id=1, source_target_pairs={{1,0},{0,1},{3,2},{2,3},{5,4},{4,5},{7,6},{6,7},{9,8},{8,9},{11,10... | collective-permute-start | bytes 18440 | tf_op jit(solution)/shard_map/ppermute | solution.py:48
  25.5 3.7 %collective-permute-start.11 = (f32[16,96]{1,0:T(8,128)S(1)}, f32[16,96]{1,0:T(8,128)S(1)}, u32[]{:S(2)}, u32[]{:S(2)}) collective-permute-start(f32[16,96]{1,0:T(8,128)S(1)} %convolution_add_fusion.5), channel_id=1, source_target_pairs={{2,0},{0,2},{6,4},{4,6},{3,1},{1,3},{7,5},{5,7},{10,8},{8,10},{14,... | collective-permute-start | bytes 18440 | tf_op jit(solution)/shard_map/ppermute | solution.py:48
  25.9 5.4 %collective-permute-start.10 = (f32[16,96]{1,0:T(8,128)S(1)}, f32[16,96]{1,0:T(8,128)S(1)}, u32[]{:S(2)}, u32[]{:S(2)}) collective-permute-start(f32[16,96]{1,0:T(8,128)S(1)} %convolution_add_fusion.5), channel_id=1, source_target_pairs={{6,0},{4,2},{2,4},{0,6},{7,1},{5,3},{3,5},{1,7},{14,8},{12,10},{10... | collective-permute-start | bytes 18440 | tf_op jit(solution)/shard_map/ppermute | solution.py:48
  31.7 3.4 %collective-permute-start.19 = (f32[16,96]{1,0:T(8,128)S(1)}, f32[16,96]{1,0:T(8,128)S(1)}, u32[]{:S(2)}, u32[]{:S(2)}) collective-permute-start(f32[16,96]{1,0:T(8,128)S(1)} %convolution_add_fusion.3), channel_id=1, source_target_pairs={{8,0},{0,8},{24,16},{16,24},{9,1},{1,9},{25,17},{17,25},{10,2},{2,... | collective-permute-start | bytes 18440 | tf_op jit(solution)/shard_map/ppermute | solution.py:48
  31.7 3.7 %collective-permute-start.18 = (f32[16,96]{1,0:T(8,128)S(1)}, f32[16,96]{1,0:T(8,128)S(1)}, u32[]{:S(2)}, u32[]{:S(2)}) collective-permute-start(f32[16,96]{1,0:T(8,128)S(1)} %convolution_add_fusion.3), channel_id=1, source_target_pairs={{16,0},{24,8},{0,16},{8,24},{17,1},{25,9},{1,17},{9,25},{18,2},{26... | collective-permute-start | bytes 18440 | tf_op jit(solution)/shard_map/ppermute | solution.py:48
  32.3 3.7 %collective-permute-start.17 = (f32[16,96]{1,0:T(8,128)S(1)}, f32[16,96]{1,0:T(8,128)S(1)}, u32[]{:S(2)}, u32[]{:S(2)}) collective-permute-start(f32[16,96]{1,0:T(8,128)S(1)} %convolution_add_fusion.3), channel_id=1, source_target_pairs={{1,0},{0,1},{3,2},{2,3},{5,4},{4,5},{7,6},{6,7},{9,8},{8,9},{11,10... | collective-permute-start | bytes 18440 | tf_op jit(solution)/shard_map/ppermute | solution.py:48
  32.9 3.7 %collective-permute-start.16 = (f32[16,96]{1,0:T(8,128)S(1)}, f32[16,96]{1,0:T(8,128)S(1)}, u32[]{:S(2)}, u32[]{:S(2)}) collective-permute-start(f32[16,96]{1,0:T(8,128)S(1)} %convolution_add_fusion.3), channel_id=1, source_target_pairs={{2,0},{0,2},{6,4},{4,6},{3,1},{1,3},{7,5},{5,7},{10,8},{8,10},{14,... | collective-permute-start | bytes 18440 | tf_op jit(solution)/shard_map/ppermute | solution.py:48
  32.9 5.4 %collective-permute-start.15 = (f32[16,96]{1,0:T(8,128)S(1)}, f32[16,96]{1,0:T(8,128)S(1)}, u32[]{:S(2)}, u32[]{:S(2)}) collective-permute-start(f32[16,96]{1,0:T(8,128)S(1)} %convolution_add_fusion.3), channel_id=1, source_target_pairs={{6,0},{4,2},{2,4},{0,6},{7,1},{5,3},{3,5},{1,7},{14,8},{12,10},{10... | collective-permute-start | bytes 18440 | tf_op jit(solution)/shard_map/ppermute | solution.py:48

commit v6 on v2

--- a/solution.py
+++ b/solution.py
@@ -46,6 +46,19 @@
     return lax.ppermute(block, axis, [(source, i) for i, source in enumerate(sources)])
 
 
+def local_term(residual, clover_inverse):
+    rhs_count, _, _, sites = residual.shape
+    rows = residual.reshape(rhs_count, 2, 2, 6, sites).astype(jnp.float32)
+    clover = clover_inverse.astype(jnp.float32)
+
+    def local_apply(left, right):
+        return sum(left[:, :, b][None] * right[:, :, b][:, :, None] for b in range(6))
+
+    local_real = local_apply(clover[0], rows[:, 0]) - local_apply(clover[1], rows[:, 1])
+    local_imag = local_apply(clover[0], rows[:, 1]) + local_apply(clover[1], rows[:, 0])
+    return local_real, local_imag
+
+
 def body(residual, null_vectors, clover_inverse, coarse_op, vector_count):
     rhs_count = residual.shape[0]
     vec_total = null_vectors.shape[1]
@@ -54,14 +67,14 @@
     in_use = (lax.iota(jnp.int32, vec_total)[None, :] < vector_count[:, None]).astype(jnp.float32)[0]
     used = jnp.tile(in_use, 4)
 
-    fine_rows = residual.transpose(2, 1, 0, 3).reshape(2, 6, 2 * rhs_count, sites)
-    vectors = null_vectors.transpose(2, 0, 1, 3).reshape(2, 6, 2 * vec_total, sites)
-    product = jnp.einsum("xcrs,xcks->xrk", fine_rows, vectors, preferred_element_type=jnp.float32)
-    product = product.reshape(2, 2, rhs_count, 2, vec_total)
-    real_part = product[:, 0, :, 0] + product[:, 1, :, 1]
-    imag_part = product[:, 1, :, 0] - product[:, 0, :, 1]
-    restricted = jnp.stack([real_part, imag_part]).transpose(2, 0, 1, 3)
-    half = omega_step * (restricted.reshape(rhs_count, 2 * coarse_dim) * used)
+    parts = residual.transpose(1, 2, 0, 3).reshape(2, 2, 6, rhs_count, sites)
+    fine_rows = jnp.stack(
+        [jnp.concatenate([parts[0], parts[1]], 2), jnp.concatenate([parts[1], -parts[0]], 2)]
+    )
+    vectors = null_vectors.transpose(0, 2, 1, 3).reshape(2, 2, 6, vec_total, sites)
+    product = jnp.einsum("pxcrs,pxcks->xrk", fine_rows, vectors, preferred_element_type=jnp.float32)
+    pieces = [product[chi, part * rhs_count : (part + 1) * rhs_count] for part in range(2) for chi in range(2)]
+    half = omega_step * (jnp.concatenate(pieces, 1) * used)
 
     operator = coarse_op.reshape(9, 2, coarse_dim, coarse_dim)
     grouped = {}
@@ -95,23 +108,17 @@
     for sweep_id in range(ITERS - 1):
         moved = [fetch(coarse, link) for link in order]
         kept = half + apply(coarse, own)
+        if sweep_id == 1:
+            rows, clover, _ = lax.optimization_barrier((residual, clover_inverse, coarse))
+            local_real, local_imag = local_term(rows, clover)
         coarse = kept + apply(jnp.concatenate(moved, 1), around)
 
-    rounded = (coarse * used).reshape(rhs_count, 2, 2, vec_total)
-    real_rows = jnp.stack([rounded[:, 0], -rounded[:, 1]], 1)
-    imag_rows = jnp.stack([rounded[:, 1], rounded[:, 0]], 1)
-    weights = jnp.stack([real_rows, imag_rows]).transpose(3, 0, 1, 2, 4)
-    weights = weights.reshape(2, 2 * rhs_count, 2 * vec_total).astype(jnp.bfloat16)
-    lift = jnp.einsum("xrk,xcks->xcrs", weights, vectors, preferred_element_type=jnp.float32)
-
-    rows = residual.reshape(rhs_count, 2, 2, 6, sites).astype(jnp.float32)
-    clover = clover_inverse.astype(jnp.float32)
-
-    def local_apply(left, right):
-        return sum(left[:, :, b][None] * right[:, :, b][:, :, None] for b in range(6))
-
-    local_real = local_apply(clover[0], rows[:, 0]) - local_apply(clover[1], rows[:, 1])
-    local_imag = local_apply(clover[0], rows[:, 1]) + local_apply(clover[1], rows[:, 0])
+    rounded = coarse * used
+    cut = [rounded[:, p * vec_total : (p + 1) * vec_total] for p in range(4)]
+    by_real = jnp.stack([jnp.concatenate([cut[chi], cut[2 + chi]], 0) for chi in range(2)])
+    by_imag = jnp.stack([jnp.concatenate([-cut[2 + chi], cut[chi]], 0) for chi in range(2)])
+    weights = jnp.stack([by_real, by_imag]).astype(jnp.bfloat16)
+    lift = jnp.einsum("pxrk,pxcks->xcrs", weights, vectors, preferred_element_type=jnp.float32)
     lift = lift.reshape(2, 6, 2, rhs_count, sites).transpose(3, 2, 0, 1, 4)
     result = jnp.stack([local_real, local_imag], 1) + lift
     return result.reshape(rhs_count, 2, 12, sites).astype(jnp.bfloat16)

time: 38.9 us -> 38.8 us (level)
  starting transfers between devices: 19.4 us -> 20.7 us
  waiting for transfers between devices: 8.74 us -> 7.5 us
    ppermute x20, waiting for transfers between devices: 8.74 us -> 7.5 us  [fetch(): lax.ppermute(block, axis, [(source, i) for i, source in enumerate(sources)])]
    ppermute x20, starting transfers between devices: 19.4 us -> 20.7 us  [fetch(): lax.ppermute(block, axis, [(source, i) for i, source in enumerate(sources)])]
    unnamed x8 -> x9, local copies, waits for them, and re-layouts: 2.59 us -> 2.42 us
  transfers between devices with their start and end apart: 20 -> 20, of which waited for: 9 -> 8; matrix products, arithmetic and copies ran while one was open for 9% -> 7% of each run, Pallas kernels for 0% -> 0%
where the time goes in v6:
time: 38.8 us; the launch traced here: 38.6 us
  starting transfers between devices  20.7 us (53%)
  waiting for transfers between devices  7.5 us (19%)
  local copies, waits for them, and re-layouts  5.61 us (14%)
  matrix products  2.32 us (6%)
  other arithmetic  1.32 us (3%)
  between operations  1.18 us (3%)
    ppermute x20, starting transfers between devices, fetch(): lax.ppermute(block, axis, [(source, i) for i, source in enumerate(sources)])  20.7 us
    ppermute x20, waiting for transfers between devices, fetch(): lax.ppermute(block, axis, [(source, i) for i, source in enumerate(sources)])  7.5 us
    unnamed x9, local copies, waits for them, and re-layouts  2.42 us
    dot_general x8, matrix products, apply(): lax.dot_general(vector, matrix, (((1,), (1,)), ((), ())), precision=exact)  1.84 us
    squeeze x12, local copies, waits for them, and re-layouts, real_form(): upper = jnp.concatenate([matrix[0], -matrix[1]], 1)  0.89 us
    convert_element_type x1, local copies, waits for them, and re-layouts, body(): return result.reshape(rhs_count, 2, 12, sites).astype(jnp.bfloat16)  0.83 us
  transfers between devices with their start and end apart: 20, of which 8 were waited for; matrix products, arithmetic and copies ran while one was open for 7% of the time, Pallas kernels for 0%

profile of v6, /device:TPU:0, one launch (start us, length us, event | category | flops | bytes accessed | tf_op | source)
XLA Modules:
  0.0 38.6 jit_solution(13121525281096687467)
XLA Ops:
  0.0 1.0 %copy.138 = bf16[16,2,12,256]{3,0,2,1:T(8,128)(2,1)S(1)} copy(bf16[16,2,12,256]{3,1,2,0:T(2,128)(2,1)} %param.5) | data formatting | bytes 393216 | tf_op args[0]
  2.6 5.1 %collective-permute-start = (f32[16,96]{1,0:T(8,128)S(1)}, f32[16,96]{1,0:T(8,128)S(1)}, u32[]{:S(2)}, u32[]{:S(2)}) collective-permute-start(f32[16,96]{1,0:T(8,128)S(1)} %fusion.15), channel_id=1, source_target_pairs={{6,0},{4,2},{2,4},{0,6},{7,1},{5,3},{3,5},{1,7},{14,8},{12,10},{10... | collective-permute-start | bytes 18440 | tf_op jit(solution)/shard_map/ppermute | solution.py:46
  7.6 1.5 %collective-permute-start.2 = (f32[16,96]{1,0:T(8,128)S(1)}, f32[16,96]{1,0:T(8,128)S(1)}, u32[]{:S(2)}, u32[]{:S(2)}) collective-permute-start(f32[16,96]{1,0:T(8,128)S(1)} %fusion.15), channel_id=1, source_target_pairs={{1,0},{0,1},{3,2},{2,3},{5,4},{4,5},{7,6},{6,7},{9,8},{8,9},{11,10... | collective-permute-start | bytes 18440 | tf_op jit(solution)/shard_map/ppermute | solution.py:46
  9.1 1.5 %collective-permute-start.3 = (f32[16,96]{1,0:T(8,128)S(1)}, f32[16,96]{1,0:T(8,128)S(1)}, u32[]{:S(2)}, u32[]{:S(2)}) collective-permute-start(f32[16,96]{1,0:T(8,128)S(1)} %fusion.15), channel_id=1, source_target_pairs={{16,0},{24,8},{0,16},{8,24},{17,1},{25,9},{1,17},{9,25},{18,2},{26... | collective-permute-start | bytes 18440 | tf_op jit(solution)/shard_map/ppermute | solution.py:46
  13.2 0.5 %copy-done.1 = bf16[16,2,12,256]{3,1,2,0:T(2,128)(2,1)S(1)} copy-done((bf16[16,2,12,256]{3,1,2,0:T(2,128)(2,1)S(1)}, bf16[16,2,12,256]{3,1,2,0:T(2,128)(2,1)}, u32[]{:S(2)}) %copy-start.1) | copy-done | bytes 196632
  13.9 0.9 %copy-done.3 = bf16[2,2,6,6,256]{4,1,3,2,0:T(2,128)(2,1)S(1)} copy-done((bf16[2,2,6,6,256]{4,1,3,2,0:T(2,128)(2,1)S(1)}, bf16[2,2,6,6,256]{4,1,3,2,0:T(2,128)(2,1)}, u32[]{:S(2)}) %copy-start.3) | copy-done | bytes 73752
  15.4 1.0 %collective-permute-start.5 = (f32[16,96]{1,0:T(8,128)S(1)}, f32[16,96]{1,0:T(8,128)S(1)}, u32[]{:S(2)}, u32[]{:S(2)}) collective-permute-start(f32[16,96]{1,0:T(8,128)S(1)} %convolution_add_fusion.7), channel_id=1, source_target_pairs={{6,0},{4,2},{2,4},{0,6},{7,1},{5,3},{3,5},{1,7},{14,8},{12,10},{10... | collective-permute-start | bytes 18440 | tf_op jit(solution)/shard_map/ppermute | solution.py:46
  16.4 1.2 %collective-permute-start.6 = (f32[16,96]{1,0:T(8,128)S(1)}, f32[16,96]{1,0:T(8,128)S(1)}, u32[]{:S(2)}, u32[]{:S(2)}) collective-permute-start(f32[16,96]{1,0:T(8,128)S(1)} %convolution_add_fusion.7), channel_id=1, source_target_pairs={{2,0},{0,2},{6,4},{4,6},{3,1},{1,3},{7,5},{5,7},{10,8},{8,10},{14,... | collective-permute-start | bytes 18440 | tf_op jit(solution)/shard_map/ppermute | solution.py:46
  17.6 0.5 %collective-permute-start.7 = (f32[16,96]{1,0:T(8,128)S(1)}, f32[16,96]{1,0:T(8,128)S(1)}, u32[]{:S(2)}, u32[]{:S(2)}) collective-permute-start(f32[16,96]{1,0:T(8,128)S(1)} %convolution_add_fusion.7), channel_id=1, source_target_pairs={{1,0},{0,1},{3,2},{2,3},{5,4},{4,5},{7,6},{6,7},{9,8},{8,9},{11,10... | collective-permute-start | bytes 18440 | tf_op jit(solution)/shard_map/ppermute | solution.py:46
  18.1 0.9 %collective-permute-start.8 = (f32[16,96]{1,0:T(8,128)S(1)}, f32[16,96]{1,0:T(8,128)S(1)}, u32[]{:S(2)}, u32[]{:S(2)}) collective-permute-start(f32[16,96]{1,0:T(8,128)S(1)} %convolution_add_fusion.7), channel_id=1, source_target_pairs={{16,0},{24,8},{0,16},{8,24},{17,1},{25,9},{1,17},{9,25},{18,2},{26... | collective-permute-start | bytes 18440 | tf_op jit(solution)/shard_map/ppermute | solution.py:46
  19.3 1.7 %collective-permute-done.5 = f32[16,96]{1,0:T(8,128)S(1)} collective-permute-done((f32[16,96]{1,0:T(8,128)S(1)}, f32[16,96]{1,0:T(8,128)S(1)}, u32[]{:S(2)}, u32[]{:S(2)}) %collective-permute-start.5) | collective-permute-done | bytes 6176 | tf_op jit(solution)/shard_map/ppermute | solution.py:46
  21.2 0.5 %collective-permute-done.8 = f32[16,96]{1,0:T(8,128)S(1)} collective-permute-done((f32[16,96]{1,0:T(8,128)S(1)}, f32[16,96]{1,0:T(8,128)S(1)}, u32[]{:S(2)}, u32[]{:S(2)}) %collective-permute-start.8) | collective-permute-done | bytes 6176 | tf_op jit(solution)/shard_map/ppermute | solution.py:46
  22.1 2.9 %collective-permute-start.10 = (f32[16,96]{1,0:T(8,128)S(1)}, f32[16,96]{1,0:T(8,128)S(1)}, u32[]{:S(2)}, u32[]{:S(2)}) collective-permute-start(f32[16,96]{1,0:T(8,128)S(1)} %convolution_add_fusion.5), channel_id=1, source_target_pairs={{6,0},{4,2},{2,4},{0,6},{7,1},{5,3},{3,5},{1,7},{14,8},{12,10},{10... | collective-permute-start | bytes 18440 | tf_op jit(solution)/shard_map/ppermute | solution.py:46
  25.0 1.5 %collective-permute-start.12 = (f32[16,96]{1,0:T(8,128)S(1)}, f32[16,96]{1,0:T(8,128)S(1)}, u32[]{:S(2)}, u32[]{:S(2)}) collective-permute-start(f32[16,96]{1,0:T(8,128)S(1)} %convolution_add_fusion.5), channel_id=1, source_target_pairs={{1,0},{0,1},{3,2},{2,3},{5,4},{4,5},{7,6},{6,7},{9,8},{8,9},{11,10... | collective-permute-start | bytes 18440 | tf_op jit(solution)/shard_map/ppermute | solution.py:46
  26.5 0.9 %collective-permute-start.13 = (f32[16,96]{1,0:T(8,128)S(1)}, f32[16,96]{1,0:T(8,128)S(1)}, u32[]{:S(2)}, u32[]{:S(2)}) collective-permute-start(f32[16,96]{1,0:T(8,128)S(1)} %convolution_add_fusion.5), channel_id=1, source_target_pairs={{16,0},{24,8},{0,16},{8,24},{17,1},{25,9},{1,17},{9,25},{18,2},{26... | collective-permute-start | bytes 18440 | tf_op jit(solution)/shard_map/ppermute | solution.py:46
  27.7 1.0 %collective-permute-done.11 = f32[16,96]{1,0:T(8,128)S(1)} collective-permute-done((f32[16,96]{1,0:T(8,128)S(1)}, f32[16,96]{1,0:T(8,128)S(1)}, u32[]{:S(2)}, u32[]{:S(2)}) %collective-permute-start.11) | collective-permute-done | bytes 6176 | tf_op jit(solution)/shard_map/ppermute | solution.py:46
  28.7 1.5 %collective-permute-done.13 = f32[16,96]{1,0:T(8,128)S(1)} collective-permute-done((f32[16,96]{1,0:T(8,128)S(1)}, f32[16,96]{1,0:T(8,128)S(1)}, u32[]{:S(2)}, u32[]{:S(2)}) %collective-permute-start.13) | collective-permute-done | bytes 6176 | tf_op jit(solution)/shard_map/ppermute | solution.py:46
  30.5 1.1 %collective-permute-start.15 = (f32[16,96]{1,0:T(8,128)S(1)}, f32[16,96]{1,0:T(8,128)S(1)}, u32[]{:S(2)}, u32[]{:S(2)}) collective-permute-start(f32[16,96]{1,0:T(8,128)S(1)} %convolution_add_fusion.3), channel_id=1, source_target_pairs={{6,0},{4,2},{2,4},{0,6},{7,1},{5,3},{3,5},{1,7},{14,8},{12,10},{10... | collective-permute-start | bytes 18440 | tf_op jit(solution)/shard_map/ppermute | solution.py:46
  31.5 1.1 %collective-permute-start.16 = (f32[16,96]{1,0:T(8,128)S(1)}, f32[16,96]{1,0:T(8,128)S(1)}, u32[]{:S(2)}, u32[]{:S(2)}) collective-permute-start(f32[16,96]{1,0:T(8,128)S(1)} %convolution_add_fusion.3), channel_id=1, source_target_pairs={{2,0},{0,2},{6,4},{4,6},{3,1},{1,3},{7,5},{5,7},{10,8},{8,10},{14,... | collective-permute-start | bytes 18440 | tf_op jit(solution)/shard_map/ppermute | solution.py:46
  32.7 0.5 %collective-permute-start.17 = (f32[16,96]{1,0:T(8,128)S(1)}, f32[16,96]{1,0:T(8,128)S(1)}, u32[]{:S(2)}, u32[]{:S(2)}) collective-permute-start(f32[16,96]{1,0:T(8,128)S(1)} %convolution_add_fusion.3), channel_id=1, source_target_pairs={{1,0},{0,1},{3,2},{2,3},{5,4},{4,5},{7,6},{6,7},{9,8},{8,9},{11,10... | collective-permute-start | bytes 18440 | tf_op jit(solution)/shard_map/ppermute | solution.py:46
  33.2 0.9 %collective-permute-start.18 = (f32[16,96]{1,0:T(8,128)S(1)}, f32[16,96]{1,0:T(8,128)S(1)}, u32[]{:S(2)}, u32[]{:S(2)}) collective-permute-start(f32[16,96]{1,0:T(8,128)S(1)} %convolution_add_fusion.3), channel_id=1, source_target_pairs={{16,0},{24,8},{0,16},{8,24},{17,1},{25,9},{1,17},{9,25},{18,2},{26... | collective-permute-start | bytes 18440 | tf_op jit(solution)/shard_map/ppermute | solution.py:46
  34.3 1.7 %collective-permute-done.15 = f32[16,96]{1,0:T(8,128)S(1)} collective-permute-done((f32[16,96]{1,0:T(8,128)S(1)}, f32[16,96]{1,0:T(8,128)S(1)}, u32[]{:S(2)}, u32[]{:S(2)}) %collective-permute-start.15) | collective-permute-done | bytes 6176 | tf_op jit(solution)/shard_map/ppermute | solution.py:46
  36.3 0.5 %collective-permute-done.18 = f32[16,96]{1,0:T(8,128)S(1)} collective-permute-done((f32[16,96]{1,0:T(8,128)S(1)}, f32[16,96]{1,0:T(8,128)S(1)}, u32[]{:S(2)}, u32[]{:S(2)}) %collective-permute-start.18) | collective-permute-done | bytes 6176 | tf_op jit(solution)/shard_map/ppermute | solution.py:46
  37.8 0.8 %copy.120 = bf16[16,2,2,6,256]{4,1,3,2,0:T(2,128)(2,1)} copy(bf16[16,2,2,6,256]{4,0,1,3,2:T(8,128)(2,1)S(1)} %fusion.4) | data formatting | bytes 393216 | tf_op jit(solution)/shard_map/convert_element_type | solution.py:124
  (110 shorter events, 6.7 us)
Async XLA Ops:
  0.0 1.1 %copy-start = (bf16[2,24,12,256]{3,1,2,0:T(8,128)(2,1)S(1)}, bf16[2,24,12,256]{3,1,2,0:T(8,128)(2,1)}, u32[]{:S(2)}) copy-start(bf16[2,24,12,256]{3,1,2,0:T(8,128)(2,1)} %param.6) | copy-start | bytes 884740
  1.3 9.3 %copy-start.2 = (f32[1,9,2,2304]{3,2,1,0:T(2,128)S(1)}, f32[1,9,2,2304]{3,2,1,0:T(2,128)}, u32[]{:S(2)}) copy-start(f32[1,9,2,2304]{3,2,1,0:T(2,128)} %param.8) | copy-start | bytes 497668
  2.6 10.3 %collective-permute-start = (f32[16,96]{1,0:T(8,128)S(1)}, f32[16,96]{1,0:T(8,128)S(1)}, u32[]{:S(2)}, u32[]{:S(2)}) collective-permute-start(f32[16,96]{1,0:T(8,128)S(1)} %fusion.15), channel_id=1, source_target_pairs={{6,0},{4,2},{2,4},{0,6},{7,1},{5,3},{3,5},{1,7},{14,8},{12,10},{10... | collective-permute-start | bytes 18440 | tf_op jit(solution)/shard_map/ppermute | solution.py:46
  7.6 5.2 %collective-permute-start.1 = (f32[16,96]{1,0:T(8,128)S(1)}, f32[16,96]{1,0:T(8,128)S(1)}, u32[]{:S(2)}, u32[]{:S(2)}) collective-permute-start(f32[16,96]{1,0:T(8,128)S(1)} %fusion.15), channel_id=1, source_target_pairs={{2,0},{0,2},{6,4},{4,6},{3,1},{1,3},{7,5},{5,7},{10,8},{8,10},{14,... | collective-permute-start | bytes 18440 | tf_op jit(solution)/shard_map/ppermute | solution.py:46
  7.6 5.2 %collective-permute-start.2 = (f32[16,96]{1,0:T(8,128)S(1)}, f32[16,96]{1,0:T(8,128)S(1)}, u32[]{:S(2)}, u32[]{:S(2)}) collective-permute-start(f32[16,96]{1,0:T(8,128)S(1)} %fusion.15), channel_id=1, source_target_pairs={{1,0},{0,1},{3,2},{2,3},{5,4},{4,5},{7,6},{6,7},{9,8},{8,9},{11,10... | collective-permute-start | bytes 18440 | tf_op jit(solution)/shard_map/ppermute | solution.py:46
  9.1 3.7 %collective-permute-start.3 = (f32[16,96]{1,0:T(8,128)S(1)}, f32[16,96]{1,0:T(8,128)S(1)}, u32[]{:S(2)}, u32[]{:S(2)}) collective-permute-start(f32[16,96]{1,0:T(8,128)S(1)} %fusion.15), channel_id=1, source_target_pairs={{16,0},{24,8},{0,16},{8,24},{17,1},{25,9},{1,17},{9,25},{18,2},{26... | collective-permute-start | bytes 18440 | tf_op jit(solution)/shard_map/ppermute | solution.py:46
  10.6 2.2 %collective-permute-start.4 = (f32[16,96]{1,0:T(8,128)S(1)}, f32[16,96]{1,0:T(8,128)S(1)}, u32[]{:S(2)}, u32[]{:S(2)}) collective-permute-start(f32[16,96]{1,0:T(8,128)S(1)} %fusion.15), channel_id=1, source_target_pairs={{8,0},{0,8},{24,16},{16,24},{9,1},{1,9},{25,17},{17,25},{10,2},{2,... | collective-permute-start | bytes 18440 | tf_op jit(solution)/shard_map/ppermute | solution.py:46
  12.8 0.9 %copy-start.1 = (bf16[16,2,12,256]{3,1,2,0:T(2,128)(2,1)S(1)}, bf16[16,2,12,256]{3,1,2,0:T(2,128)(2,1)}, u32[]{:S(2)}) copy-start(bf16[16,2,12,256]{3,1,2,0:T(2,128)(2,1)} %param.5) | copy-start | bytes 589828
  13.8 0.9 %copy-start.3 = (bf16[2,2,6,6,256]{4,1,3,2,0:T(2,128)(2,1)S(1)}, bf16[2,2,6,6,256]{4,1,3,2,0:T(2,128)(2,1)}, u32[]{:S(2)}) copy-start(bf16[2,2,6,6,256]{4,1,3,2,0:T(2,128)(2,1)} %param.7) | copy-start | bytes 221188
  15.4 5.5 %collective-permute-start.5 = (f32[16,96]{1,0:T(8,128)S(1)}, f32[16,96]{1,0:T(8,128)S(1)}, u32[]{:S(2)}, u32[]{:S(2)}) collective-permute-start(f32[16,96]{1,0:T(8,128)S(1)} %convolution_add_fusion.7), channel_id=1, source_target_pairs={{6,0},{4,2},{2,4},{0,6},{7,1},{5,3},{3,5},{1,7},{14,8},{12,10},{10... | collective-permute-start | bytes 18440 | tf_op jit(solution)/shard_map/ppermute | solution.py:46
  16.4 4.6 %collective-permute-start.6 = (f32[16,96]{1,0:T(8,128)S(1)}, f32[16,96]{1,0:T(8,128)S(1)}, u32[]{:S(2)}, u32[]{:S(2)}) collective-permute-start(f32[16,96]{1,0:T(8,128)S(1)} %convolution_add_fusion.7), channel_id=1, source_target_pairs={{2,0},{0,2},{6,4},{4,6},{3,1},{1,3},{7,5},{5,7},{10,8},{8,10},{14,... | collective-permute-start | bytes 18440 | tf_op jit(solution)/shard_map/ppermute | solution.py:46
  17.6 3.7 %collective-permute-start.7 = (f32[16,96]{1,0:T(8,128)S(1)}, f32[16,96]{1,0:T(8,128)S(1)}, u32[]{:S(2)}, u32[]{:S(2)}) collective-permute-start(f32[16,96]{1,0:T(8,128)S(1)} %convolution_add_fusion.7), channel_id=1, source_target_pairs={{1,0},{0,1},{3,2},{2,3},{5,4},{4,5},{7,6},{6,7},{9,8},{8,9},{11,10... | collective-permute-start | bytes 18440 | tf_op jit(solution)/shard_map/ppermute | solution.py:46
  18.1 3.7 %collective-permute-start.8 = (f32[16,96]{1,0:T(8,128)S(1)}, f32[16,96]{1,0:T(8,128)S(1)}, u32[]{:S(2)}, u32[]{:S(2)}) collective-permute-start(f32[16,96]{1,0:T(8,128)S(1)} %convolution_add_fusion.7), channel_id=1, source_target_pairs={{16,0},{24,8},{0,16},{8,24},{17,1},{25,9},{1,17},{9,25},{18,2},{26... | collective-permute-start | bytes 18440 | tf_op jit(solution)/shard_map/ppermute | solution.py:46
  19.0 2.7 %collective-permute-start.9 = (f32[16,96]{1,0:T(8,128)S(1)}, f32[16,96]{1,0:T(8,128)S(1)}, u32[]{:S(2)}, u32[]{:S(2)}) collective-permute-start(f32[16,96]{1,0:T(8,128)S(1)} %convolution_add_fusion.7), channel_id=1, source_target_pairs={{8,0},{0,8},{24,16},{16,24},{9,1},{1,9},{25,17},{17,25},{10,2},{2,... | collective-permute-start | bytes 18440 | tf_op jit(solution)/shard_map/ppermute | solution.py:46
  22.1 5.6 %collective-permute-start.10 = (f32[16,96]{1,0:T(8,128)S(1)}, f32[16,96]{1,0:T(8,128)S(1)}, u32[]{:S(2)}, u32[]{:S(2)}) collective-permute-start(f32[16,96]{1,0:T(8,128)S(1)} %convolution_add_fusion.5), channel_id=1, source_target_pairs={{6,0},{4,2},{2,4},{0,6},{7,1},{5,3},{3,5},{1,7},{14,8},{12,10},{10... | collective-permute-start | bytes 18440 | tf_op jit(solution)/shard_map/ppermute | solution.py:46
  25.0 3.7 %collective-permute-start.11 = (f32[16,96]{1,0:T(8,128)S(1)}, f32[16,96]{1,0:T(8,128)S(1)}, u32[]{:S(2)}, u32[]{:S(2)}) collective-permute-start(f32[16,96]{1,0:T(8,128)S(1)} %convolution_add_fusion.5), channel_id=1, source_target_pairs={{2,0},{0,2},{6,4},{4,6},{3,1},{1,3},{7,5},{5,7},{10,8},{8,10},{14,... | collective-permute-start | bytes 18440 | tf_op jit(solution)/shard_map/ppermute | solution.py:46
  25.0 3.7 %collective-permute-start.12 = (f32[16,96]{1,0:T(8,128)S(1)}, f32[16,96]{1,0:T(8,128)S(1)}, u32[]{:S(2)}, u32[]{:S(2)}) collective-permute-start(f32[16,96]{1,0:T(8,128)S(1)} %convolution_add_fusion.5), channel_id=1, source_target_pairs={{1,0},{0,1},{3,2},{2,3},{5,4},{4,5},{7,6},{6,7},{9,8},{8,9},{11,10... | collective-permute-start | bytes 18440 | tf_op jit(solution)/shard_map/ppermute | solution.py:46
  26.5 3.7 %collective-permute-start.13 = (f32[16,96]{1,0:T(8,128)S(1)}, f32[16,96]{1,0:T(8,128)S(1)}, u32[]{:S(2)}, u32[]{:S(2)}) collective-permute-start(f32[16,96]{1,0:T(8,128)S(1)} %convolution_add_fusion.5), channel_id=1, source_target_pairs={{16,0},{24,8},{0,16},{8,24},{17,1},{25,9},{1,17},{9,25},{18,2},{26... | collective-permute-start | bytes 18440 | tf_op jit(solution)/shard_map/ppermute | solution.py:46
  27.4 2.7 %collective-permute-start.14 = (f32[16,96]{1,0:T(8,128)S(1)}, f32[16,96]{1,0:T(8,128)S(1)}, u32[]{:S(2)}, u32[]{:S(2)}) collective-permute-start(f32[16,96]{1,0:T(8,128)S(1)} %convolution_add_fusion.5), channel_id=1, source_target_pairs={{8,0},{0,8},{24,16},{16,24},{9,1},{1,9},{25,17},{17,25},{10,2},{2,... | collective-permute-start | bytes 18440 | tf_op jit(solution)/shard_map/ppermute | solution.py:46
  30.5 5.5 %collective-permute-start.15 = (f32[16,96]{1,0:T(8,128)S(1)}, f32[16,96]{1,0:T(8,128)S(1)}, u32[]{:S(2)}, u32[]{:S(2)}) collective-permute-start(f32[16,96]{1,0:T(8,128)S(1)} %convolution_add_fusion.3), channel_id=1, source_target_pairs={{6,0},{4,2},{2,4},{0,6},{7,1},{5,3},{3,5},{1,7},{14,8},{12,10},{10... | collective-permute-start | bytes 18440 | tf_op jit(solution)/shard_map/ppermute | solution.py:46
  31.5 4.5 %collective-permute-start.16 = (f32[16,96]{1,0:T(8,128)S(1)}, f32[16,96]{1,0:T(8,128)S(1)}, u32[]{:S(2)}, u32[]{:S(2)}) collective-permute-start(f32[16,96]{1,0:T(8,128)S(1)} %convolution_add_fusion.3), channel_id=1, source_target_pairs={{2,0},{0,2},{6,4},{4,6},{3,1},{1,3},{7,5},{5,7},{10,8},{8,10},{14,... | collective-permute-start | bytes 18440 | tf_op jit(solution)/shard_map/ppermute | solution.py:46
  32.7 3.7 %collective-permute-start.17 = (f32[16,96]{1,0:T(8,128)S(1)}, f32[16,96]{1,0:T(8,128)S(1)}, u32[]{:S(2)}, u32[]{:S(2)}) collective-permute-start(f32[16,96]{1,0:T(8,128)S(1)} %convolution_add_fusion.3), channel_id=1, source_target_pairs={{1,0},{0,1},{3,2},{2,3},{5,4},{4,5},{7,6},{6,7},{9,8},{8,9},{11,10... | collective-permute-start | bytes 18440 | tf_op jit(solution)/shard_map/ppermute | solution.py:46
  33.2 3.7 %collective-permute-start.18 = (f32[16,96]{1,0:T(8,128)S(1)}, f32[16,96]{1,0:T(8,128)S(1)}, u32[]{:S(2)}, u32[]{:S(2)}) collective-permute-start(f32[16,96]{1,0:T(8,128)S(1)} %convolution_add_fusion.3), channel_id=1, source_target_pairs={{16,0},{24,8},{0,16},{8,24},{17,1},{25,9},{1,17},{9,25},{18,2},{26... | collective-permute-start | bytes 18440 | tf_op jit(solution)/shard_map/ppermute | solution.py:46
  34.1 2.7 %collective-permute-start.19 = (f32[16,96]{1,0:T(8,128)S(1)}, f32[16,96]{1,0:T(8,128)S(1)}, u32[]{:S(2)}, u32[]{:S(2)}) collective-permute-start(f32[16,96]{1,0:T(8,128)S(1)} %convolution_add_fusion.3), channel_id=1, source_target_pairs={{8,0},{0,8},{24,16},{16,24},{9,1},{1,9},{25,17},{17,25},{10,2},{2,... | collective-permute-start | bytes 18440 | tf_op jit(solution)/shard_map/ppermute | solution.py:46

commit v7 on v6

--- a/solution.py
+++ b/solution.py
@@ -66,8 +66,9 @@
     sites = residual.shape[3]
     in_use = (lax.iota(jnp.int32, vec_total)[None, :] < vector_count[:, None]).astype(jnp.float32)[0]
     used = jnp.tile(in_use, 4)
+    used, fine = lax.optimization_barrier((used, residual))
 
-    parts = residual.transpose(1, 2, 0, 3).reshape(2, 2, 6, rhs_count, sites)
+    parts = fine.transpose(1, 2, 0, 3).reshape(2, 2, 6, rhs_count, sites)
     fine_rows = jnp.stack(
         [jnp.concatenate([parts[0], parts[1]], 2), jnp.concatenate([parts[1], -parts[0]], 2)]
     )
@@ -109,7 +110,7 @@
         moved = [fetch(coarse, link) for link in order]
         kept = half + apply(coarse, own)
         if sweep_id == 1:
-            rows, clover, _ = lax.optimization_barrier((residual, clover_inverse, coarse))
+            rows, clover, kept = lax.optimization_barrier((residual, clover_inverse, kept))
             local_real, local_imag = local_term(rows, clover)
         coarse = kept + apply(jnp.concatenate(moved, 1), around)
 

time: 38.8 us -> 36.8 us (0.948)
  waiting for transfers between devices: 7.5 us -> 4.49 us
  starting transfers between devices: 20.7 us -> 22.2 us
  local copies, waits for them, and re-layouts: 5.61 us -> 5.02 us
    ppermute x20, waiting for transfers between devices: 7.5 us -> 4.49 us  [fetch(): lax.ppermute(block, axis, [(source, i) for i, source in enumerate(sources)])]
    unnamed x9 -> x8, local copies, waits for them, and re-layouts: 2.42 us -> 0.87 us
    ppermute x20, starting transfers between devices: 20.7 us -> 22.2 us  [fetch(): lax.ppermute(block, axis, [(source, i) for i, source in enumerate(sources)])]
    optimization_barrier x0 -> x1, local copies, waits for them, and re-layouts: none -> 0.96 us  [body(): used, fine = lax.optimization_barrier((used, residual))]
  transfers between devices with their start and end apart: 20 -> 20, of which waited for: 8 -> 6; matrix products, arithmetic and copies ran while one was open for 7% -> 9% of each run, Pallas kernels for 0% -> 0%
where the time goes in v7:
time: 36.8 us; the launch traced here: 36.6 us
  starting transfers between devices  22.2 us (60%)
  local copies, waits for them, and re-layouts  5.02 us (14%)
  waiting for transfers between devices  4.49 us (12%)
  matrix products  2.37 us (6%)
  other arithmetic  1.34 us (4%)
  between operations  1.22 us (3%)
    ppermute x20, starting transfers between devices, fetch(): lax.ppermute(block, axis, [(source, i) for i, source in enumerate(sources)])  22.2 us
    ppermute x20, waiting for transfers between devices, fetch(): lax.ppermute(block, axis, [(source, i) for i, source in enumerate(sources)])  4.49 us
    dot_general x8, matrix products, apply(): lax.dot_general(vector, matrix, (((1,), (1,)), ((), ())), precision=exact)  1.89 us
    optimization_barrier x1, local copies, waits for them, and re-layouts, body(): used, fine = lax.optimization_barrier((used, residual))  0.96 us
    squeeze x12, local copies, waits for them, and re-layouts, real_form(): upper = jnp.concatenate([matrix[0], -matrix[1]], 1)  0.89 us
    unnamed x8, local copies, waits for them, and re-layouts  0.87 us
    convert_element_type x1, local copies, waits for them, and re-layouts, body(): return result.reshape(rhs_count, 2, 12, sites).astype(jnp.bfloat16)  0.83 us
  transfers between devices with their start and end apart: 20, of which 6 were waited for; matrix products, arithmetic and copies ran while one was open for 9% of the time, Pallas kernels for 0%

profile of v7, /device:TPU:0, one launch (start us, length us, event | category | flops | bytes accessed | tf_op | source)
XLA Modules:
  0.0 36.6 jit_solution(4088141477861162874)
XLA Ops:
  0.8 1.0 %copy.138 = bf16[16,2,12,256]{3,0,2,1:T(8,128)(2,1)S(1)} copy(bf16[16,2,12,256]{3,1,2,0:T(2,128)(2,1)} %param.5) | data formatting | bytes 393216 | tf_op jit(solution)/shard_map/optimization_barrier | solution.py:69
  2.6 5.1 %collective-permute-start = (f32[16,96]{1,0:T(8,128)S(1)}, f32[16,96]{1,0:T(8,128)S(1)}, u32[]{:S(2)}, u32[]{:S(2)}) collective-permute-start(f32[16,96]{1,0:T(8,128)S(1)} %fusion.15), channel_id=1, source_target_pairs={{6,0},{4,2},{2,4},{0,6},{7,1},{5,3},{3,5},{1,7},{14,8},{12,10},{10... | collective-permute-start | bytes 18440 | tf_op jit(solution)/shard_map/ppermute | solution.py:46
  7.6 1.5 %collective-permute-start.2 = (f32[16,96]{1,0:T(8,128)S(1)}, f32[16,96]{1,0:T(8,128)S(1)}, u32[]{:S(2)}, u32[]{:S(2)}) collective-permute-start(f32[16,96]{1,0:T(8,128)S(1)} %fusion.15), channel_id=1, source_target_pairs={{1,0},{0,1},{3,2},{2,3},{5,4},{4,5},{7,6},{6,7},{9,8},{8,9},{11,10... | collective-permute-start | bytes 18440 | tf_op jit(solution)/shard_map/ppermute | solution.py:46
  9.1 1.5 %collective-permute-start.3 = (f32[16,96]{1,0:T(8,128)S(1)}, f32[16,96]{1,0:T(8,128)S(1)}, u32[]{:S(2)}, u32[]{:S(2)}) collective-permute-start(f32[16,96]{1,0:T(8,128)S(1)} %fusion.15), channel_id=1, source_target_pairs={{16,0},{24,8},{0,16},{8,24},{17,1},{25,9},{1,17},{9,25},{18,2},{26... | collective-permute-start | bytes 18440 | tf_op jit(solution)/shard_map/ppermute | solution.py:46
  13.2 0.3 convolution_add_fusion.6
  13.5 0.9 %collective-permute-start.5 = (f32[16,96]{1,0:T(8,128)S(1)}, f32[16,96]{1,0:T(8,128)S(1)}, u32[]{:S(2)}, u32[]{:S(2)}) collective-permute-start(f32[16,96]{1,0:T(8,128)S(1)} %convolution_add_fusion.7), channel_id=1, source_target_pairs={{6,0},{4,2},{2,4},{0,6},{7,1},{5,3},{3,5},{1,7},{14,8},{12,10},{10... | collective-permute-start | bytes 18440 | tf_op jit(solution)/shard_map/ppermute | solution.py:46
  14.4 1.2 %collective-permute-start.6 = (f32[16,96]{1,0:T(8,128)S(1)}, f32[16,96]{1,0:T(8,128)S(1)}, u32[]{:S(2)}, u32[]{:S(2)}) collective-permute-start(f32[16,96]{1,0:T(8,128)S(1)} %convolution_add_fusion.7), channel_id=1, source_target_pairs={{2,0},{0,2},{6,4},{4,6},{3,1},{1,3},{7,5},{5,7},{10,8},{8,10},{14,... | collective-permute-start | bytes 18440 | tf_op jit(solution)/shard_map/ppermute | solution.py:46
  15.6 0.5 %collective-permute-start.7 = (f32[16,96]{1,0:T(8,128)S(1)}, f32[16,96]{1,0:T(8,128)S(1)}, u32[]{:S(2)}, u32[]{:S(2)}) collective-permute-start(f32[16,96]{1,0:T(8,128)S(1)} %convolution_add_fusion.7), channel_id=1, source_target_pairs={{1,0},{0,1},{3,2},{2,3},{5,4},{4,5},{7,6},{6,7},{9,8},{8,9},{11,10... | collective-permute-start | bytes 18440 | tf_op jit(solution)/shard_map/ppermute | solution.py:46
  16.1 1.4 %collective-permute-start.8 = (f32[16,96]{1,0:T(8,128)S(1)}, f32[16,96]{1,0:T(8,128)S(1)}, u32[]{:S(2)}, u32[]{:S(2)}) collective-permute-start(f32[16,96]{1,0:T(8,128)S(1)} %convolution_add_fusion.7), channel_id=1, source_target_pairs={{16,0},{24,8},{0,16},{8,24},{17,1},{25,9},{1,17},{9,25},{18,2},{26... | collective-permute-start | bytes 18440 | tf_op jit(solution)/shard_map/ppermute | solution.py:46
  17.7 0.9 %copy-done.3 = bf16[2,2,6,6,256]{4,1,3,2,0:T(2,128)(2,1)S(1)} copy-done((bf16[2,2,6,6,256]{4,1,3,2,0:T(2,128)(2,1)S(1)}, bf16[2,2,6,6,256]{4,1,3,2,0:T(2,128)(2,1)}, u32[]{:S(2)}) %copy-start.3) | copy-done | bytes 73752
  19.3 0.5 %collective-permute-done.8 = f32[16,96]{1,0:T(8,128)S(1)} collective-permute-done((f32[16,96]{1,0:T(8,128)S(1)}, f32[16,96]{1,0:T(8,128)S(1)}, u32[]{:S(2)}, u32[]{:S(2)}) %collective-permute-start.8) | collective-permute-done | bytes 6176 | tf_op jit(solution)/shard_map/ppermute | solution.py:46
  20.1 2.9 %collective-permute-start.10 = (f32[16,96]{1,0:T(8,128)S(1)}, f32[16,96]{1,0:T(8,128)S(1)}, u32[]{:S(2)}, u32[]{:S(2)}) collective-permute-start(f32[16,96]{1,0:T(8,128)S(1)} %convolution_add_fusion.5), channel_id=1, source_target_pairs={{6,0},{4,2},{2,4},{0,6},{7,1},{5,3},{3,5},{1,7},{14,8},{12,10},{10... | collective-permute-start | bytes 18440 | tf_op jit(solution)/shard_map/ppermute | solution.py:46
  23.0 1.5 %collective-permute-start.12 = (f32[16,96]{1,0:T(8,128)S(1)}, f32[16,96]{1,0:T(8,128)S(1)}, u32[]{:S(2)}, u32[]{:S(2)}) collective-permute-start(f32[16,96]{1,0:T(8,128)S(1)} %convolution_add_fusion.5), channel_id=1, source_target_pairs={{1,0},{0,1},{3,2},{2,3},{5,4},{4,5},{7,6},{6,7},{9,8},{8,9},{11,10... | collective-permute-start | bytes 18440 | tf_op jit(solution)/shard_map/ppermute | solution.py:46
  24.5 1.4 %collective-permute-start.13 = (f32[16,96]{1,0:T(8,128)S(1)}, f32[16,96]{1,0:T(8,128)S(1)}, u32[]{:S(2)}, u32[]{:S(2)}) collective-permute-start(f32[16,96]{1,0:T(8,128)S(1)} %convolution_add_fusion.5), channel_id=1, source_target_pairs={{16,0},{24,8},{0,16},{8,24},{17,1},{25,9},{1,17},{9,25},{18,2},{26... | collective-permute-start | bytes 18440 | tf_op jit(solution)/shard_map/ppermute | solution.py:46
  26.2 0.4 %collective-permute-done.11 = f32[16,96]{1,0:T(8,128)S(1)} collective-permute-done((f32[16,96]{1,0:T(8,128)S(1)}, f32[16,96]{1,0:T(8,128)S(1)}, u32[]{:S(2)}, u32[]{:S(2)}) %collective-permute-start.11) | collective-permute-done | bytes 6176 | tf_op jit(solution)/shard_map/ppermute | solution.py:46
  26.7 1.5 %collective-permute-done.13 = f32[16,96]{1,0:T(8,128)S(1)} collective-permute-done((f32[16,96]{1,0:T(8,128)S(1)}, f32[16,96]{1,0:T(8,128)S(1)}, u32[]{:S(2)}, u32[]{:S(2)}) %collective-permute-start.13) | collective-permute-done | bytes 6176 | tf_op jit(solution)/shard_map/ppermute | solution.py:46
  28.5 1.1 %collective-permute-start.15 = (f32[16,96]{1,0:T(8,128)S(1)}, f32[16,96]{1,0:T(8,128)S(1)}, u32[]{:S(2)}, u32[]{:S(2)}) collective-permute-start(f32[16,96]{1,0:T(8,128)S(1)} %convolution_add_fusion.3), channel_id=1, source_target_pairs={{6,0},{4,2},{2,4},{0,6},{7,1},{5,3},{3,5},{1,7},{14,8},{12,10},{10... | collective-permute-start | bytes 18440 | tf_op jit(solution)/shard_map/ppermute | solution.py:46
  29.5 1.1 %collective-permute-start.16 = (f32[16,96]{1,0:T(8,128)S(1)}, f32[16,96]{1,0:T(8,128)S(1)}, u32[]{:S(2)}, u32[]{:S(2)}) collective-permute-start(f32[16,96]{1,0:T(8,128)S(1)} %convolution_add_fusion.3), channel_id=1, source_target_pairs={{2,0},{0,2},{6,4},{4,6},{3,1},{1,3},{7,5},{5,7},{10,8},{8,10},{14,... | collective-permute-start | bytes 18440 | tf_op jit(solution)/shard_map/ppermute | solution.py:46
  30.7 0.5 %collective-permute-start.17 = (f32[16,96]{1,0:T(8,128)S(1)}, f32[16,96]{1,0:T(8,128)S(1)}, u32[]{:S(2)}, u32[]{:S(2)}) collective-permute-start(f32[16,96]{1,0:T(8,128)S(1)} %convolution_add_fusion.3), channel_id=1, source_target_pairs={{1,0},{0,1},{3,2},{2,3},{5,4},{4,5},{7,6},{6,7},{9,8},{8,9},{11,10... | collective-permute-start | bytes 18440 | tf_op jit(solution)/shard_map/ppermute | solution.py:46
  31.2 1.4 %collective-permute-start.18 = (f32[16,96]{1,0:T(8,128)S(1)}, f32[16,96]{1,0:T(8,128)S(1)}, u32[]{:S(2)}, u32[]{:S(2)}) collective-permute-start(f32[16,96]{1,0:T(8,128)S(1)} %convolution_add_fusion.3), channel_id=1, source_target_pairs={{16,0},{24,8},{0,16},{8,24},{17,1},{25,9},{1,17},{9,25},{18,2},{26... | collective-permute-start | bytes 18440 | tf_op jit(solution)/shard_map/ppermute | solution.py:46
  32.9 1.1 %collective-permute-done.15 = f32[16,96]{1,0:T(8,128)S(1)} collective-permute-done((f32[16,96]{1,0:T(8,128)S(1)}, f32[16,96]{1,0:T(8,128)S(1)}, u32[]{:S(2)}, u32[]{:S(2)}) %collective-permute-start.15) | collective-permute-done | bytes 6176 | tf_op jit(solution)/shard_map/ppermute | solution.py:46
  34.0 0.3 collective-permute-done.17
  34.3 0.5 %collective-permute-done.18 = f32[16,96]{1,0:T(8,128)S(1)} collective-permute-done((f32[16,96]{1,0:T(8,128)S(1)}, f32[16,96]{1,0:T(8,128)S(1)}, u32[]{:S(2)}, u32[]{:S(2)}) %collective-permute-start.18) | collective-permute-done | bytes 6176 | tf_op jit(solution)/shard_map/ppermute | solution.py:46
  35.8 0.8 %copy.120 = bf16[16,2,2,6,256]{4,1,3,2,0:T(2,128)(2,1)} copy(bf16[16,2,2,6,256]{4,0,1,3,2:T(8,128)(2,1)S(1)} %fusion.4) | data formatting | bytes 393216 | tf_op jit(solution)/shard_map/convert_element_type | solution.py:125
  (110 shorter events, 5.9 us)
Async XLA Ops:
  0.0 1.9 %copy-start = (bf16[2,24,12,256]{3,1,2,0:T(8,128)(2,1)S(1)}, bf16[2,24,12,256]{3,1,2,0:T(8,128)(2,1)}, u32[]{:S(2)}) copy-start(bf16[2,24,12,256]{3,1,2,0:T(8,128)(2,1)} %param.6) | copy-start | bytes 884740
  2.1 8.5 %copy-start.2 = (f32[1,9,2,2304]{3,2,1,0:T(2,128)S(1)}, f32[1,9,2,2304]{3,2,1,0:T(2,128)}, u32[]{:S(2)}) copy-start(f32[1,9,2,2304]{3,2,1,0:T(2,128)} %param.8) | copy-start | bytes 497668
  2.6 10.2 %collective-permute-start = (f32[16,96]{1,0:T(8,128)S(1)}, f32[16,96]{1,0:T(8,128)S(1)}, u32[]{:S(2)}, u32[]{:S(2)}) collective-permute-start(f32[16,96]{1,0:T(8,128)S(1)} %fusion.15), channel_id=1, source_target_pairs={{6,0},{4,2},{2,4},{0,6},{7,1},{5,3},{3,5},{1,7},{14,8},{12,10},{10... | collective-permute-start | bytes 18440 | tf_op jit(solution)/shard_map/ppermute | solution.py:46
  7.6 5.2 %collective-permute-start.1 = (f32[16,96]{1,0:T(8,128)S(1)}, f32[16,96]{1,0:T(8,128)S(1)}, u32[]{:S(2)}, u32[]{:S(2)}) collective-permute-start(f32[16,96]{1,0:T(8,128)S(1)} %fusion.15), channel_id=1, source_target_pairs={{2,0},{0,2},{6,4},{4,6},{3,1},{1,3},{7,5},{5,7},{10,8},{8,10},{14,... | collective-permute-start | bytes 18440 | tf_op jit(solution)/shard_map/ppermute | solution.py:46
  7.6 5.2 %collective-permute-start.2 = (f32[16,96]{1,0:T(8,128)S(1)}, f32[16,96]{1,0:T(8,128)S(1)}, u32[]{:S(2)}, u32[]{:S(2)}) collective-permute-start(f32[16,96]{1,0:T(8,128)S(1)} %fusion.15), channel_id=1, source_target_pairs={{1,0},{0,1},{3,2},{2,3},{5,4},{4,5},{7,6},{6,7},{9,8},{8,9},{11,10... | collective-permute-start | bytes 18440 | tf_op jit(solution)/shard_map/ppermute | solution.py:46
  9.1 3.7 %collective-permute-start.3 = (f32[16,96]{1,0:T(8,128)S(1)}, f32[16,96]{1,0:T(8,128)S(1)}, u32[]{:S(2)}, u32[]{:S(2)}) collective-permute-start(f32[16,96]{1,0:T(8,128)S(1)} %fusion.15), channel_id=1, source_target_pairs={{16,0},{24,8},{0,16},{8,24},{17,1},{25,9},{1,17},{9,25},{18,2},{26... | collective-permute-start | bytes 18440 | tf_op jit(solution)/shard_map/ppermute | solution.py:46
  10.6 2.2 %collective-permute-start.4 = (f32[16,96]{1,0:T(8,128)S(1)}, f32[16,96]{1,0:T(8,128)S(1)}, u32[]{:S(2)}, u32[]{:S(2)}) collective-permute-start(f32[16,96]{1,0:T(8,128)S(1)} %fusion.15), channel_id=1, source_target_pairs={{8,0},{0,8},{24,16},{16,24},{9,1},{1,9},{25,17},{17,25},{10,2},{2,... | collective-permute-start | bytes 18440 | tf_op jit(solution)/shard_map/ppermute | solution.py:46
  12.9 4.6 %copy-start.1 = (bf16[16,2,12,256]{3,1,2,0:T(2,128)(2,1)S(1)}, bf16[16,2,12,256]{3,1,2,0:T(2,128)(2,1)}, u32[]{:S(2)}) copy-start(bf16[16,2,12,256]{3,1,2,0:T(2,128)(2,1)} %param.5) | copy-start | bytes 589828
  13.5 5.8 %collective-permute-start.5 = (f32[16,96]{1,0:T(8,128)S(1)}, f32[16,96]{1,0:T(8,128)S(1)}, u32[]{:S(2)}, u32[]{:S(2)}) collective-permute-start(f32[16,96]{1,0:T(8,128)S(1)} %convolution_add_fusion.7), channel_id=1, source_target_pairs={{6,0},{4,2},{2,4},{0,6},{7,1},{5,3},{3,5},{1,7},{14,8},{12,10},{10... | collective-permute-start | bytes 18440 | tf_op jit(solution)/shard_map/ppermute | solution.py:46
  14.4 4.9 %collective-permute-start.6 = (f32[16,96]{1,0:T(8,128)S(1)}, f32[16,96]{1,0:T(8,128)S(1)}, u32[]{:S(2)}, u32[]{:S(2)}) collective-permute-start(f32[16,96]{1,0:T(8,128)S(1)} %convolution_add_fusion.7), channel_id=1, source_target_pairs={{2,0},{0,2},{6,4},{4,6},{3,1},{1,3},{7,5},{5,7},{10,8},{8,10},{14,... | collective-permute-start | bytes 18440 | tf_op jit(solution)/shard_map/ppermute | solution.py:46
  15.6 3.7 %collective-permute-start.7 = (f32[16,96]{1,0:T(8,128)S(1)}, f32[16,96]{1,0:T(8,128)S(1)}, u32[]{:S(2)}, u32[]{:S(2)}) collective-permute-start(f32[16,96]{1,0:T(8,128)S(1)} %convolution_add_fusion.7), channel_id=1, source_target_pairs={{1,0},{0,1},{3,2},{2,3},{5,4},{4,5},{7,6},{6,7},{9,8},{8,9},{11,10... | collective-permute-start | bytes 18440 | tf_op jit(solution)/shard_map/ppermute | solution.py:46
  16.1 3.7 %collective-permute-start.8 = (f32[16,96]{1,0:T(8,128)S(1)}, f32[16,96]{1,0:T(8,128)S(1)}, u32[]{:S(2)}, u32[]{:S(2)}) collective-permute-start(f32[16,96]{1,0:T(8,128)S(1)} %convolution_add_fusion.7), channel_id=1, source_target_pairs={{16,0},{24,8},{0,16},{8,24},{17,1},{25,9},{1,17},{9,25},{18,2},{26... | collective-permute-start | bytes 18440 | tf_op jit(solution)/shard_map/ppermute | solution.py:46
  17.6 2.2 %collective-permute-start.9 = (f32[16,96]{1,0:T(8,128)S(1)}, f32[16,96]{1,0:T(8,128)S(1)}, u32[]{:S(2)}, u32[]{:S(2)}) collective-permute-start(f32[16,96]{1,0:T(8,128)S(1)} %convolution_add_fusion.7), channel_id=1, source_target_pairs={{8,0},{0,8},{24,16},{16,24},{9,1},{1,9},{25,17},{17,25},{10,2},{2,... | collective-permute-start | bytes 18440 | tf_op jit(solution)/shard_map/ppermute | solution.py:46
  17.7 0.9 %copy-start.3 = (bf16[2,2,6,6,256]{4,1,3,2,0:T(2,128)(2,1)S(1)}, bf16[2,2,6,6,256]{4,1,3,2,0:T(2,128)(2,1)}, u32[]{:S(2)}) copy-start(bf16[2,2,6,6,256]{4,1,3,2,0:T(2,128)(2,1)} %param.7) | copy-start | bytes 221188
  20.1 6.1 %collective-permute-start.10 = (f32[16,96]{1,0:T(8,128)S(1)}, f32[16,96]{1,0:T(8,128)S(1)}, u32[]{:S(2)}, u32[]{:S(2)}) collective-permute-start(f32[16,96]{1,0:T(8,128)S(1)} %convolution_add_fusion.5), channel_id=1, source_target_pairs={{6,0},{4,2},{2,4},{0,6},{7,1},{5,3},{3,5},{1,7},{14,8},{12,10},{10... | collective-permute-start | bytes 18440 | tf_op jit(solution)/shard_map/ppermute | solution.py:46
  23.0 3.7 %collective-permute-start.11 = (f32[16,96]{1,0:T(8,128)S(1)}, f32[16,96]{1,0:T(8,128)S(1)}, u32[]{:S(2)}, u32[]{:S(2)}) collective-permute-start(f32[16,96]{1,0:T(8,128)S(1)} %convolution_add_fusion.5), channel_id=1, source_target_pairs={{2,0},{0,2},{6,4},{4,6},{3,1},{1,3},{7,5},{5,7},{10,8},{8,10},{14,... | collective-permute-start | bytes 18440 | tf_op jit(solution)/shard_map/ppermute | solution.py:46
  23.0 3.7 %collective-permute-start.12 = (f32[16,96]{1,0:T(8,128)S(1)}, f32[16,96]{1,0:T(8,128)S(1)}, u32[]{:S(2)}, u32[]{:S(2)}) collective-permute-start(f32[16,96]{1,0:T(8,128)S(1)} %convolution_add_fusion.5), channel_id=1, source_target_pairs={{1,0},{0,1},{3,2},{2,3},{5,4},{4,5},{7,6},{6,7},{9,8},{8,9},{11,10... | collective-permute-start | bytes 18440 | tf_op jit(solution)/shard_map/ppermute | solution.py:46
  24.5 3.7 %collective-permute-start.13 = (f32[16,96]{1,0:T(8,128)S(1)}, f32[16,96]{1,0:T(8,128)S(1)}, u32[]{:S(2)}, u32[]{:S(2)}) collective-permute-start(f32[16,96]{1,0:T(8,128)S(1)} %convolution_add_fusion.5), channel_id=1, source_target_pairs={{16,0},{24,8},{0,16},{8,24},{17,1},{25,9},{1,17},{9,25},{18,2},{26... | collective-permute-start | bytes 18440 | tf_op jit(solution)/shard_map/ppermute | solution.py:46
  26.0 2.2 %collective-permute-start.14 = (f32[16,96]{1,0:T(8,128)S(1)}, f32[16,96]{1,0:T(8,128)S(1)}, u32[]{:S(2)}, u32[]{:S(2)}) collective-permute-start(f32[16,96]{1,0:T(8,128)S(1)} %convolution_add_fusion.5), channel_id=1, source_target_pairs={{8,0},{0,8},{24,16},{16,24},{9,1},{1,9},{25,17},{17,25},{10,2},{2,... | collective-permute-start | bytes 18440 | tf_op jit(solution)/shard_map/ppermute | solution.py:46
  28.5 5.5 %collective-permute-start.15 = (f32[16,96]{1,0:T(8,128)S(1)}, f32[16,96]{1,0:T(8,128)S(1)}, u32[]{:S(2)}, u32[]{:S(2)}) collective-permute-start(f32[16,96]{1,0:T(8,128)S(1)} %convolution_add_fusion.3), channel_id=1, source_target_pairs={{6,0},{4,2},{2,4},{0,6},{7,1},{5,3},{3,5},{1,7},{14,8},{12,10},{10... | collective-permute-start | bytes 18440 | tf_op jit(solution)/shard_map/ppermute | solution.py:46
  29.5 4.5 %collective-permute-start.16 = (f32[16,96]{1,0:T(8,128)S(1)}, f32[16,96]{1,0:T(8,128)S(1)}, u32[]{:S(2)}, u32[]{:S(2)}) collective-permute-start(f32[16,96]{1,0:T(8,128)S(1)} %convolution_add_fusion.3), channel_id=1, source_target_pairs={{2,0},{0,2},{6,4},{4,6},{3,1},{1,3},{7,5},{5,7},{10,8},{8,10},{14,... | collective-permute-start | bytes 18440 | tf_op jit(solution)/shard_map/ppermute | solution.py:46
  30.7 3.7 %collective-permute-start.17 = (f32[16,96]{1,0:T(8,128)S(1)}, f32[16,96]{1,0:T(8,128)S(1)}, u32[]{:S(2)}, u32[]{:S(2)}) collective-permute-start(f32[16,96]{1,0:T(8,128)S(1)} %convolution_add_fusion.3), channel_id=1, source_target_pairs={{1,0},{0,1},{3,2},{2,3},{5,4},{4,5},{7,6},{6,7},{9,8},{8,9},{11,10... | collective-permute-start | bytes 18440 | tf_op jit(solution)/shard_map/ppermute | solution.py:46
  31.2 3.7 %collective-permute-start.18 = (f32[16,96]{1,0:T(8,128)S(1)}, f32[16,96]{1,0:T(8,128)S(1)}, u32[]{:S(2)}, u32[]{:S(2)}) collective-permute-start(f32[16,96]{1,0:T(8,128)S(1)} %convolution_add_fusion.3), channel_id=1, source_target_pairs={{16,0},{24,8},{0,16},{8,24},{17,1},{25,9},{1,17},{9,25},{18,2},{26... | collective-permute-start | bytes 18440 | tf_op jit(solution)/shard_map/ppermute | solution.py:46
  32.6 2.2 %collective-permute-start.19 = (f32[16,96]{1,0:T(8,128)S(1)}, f32[16,96]{1,0:T(8,128)S(1)}, u32[]{:S(2)}, u32[]{:S(2)}) collective-permute-start(f32[16,96]{1,0:T(8,128)S(1)} %convolution_add_fusion.3), channel_id=1, source_target_pairs={{8,0},{0,8},{24,16},{16,24},{9,1},{1,9},{25,17},{17,25},{10,2},{2,... | collective-permute-start | bytes 18440 | tf_op jit(solution)/shard_map/ppermute | solution.py:46

commit v8 on v7

--- a/solution.py
+++ b/solution.py
@@ -35,9 +35,8 @@
         [("gx", tuple((g // plane_y) * plane_y + way[g % plane_y] for g in range(total))) for way in (first, second)]
         + [paired, lax.axis_index("gx") % plane_y]
     )
-    for axis in ("gz", "ta"):
-        first, second, paired = ring(lax.axis_size(axis))
-        links.append([(axis, tuple(first)), (axis, tuple(second)), paired, lax.axis_index(axis)])
+    first, second, paired = ring(lax.axis_size("ta"))
+    links.append([("ta", tuple(first)), ("ta", tuple(second)), paired, lax.axis_index("ta")])
     return links
 
 
@@ -79,7 +78,7 @@
 
     operator = coarse_op.reshape(9, 2, coarse_dim, coarse_dim)
     grouped = {}
-    for way, (first, second, paired, place) in enumerate(routes()):
+    for way, (first, second, paired, place) in zip((0, 1, 3), routes()):
         plus, minus = operator[2 * way + 1], operator[2 * way + 2]
         if first == second:
             grouped[first] = plus + minus
@@ -87,12 +86,15 @@
             swap = (place % 2 == 1) & paired
             grouped[first] = jnp.where(swap, minus, plus)
             grouped[second] = jnp.where(swap, plus, minus)
+    order = sorted(grouped, key=lambda link: ("ta", "gx").index(link[0]))
 
-    def reach(link):
-        axis, sources = link
-        return ("gz", "ta", "gx").index(axis), -max(abs(source - i) for i, source in enumerate(sources))
-
-    order = sorted(grouped, key=reach)
+    depth = lax.axis_size("gz")
+    place = lax.axis_index("gz")
+    column = []
+    for source in range(depth):
+        above = jnp.where(source == (place + 1) % depth, 1.0, 0.0)
+        below = jnp.where(source == (place + depth - 1) % depth, 1.0, 0.0)
+        column.append(above * operator[5] + below * operator[6])
 
     def real_form(matrix):
         upper = jnp.concatenate([matrix[0], -matrix[1]], 1)
@@ -100,14 +102,15 @@
         return omega_step * jnp.concatenate([upper, lower], 0)
 
     own = jnp.eye(2 * coarse_dim, dtype=jnp.float32) - real_form(operator[0])
-    around = jnp.concatenate([-real_form(grouped[link]) for link in order], 1)
+    around = jnp.concatenate([-real_form(part) for part in column + [grouped[link] for link in order]], 1)
 
     def apply(vector, matrix):
         return lax.dot_general(vector, matrix, (((1,), (1,)), ((), ())), precision=exact)
 
     coarse = half
     for sweep_id in range(ITERS - 1):
-        moved = [fetch(coarse, link) for link in order]
+        line = lax.all_to_all(jnp.broadcast_to(coarse, (depth,) + coarse.shape), "gz", 0, 0)
+        moved = [line[source] for source in range(depth)] + [fetch(coarse, link) for link in order]
         kept = half + apply(coarse, own)
         if sweep_id == 1:
             rows, clover, kept = lax.optimization_barrier((residual, clover_inverse, kept))

time: 36.8 us -> 53.4 us (1.45)
  waiting for transfers between devices: 4.49 us -> 12.4 us
  starting transfers between devices: 22.2 us -> 26.9 us
  local copies, waits for them, and re-layouts: 5.02 us -> 8.01 us
    all_to_all x0 -> x4, starting transfers between devices: none -> 16.2 us  [body(): lax.all_to_all(jnp.broadcast_to(coarse, (depth,) + coarse.shape), 'gz', 0...]
    all_to_all x0 -> x4, waiting for transfers between devices: none -> 12.4 us  [body(): lax.all_to_all(jnp.broadcast_to(coarse, (depth,) + coarse.shape), 'gz', 0...]
    ppermute x20 -> x12, starting transfers between devices: 22.2 us -> 10.7 us  [fetch(): lax.ppermute(block, axis, [(source, i) for i, source in enumerate(sources)])]
    ppermute x20 -> x12, waiting for transfers between devices: 4.49 us -> 0.03 us  [fetch(): lax.ppermute(block, axis, [(source, i) for i, source in enumerate(sources)])]
    broadcast_in_dim x0 -> x4, local copies, waits for them, and re-layouts: none -> 2.52 us  [body(): jnp.broadcast_to(coarse, (depth,) + coarse.shape)]
    squeeze x12 -> x16, local copies, waits for them, and re-layouts: 0.89 us -> 1.18 us  [real_form(): upper = jnp.concatenate([matrix[0], -matrix[1]], 1)]
  transfers between devices with their start and end apart: 20 -> 16, of which waited for: 6 -> 4; matrix products, arithmetic and copies ran while one was open for 9% -> 10% of each run, Pallas kernels for 0% -> 0%
where the time goes in v8:
time: 53.4 us; the launch traced here: 52.9 us
  starting transfers between devices  26.9 us (50%)
  waiting for transfers between devices  12.4 us (23%)
  local copies, waits for them, and re-layouts  8.01 us (15%)
  matrix products  2.72 us (5%)
  other arithmetic  1.54 us (3%)
  between operations  1.3 us (2%)
    all_to_all x4, starting transfers between devices, body(): lax.all_to_all(jnp.broadcast_to(coarse, (depth,) + coarse.shape), 'gz', 0...  16.2 us
    all_to_all x4, waiting for transfers between devices, body(): lax.all_to_all(jnp.broadcast_to(coarse, (depth,) + coarse.shape), 'gz', 0...  12.4 us
    ppermute x12, starting transfers between devices, fetch(): lax.ppermute(block, axis, [(source, i) for i, source in enumerate(sources)])  10.7 us
    broadcast_in_dim x4, local copies, waits for them, and re-layouts, body(): jnp.broadcast_to(coarse, (depth,) + coarse.shape)  2.52 us
    dot_general x8, matrix products, apply(): lax.dot_general(vector, matrix, (((1,), (1,)), ((), ())), precision=exact)  2.24 us
    squeeze x16, local copies, waits for them, and re-layouts, real_form(): upper = jnp.concatenate([matrix[0], -matrix[1]], 1)  1.18 us
  transfers between devices with their start and end apart: 16, of which 4 were waited for; matrix products, arithmetic and copies ran while one was open for 10% of the time, Pallas kernels for 0%

profile of v8, /device:TPU:0, one launch (start us, length us, event | category | flops | bytes accessed | tf_op | source)
XLA Modules:
  0.0 52.9 jit_solution(3781871917741997945)
XLA Ops:
  0.8 1.0 %copy.138 = bf16[16,2,12,256]{3,0,2,1:T(8,128)(2,1)S(1)} copy(bf16[16,2,12,256]{3,1,2,0:T(2,128)(2,1)} %param.5) | data formatting | bytes 393216 | tf_op jit(solution)/shard_map/optimization_barrier | solution.py:68
  2.6 2.9 %collective-permute-start = (f32[16,96]{1,0:T(8,128)S(1)}, f32[16,96]{1,0:T(8,128)S(1)}, u32[]{:S(2)}, u32[]{:S(2)}) collective-permute-start(f32[16,96]{1,0:T(8,128)S(1)} %fusion.17), channel_id=1, source_target_pairs={{1,0},{0,1},{3,2},{2,3},{5,4},{4,5},{7,6},{6,7},{9,8},{8,9},{11,10... | collective-permute-start | bytes 18440 | tf_op jit(solution)/shard_map/ppermute | solution.py:45
  5.5 1.5 %collective-permute-start.1 = (f32[16,96]{1,0:T(8,128)S(1)}, f32[16,96]{1,0:T(8,128)S(1)}, u32[]{:S(2)}, u32[]{:S(2)}) collective-permute-start(f32[16,96]{1,0:T(8,128)S(1)} %fusion.17), channel_id=1, source_target_pairs={{16,0},{24,8},{0,16},{8,24},{17,1},{25,9},{1,17},{9,25},{18,2},{26... | collective-permute-start | bytes 18440 | tf_op jit(solution)/shard_map/ppermute | solution.py:45
  7.0 0.6 %broadcast_in_dim.16 = f32[4,16,96]{2,1,0:T(8,128)} broadcast(f32[16,96]{1,0:T(8,128)S(1)} %fusion.17), dimensions={1,2} | broadcast | bytes 30720 | tf_op jit(solution)/shard_map/broadcast_in_dim | solution.py:112
  7.6 4.9 %all-to-all-start = ((f32[4,16,96]{2,1,0:T(8,128)}), f32[4,16,96]{2,1,0:T(8,128)S(1)}, u32[]{:S(2)}, u32[]{:S(2)}) async-start(f32[4,16,96]{2,1,0:T(8,128)} %broadcast_in_dim.16), calls=%async_computation | async-start | bytes 65536 | tf_op jit(solution)/shard_map/all_to_all | solution.py:112
  15.4 2.8 %all-to-all-done = f32[4,16,96]{2,1,0:T(8,128)S(1)} async-done(((f32[4,16,96]{2,1,0:T(8,128)}), f32[4,16,96]{2,1,0:T(8,128)S(1)}, u32[]{:S(2)}, u32[]{:S(2)}) %all-to-all-start) | async-done | bytes 24608 | tf_op jit(solution)/shard_map/all_to_all | solution.py:112
  18.9 0.6 %collective-permute-start.3 = (f32[16,96]{1,0:T(8,128)S(1)}, f32[16,96]{1,0:T(8,128)S(1)}, u32[]{:S(2)}, u32[]{:S(2)}) collective-permute-start(f32[16,96]{1,0:T(8,128)S(1)} %convolution_add_fusion.7), channel_id=1, source_target_pairs={{1,0},{0,1},{3,2},{2,3},{5,4},{4,5},{7,6},{6,7},{9,8},{8,9},{11,10... | collective-permute-start | bytes 18440 | tf_op jit(solution)/shard_map/ppermute | solution.py:45
  19.5 0.5 collective-permute-start.4
  20.0 0.6 %broadcast_in_dim.17 = f32[4,16,96]{2,1,0:T(8,128)} broadcast(f32[16,96]{1,0:T(8,128)S(1)} %convolution_add_fusion.7), dimensions={1,2} | broadcast | bytes 30720 | tf_op jit(solution)/shard_map/broadcast_in_dim | solution.py:112
  20.6 3.3 %all-to-all-start.1 = ((f32[4,16,96]{2,1,0:T(8,128)}), f32[4,16,96]{2,1,0:T(8,128)S(1)}, u32[]{:S(2)}, u32[]{:S(2)}) async-start(f32[4,16,96]{2,1,0:T(8,128)} %broadcast_in_dim.17), calls=%async_computation.1 | async-start | bytes 65536 | tf_op jit(solution)/shard_map/all_to_all | solution.py:112
  24.0 0.9 %copy-done.3 = bf16[2,2,6,6,256]{4,1,3,2,0:T(2,128)(2,1)S(1)} copy-done((bf16[2,2,6,6,256]{4,1,3,2,0:T(2,128)(2,1)S(1)}, bf16[2,2,6,6,256]{4,1,3,2,0:T(2,128)(2,1)}, u32[]{:S(2)}) %copy-start.3) | copy-done | bytes 73752
  25.6 3.9 %all-to-all-done.1 = f32[4,16,96]{2,1,0:T(8,128)S(1)} async-done(((f32[4,16,96]{2,1,0:T(8,128)}), f32[4,16,96]{2,1,0:T(8,128)S(1)}, u32[]{:S(2)}, u32[]{:S(2)}) %all-to-all-start.1) | async-done | bytes 24608 | tf_op jit(solution)/shard_map/all_to_all | solution.py:112
  29.9 0.6 %broadcast_in_dim.18 = f32[4,16,96]{2,1,0:T(8,128)} broadcast(f32[16,96]{1,0:T(8,128)S(1)} %convolution_add_fusion.5), dimensions={1,2} | broadcast | bytes 30720 | tf_op jit(solution)/shard_map/broadcast_in_dim | solution.py:112
  30.6 3.3 %all-to-all-start.2 = ((f32[4,16,96]{2,1,0:T(8,128)}), f32[4,16,96]{2,1,0:T(8,128)S(1)}, u32[]{:S(2)}, u32[]{:S(2)}) async-start(f32[4,16,96]{2,1,0:T(8,128)} %broadcast_in_dim.18), calls=%async_computation.2 | async-start | bytes 65536 | tf_op jit(solution)/shard_map/all_to_all | solution.py:112
  34.1 1.5 %collective-permute-start.6 = (f32[16,96]{1,0:T(8,128)S(1)}, f32[16,96]{1,0:T(8,128)S(1)}, u32[]{:S(2)}, u32[]{:S(2)}) collective-permute-start(f32[16,96]{1,0:T(8,128)S(1)} %convolution_add_fusion.5), channel_id=1, source_target_pairs={{1,0},{0,1},{3,2},{2,3},{5,4},{4,5},{7,6},{6,7},{9,8},{8,9},{11,10... | collective-permute-start | bytes 18440 | tf_op jit(solution)/shard_map/ppermute | solution.py:45
  35.6 1.5 %collective-permute-start.7 = (f32[16,96]{1,0:T(8,128)S(1)}, f32[16,96]{1,0:T(8,128)S(1)}, u32[]{:S(2)}, u32[]{:S(2)}) collective-permute-start(f32[16,96]{1,0:T(8,128)S(1)} %convolution_add_fusion.5), channel_id=1, source_target_pairs={{16,0},{24,8},{0,16},{8,24},{17,1},{25,9},{1,17},{9,25},{18,2},{26... | collective-permute-start | bytes 18440 | tf_op jit(solution)/shard_map/ppermute | solution.py:45
  37.1 2.3 %all-to-all-done.2 = f32[4,16,96]{2,1,0:T(8,128)S(1)} async-done(((f32[4,16,96]{2,1,0:T(8,128)}), f32[4,16,96]{2,1,0:T(8,128)S(1)}, u32[]{:S(2)}, u32[]{:S(2)}) %all-to-all-start.2) | async-done | bytes 24608 | tf_op jit(solution)/shard_map/all_to_all | solution.py:112
  39.9 0.6 %broadcast_in_dim.19 = f32[4,16,96]{2,1,0:T(8,128)} broadcast(f32[16,96]{1,0:T(8,128)S(1)} %convolution_add_fusion.3), dimensions={1,2} | broadcast | bytes 30720 | tf_op jit(solution)/shard_map/broadcast_in_dim | solution.py:112
  40.6 4.8 %all-to-all-start.3 = ((f32[4,16,96]{2,1,0:T(8,128)}), f32[4,16,96]{2,1,0:T(8,128)S(1)}, u32[]{:S(2)}, u32[]{:S(2)}) async-start(f32[4,16,96]{2,1,0:T(8,128)} %broadcast_in_dim.19), calls=%async_computation.3 | async-start | bytes 65536 | tf_op jit(solution)/shard_map/all_to_all | solution.py:112
  45.6 0.6 %collective-permute-start.9 = (f32[16,96]{1,0:T(8,128)S(1)}, f32[16,96]{1,0:T(8,128)S(1)}, u32[]{:S(2)}, u32[]{:S(2)}) collective-permute-start(f32[16,96]{1,0:T(8,128)S(1)} %convolution_add_fusion.3), channel_id=1, source_target_pairs={{1,0},{0,1},{3,2},{2,3},{5,4},{4,5},{7,6},{6,7},{9,8},{8,9},{11,10... | collective-permute-start | bytes 18440 | tf_op jit(solution)/shard_map/ppermute | solution.py:45
  46.2 1.5 %collective-permute-start.10 = (f32[16,96]{1,0:T(8,128)S(1)}, f32[16,96]{1,0:T(8,128)S(1)}, u32[]{:S(2)}, u32[]{:S(2)}) collective-permute-start(f32[16,96]{1,0:T(8,128)S(1)} %convolution_add_fusion.3), channel_id=1, source_target_pairs={{16,0},{24,8},{0,16},{8,24},{17,1},{25,9},{1,17},{9,25},{18,2},{26... | collective-permute-start | bytes 18440 | tf_op jit(solution)/shard_map/ppermute | solution.py:45
  47.7 3.3 %all-to-all-done.3 = f32[4,16,96]{2,1,0:T(8,128)S(1)} async-done(((f32[4,16,96]{2,1,0:T(8,128)}), f32[4,16,96]{2,1,0:T(8,128)S(1)}, u32[]{:S(2)}, u32[]{:S(2)}) %all-to-all-start.3) | async-done | bytes 24608 | tf_op jit(solution)/shard_map/all_to_all | solution.py:112
  51.2 0.3 fusion
  52.1 0.8 %copy.120 = bf16[16,2,2,6,256]{4,1,3,2,0:T(2,128)(2,1)} copy(bf16[16,2,2,6,256]{4,0,1,3,2:T(8,128)(2,1)S(1)} %fusion.4) | data formatting | bytes 393216 | tf_op jit(solution)/shard_map/convert_element_type | solution.py:128
  (120 shorter events, 6.8 us)
Async XLA Ops:
  0.0 1.9 %copy-start = (bf16[2,24,12,256]{3,1,2,0:T(8,128)(2,1)S(1)}, bf16[2,24,12,256]{3,1,2,0:T(8,128)(2,1)}, u32[]{:S(2)}) copy-start(bf16[2,24,12,256]{3,1,2,0:T(8,128)(2,1)} %param.6) | copy-start | bytes 884740
  2.2 10.3 %copy-start.2 = (f32[1,9,2,2304]{3,2,1,0:T(2,128)S(1)}, f32[1,9,2,2304]{3,2,1,0:T(2,128)}, u32[]{:S(2)}) copy-start(f32[1,9,2,2304]{3,2,1,0:T(2,128)} %param.8) | copy-start | bytes 497668
  2.6 15.6 %collective-permute-start = (f32[16,96]{1,0:T(8,128)S(1)}, f32[16,96]{1,0:T(8,128)S(1)}, u32[]{:S(2)}, u32[]{:S(2)}) collective-permute-start(f32[16,96]{1,0:T(8,128)S(1)} %fusion.17), channel_id=1, source_target_pairs={{1,0},{0,1},{3,2},{2,3},{5,4},{4,5},{7,6},{6,7},{9,8},{8,9},{11,10... | collective-permute-start | bytes 18440 | tf_op jit(solution)/shard_map/ppermute | solution.py:45
  5.5 12.7 %collective-permute-start.1 = (f32[16,96]{1,0:T(8,128)S(1)}, f32[16,96]{1,0:T(8,128)S(1)}, u32[]{:S(2)}, u32[]{:S(2)}) collective-permute-start(f32[16,96]{1,0:T(8,128)S(1)} %fusion.17), channel_id=1, source_target_pairs={{16,0},{24,8},{0,16},{8,24},{17,1},{25,9},{1,17},{9,25},{18,2},{26... | collective-permute-start | bytes 18440 | tf_op jit(solution)/shard_map/ppermute | solution.py:45
  7.0 11.2 %collective-permute-start.2 = (f32[16,96]{1,0:T(8,128)S(1)}, f32[16,96]{1,0:T(8,128)S(1)}, u32[]{:S(2)}, u32[]{:S(2)}) collective-permute-start(f32[16,96]{1,0:T(8,128)S(1)} %fusion.17), channel_id=1, source_target_pairs={{8,0},{0,8},{24,16},{16,24},{9,1},{1,9},{25,17},{17,25},{10,2},{2,... | collective-permute-start | bytes 18440 | tf_op jit(solution)/shard_map/ppermute | solution.py:45
  7.6 10.5 %all-to-all-start = ((f32[4,16,96]{2,1,0:T(8,128)}), f32[4,16,96]{2,1,0:T(8,128)S(1)}, u32[]{:S(2)}, u32[]{:S(2)}) async-start(f32[4,16,96]{2,1,0:T(8,128)} %broadcast_in_dim.16), calls=%async_computation | async-start | bytes 65536 | tf_op jit(solution)/shard_map/all_to_all | solution.py:112
  18.6 5.2 %copy-start.1 = (bf16[16,2,12,256]{3,1,2,0:T(2,128)(2,1)S(1)}, bf16[16,2,12,256]{3,1,2,0:T(2,128)(2,1)}, u32[]{:S(2)}) copy-start(bf16[16,2,12,256]{3,1,2,0:T(2,128)(2,1)} %param.5) | copy-start | bytes 589828
  18.9 10.6 %collective-permute-start.3 = (f32[16,96]{1,0:T(8,128)S(1)}, f32[16,96]{1,0:T(8,128)S(1)}, u32[]{:S(2)}, u32[]{:S(2)}) collective-permute-start(f32[16,96]{1,0:T(8,128)S(1)} %convolution_add_fusion.7), channel_id=1, source_target_pairs={{1,0},{0,1},{3,2},{2,3},{5,4},{4,5},{7,6},{6,7},{9,8},{8,9},{11,10... | collective-permute-start | bytes 18440 | tf_op jit(solution)/shard_map/ppermute | solution.py:45
  19.5 10.0 %collective-permute-start.4 = (f32[16,96]{1,0:T(8,128)S(1)}, f32[16,96]{1,0:T(8,128)S(1)}, u32[]{:S(2)}, u32[]{:S(2)}) collective-permute-start(f32[16,96]{1,0:T(8,128)S(1)} %convolution_add_fusion.7), channel_id=1, source_target_pairs={{16,0},{24,8},{0,16},{8,24},{17,1},{25,9},{1,17},{9,25},{18,2},{26... | collective-permute-start | bytes 18440 | tf_op jit(solution)/shard_map/ppermute | solution.py:45
  20.0 9.5 %collective-permute-start.5 = (f32[16,96]{1,0:T(8,128)S(1)}, f32[16,96]{1,0:T(8,128)S(1)}, u32[]{:S(2)}, u32[]{:S(2)}) collective-permute-start(f32[16,96]{1,0:T(8,128)S(1)} %convolution_add_fusion.7), channel_id=1, source_target_pairs={{8,0},{0,8},{24,16},{16,24},{9,1},{1,9},{25,17},{17,25},{10,2},{2,... | collective-permute-start | bytes 18440 | tf_op jit(solution)/shard_map/ppermute | solution.py:45
  20.6 8.9 %all-to-all-start.1 = ((f32[4,16,96]{2,1,0:T(8,128)}), f32[4,16,96]{2,1,0:T(8,128)S(1)}, u32[]{:S(2)}, u32[]{:S(2)}) async-start(f32[4,16,96]{2,1,0:T(8,128)} %broadcast_in_dim.17), calls=%async_computation.1 | async-start | bytes 65536 | tf_op jit(solution)/shard_map/all_to_all | solution.py:112
  24.0 0.9 %copy-start.3 = (bf16[2,2,6,6,256]{4,1,3,2,0:T(2,128)(2,1)S(1)}, bf16[2,2,6,6,256]{4,1,3,2,0:T(2,128)(2,1)}, u32[]{:S(2)}) copy-start(bf16[2,2,6,6,256]{4,1,3,2,0:T(2,128)(2,1)} %param.7) | copy-start | bytes 221188
  30.6 8.9 %all-to-all-start.2 = ((f32[4,16,96]{2,1,0:T(8,128)}), f32[4,16,96]{2,1,0:T(8,128)S(1)}, u32[]{:S(2)}, u32[]{:S(2)}) async-start(f32[4,16,96]{2,1,0:T(8,128)} %broadcast_in_dim.18), calls=%async_computation.2 | async-start | bytes 65536 | tf_op jit(solution)/shard_map/all_to_all | solution.py:112
  34.1 5.4 %collective-permute-start.6 = (f32[16,96]{1,0:T(8,128)S(1)}, f32[16,96]{1,0:T(8,128)S(1)}, u32[]{:S(2)}, u32[]{:S(2)}) collective-permute-start(f32[16,96]{1,0:T(8,128)S(1)} %convolution_add_fusion.5), channel_id=1, source_target_pairs={{1,0},{0,1},{3,2},{2,3},{5,4},{4,5},{7,6},{6,7},{9,8},{8,9},{11,10... | collective-permute-start | bytes 18440 | tf_op jit(solution)/shard_map/ppermute | solution.py:45
  35.6 3.9 %collective-permute-start.7 = (f32[16,96]{1,0:T(8,128)S(1)}, f32[16,96]{1,0:T(8,128)S(1)}, u32[]{:S(2)}, u32[]{:S(2)}) collective-permute-start(f32[16,96]{1,0:T(8,128)S(1)} %convolution_add_fusion.5), channel_id=1, source_target_pairs={{16,0},{24,8},{0,16},{8,24},{17,1},{25,9},{1,17},{9,25},{18,2},{26... | collective-permute-start | bytes 18440 | tf_op jit(solution)/shard_map/ppermute | solution.py:45
  37.1 2.3 %collective-permute-start.8 = (f32[16,96]{1,0:T(8,128)S(1)}, f32[16,96]{1,0:T(8,128)S(1)}, u32[]{:S(2)}, u32[]{:S(2)}) collective-permute-start(f32[16,96]{1,0:T(8,128)S(1)} %convolution_add_fusion.5), channel_id=1, source_target_pairs={{8,0},{0,8},{24,16},{16,24},{9,1},{1,9},{25,17},{17,25},{10,2},{2,... | collective-permute-start | bytes 18440 | tf_op jit(solution)/shard_map/ppermute | solution.py:45
  40.6 10.5 %all-to-all-start.3 = ((f32[4,16,96]{2,1,0:T(8,128)}), f32[4,16,96]{2,1,0:T(8,128)S(1)}, u32[]{:S(2)}, u32[]{:S(2)}) async-start(f32[4,16,96]{2,1,0:T(8,128)} %broadcast_in_dim.19), calls=%async_computation.3 | async-start | bytes 65536 | tf_op jit(solution)/shard_map/all_to_all | solution.py:112
  45.6 5.4 %collective-permute-start.9 = (f32[16,96]{1,0:T(8,128)S(1)}, f32[16,96]{1,0:T(8,128)S(1)}, u32[]{:S(2)}, u32[]{:S(2)}) collective-permute-start(f32[16,96]{1,0:T(8,128)S(1)} %convolution_add_fusion.3), channel_id=1, source_target_pairs={{1,0},{0,1},{3,2},{2,3},{5,4},{4,5},{7,6},{6,7},{9,8},{8,9},{11,10... | collective-permute-start | bytes 18440 | tf_op jit(solution)/shard_map/ppermute | solution.py:45
  46.2 4.9 %collective-permute-start.10 = (f32[16,96]{1,0:T(8,128)S(1)}, f32[16,96]{1,0:T(8,128)S(1)}, u32[]{:S(2)}, u32[]{:S(2)}) collective-permute-start(f32[16,96]{1,0:T(8,128)S(1)} %convolution_add_fusion.3), channel_id=1, source_target_pairs={{16,0},{24,8},{0,16},{8,24},{17,1},{25,9},{1,17},{9,25},{18,2},{26... | collective-permute-start | bytes 18440 | tf_op jit(solution)/shard_map/ppermute | solution.py:45
  47.7 3.3 %collective-permute-start.11 = (f32[16,96]{1,0:T(8,128)S(1)}, f32[16,96]{1,0:T(8,128)S(1)}, u32[]{:S(2)}, u32[]{:S(2)}) collective-permute-start(f32[16,96]{1,0:T(8,128)S(1)} %convolution_add_fusion.3), channel_id=1, source_target_pairs={{8,0},{0,8},{24,16},{16,24},{9,1},{1,9},{25,17},{17,25},{10,2},{2,... | collective-permute-start | bytes 18440 | tf_op jit(solution)/shard_map/ppermute | solution.py:45

commit v9 on v7

--- a/solution.py
+++ b/solution.py
@@ -10,40 +10,64 @@
 exact = lax.Precision.HIGHEST
 
 
-def routes():
-    total = lax.axis_size("gx")
-    plane_y = min(8, total // 2)
-    plane_x = total // plane_y
-
-    def ring(count):
-        up = [(i + 1) % count for i in range(count)]
-        down = [(i - 1) % count for i in range(count)]
-        if count % 2:
-            return up, down, False
-        even = [(up if i % 2 == 0 else down)[i] for i in range(count)]
-        odd = [(down if i % 2 == 0 else up)[i] for i in range(count)]
-        return even, odd, True
-
-    links = []
-    first, second, paired = ring(plane_x)
-    links.append(
-        [("gx", tuple(way[g // plane_y] * plane_y + g % plane_y for g in range(total))) for way in (first, second)]
-        + [paired, lax.axis_index("gx") // plane_y]
-    )
-    first, second, paired = ring(plane_y)
-    links.append(
-        [("gx", tuple((g // plane_y) * plane_y + way[g % plane_y] for g in range(total))) for way in (first, second)]
-        + [paired, lax.axis_index("gx") % plane_y]
-    )
-    for axis in ("gz", "ta"):
-        first, second, paired = ring(lax.axis_size(axis))
-        links.append([(axis, tuple(first)), (axis, tuple(second)), paired, lax.axis_index(axis)])
-    return links
+axes = ("gx", "gz", "ta")
 
 
-def fetch(block, link):
-    axis, sources = link
-    return lax.ppermute(block, axis, [(source, i) for i, source in enumerate(sources)])
+def plan():
+    total, depth, slabs = (lax.axis_size(axis) for axis in axes)
+    plane_y = min(8, total // 2)
+    extents = (total // plane_y, plane_y, depth, slabs)
+    count = total * depth * slabs
+
+    def coordinates(device):
+        group, rest = divmod(device, depth * slabs)
+        return [group // plane_y, group % plane_y, rest // slabs, rest % slabs]
+
+    def device_at(x, y, z, t):
+        return ((x * plane_y + y) * depth + z) * slabs + t
+
+    places = [coordinates(device) for device in range(count)]
+    parity = [sum(place) % 2 for place in places]
+    links = []
+    for dim, extent in enumerate(extents):
+        for first in (0, 1):
+            sources, plus = [], []
+            for place in places:
+                step = 1 if extent % 2 or place[dim] % 2 == 0 else -1
+                step = -step if first == 0 else step
+                moved = list(place)
+                moved[dim] = (place[dim] + step) % extent
+                sources.append(device_at(*moved))
+                plus.append(step == 1)
+            links.append((dim, sources, plus, extent == 2, extent % 2 == 0))
+            if extent == 2:
+                break
+    return links, parity
+
+
+def fetch(block, sources, senders):
+    pairs = [(source, i) for i, source in enumerate(sources) if senders(source)]
+    return lax.ppermute(block, axes, pairs)
+
+
+def exchange(block, links, parity, odd):
+    split = [i for i, (dim, _, _, _, paired) in enumerate(links) if paired and dim in (0, 3)]
+    along_z = [i for i, link in enumerate(links) if link[0] == 2]
+    split += [i for i in along_z[1:] if links[i][4]]
+    middle = [i for i in range(len(links)) if i not in split and links[i][0] != 1]
+    last = [i for i in range(len(links)) if links[i][0] == 1]
+
+    def send(block, chosen, senders):
+        return [fetch(block, links[i][1], senders) for i in chosen]
+
+    from_odd = send(block, split, lambda device: parity[device] == 1)
+    got = dict(zip(middle, send(block, middle, lambda device: True)))
+    block, from_odd = lax.optimization_barrier((block, from_odd))
+    from_even = send(block, split, lambda device: parity[device] == 0)
+    got.update(zip(last, send(block, last, lambda device: True)))
+    for i, first, second in zip(split, from_odd, from_even):
+        got[i] = jnp.where(odd, second, first)
+    return [got[i] for i in range(len(links))]
 
 
 def local_term(residual, clover_inverse):
@@ -78,21 +102,17 @@
     half = omega_step * (jnp.concatenate(pieces, 1) * used)
 
     operator = coarse_op.reshape(9, 2, coarse_dim, coarse_dim)
-    grouped = {}
-    for way, (first, second, paired, place) in enumerate(routes()):
-        plus, minus = operator[2 * way + 1], operator[2 * way + 2]
-        if first == second:
-            grouped[first] = plus + minus
+    links, parity = plan()
+    me = (lax.axis_index("gx") * lax.axis_size("gz") + lax.axis_index("gz")) * lax.axis_size("ta")
+    me = me + lax.axis_index("ta")
+    odd = jnp.asarray(parity, jnp.int32)[me] == 1
+    reached = []
+    for dim, _, plus, merged, _ in links:
+        above, below = operator[2 * dim + 1], operator[2 * dim + 2]
+        if merged:
+            reached.append(above + below)
         else:
-            swap = (place % 2 == 1) & paired
-            grouped[first] = jnp.where(swap, minus, plus)
-            grouped[second] = jnp.where(swap, plus, minus)
-
-    def reach(link):
-        axis, sources = link
-        return ("gz", "ta", "gx").index(axis), -max(abs(source - i) for i, source in enumerate(sources))
-
-    order = sorted(grouped, key=reach)
+            reached.append(jnp.where(jnp.asarray(plus)[me], above, below))
 
     def real_form(matrix):
         upper = jnp.concatenate([matrix[0], -matrix[1]], 1)
@@ -100,14 +120,14 @@
         return omega_step * jnp.concatenate([upper, lower], 0)
 
     own = jnp.eye(2 * coarse_dim, dtype=jnp.float32) - real_form(operator[0])
-    around = jnp.concatenate([-real_form(grouped[link]) for link in order], 1)
+    around = jnp.concatenate([-real_form(part) for part in reached], 1)
 
     def apply(vector, matrix):
         return lax.dot_general(vector, matrix, (((1,), (1,)), ((), ())), precision=exact)
 
     coarse = half
     for sweep_id in range(ITERS - 1):
-        moved = [fetch(coarse, link) for link in order]
+        moved = exchange(coarse, links, parity, odd)
         kept = half + apply(coarse, own)
         if sweep_id == 1:
             rows, clover, kept = lax.optimization_barrier((residual, clover_inverse, kept))

time: 36.8 us -> 71.3 us (1.94)
  starting transfers between devices: 22.2 us -> 50.3 us
  local copies, waits for them, and re-layouts: 5.02 us -> 7.51 us
  other arithmetic: 1.34 us -> 2.66 us
  waiting for transfers between devices: 4.49 us -> 5.51 us
  between operations: 1.22 us -> 2.2 us
    ppermute x20 -> x32, starting transfers between devices: 22.2 us -> 50.3 us  [fetch(): return lax.ppermute(block, axes, pairs)]
    dynamic_slice x0 -> x3, local copies, waits for them, and re-layouts: none -> 1.77 us  [the longest x2 1.18 us: body(): reached.append(jnp.where(jnp.asarray(plus)[me], above, below))]
    add x1, other arithmetic: 0.04 us -> 1.31 us  [body(): reached.append(above + below)]
    ppermute x20 -> x32, waiting for transfers between devices: 4.49 us -> 5.51 us  [fetch(): return lax.ppermute(block, axes, pairs)]
    unnamed x8 -> x14, local copies, waits for them, and re-layouts: 0.87 us -> 1.58 us
  transfers between devices with their start and end apart: 20 -> 32, of which waited for: 6 -> 6; matrix products, arithmetic and copies ran while one was open for 9% -> 9% of each run, Pallas kernels for 0% -> 0%
where the time goes in v9:
time: 71.3 us; the launch traced here: 70.6 us
  starting transfers between devices  50.3 us (71%)
  local copies, waits for them, and re-layouts  7.51 us (11%)
  waiting for transfers between devices  5.51 us (8%)
  other arithmetic  2.66 us (4%)
  matrix products  2.37 us (3%)
  between operations  2.2 us (3%)
    ppermute x32, starting transfers between devices, fetch(): return lax.ppermute(block, axes, pairs)  50.3 us
    ppermute x32, waiting for transfers between devices, fetch(): return lax.ppermute(block, axes, pairs)  5.51 us
    dot_general x8, matrix products, apply(): lax.dot_general(vector, matrix, (((1,), (1,)), ((), ())), precision=exact)  1.89 us
    unnamed x14, local copies, waits for them, and re-layouts  1.58 us
  transfers between devices with their start and end apart: 32, of which 6 were waited for; matrix products, arithmetic and copies ran while one was open for 9% of the time, Pallas kernels for 0%

profile of v9, /device:TPU:0, one launch (start us, length us, event | category | flops | bytes accessed | tf_op | source)
XLA Modules:
  0.0 70.6 jit_solution(13558575598808796864)
XLA Ops:
  3.9 1.3 %collective-permute-start.1 = (f32[16,96]{1,0:T(8,128)S(1)}, f32[16,96]{1,0:T(8,128)S(1)}, u32[]{:S(2)}, u32[]{:S(2)}) collective-permute-start(f32[16,96]{1,0:T(8,128)S(1)} %fusion.15), channel_id=1, source_target_pairs={{1,0},{2,3},{5,4},{6,7},{8,9},{11,10},{12,13},{15,14},{16,17},{19,... | collective-permute-start | bytes 18440 | tf_op jit(solution)/shard_map/ppermute | solution.py:50
  5.2 1.3 %collective-permute-start.2 = (f32[16,96]{1,0:T(8,128)S(1)}, f32[16,96]{1,0:T(8,128)S(1)}, u32[]{:S(2)}, u32[]{:S(2)}) collective-permute-start(f32[16,96]{1,0:T(8,128)S(1)} %fusion.15), channel_id=1, source_target_pairs={{2,0},{1,3},{6,4},{5,7},{11,9},{8,10},{15,13},{12,14},{19,17},{16,... | collective-permute-start | bytes 18440 | tf_op jit(solution)/shard_map/ppermute | solution.py:50
  6.5 7.2 %collective-permute-start.5 = (f32[16,96]{1,0:T(8,128)S(1)}, f32[16,96]{1,0:T(8,128)S(1)}, u32[]{:S(2)}, u32[]{:S(2)}) collective-permute-start(f32[16,96]{1,0:T(8,128)S(1)} %fusion.15), channel_id=1, source_target_pairs={{6,0},{7,1},{4,2},{5,3},{2,4},{3,5},{0,6},{1,7},{14,8},{15,9},{12,... | collective-permute-start | bytes 18440 | tf_op jit(solution)/shard_map/ppermute | solution.py:50
  15.6 1.3 %slice_add_fusion = (f32[1,1,2,2304]{3,2,1,0:T(2,128)S(1)}, f32[1,1,2,2304]{3,2,1,0:T(2,128)S(1)}, f32[1,1,2,2304]{3,2,1,0:T(2,128)S(1)}, f32[1,1,2,2304]{3,2,1,0:T(2,128)S(1)}, f32[1,1,2,2304]{3,2,1,0:T(2,128)S(1)}) fusion(f32[1,9,2,2304]{3,2,1,0:T(2,128)S(1)} %copy-done.2, pred[]{:T(512)} %bitcast.17, pred[]{:T(512)} %bitcast.16), kind=kLoop, calls=%fused_computation.56 | loop fusion | flops 23040 | bytes 239618 | tf_op jit(solution)/shard_map/add | solution.py:113
  22.9 1.3 %collective-permute-start.3 = (f32[16,96]{1,0:T(8,128)S(1)}, f32[16,96]{1,0:T(8,128)S(1)}, u32[]{:S(2)}, u32[]{:S(2)}) collective-permute-start(f32[16,96]{1,0:T(8,128)S(1)} %fusion.15), channel_id=1, source_target_pairs={{17,1},{18,2},{21,5},{22,6},{24,8},{27,11},{28,12},{31,15},{0,16},... | collective-permute-start | bytes 18440 | tf_op jit(solution)/shard_map/ppermute | solution.py:50
  26.2 1.3 %collective-permute-start.10 = (f32[16,96]{1,0:T(8,128)S(1)}, f32[16,96]{1,0:T(8,128)S(1)}, u32[]{:S(2)}, u32[]{:S(2)}) collective-permute-start(f32[16,96]{1,0:T(8,128)S(1)} %convolution_add_fusion.7), channel_id=1, source_target_pairs={{2,0},{1,3},{6,4},{5,7},{11,9},{8,10},{15,13},{12,14},{19,17},{16,... | collective-permute-start | bytes 18440 | tf_op jit(solution)/shard_map/ppermute | solution.py:50
  27.5 1.3 %collective-permute-start.8 = (f32[16,96]{1,0:T(8,128)S(1)}, f32[16,96]{1,0:T(8,128)S(1)}, u32[]{:S(2)}, u32[]{:S(2)}) collective-permute-start(f32[16,96]{1,0:T(8,128)S(1)} %convolution_add_fusion.7), channel_id=1, source_target_pairs={{16,0},{19,3},{20,4},{23,7},{25,9},{26,10},{29,13},{30,14},{1,17},... | collective-permute-start | bytes 18440 | tf_op jit(solution)/shard_map/ppermute | solution.py:50
  28.8 1.3 %collective-permute-start.9 = (f32[16,96]{1,0:T(8,128)S(1)}, f32[16,96]{1,0:T(8,128)S(1)}, u32[]{:S(2)}, u32[]{:S(2)}) collective-permute-start(f32[16,96]{1,0:T(8,128)S(1)} %convolution_add_fusion.7), channel_id=1, source_target_pairs={{1,0},{2,3},{5,4},{6,7},{8,9},{11,10},{12,13},{15,14},{16,17},{19,... | collective-permute-start | bytes 18440 | tf_op jit(solution)/shard_map/ppermute | solution.py:50
  30.1 3.3 %collective-permute-start.13 = (f32[16,96]{1,0:T(8,128)S(1)}, f32[16,96]{1,0:T(8,128)S(1)}, u32[]{:S(2)}, u32[]{:S(2)}) collective-permute-start(f32[16,96]{1,0:T(8,128)S(1)} %convolution_add_fusion.7), channel_id=1, source_target_pairs={{6,0},{7,1},{4,2},{5,3},{2,4},{3,5},{0,6},{1,7},{14,8},{15,9},{12,... | collective-permute-start | bytes 18440 | tf_op jit(solution)/shard_map/ppermute | solution.py:50
  34.6 1.4 %collective-permute-start.15 = (f32[16,96]{1,0:T(8,128)S(1)}, f32[16,96]{1,0:T(8,128)S(1)}, u32[]{:S(2)}, u32[]{:S(2)}) collective-permute-start(f32[16,96]{1,0:T(8,128)S(1)} %convolution_add_fusion.7), channel_id=1, source_target_pairs={{0,1},{3,2},{4,5},{7,6},{9,8},{10,11},{13,12},{14,15},{17,16},{18,... | collective-permute-start | bytes 18440 | tf_op jit(solution)/shard_map/ppermute | solution.py:50
  37.5 1.3 %collective-permute-start.11 = (f32[16,96]{1,0:T(8,128)S(1)}, f32[16,96]{1,0:T(8,128)S(1)}, u32[]{:S(2)}, u32[]{:S(2)}) collective-permute-start(f32[16,96]{1,0:T(8,128)S(1)} %convolution_add_fusion.7), channel_id=1, source_target_pairs={{17,1},{18,2},{21,5},{22,6},{24,8},{27,11},{28,12},{31,15},{0,16},... | collective-permute-start | bytes 18440 | tf_op jit(solution)/shard_map/ppermute | solution.py:50
  40.4 1.3 %collective-permute-start.16 = (f32[16,96]{1,0:T(8,128)S(1)}, f32[16,96]{1,0:T(8,128)S(1)}, u32[]{:S(2)}, u32[]{:S(2)}) collective-permute-start(f32[16,96]{1,0:T(8,128)S(1)} %convolution_add_fusion.5), channel_id=1, source_target_pairs={{16,0},{19,3},{20,4},{23,7},{25,9},{26,10},{29,13},{30,14},{1,17},... | collective-permute-start | bytes 18440 | tf_op jit(solution)/shard_map/ppermute | solution.py:50
  41.8 1.3 %collective-permute-start.17 = (f32[16,96]{1,0:T(8,128)S(1)}, f32[16,96]{1,0:T(8,128)S(1)}, u32[]{:S(2)}, u32[]{:S(2)}) collective-permute-start(f32[16,96]{1,0:T(8,128)S(1)} %convolution_add_fusion.5), channel_id=1, source_target_pairs={{1,0},{2,3},{5,4},{6,7},{8,9},{11,10},{12,13},{15,14},{16,17},{19,... | collective-permute-start | bytes 18440 | tf_op jit(solution)/shard_map/ppermute | solution.py:50
  43.1 1.3 %collective-permute-start.18 = (f32[16,96]{1,0:T(8,128)S(1)}, f32[16,96]{1,0:T(8,128)S(1)}, u32[]{:S(2)}, u32[]{:S(2)}) collective-permute-start(f32[16,96]{1,0:T(8,128)S(1)} %convolution_add_fusion.5), channel_id=1, source_target_pairs={{2,0},{1,3},{6,4},{5,7},{11,9},{8,10},{15,13},{12,14},{19,17},{16,... | collective-permute-start | bytes 18440 | tf_op jit(solution)/shard_map/ppermute | solution.py:50
  44.6 3.7 %collective-permute-start.21 = (f32[16,96]{1,0:T(8,128)S(1)}, f32[16,96]{1,0:T(8,128)S(1)}, u32[]{:S(2)}, u32[]{:S(2)}) collective-permute-start(f32[16,96]{1,0:T(8,128)S(1)} %convolution_add_fusion.5), channel_id=1, source_target_pairs={{6,0},{7,1},{4,2},{5,3},{2,4},{3,5},{0,6},{1,7},{14,8},{15,9},{12,... | collective-permute-start | bytes 18440 | tf_op jit(solution)/shard_map/ppermute | solution.py:50
  48.6 1.6 %collective-permute-start.23 = (f32[16,96]{1,0:T(8,128)S(1)}, f32[16,96]{1,0:T(8,128)S(1)}, u32[]{:S(2)}, u32[]{:S(2)}) collective-permute-start(f32[16,96]{1,0:T(8,128)S(1)} %convolution_add_fusion.5), channel_id=1, source_target_pairs={{0,1},{3,2},{4,5},{7,6},{9,8},{10,11},{13,12},{14,15},{17,16},{18,... | collective-permute-start | bytes 18440 | tf_op jit(solution)/shard_map/ppermute | solution.py:50
  50.5 1.3 %collective-permute-start.22 = (f32[16,96]{1,0:T(8,128)S(1)}, f32[16,96]{1,0:T(8,128)S(1)}, u32[]{:S(2)}, u32[]{:S(2)}) collective-permute-start(f32[16,96]{1,0:T(8,128)S(1)} %convolution_add_fusion.5), channel_id=1, source_target_pairs={{3,1},{0,2},{7,5},{4,6},{10,8},{9,11},{14,12},{13,15},{18,16},{17,... | collective-permute-start | bytes 18440 | tf_op jit(solution)/shard_map/ppermute | solution.py:50
  51.8 1.3 %collective-permute-start.19 = (f32[16,96]{1,0:T(8,128)S(1)}, f32[16,96]{1,0:T(8,128)S(1)}, u32[]{:S(2)}, u32[]{:S(2)}) collective-permute-start(f32[16,96]{1,0:T(8,128)S(1)} %convolution_add_fusion.5), channel_id=1, source_target_pairs={{17,1},{18,2},{21,5},{22,6},{24,8},{27,11},{28,12},{31,15},{0,16},... | collective-permute-start | bytes 18440 | tf_op jit(solution)/shard_map/ppermute | solution.py:50
  54.8 1.3 %collective-permute-start.24 = (f32[16,96]{1,0:T(8,128)S(1)}, f32[16,96]{1,0:T(8,128)S(1)}, u32[]{:S(2)}, u32[]{:S(2)}) collective-permute-start(f32[16,96]{1,0:T(8,128)S(1)} %convolution_add_fusion.3), channel_id=1, source_target_pairs={{16,0},{19,3},{20,4},{23,7},{25,9},{26,10},{29,13},{30,14},{1,17},... | collective-permute-start | bytes 18440 | tf_op jit(solution)/shard_map/ppermute | solution.py:50
  56.1 1.3 %collective-permute-start.25 = (f32[16,96]{1,0:T(8,128)S(1)}, f32[16,96]{1,0:T(8,128)S(1)}, u32[]{:S(2)}, u32[]{:S(2)}) collective-permute-start(f32[16,96]{1,0:T(8,128)S(1)} %convolution_add_fusion.3), channel_id=1, source_target_pairs={{1,0},{2,3},{5,4},{6,7},{8,9},{11,10},{12,13},{15,14},{16,17},{19,... | collective-permute-start | bytes 18440 | tf_op jit(solution)/shard_map/ppermute | solution.py:50
  57.4 1.3 %collective-permute-start.26 = (f32[16,96]{1,0:T(8,128)S(1)}, f32[16,96]{1,0:T(8,128)S(1)}, u32[]{:S(2)}, u32[]{:S(2)}) collective-permute-start(f32[16,96]{1,0:T(8,128)S(1)} %convolution_add_fusion.3), channel_id=1, source_target_pairs={{2,0},{1,3},{6,4},{5,7},{11,9},{8,10},{15,13},{12,14},{19,17},{16,... | collective-permute-start | bytes 18440 | tf_op jit(solution)/shard_map/ppermute | solution.py:50
  58.9 3.8 %collective-permute-start.29 = (f32[16,96]{1,0:T(8,128)S(1)}, f32[16,96]{1,0:T(8,128)S(1)}, u32[]{:S(2)}, u32[]{:S(2)}) collective-permute-start(f32[16,96]{1,0:T(8,128)S(1)} %convolution_add_fusion.3), channel_id=1, source_target_pairs={{6,0},{7,1},{4,2},{5,3},{2,4},{3,5},{0,6},{1,7},{14,8},{15,9},{12,... | collective-permute-start | bytes 18440 | tf_op jit(solution)/shard_map/ppermute | solution.py:50
  63.0 1.6 %collective-permute-start.31 = (f32[16,96]{1,0:T(8,128)S(1)}, f32[16,96]{1,0:T(8,128)S(1)}, u32[]{:S(2)}, u32[]{:S(2)}) collective-permute-start(f32[16,96]{1,0:T(8,128)S(1)} %convolution_add_fusion.3), channel_id=1, source_target_pairs={{0,1},{3,2},{4,5},{7,6},{9,8},{10,11},{13,12},{14,15},{17,16},{18,... | collective-permute-start | bytes 18440 | tf_op jit(solution)/shard_map/ppermute | solution.py:50
  64.9 1.3 %collective-permute-start.30 = (f32[16,96]{1,0:T(8,128)S(1)}, f32[16,96]{1,0:T(8,128)S(1)}, u32[]{:S(2)}, u32[]{:S(2)}) collective-permute-start(f32[16,96]{1,0:T(8,128)S(1)} %convolution_add_fusion.3), channel_id=1, source_target_pairs={{3,1},{0,2},{7,5},{4,6},{10,8},{9,11},{14,12},{13,15},{18,16},{17,... | collective-permute-start | bytes 18440 | tf_op jit(solution)/shard_map/ppermute | solution.py:50
  (155 shorter events, 23.5 us)
Async XLA Ops:
  2.6 16.3 %collective-permute-start = (f32[16,96]{1,0:T(8,128)S(1)}, f32[16,96]{1,0:T(8,128)S(1)}, u32[]{:S(2)}, u32[]{:S(2)}) collective-permute-start(f32[16,96]{1,0:T(8,128)S(1)} %fusion.15), channel_id=1, source_target_pairs={{16,0},{19,3},{20,4},{23,7},{25,9},{26,10},{29,13},{30,14},{1,17},... | collective-permute-start | bytes 18440 | tf_op jit(solution)/shard_map/ppermute | solution.py:50
  3.9 15.0 %collective-permute-start.1 = (f32[16,96]{1,0:T(8,128)S(1)}, f32[16,96]{1,0:T(8,128)S(1)}, u32[]{:S(2)}, u32[]{:S(2)}) collective-permute-start(f32[16,96]{1,0:T(8,128)S(1)} %fusion.15), channel_id=1, source_target_pairs={{1,0},{2,3},{5,4},{6,7},{8,9},{11,10},{12,13},{15,14},{16,17},{19,... | collective-permute-start | bytes 18440 | tf_op jit(solution)/shard_map/ppermute | solution.py:50
  5.2 13.7 %collective-permute-start.2 = (f32[16,96]{1,0:T(8,128)S(1)}, f32[16,96]{1,0:T(8,128)S(1)}, u32[]{:S(2)}, u32[]{:S(2)}) collective-permute-start(f32[16,96]{1,0:T(8,128)S(1)} %fusion.15), channel_id=1, source_target_pairs={{2,0},{1,3},{6,4},{5,7},{11,9},{8,10},{15,13},{12,14},{19,17},{16,... | collective-permute-start | bytes 18440 | tf_op jit(solution)/shard_map/ppermute | solution.py:50
  6.5 19.1 %collective-permute-start.5 = (f32[16,96]{1,0:T(8,128)S(1)}, f32[16,96]{1,0:T(8,128)S(1)}, u32[]{:S(2)}, u32[]{:S(2)}) collective-permute-start(f32[16,96]{1,0:T(8,128)S(1)} %fusion.15), channel_id=1, source_target_pairs={{6,0},{7,1},{4,2},{5,3},{2,4},{3,5},{0,6},{1,7},{14,8},{15,9},{12,... | collective-permute-start | bytes 18440 | tf_op jit(solution)/shard_map/ppermute | solution.py:50
  18.8 5.5 %collective-permute-start.7 = (f32[16,96]{1,0:T(8,128)S(1)}, f32[16,96]{1,0:T(8,128)S(1)}, u32[]{:S(2)}, u32[]{:S(2)}) collective-permute-start(f32[16,96]{1,0:T(8,128)S(1)} %fusion.15), channel_id=1, source_target_pairs={{0,1},{3,2},{4,5},{7,6},{9,8},{10,11},{13,12},{14,15},{17,16},{18,... | collective-permute-start | bytes 18440 | tf_op jit(solution)/shard_map/ppermute | solution.py:50
  21.6 2.7 %collective-permute-start.6 = (f32[16,96]{1,0:T(8,128)S(1)}, f32[16,96]{1,0:T(8,128)S(1)}, u32[]{:S(2)}, u32[]{:S(2)}) collective-permute-start(f32[16,96]{1,0:T(8,128)S(1)} %fusion.15), channel_id=1, source_target_pairs={{3,1},{0,2},{7,5},{4,6},{10,8},{9,11},{14,12},{13,15},{18,16},{17,... | collective-permute-start | bytes 18440 | tf_op jit(solution)/shard_map/ppermute | solution.py:50
  26.2 8.4 %collective-permute-start.10 = (f32[16,96]{1,0:T(8,128)S(1)}, f32[16,96]{1,0:T(8,128)S(1)}, u32[]{:S(2)}, u32[]{:S(2)}) collective-permute-start(f32[16,96]{1,0:T(8,128)S(1)} %convolution_add_fusion.7), channel_id=1, source_target_pairs={{2,0},{1,3},{6,4},{5,7},{11,9},{8,10},{15,13},{12,14},{19,17},{16,... | collective-permute-start | bytes 18440 | tf_op jit(solution)/shard_map/ppermute | solution.py:50
  27.5 7.1 %collective-permute-start.8 = (f32[16,96]{1,0:T(8,128)S(1)}, f32[16,96]{1,0:T(8,128)S(1)}, u32[]{:S(2)}, u32[]{:S(2)}) collective-permute-start(f32[16,96]{1,0:T(8,128)S(1)} %convolution_add_fusion.7), channel_id=1, source_target_pairs={{16,0},{19,3},{20,4},{23,7},{25,9},{26,10},{29,13},{30,14},{1,17},... | collective-permute-start | bytes 18440 | tf_op jit(solution)/shard_map/ppermute | solution.py:50
  28.8 5.8 %collective-permute-start.9 = (f32[16,96]{1,0:T(8,128)S(1)}, f32[16,96]{1,0:T(8,128)S(1)}, u32[]{:S(2)}, u32[]{:S(2)}) collective-permute-start(f32[16,96]{1,0:T(8,128)S(1)} %convolution_add_fusion.7), channel_id=1, source_target_pairs={{1,0},{2,3},{5,4},{6,7},{8,9},{11,10},{12,13},{15,14},{16,17},{19,... | collective-permute-start | bytes 18440 | tf_op jit(solution)/shard_map/ppermute | solution.py:50
  30.1 10.0 %collective-permute-start.13 = (f32[16,96]{1,0:T(8,128)S(1)}, f32[16,96]{1,0:T(8,128)S(1)}, u32[]{:S(2)}, u32[]{:S(2)}) collective-permute-start(f32[16,96]{1,0:T(8,128)S(1)} %convolution_add_fusion.7), channel_id=1, source_target_pairs={{6,0},{7,1},{4,2},{5,3},{2,4},{3,5},{0,6},{1,7},{14,8},{15,9},{12,... | collective-permute-start | bytes 18440 | tf_op jit(solution)/shard_map/ppermute | solution.py:50
  34.6 4.3 %collective-permute-start.15 = (f32[16,96]{1,0:T(8,128)S(1)}, f32[16,96]{1,0:T(8,128)S(1)}, u32[]{:S(2)}, u32[]{:S(2)}) collective-permute-start(f32[16,96]{1,0:T(8,128)S(1)} %convolution_add_fusion.7), channel_id=1, source_target_pairs={{0,1},{3,2},{4,5},{7,6},{9,8},{10,11},{13,12},{14,15},{17,16},{18,... | collective-permute-start | bytes 18440 | tf_op jit(solution)/shard_map/ppermute | solution.py:50
  36.2 2.7 %collective-permute-start.14 = (f32[16,96]{1,0:T(8,128)S(1)}, f32[16,96]{1,0:T(8,128)S(1)}, u32[]{:S(2)}, u32[]{:S(2)}) collective-permute-start(f32[16,96]{1,0:T(8,128)S(1)} %convolution_add_fusion.7), channel_id=1, source_target_pairs={{3,1},{0,2},{7,5},{4,6},{10,8},{9,11},{14,12},{13,15},{18,16},{17,... | collective-permute-start | bytes 18440 | tf_op jit(solution)/shard_map/ppermute | solution.py:50
  40.4 7.9 %collective-permute-start.16 = (f32[16,96]{1,0:T(8,128)S(1)}, f32[16,96]{1,0:T(8,128)S(1)}, u32[]{:S(2)}, u32[]{:S(2)}) collective-permute-start(f32[16,96]{1,0:T(8,128)S(1)} %convolution_add_fusion.5), channel_id=1, source_target_pairs={{16,0},{19,3},{20,4},{23,7},{25,9},{26,10},{29,13},{30,14},{1,17},... | collective-permute-start | bytes 18440 | tf_op jit(solution)/shard_map/ppermute | solution.py:50
  41.8 6.6 %collective-permute-start.17 = (f32[16,96]{1,0:T(8,128)S(1)}, f32[16,96]{1,0:T(8,128)S(1)}, u32[]{:S(2)}, u32[]{:S(2)}) collective-permute-start(f32[16,96]{1,0:T(8,128)S(1)} %convolution_add_fusion.5), channel_id=1, source_target_pairs={{1,0},{2,3},{5,4},{6,7},{8,9},{11,10},{12,13},{15,14},{16,17},{19,... | collective-permute-start | bytes 18440 | tf_op jit(solution)/shard_map/ppermute | solution.py:50
  43.1 5.5 %collective-permute-start.18 = (f32[16,96]{1,0:T(8,128)S(1)}, f32[16,96]{1,0:T(8,128)S(1)}, u32[]{:S(2)}, u32[]{:S(2)}) collective-permute-start(f32[16,96]{1,0:T(8,128)S(1)} %convolution_add_fusion.5), channel_id=1, source_target_pairs={{2,0},{1,3},{6,4},{5,7},{11,9},{8,10},{15,13},{12,14},{19,17},{16,... | collective-permute-start | bytes 18440 | tf_op jit(solution)/shard_map/ppermute | solution.py:50
  44.6 9.9 %collective-permute-start.21 = (f32[16,96]{1,0:T(8,128)S(1)}, f32[16,96]{1,0:T(8,128)S(1)}, u32[]{:S(2)}, u32[]{:S(2)}) collective-permute-start(f32[16,96]{1,0:T(8,128)S(1)} %convolution_add_fusion.5), channel_id=1, source_target_pairs={{6,0},{7,1},{4,2},{5,3},{2,4},{3,5},{0,6},{1,7},{14,8},{15,9},{12,... | collective-permute-start | bytes 18440 | tf_op jit(solution)/shard_map/ppermute | solution.py:50
  48.6 4.6 %collective-permute-start.23 = (f32[16,96]{1,0:T(8,128)S(1)}, f32[16,96]{1,0:T(8,128)S(1)}, u32[]{:S(2)}, u32[]{:S(2)}) collective-permute-start(f32[16,96]{1,0:T(8,128)S(1)} %convolution_add_fusion.5), channel_id=1, source_target_pairs={{0,1},{3,2},{4,5},{7,6},{9,8},{10,11},{13,12},{14,15},{17,16},{18,... | collective-permute-start | bytes 18440 | tf_op jit(solution)/shard_map/ppermute | solution.py:50
  50.5 2.7 %collective-permute-start.22 = (f32[16,96]{1,0:T(8,128)S(1)}, f32[16,96]{1,0:T(8,128)S(1)}, u32[]{:S(2)}, u32[]{:S(2)}) collective-permute-start(f32[16,96]{1,0:T(8,128)S(1)} %convolution_add_fusion.5), channel_id=1, source_target_pairs={{3,1},{0,2},{7,5},{4,6},{10,8},{9,11},{14,12},{13,15},{18,16},{17,... | collective-permute-start | bytes 18440 | tf_op jit(solution)/shard_map/ppermute | solution.py:50
  54.8 7.9 %collective-permute-start.24 = (f32[16,96]{1,0:T(8,128)S(1)}, f32[16,96]{1,0:T(8,128)S(1)}, u32[]{:S(2)}, u32[]{:S(2)}) collective-permute-start(f32[16,96]{1,0:T(8,128)S(1)} %convolution_add_fusion.3), channel_id=1, source_target_pairs={{16,0},{19,3},{20,4},{23,7},{25,9},{26,10},{29,13},{30,14},{1,17},... | collective-permute-start | bytes 18440 | tf_op jit(solution)/shard_map/ppermute | solution.py:50
  56.1 6.6 %collective-permute-start.25 = (f32[16,96]{1,0:T(8,128)S(1)}, f32[16,96]{1,0:T(8,128)S(1)}, u32[]{:S(2)}, u32[]{:S(2)}) collective-permute-start(f32[16,96]{1,0:T(8,128)S(1)} %convolution_add_fusion.3), channel_id=1, source_target_pairs={{1,0},{2,3},{5,4},{6,7},{8,9},{11,10},{12,13},{15,14},{16,17},{19,... | collective-permute-start | bytes 18440 | tf_op jit(solution)/shard_map/ppermute | solution.py:50
  57.4 5.5 %collective-permute-start.26 = (f32[16,96]{1,0:T(8,128)S(1)}, f32[16,96]{1,0:T(8,128)S(1)}, u32[]{:S(2)}, u32[]{:S(2)}) collective-permute-start(f32[16,96]{1,0:T(8,128)S(1)} %convolution_add_fusion.3), channel_id=1, source_target_pairs={{2,0},{1,3},{6,4},{5,7},{11,9},{8,10},{15,13},{12,14},{19,17},{16,... | collective-permute-start | bytes 18440 | tf_op jit(solution)/shard_map/ppermute | solution.py:50
  58.9 9.9 %collective-permute-start.29 = (f32[16,96]{1,0:T(8,128)S(1)}, f32[16,96]{1,0:T(8,128)S(1)}, u32[]{:S(2)}, u32[]{:S(2)}) collective-permute-start(f32[16,96]{1,0:T(8,128)S(1)} %convolution_add_fusion.3), channel_id=1, source_target_pairs={{6,0},{7,1},{4,2},{5,3},{2,4},{3,5},{0,6},{1,7},{14,8},{15,9},{12,... | collective-permute-start | bytes 18440 | tf_op jit(solution)/shard_map/ppermute | solution.py:50
  63.0 4.6 %collective-permute-start.31 = (f32[16,96]{1,0:T(8,128)S(1)}, f32[16,96]{1,0:T(8,128)S(1)}, u32[]{:S(2)}, u32[]{:S(2)}) collective-permute-start(f32[16,96]{1,0:T(8,128)S(1)} %convolution_add_fusion.3), channel_id=1, source_target_pairs={{0,1},{3,2},{4,5},{7,6},{9,8},{10,11},{13,12},{14,15},{17,16},{18,... | collective-permute-start | bytes 18440 | tf_op jit(solution)/shard_map/ppermute | solution.py:50
  64.9 2.7 %collective-permute-start.30 = (f32[16,96]{1,0:T(8,128)S(1)}, f32[16,96]{1,0:T(8,128)S(1)}, u32[]{:S(2)}, u32[]{:S(2)}) collective-permute-start(f32[16,96]{1,0:T(8,128)S(1)} %convolution_add_fusion.3), channel_id=1, source_target_pairs={{3,1},{0,2},{7,5},{4,6},{10,8},{9,11},{14,12},{13,15},{18,16},{17,... | collective-permute-start | bytes 18440 | tf_op jit(solution)/shard_map/ppermute | solution.py:50
  (15 other events, 42.8 us)

commit v10 on v6

--- a/solution.py
+++ b/solution.py
@@ -8,6 +8,7 @@
 
 omega_step = 0.5
 exact = lax.Precision.HIGHEST
+axes = ("gx", "gz", "ta")
 
 
 def routes():
@@ -59,24 +60,22 @@
     return local_real, local_imag
 
 
-def body(residual, null_vectors, clover_inverse, coarse_op, vector_count):
-    rhs_count = residual.shape[0]
-    vec_total = null_vectors.shape[1]
-    coarse_dim = 2 * vec_total
-    sites = residual.shape[3]
-    in_use = (lax.iota(jnp.int32, vec_total)[None, :] < vector_count[:, None]).astype(jnp.float32)[0]
-    used = jnp.tile(in_use, 4)
-
-    parts = residual.transpose(1, 2, 0, 3).reshape(2, 2, 6, rhs_count, sites)
-    fine_rows = jnp.stack(
-        [jnp.concatenate([parts[0], parts[1]], 2), jnp.concatenate([parts[1], -parts[0]], 2)]
-    )
-    vectors = null_vectors.transpose(0, 2, 1, 3).reshape(2, 2, 6, vec_total, sites)
-    product = jnp.einsum("pxcrs,pxcks->xrk", fine_rows, vectors, preferred_element_type=jnp.float32)
-    pieces = [product[chi, part * rhs_count : (part + 1) * rhs_count] for part in range(2) for chi in range(2)]
-    half = omega_step * (jnp.concatenate(pieces, 1) * used)
-
-    operator = coarse_op.reshape(9, 2, coarse_dim, coarse_dim)
+def real_form(matrix, dim):
+    matrix = matrix.reshape(2, dim, dim)
+    upper = jnp.concatenate([matrix[0], -matrix[1]], 1)
+    lower = jnp.concatenate([matrix[1], matrix[0]], 1)
+    return omega_step * jnp.concatenate([upper, lower], 0)
+
+
+def apply(vector, matrix):
+    return lax.dot_general(vector, matrix, (((1,), (1,)), ((), ())), precision=exact)
+
+
+def own_form(operator, dim):
+    return jnp.eye(2 * dim, dtype=jnp.float32) - real_form(operator, dim)
+
+
+def sweep_alone(half, operator, dim, held):
     grouped = {}
     for way, (first, second, paired, place) in enumerate(routes()):
         plus, minus = operator[2 * way + 1], operator[2 * way + 2]
@@ -92,26 +91,109 @@
         return ("gz", "ta", "gx").index(axis), -max(abs(source - i) for i, source in enumerate(sources))
 
     order = sorted(grouped, key=reach)
-
-    def real_form(matrix):
-        upper = jnp.concatenate([matrix[0], -matrix[1]], 1)
-        lower = jnp.concatenate([matrix[1], matrix[0]], 1)
-        return omega_step * jnp.concatenate([upper, lower], 0)
-
-    own = jnp.eye(2 * coarse_dim, dtype=jnp.float32) - real_form(operator[0])
-    around = jnp.concatenate([-real_form(grouped[link]) for link in order], 1)
-
-    def apply(vector, matrix):
-        return lax.dot_general(vector, matrix, (((1,), (1,)), ((), ())), precision=exact)
-
+    own = own_form(operator[0], dim)
+    around = jnp.concatenate([-real_form(grouped[link], dim) for link in order], 1)
     coarse = half
     for sweep_id in range(ITERS - 1):
         moved = [fetch(coarse, link) for link in order]
         kept = half + apply(coarse, own)
         if sweep_id == 1:
-            rows, clover, _ = lax.optimization_barrier((residual, clover_inverse, coarse))
-            local_real, local_imag = local_term(rows, clover)
+            rows, clover, kept = lax.optimization_barrier((*held, kept))
+            local = local_term(rows, clover)
         coarse = kept + apply(jnp.concatenate(moved, 1), around)
+    return coarse, local
+
+
+def shares_chip():
+    total, depth, slabs = (lax.axis_size(axis) for axis in axes)
+    return total == 4 and depth == 4 and slabs == 2
+
+
+def pair_routes():
+    total, depth, slabs = (lax.axis_size(axis) for axis in axes)
+
+    def device_at(group, level, slab):
+        return (group * depth + level) * slabs + slab
+
+    first, second, mate = [], [], []
+    for group in range(total):
+        for level in range(depth):
+            for slab in range(slabs):
+                step = 1 if level % 2 == 0 else -1
+                if group % 2 == 0:
+                    first.append(device_at(group, level, 1 - slab))
+                    second.append(device_at(group ^ 2, level, slab))
+                else:
+                    first.append(device_at(group, (level - step) % depth, slab))
+                    second.append(device_at(group, (level + step) % depth, slab))
+                mate.append(device_at(group ^ 1, level, slab))
+    return first, second, mate
+
+
+def sweep_in_pairs(half, operator, dim, held):
+    first, second, mate = pair_routes()
+
+    def swap(block, sources):
+        return lax.ppermute(block, axes, [(source, i) for i, source in enumerate(sources)])
+
+    along_t_x = jnp.stack([operator[7] + operator[8], operator[1] + operator[2]])
+    odd_level = lax.axis_index("gz") % 2 == 1
+    along_z = jnp.stack(
+        [jnp.where(odd_level, operator[5], operator[6]), jnp.where(odd_level, operator[6], operator[5])]
+    )
+    upper = lax.axis_index("gx") % 2 == 1
+    mine = jnp.where(upper, along_z, along_t_x)
+    theirs = swap(jnp.where(upper, along_t_x, along_z), mate)
+    inside = jnp.concatenate([own_form(operator[0], dim), -real_form(operator[3] + operator[4], dim)], 1)
+    around = jnp.stack(
+        [
+            jnp.concatenate([-real_form(part[0], dim), -real_form(part[1], dim)], 1)
+            for part in (mine, theirs)
+        ]
+    )
+
+    pair = jnp.stack([half, swap(half, mate)])
+    for sweep_id in range(ITERS - 1):
+        moved = [swap(pair, first), swap(pair, second)]
+        kept = half + apply(jnp.concatenate([pair[0], pair[1]], 1), inside)
+        if sweep_id == 1:
+            rows, clover, kept = lax.optimization_barrier((*held, kept))
+            local = local_term(rows, clover)
+        part = lax.dot_general(
+            jnp.concatenate(moved, 2), around, (((2,), (2,)), ((0,), (0,))), precision=exact
+        )
+        part = part + jnp.stack([kept, jnp.zeros_like(kept)])
+        if sweep_id < ITERS - 2:
+            other = swap(part, mate)
+            pair = part + jnp.stack([other[1], other[0]])
+    return part[0] + swap(part[1], mate), local
+
+
+def body(residual, null_vectors, clover_inverse, coarse_op, vector_count):
+    rhs_count = residual.shape[0]
+    vec_total = null_vectors.shape[1]
+    coarse_dim = 2 * vec_total
+    sites = residual.shape[3]
+    in_use = (lax.iota(jnp.int32, vec_total)[None, :] < vector_count[:, None]).astype(jnp.float32)[0]
+    used = jnp.tile(in_use, 4)
+    used, fine = lax.optimization_barrier((used, residual))
+
+    parts = fine.transpose(1, 2, 0, 3).reshape(2, 2, 6, rhs_count, sites)
+    fine_rows = jnp.stack(
+        [jnp.concatenate([parts[0], parts[1]], 2), jnp.concatenate([parts[1], -parts[0]], 2)]
+    )
+    vectors = null_vectors.transpose(0, 2, 1, 3).reshape(2, 2, 6, vec_total, sites)
+    product = jnp.einsum("pxcrs,pxcks->xrk", fine_rows, vectors, preferred_element_type=jnp.float32)
+    pieces = [product[chi, part * rhs_count : (part + 1) * rhs_count] for part in range(2) for chi in range(2)]
+    half = omega_step * (jnp.concatenate(pieces, 1) * used)
+
+    operator = coarse_op.reshape(9, 2, coarse_dim * coarse_dim)
+    held = (residual, clover_inverse)
+    if shares_chip():
+        coarse, local = sweep_in_pairs(half, operator, coarse_dim, held)
+    else:
+        coarse, local = sweep_alone(half, operator, coarse_dim, held)
+    local_real, local_imag = local
 
     rounded = coarse * used
     cut = [rounded[:, p * vec_total : (p + 1) * vec_total] for p in range(4)]

time: 38.8 us -> 35.1 us (0.905)
  starting transfers between devices: 20.7 us -> 15.1 us
  waiting for transfers between devices: 7.5 us -> 9.56 us
  local copies, waits for them, and re-layouts: 5.61 us -> 4.9 us
    ppermute x20 -> x14, starting transfers between devices: 20.7 us -> 15.1 us  [swap(): lax.ppermute(block, axes, [(source, i) for i, source in enumerate(sources)])]
    ppermute x20 -> x14, waiting for transfers between devices: 7.5 us -> 9.56 us  [swap(): lax.ppermute(block, axes, [(source, i) for i, source in enumerate(sources)])]
    unnamed x9 -> x8, local copies, waits for them, and re-layouts: 2.42 us -> 0.89 us
    dot_general x0 -> x4, matrix products: none -> 1.24 us  [sweep_in_pairs(): lax.dot_general(jnp.concatenate(moved, 2), around, (((2,), (2,)), ((0,),...]
    optimization_barrier x0 -> x1, local copies, waits for them, and re-layouts: none -> 0.96 us  [body(): used, fine = lax.optimization_barrier((used, residual))]
    dot_general x8 -> x4, matrix products: 1.84 us -> 0.92 us  [apply(): lax.dot_general(vector, matrix, (((1,), (1,)), ((), ())), precision=exact)]
    concatenate x5 -> x0, local copies, waits for them, and re-layouts: 0.45 us -> none  [the longest x4 0.33 us: body(): coarse = kept + apply(jnp.concatenate(moved, 1), around)]
  transfers between devices with their start and end apart: 20 -> 14, of which waited for: 8 -> 10; matrix products, arithmetic and copies ran while one was open for 7% -> 11% of each run, Pallas kernels for 0% -> 0%
where the time goes in v10:
time: 35.1 us; the launch traced here: 34.9 us
  starting transfers between devices  15.1 us (43%)
  waiting for transfers between devices  9.56 us (27%)
  local copies, waits for them, and re-layouts  4.9 us (14%)
  matrix products  2.65 us (8%)
  other arithmetic  1.51 us (4%)
  between operations  1.16 us (3%)
    ppermute x14, starting transfers between devices, swap(): lax.ppermute(block, axes, [(source, i) for i, source in enumerate(sources)])  15.1 us
    ppermute x14, waiting for transfers between devices, swap(): lax.ppermute(block, axes, [(source, i) for i, source in enumerate(sources)])  9.56 us
    dot_general x4, matrix products, sweep_in_pairs(): lax.dot_general(jnp.concatenate(moved, 2), around, (((2,), (2,)), ((0,),...  1.24 us
    optimization_barrier x1, local copies, waits for them, and re-layouts, body(): used, fine = lax.optimization_barrier((used, residual))  0.96 us
    dot_general x4, matrix products, apply(): lax.dot_general(vector, matrix, (((1,), (1,)), ((), ())), precision=exact)  0.92 us
    unnamed x8, local copies, waits for them, and re-layouts  0.89 us
    squeeze x12, local copies, waits for them, and re-layouts, real_form(): upper = jnp.concatenate([matrix[0], -matrix[1]], 1)  0.89 us
    convert_element_type x1, local copies, waits for them, and re-layouts, body(): return result.reshape(rhs_count, 2, 12, sites).astype(jnp.bfloat16)  0.83 us
  transfers between devices with their start and end apart: 14, of which 10 were waited for; matrix products, arithmetic and copies ran while one was open for 11% of the time, Pallas kernels for 0%

profile of v10, /device:TPU:0, one launch (start us, length us, event | category | flops | bytes accessed | tf_op | source)
XLA Modules:
  0.0 34.9 jit_solution(17410619370731584820)
XLA Ops:
  0.8 1.0 %copy.154 = bf16[16,2,12,256]{3,0,2,1:T(8,128)(2,1)S(1)} copy(bf16[16,2,12,256]{3,1,2,0:T(2,128)(2,1)} %param.5) | data formatting | bytes 393216 | tf_op jit(solution)/shard_map/optimization_barrier | solution.py:179
  2.6 0.5 %collective-permute-start = (f32[16,96]{1,0:T(8,128)S(1)}, f32[16,96]{1,0:T(8,128)S(1)}, u32[]{:S(2)}, u32[]{:S(2)}) collective-permute-start(f32[16,96]{1,0:T(8,128)S(1)} %fusion.43), channel_id=1, source_target_pairs={{8,0},{9,1},{10,2},{11,3},{12,4},{13,5},{14,6},{15,7},{0,8},{1,9},... | collective-permute-start | bytes 18440 | tf_op jit(solution)/shard_map/ppermute | solution.py:137
  3.1 0.5 %collective-permute-start.3 = (f32[2,2,2304]{2,1,0:T(2,128)S(1)}, f32[2,2,2304]{2,1,0:T(2,128)S(1)}, u32[]{:S(2)}, u32[]{:S(2)}) collective-permute-start(f32[2,2,2304]{2,1,0:T(2,128)S(1)} %get-tuple-element.63), channel_id=1, source_target_pairs={{8,0},{9,1},{10,2},{11,3},{12,4},{13,5},{14,6},{15,7},{0,8},{1,9},... | collective-permute-start | bytes 110600 | tf_op jit(solution)/shard_map/ppermute | solution.py:137
  5.2 2.6 %collective-permute-start.1 = (f32[2,16,96]{2,1,0:T(8,128)S(1)}, f32[2,16,96]{2,1,0:T(8,128)S(1)}, u32[]{:S(2)}, u32[]{:S(2)}) collective-permute-start(f32[2,16,96]{2,1,0:T(8,128)S(1)} %pad_maximum_fusion.13), channel_id=1, source_target_pairs={{1,0},{0,1},{3,2},{2,3},{5,4},{4,5},{7,6},{6,7},{14,8},{15,9},{12,... | collective-permute-start | bytes 36872 | tf_op jit(solution)/shard_map/ppermute | solution.py:137
  7.8 1.5 %collective-permute-start.2 = (f32[2,16,96]{2,1,0:T(8,128)S(1)}, f32[2,16,96]{2,1,0:T(8,128)S(1)}, u32[]{:S(2)}, u32[]{:S(2)}) collective-permute-start(f32[2,16,96]{2,1,0:T(8,128)S(1)} %pad_maximum_fusion.13), channel_id=1, source_target_pairs={{16,0},{17,1},{18,2},{19,3},{20,4},{21,5},{22,6},{23,7},{10,8},{11... | collective-permute-start | bytes 36872 | tf_op jit(solution)/shard_map/ppermute | solution.py:137
  10.2 1.3 %collective-permute-done.2 = f32[2,16,96]{2,1,0:T(8,128)S(1)} collective-permute-done((f32[2,16,96]{2,1,0:T(8,128)S(1)}, f32[2,16,96]{2,1,0:T(8,128)S(1)}, u32[]{:S(2)}, u32[]{:S(2)}) %collective-permute-start.2) | collective-permute-done | bytes 12320 | tf_op jit(solution)/shard_map/ppermute | solution.py:137
  11.8 1.2 %collective-permute-start.4 = (f32[2,16,96]{2,1,0:T(8,128)S(1)}, f32[2,16,96]{2,1,0:T(8,128)S(1)}, u32[]{:S(2)}, u32[]{:S(2)}) collective-permute-start(f32[2,16,96]{2,1,0:T(8,128)S(1)} %convolution_add_fusion.3), channel_id=1, source_target_pairs={{8,0},{9,1},{10,2},{11,3},{12,4},{13,5},{14,6},{15,7},{0,8},{1,9},... | collective-permute-start | bytes 36872 | tf_op jit(solution)/shard_map/ppermute | solution.py:137
  13.0 0.8 %collective-permute-done.4 = f32[2,16,96]{2,1,0:T(8,128)S(1)} collective-permute-done((f32[2,16,96]{2,1,0:T(8,128)S(1)}, f32[2,16,96]{2,1,0:T(8,128)S(1)}, u32[]{:S(2)}, u32[]{:S(2)}) %collective-permute-start.4) | collective-permute-done | bytes 12320 | tf_op jit(solution)/shard_map/ppermute | solution.py:137
  13.9 1.6 %collective-permute-start.5 = (f32[2,16,96]{2,1,0:T(8,128)S(1)}, f32[2,16,96]{2,1,0:T(8,128)S(1)}, u32[]{:S(2)}, u32[]{:S(2)}) collective-permute-start(f32[2,16,96]{2,1,0:T(8,128)S(1)} %maximum_add_fusion.1), channel_id=1, source_target_pairs={{1,0},{0,1},{3,2},{2,3},{5,4},{4,5},{7,6},{6,7},{14,8},{15,9},{12,... | collective-permute-start | bytes 36872 | tf_op jit(solution)/shard_map/ppermute | solution.py:137
  15.4 1.5 %collective-permute-start.6 = (f32[2,16,96]{2,1,0:T(8,128)S(1)}, f32[2,16,96]{2,1,0:T(8,128)S(1)}, u32[]{:S(2)}, u32[]{:S(2)}) collective-permute-start(f32[2,16,96]{2,1,0:T(8,128)S(1)} %maximum_add_fusion.1), channel_id=1, source_target_pairs={{16,0},{17,1},{18,2},{19,3},{20,4},{21,5},{22,6},{23,7},{10,8},{11... | collective-permute-start | bytes 36872 | tf_op jit(solution)/shard_map/ppermute | solution.py:137
  17.4 0.9 %copy-done.3 = bf16[2,2,6,6,256]{4,1,3,2,0:T(2,128)(2,1)S(1)} copy-done((bf16[2,2,6,6,256]{4,1,3,2,0:T(2,128)(2,1)S(1)}, bf16[2,2,6,6,256]{4,1,3,2,0:T(2,128)(2,1)}, u32[]{:S(2)}) %copy-start.3) | copy-done | bytes 73752
  18.4 0.8 %collective-permute-done.6 = f32[2,16,96]{2,1,0:T(8,128)S(1)} collective-permute-done((f32[2,16,96]{2,1,0:T(8,128)S(1)}, f32[2,16,96]{2,1,0:T(8,128)S(1)}, u32[]{:S(2)}, u32[]{:S(2)}) %collective-permute-start.6) | collective-permute-done | bytes 12320 | tf_op jit(solution)/shard_map/ppermute | solution.py:137
  19.8 0.9 %collective-permute-done.7 = f32[2,16,96]{2,1,0:T(8,128)S(1)} collective-permute-done((f32[2,16,96]{2,1,0:T(8,128)S(1)}, f32[2,16,96]{2,1,0:T(8,128)S(1)}, u32[]{:S(2)}, u32[]{:S(2)}) %collective-permute-start.7) | collective-permute-done | bytes 12320 | tf_op jit(solution)/shard_map/ppermute | solution.py:137
  20.8 0.9 %collective-permute-start.8 = (f32[2,16,96]{2,1,0:T(8,128)S(1)}, f32[2,16,96]{2,1,0:T(8,128)S(1)}, u32[]{:S(2)}, u32[]{:S(2)}) collective-permute-start(f32[2,16,96]{2,1,0:T(8,128)S(1)} %maximum_add_fusion.2), channel_id=1, source_target_pairs={{1,0},{0,1},{3,2},{2,3},{5,4},{4,5},{7,6},{6,7},{14,8},{15,9},{12,... | collective-permute-start | bytes 36872 | tf_op jit(solution)/shard_map/ppermute | solution.py:137
  21.6 1.5 %collective-permute-start.9 = (f32[2,16,96]{2,1,0:T(8,128)S(1)}, f32[2,16,96]{2,1,0:T(8,128)S(1)}, u32[]{:S(2)}, u32[]{:S(2)}) collective-permute-start(f32[2,16,96]{2,1,0:T(8,128)S(1)} %maximum_add_fusion.2), channel_id=1, source_target_pairs={{16,0},{17,1},{18,2},{19,3},{20,4},{21,5},{22,6},{23,7},{10,8},{11... | collective-permute-start | bytes 36872 | tf_op jit(solution)/shard_map/ppermute | solution.py:137
  23.4 1.2 %collective-permute-done.8 = f32[2,16,96]{2,1,0:T(8,128)S(1)} collective-permute-done((f32[2,16,96]{2,1,0:T(8,128)S(1)}, f32[2,16,96]{2,1,0:T(8,128)S(1)}, u32[]{:S(2)}, u32[]{:S(2)}) %collective-permute-start.8) | collective-permute-done | bytes 12320 | tf_op jit(solution)/shard_map/ppermute | solution.py:137
  24.6 0.8 %collective-permute-done.9 = f32[2,16,96]{2,1,0:T(8,128)S(1)} collective-permute-done((f32[2,16,96]{2,1,0:T(8,128)S(1)}, f32[2,16,96]{2,1,0:T(8,128)S(1)}, u32[]{:S(2)}, u32[]{:S(2)}) %collective-permute-start.9) | collective-permute-done | bytes 12320 | tf_op jit(solution)/shard_map/ppermute | solution.py:137
  26.1 0.8 %collective-permute-done.10 = f32[2,16,96]{2,1,0:T(8,128)S(1)} collective-permute-done((f32[2,16,96]{2,1,0:T(8,128)S(1)}, f32[2,16,96]{2,1,0:T(8,128)S(1)}, u32[]{:S(2)}, u32[]{:S(2)}) %collective-permute-start.10) | collective-permute-done | bytes 12320 | tf_op jit(solution)/shard_map/ppermute | solution.py:137
  27.0 1.3 %collective-permute-start.11 = (f32[2,16,96]{2,1,0:T(8,128)S(1)}, f32[2,16,96]{2,1,0:T(8,128)S(1)}, u32[]{:S(2)}, u32[]{:S(2)}) collective-permute-start(f32[2,16,96]{2,1,0:T(8,128)S(1)} %maximum_add_fusion.3), channel_id=1, source_target_pairs={{1,0},{0,1},{3,2},{2,3},{5,4},{4,5},{7,6},{6,7},{14,8},{15,9},{12,... | collective-permute-start | bytes 36872 | tf_op jit(solution)/shard_map/ppermute | solution.py:137
  28.2 1.5 %collective-permute-start.12 = (f32[2,16,96]{2,1,0:T(8,128)S(1)}, f32[2,16,96]{2,1,0:T(8,128)S(1)}, u32[]{:S(2)}, u32[]{:S(2)}) collective-permute-start(f32[2,16,96]{2,1,0:T(8,128)S(1)} %maximum_add_fusion.3), channel_id=1, source_target_pairs={{16,0},{17,1},{18,2},{19,3},{20,4},{21,5},{22,6},{23,7},{10,8},{11... | collective-permute-start | bytes 36872 | tf_op jit(solution)/shard_map/ppermute | solution.py:137
  30.0 0.8 %collective-permute-done.11 = f32[2,16,96]{2,1,0:T(8,128)S(1)} collective-permute-done((f32[2,16,96]{2,1,0:T(8,128)S(1)}, f32[2,16,96]{2,1,0:T(8,128)S(1)}, u32[]{:S(2)}, u32[]{:S(2)}) %collective-permute-start.11) | collective-permute-done | bytes 12320 | tf_op jit(solution)/shard_map/ppermute | solution.py:137
  30.8 1.2 %collective-permute-done.12 = f32[2,16,96]{2,1,0:T(8,128)S(1)} collective-permute-done((f32[2,16,96]{2,1,0:T(8,128)S(1)}, f32[2,16,96]{2,1,0:T(8,128)S(1)}, u32[]{:S(2)}, u32[]{:S(2)}) %collective-permute-start.12) | collective-permute-done | bytes 12320 | tf_op jit(solution)/shard_map/ppermute | solution.py:137
  32.7 0.9 %collective-permute-done.13 = f32[16,96]{1,0:T(8,128)S(1)} collective-permute-done((f32[16,96]{1,0:T(8,128)S(1)}, f32[16,96]{1,0:T(8,128)S(1)}, u32[]{:S(2)}, u32[]{:S(2)}) %collective-permute-start.13) | collective-permute-done | bytes 6176 | tf_op jit(solution)/shard_map/ppermute | solution.py:137
  34.1 0.8 %copy.136 = bf16[16,2,2,6,256]{4,1,3,2,0:T(2,128)(2,1)} copy(bf16[16,2,2,6,256]{4,0,1,3,2:T(8,128)(2,1)S(1)} %fusion.6) | data formatting | bytes 393216 | tf_op jit(solution)/shard_map/convert_element_type | solution.py:206
  (111 shorter events, 7.0 us)
Async XLA Ops:
  0.0 1.9 %copy-start = (bf16[2,24,12,256]{3,1,2,0:T(8,128)(2,1)S(1)}, bf16[2,24,12,256]{3,1,2,0:T(8,128)(2,1)}, u32[]{:S(2)}) copy-start(bf16[2,24,12,256]{3,1,2,0:T(8,128)(2,1)} %param.6) | copy-start | bytes 884740
  2.1 0.9 %copy-start.2 = (f32[1,9,2,2304]{3,2,1,0:T(2,128)S(1)}, f32[1,9,2,2304]{3,2,1,0:T(2,128)}, u32[]{:S(2)}) copy-start(f32[1,9,2,2304]{3,2,1,0:T(2,128)} %param.8) | copy-start | bytes 497668
  2.6 2.6 %collective-permute-start = (f32[16,96]{1,0:T(8,128)S(1)}, f32[16,96]{1,0:T(8,128)S(1)}, u32[]{:S(2)}, u32[]{:S(2)}) collective-permute-start(f32[16,96]{1,0:T(8,128)S(1)} %fusion.43), channel_id=1, source_target_pairs={{8,0},{9,1},{10,2},{11,3},{12,4},{13,5},{14,6},{15,7},{0,8},{1,9},... | collective-permute-start | bytes 18440 | tf_op jit(solution)/shard_map/ppermute | solution.py:137
  3.1 6.4 %collective-permute-start.3 = (f32[2,2,2304]{2,1,0:T(2,128)S(1)}, f32[2,2,2304]{2,1,0:T(2,128)S(1)}, u32[]{:S(2)}, u32[]{:S(2)}) collective-permute-start(f32[2,2,2304]{2,1,0:T(2,128)S(1)} %get-tuple-element.63), channel_id=1, source_target_pairs={{8,0},{9,1},{10,2},{11,3},{12,4},{13,5},{14,6},{15,7},{0,8},{1,9},... | collective-permute-start | bytes 110600 | tf_op jit(solution)/shard_map/ppermute | solution.py:137
  5.2 5.0 %collective-permute-start.1 = (f32[2,16,96]{2,1,0:T(8,128)S(1)}, f32[2,16,96]{2,1,0:T(8,128)S(1)}, u32[]{:S(2)}, u32[]{:S(2)}) collective-permute-start(f32[2,16,96]{2,1,0:T(8,128)S(1)} %pad_maximum_fusion.13), channel_id=1, source_target_pairs={{1,0},{0,1},{3,2},{2,3},{5,4},{4,5},{7,6},{6,7},{14,8},{15,9},{12,... | collective-permute-start | bytes 36872 | tf_op jit(solution)/shard_map/ppermute | solution.py:137
  7.8 3.7 %collective-permute-start.2 = (f32[2,16,96]{2,1,0:T(8,128)S(1)}, f32[2,16,96]{2,1,0:T(8,128)S(1)}, u32[]{:S(2)}, u32[]{:S(2)}) collective-permute-start(f32[2,16,96]{2,1,0:T(8,128)S(1)} %pad_maximum_fusion.13), channel_id=1, source_target_pairs={{16,0},{17,1},{18,2},{19,3},{20,4},{21,5},{22,6},{23,7},{10,8},{11... | collective-permute-start | bytes 36872 | tf_op jit(solution)/shard_map/ppermute | solution.py:137
  10.2 7.0 %copy-start.1 = (bf16[16,2,12,256]{3,1,2,0:T(2,128)(2,1)S(1)}, bf16[16,2,12,256]{3,1,2,0:T(2,128)(2,1)}, u32[]{:S(2)}) copy-start(bf16[16,2,12,256]{3,1,2,0:T(2,128)(2,1)} %param.5) | copy-start | bytes 589828
  11.8 2.0 %collective-permute-start.4 = (f32[2,16,96]{2,1,0:T(8,128)S(1)}, f32[2,16,96]{2,1,0:T(8,128)S(1)}, u32[]{:S(2)}, u32[]{:S(2)}) collective-permute-start(f32[2,16,96]{2,1,0:T(8,128)S(1)} %convolution_add_fusion.3), channel_id=1, source_target_pairs={{8,0},{9,1},{10,2},{11,3},{12,4},{13,5},{14,6},{15,7},{0,8},{1,9},... | collective-permute-start | bytes 36872 | tf_op jit(solution)/shard_map/ppermute | solution.py:137
  13.9 4.4 %collective-permute-start.5 = (f32[2,16,96]{2,1,0:T(8,128)S(1)}, f32[2,16,96]{2,1,0:T(8,128)S(1)}, u32[]{:S(2)}, u32[]{:S(2)}) collective-permute-start(f32[2,16,96]{2,1,0:T(8,128)S(1)} %maximum_add_fusion.1), channel_id=1, source_target_pairs={{1,0},{0,1},{3,2},{2,3},{5,4},{4,5},{7,6},{6,7},{14,8},{15,9},{12,... | collective-permute-start | bytes 36872 | tf_op jit(solution)/shard_map/ppermute | solution.py:137
  15.4 3.7 %collective-permute-start.6 = (f32[2,16,96]{2,1,0:T(8,128)S(1)}, f32[2,16,96]{2,1,0:T(8,128)S(1)}, u32[]{:S(2)}, u32[]{:S(2)}) collective-permute-start(f32[2,16,96]{2,1,0:T(8,128)S(1)} %maximum_add_fusion.1), channel_id=1, source_target_pairs={{16,0},{17,1},{18,2},{19,3},{20,4},{21,5},{22,6},{23,7},{10,8},{11... | collective-permute-start | bytes 36872 | tf_op jit(solution)/shard_map/ppermute | solution.py:137
  17.4 0.9 %copy-start.3 = (bf16[2,2,6,6,256]{4,1,3,2,0:T(2,128)(2,1)S(1)}, bf16[2,2,6,6,256]{4,1,3,2,0:T(2,128)(2,1)}, u32[]{:S(2)}) copy-start(bf16[2,2,6,6,256]{4,1,3,2,0:T(2,128)(2,1)} %param.7) | copy-start | bytes 221188
  19.5 1.2 %collective-permute-start.7 = (f32[2,16,96]{2,1,0:T(8,128)S(1)}, f32[2,16,96]{2,1,0:T(8,128)S(1)}, u32[]{:S(2)}, u32[]{:S(2)}) collective-permute-start(f32[2,16,96]{2,1,0:T(8,128)S(1)} %convolution_add_fusion.2), channel_id=1, source_target_pairs={{8,0},{9,1},{10,2},{11,3},{12,4},{13,5},{14,6},{15,7},{0,8},{1,9},... | collective-permute-start | bytes 36872 | tf_op jit(solution)/shard_map/ppermute | solution.py:137
  20.8 3.8 %collective-permute-start.8 = (f32[2,16,96]{2,1,0:T(8,128)S(1)}, f32[2,16,96]{2,1,0:T(8,128)S(1)}, u32[]{:S(2)}, u32[]{:S(2)}) collective-permute-start(f32[2,16,96]{2,1,0:T(8,128)S(1)} %maximum_add_fusion.2), channel_id=1, source_target_pairs={{1,0},{0,1},{3,2},{2,3},{5,4},{4,5},{7,6},{6,7},{14,8},{15,9},{12,... | collective-permute-start | bytes 36872 | tf_op jit(solution)/shard_map/ppermute | solution.py:137
  21.6 3.7 %collective-permute-start.9 = (f32[2,16,96]{2,1,0:T(8,128)S(1)}, f32[2,16,96]{2,1,0:T(8,128)S(1)}, u32[]{:S(2)}, u32[]{:S(2)}) collective-permute-start(f32[2,16,96]{2,1,0:T(8,128)S(1)} %maximum_add_fusion.2), channel_id=1, source_target_pairs={{16,0},{17,1},{18,2},{19,3},{20,4},{21,5},{22,6},{23,7},{10,8},{11... | collective-permute-start | bytes 36872 | tf_op jit(solution)/shard_map/ppermute | solution.py:137
  25.7 1.2 %collective-permute-start.10 = (f32[2,16,96]{2,1,0:T(8,128)S(1)}, f32[2,16,96]{2,1,0:T(8,128)S(1)}, u32[]{:S(2)}, u32[]{:S(2)}) collective-permute-start(f32[2,16,96]{2,1,0:T(8,128)S(1)} %convolution_add_fusion.1), channel_id=1, source_target_pairs={{8,0},{9,1},{10,2},{11,3},{12,4},{13,5},{14,6},{15,7},{0,8},{1,9},... | collective-permute-start | bytes 36872 | tf_op jit(solution)/shard_map/ppermute | solution.py:137
  27.0 3.8 %collective-permute-start.11 = (f32[2,16,96]{2,1,0:T(8,128)S(1)}, f32[2,16,96]{2,1,0:T(8,128)S(1)}, u32[]{:S(2)}, u32[]{:S(2)}) collective-permute-start(f32[2,16,96]{2,1,0:T(8,128)S(1)} %maximum_add_fusion.3), channel_id=1, source_target_pairs={{1,0},{0,1},{3,2},{2,3},{5,4},{4,5},{7,6},{6,7},{14,8},{15,9},{12,... | collective-permute-start | bytes 36872 | tf_op jit(solution)/shard_map/ppermute | solution.py:137
  28.2 3.7 %collective-permute-start.12 = (f32[2,16,96]{2,1,0:T(8,128)S(1)}, f32[2,16,96]{2,1,0:T(8,128)S(1)}, u32[]{:S(2)}, u32[]{:S(2)}) collective-permute-start(f32[2,16,96]{2,1,0:T(8,128)S(1)} %maximum_add_fusion.3), channel_id=1, source_target_pairs={{16,0},{17,1},{18,2},{19,3},{20,4},{21,5},{22,6},{23,7},{10,8},{11... | collective-permute-start | bytes 36872 | tf_op jit(solution)/shard_map/ppermute | solution.py:137
  32.3 1.2 %collective-permute-start.13 = (f32[16,96]{1,0:T(8,128)S(1)}, f32[16,96]{1,0:T(8,128)S(1)}, u32[]{:S(2)}, u32[]{:S(2)}) collective-permute-start(f32[16,96]{1,0:T(8,128)S(1)} %slice_bitcast_fusion.28), channel_id=1, source_target_pairs={{8,0},{9,1},{10,2},{11,3},{12,4},{13,5},{14,6},{15,7},{0,8},{1,9},... | collective-permute-start | bytes 18440 | tf_op jit(solution)/shard_map/ppermute | solution.py:137

commit v11 on v10

--- a/solution.py
+++ b/solution.py
@@ -1,6 +1,8 @@
 import jax
 import jax.numpy as jnp
 from jax import lax
+from jax.experimental import pallas as pl
+from jax.experimental.pallas import tpu as pltpu
 from jax.sharding import PartitionSpec as P
 
 ITERS = 5
@@ -130,6 +132,42 @@
     return first, second, mate
 
 
+def real_blocks(flat, dim, has_own):
+    blocks = flat.shape[0]
+
+    def kernel(flat_ref, out_ref, rows_ref):
+        packed = jnp.concatenate([flat_ref[block, link] for block in range(blocks) for link in range(2)], 0)
+        for i in range(dim):
+            rows_ref[pl.ds(i, 4 * blocks, stride=dim), :] = packed[:, i * dim : (i + 1) * dim]
+        row = lax.broadcasted_iota(jnp.int32, (dim, dim), 0)
+        col = lax.broadcasted_iota(jnp.int32, (dim, dim), 1)
+        for block in range(blocks):
+            for link in range(2):
+                base = (2 * block + link) * 2 * dim
+                real = -omega_step * rows_ref[base : base + dim]
+                imag = omega_step * rows_ref[base + dim : base + 2 * dim]
+                if has_own and link == 0:
+                    real = real + jnp.where(row == col, 1.0, 0.0)
+                place, left = ((block,), 2 * dim * link) if has_own else ((block, link), 0)
+                low, high = pl.ds(0, dim), pl.ds(dim, dim)
+                near, beyond = pl.ds(left, dim), pl.ds(left + dim, dim)
+                out_ref[(*place, low, near)] = real
+                out_ref[(*place, low, beyond)] = imag
+                out_ref[(*place, high, near)] = -imag
+                out_ref[(*place, high, beyond)] = real
+
+    shape = (blocks, 2 * dim, 4 * dim) if has_own else (blocks, 2, 2 * dim, 2 * dim)
+    return pl.pallas_call(
+        kernel,
+        out_shape=jax.ShapeDtypeStruct(shape, jnp.float32),
+        in_specs=[pl.BlockSpec(memory_space=pltpu.VMEM)],
+        out_specs=pl.BlockSpec(memory_space=pltpu.VMEM),
+        scratch_shapes=[pltpu.VMEM((4 * blocks * dim, dim), jnp.float32)],
+        compiler_params=pltpu.CompilerParams(vmem_limit_bytes=8 * 2**20),
+        cost_estimate=pl.CostEstimate(flops=10**5, bytes_accessed=10**5, transcendentals=0),
+    )(flat)
+
+
 def sweep_in_pairs(half, operator, dim, held):
     first, second, mate = pair_routes()
 
@@ -144,13 +182,8 @@
     upper = lax.axis_index("gx") % 2 == 1
     mine = jnp.where(upper, along_z, along_t_x)
     theirs = swap(jnp.where(upper, along_t_x, along_z), mate)
-    inside = jnp.concatenate([own_form(operator[0], dim), -real_form(operator[3] + operator[4], dim)], 1)
-    around = jnp.stack(
-        [
-            jnp.concatenate([-real_form(part[0], dim), -real_form(part[1], dim)], 1)
-            for part in (mine, theirs)
-        ]
-    )
+    inside = real_blocks(jnp.stack([operator[0], operator[3] + operator[4]])[None], dim, True)[0]
+    around = real_blocks(jnp.stack([mine, theirs]), dim, False)
 
     pair = jnp.stack([half, swap(half, mate)])
     for sweep_id in range(ITERS - 1):
@@ -159,10 +192,11 @@
         if sweep_id == 1:
             rows, clover, kept = lax.optimization_barrier((*held, kept))
             local = local_term(rows, clover)
-        part = lax.dot_general(
-            jnp.concatenate(moved, 2), around, (((2,), (2,)), ((0,), (0,))), precision=exact
-        )
-        part = part + jnp.stack([kept, jnp.zeros_like(kept)])
+        part = jnp.stack([kept, jnp.zeros_like(kept)])
+        for link, vectors in enumerate(moved):
+            part = part + lax.dot_general(
+                vectors, around[:, link], (((2,), (2,)), ((0,), (0,))), precision=exact
+            )
         if sweep_id < ITERS - 2:
             other = swap(part, mate)
             pair = part + jnp.stack([other[1], other[0]])

time: 35.1 us -> 33.7 us (0.960)
  local copies, waits for them, and re-layouts: 4.9 us -> 3.71 us
  matrix products: 2.65 us -> 3.27 us
  Pallas kernels: 0 us -> 0.54 us
  starting transfers between devices: 15.1 us -> 14.6 us
  other arithmetic: 1.51 us -> 1.06 us
    squeeze x12 -> x0, local copies, waits for them, and re-layouts: 0.89 us -> none  [real_form(): upper = jnp.concatenate([matrix[0], -matrix[1]], 1)]
    dot_general x4 -> x8, matrix products: 1.24 us -> 1.95 us  [sweep_in_pairs(): lax.dot_general(vectors, around[:, link], (((2,), (2,)), ((0,), (0,))), p...]
    ppermute x14, starting transfers between devices: 15.1 us -> 14.6 us  [swap(): lax.ppermute(block, axes, [(source, i) for i, source in enumerate(sources)])]
    pallas_call x0 -> x2, Pallas kernels: none -> 0.54 us  [real_blocks(): pl.pallas_call(kernel, out_shape=jax.ShapeDtypeStruct(shape, jnp.float32)...]
  transfers between devices with their start and end apart: 14 -> 14, of which waited for: 10 -> 10; matrix products, arithmetic and copies ran while one was open for 11% -> 9% of each run, Pallas kernels for 0% -> 2%
where the time goes in v11:
time: 33.7 us; the launch traced here: 33.5 us
  starting transfers between devices  14.6 us (43%)
  waiting for transfers between devices  9.25 us (27%)
  local copies, waits for them, and re-layouts  3.71 us (11%)
  matrix products  3.27 us (10%)
  between operations  1.08 us (3%)
  other arithmetic  1.06 us (3%)
  Pallas kernels  0.54 us (2%)
    ppermute x14, starting transfers between devices, swap(): lax.ppermute(block, axes, [(source, i) for i, source in enumerate(sources)])  14.6 us
    ppermute x14, waiting for transfers between devices, swap(): lax.ppermute(block, axes, [(source, i) for i, source in enumerate(sources)])  9.25 us
    dot_general x8, matrix products, sweep_in_pairs(): lax.dot_general(vectors, around[:, link], (((2,), (2,)), ((0,), (0,))), p...  1.95 us
    optimization_barrier x1, local copies, waits for them, and re-layouts, body(): used, fine = lax.optimization_barrier((used, residual))  0.96 us
    unnamed x8, local copies, waits for them, and re-layouts  0.89 us
    dot_general x4, matrix products, apply(): lax.dot_general(vector, matrix, (((1,), (1,)), ((), ())), precision=exact)  0.84 us
    convert_element_type x1, local copies, waits for them, and re-layouts, body(): return result.reshape(rhs_count, 2, 12, sites).astype(jnp.bfloat16)  0.83 us
  transfers between devices with their start and end apart: 14, of which 10 were waited for; matrix products, arithmetic and copies ran while one was open for 9% of the time, Pallas kernels for 2%

profile of v11, /device:TPU:0, one launch (start us, length us, event | category | flops | bytes accessed | tf_op | source)
XLA Modules:
  0.0 33.5 jit_solution(1000984302225466450)
XLA Ops:
  0.8 1.0 %copy.170 = bf16[16,2,12,256]{3,0,2,1:T(8,128)(2,1)S(1)} copy(bf16[16,2,12,256]{3,1,2,0:T(2,128)(2,1)} %param.5) | data formatting | bytes 393216 | tf_op jit(solution)/shard_map/optimization_barrier | solution.py:213
  2.6 0.5 %collective-permute-start = (f32[16,96]{1,0:T(8,128)S(1)}, f32[16,96]{1,0:T(8,128)S(1)}, u32[]{:S(2)}, u32[]{:S(2)}) collective-permute-start(f32[16,96]{1,0:T(8,128)S(1)} %fusion.37), channel_id=1, source_target_pairs={{8,0},{9,1},{10,2},{11,3},{12,4},{13,5},{14,6},{15,7},{0,8},{1,9},... | collective-permute-start | bytes 18440 | tf_op jit(solution)/shard_map/ppermute | solution.py:175
  3.1 0.5 %collective-permute-start.2 = (f32[2,2,2304]{2,1,0:T(2,128)S(1)}, f32[2,2,2304]{2,1,0:T(2,128)S(1)}, u32[]{:S(2)}, u32[]{:S(2)}) collective-permute-start(f32[2,2,2304]{2,1,0:T(2,128)S(1)} %maximum_select_fusion.1), channel_id=1, source_target_pairs={{8,0},{9,1},{10,2},{11,3},{12,4},{13,5},{14,6},{15,7},{0,8},{1,9},... | collective-permute-start | bytes 110600 | tf_op jit(solution)/shard_map/ppermute | solution.py:175
  4.3 2.6 %collective-permute-start.3 = (f32[2,16,96]{2,1,0:T(8,128)S(1)}, f32[2,16,96]{2,1,0:T(8,128)S(1)}, u32[]{:S(2)}, u32[]{:S(2)}) collective-permute-start(f32[2,16,96]{2,1,0:T(8,128)S(1)} %pad_maximum_fusion.2), channel_id=1, source_target_pairs={{16,0},{17,1},{18,2},{19,3},{20,4},{21,5},{22,6},{23,7},{10,8},{11... | collective-permute-start | bytes 36872 | tf_op jit(solution)/shard_map/ppermute | solution.py:175
  7.0 1.5 %collective-permute-start.1 = (f32[2,16,96]{2,1,0:T(8,128)S(1)}, f32[2,16,96]{2,1,0:T(8,128)S(1)}, u32[]{:S(2)}, u32[]{:S(2)}) collective-permute-start(f32[2,16,96]{2,1,0:T(8,128)S(1)} %pad_maximum_fusion.2), channel_id=1, source_target_pairs={{1,0},{0,1},{3,2},{2,3},{5,4},{4,5},{7,6},{6,7},{14,8},{15,9},{12,... | collective-permute-start | bytes 36872 | tf_op jit(solution)/shard_map/ppermute | solution.py:175
  9.3 1.4 %collective-permute-done.1 = f32[2,16,96]{2,1,0:T(8,128)S(1)} collective-permute-done((f32[2,16,96]{2,1,0:T(8,128)S(1)}, f32[2,16,96]{2,1,0:T(8,128)S(1)}, u32[]{:S(2)}, u32[]{:S(2)}) %collective-permute-start.1) | collective-permute-done | bytes 12320 | tf_op jit(solution)/shard_map/ppermute | solution.py:175
  10.9 0.9 %collective-permute-start.4 = (f32[2,16,96]{2,1,0:T(8,128)S(1)}, f32[2,16,96]{2,1,0:T(8,128)S(1)}, u32[]{:S(2)}, u32[]{:S(2)}) collective-permute-start(f32[2,16,96]{2,1,0:T(8,128)S(1)} %fusion.3), channel_id=1, source_target_pairs={{8,0},{9,1},{10,2},{11,3},{12,4},{13,5},{14,6},{15,7},{0,8},{1,9},... | collective-permute-start | bytes 36872 | tf_op jit(solution)/shard_map/ppermute | solution.py:175
  11.9 0.8 %collective-permute-done.4 = f32[2,16,96]{2,1,0:T(8,128)S(1)} collective-permute-done((f32[2,16,96]{2,1,0:T(8,128)S(1)}, f32[2,16,96]{2,1,0:T(8,128)S(1)}, u32[]{:S(2)}, u32[]{:S(2)}) %collective-permute-start.4) | collective-permute-done | bytes 12320 | tf_op jit(solution)/shard_map/ppermute | solution.py:175
  12.7 1.6 %collective-permute-start.6 = (f32[2,16,96]{2,1,0:T(8,128)S(1)}, f32[2,16,96]{2,1,0:T(8,128)S(1)}, u32[]{:S(2)}, u32[]{:S(2)}) collective-permute-start(f32[2,16,96]{2,1,0:T(8,128)S(1)} %maximum_add_fusion.1), channel_id=1, source_target_pairs={{16,0},{17,1},{18,2},{19,3},{20,4},{21,5},{22,6},{23,7},{10,8},{11... | collective-permute-start | bytes 36872 | tf_op jit(solution)/shard_map/ppermute | solution.py:175
  14.3 1.5 %collective-permute-start.5 = (f32[2,16,96]{2,1,0:T(8,128)S(1)}, f32[2,16,96]{2,1,0:T(8,128)S(1)}, u32[]{:S(2)}, u32[]{:S(2)}) collective-permute-start(f32[2,16,96]{2,1,0:T(8,128)S(1)} %maximum_add_fusion.1), channel_id=1, source_target_pairs={{1,0},{0,1},{3,2},{2,3},{5,4},{4,5},{7,6},{6,7},{14,8},{15,9},{12,... | collective-permute-start | bytes 36872 | tf_op jit(solution)/shard_map/ppermute | solution.py:175
  16.2 0.9 %copy-done.3 = bf16[2,2,6,6,256]{4,1,3,2,0:T(2,128)(2,1)S(1)} copy-done((bf16[2,2,6,6,256]{4,1,3,2,0:T(2,128)(2,1)S(1)}, bf16[2,2,6,6,256]{4,1,3,2,0:T(2,128)(2,1)}, u32[]{:S(2)}) %copy-start.3) | copy-done | bytes 73752
  17.4 0.6 %collective-permute-done.5 = f32[2,16,96]{2,1,0:T(8,128)S(1)} collective-permute-done((f32[2,16,96]{2,1,0:T(8,128)S(1)}, f32[2,16,96]{2,1,0:T(8,128)S(1)}, u32[]{:S(2)}, u32[]{:S(2)}) %collective-permute-start.5) | collective-permute-done | bytes 12320 | tf_op jit(solution)/shard_map/ppermute | solution.py:175
  18.5 1.0 %collective-permute-done.7 = f32[2,16,96]{2,1,0:T(8,128)S(1)} collective-permute-done((f32[2,16,96]{2,1,0:T(8,128)S(1)}, f32[2,16,96]{2,1,0:T(8,128)S(1)}, u32[]{:S(2)}, u32[]{:S(2)}) %collective-permute-start.7) | collective-permute-done | bytes 12320 | tf_op jit(solution)/shard_map/ppermute | solution.py:175
  19.5 0.8 %collective-permute-start.9 = (f32[2,16,96]{2,1,0:T(8,128)S(1)}, f32[2,16,96]{2,1,0:T(8,128)S(1)}, u32[]{:S(2)}, u32[]{:S(2)}) collective-permute-start(f32[2,16,96]{2,1,0:T(8,128)S(1)} %maximum_add_fusion.2), channel_id=1, source_target_pairs={{16,0},{17,1},{18,2},{19,3},{20,4},{21,5},{22,6},{23,7},{10,8},{11... | collective-permute-start | bytes 36872 | tf_op jit(solution)/shard_map/ppermute | solution.py:175
  20.3 1.5 %collective-permute-start.8 = (f32[2,16,96]{2,1,0:T(8,128)S(1)}, f32[2,16,96]{2,1,0:T(8,128)S(1)}, u32[]{:S(2)}, u32[]{:S(2)}) collective-permute-start(f32[2,16,96]{2,1,0:T(8,128)S(1)} %maximum_add_fusion.2), channel_id=1, source_target_pairs={{1,0},{0,1},{3,2},{2,3},{5,4},{4,5},{7,6},{6,7},{14,8},{15,9},{12,... | collective-permute-start | bytes 36872 | tf_op jit(solution)/shard_map/ppermute | solution.py:175
  22.0 1.3 %collective-permute-done.9 = f32[2,16,96]{2,1,0:T(8,128)S(1)} collective-permute-done((f32[2,16,96]{2,1,0:T(8,128)S(1)}, f32[2,16,96]{2,1,0:T(8,128)S(1)}, u32[]{:S(2)}, u32[]{:S(2)}) %collective-permute-start.9) | collective-permute-done | bytes 12320 | tf_op jit(solution)/shard_map/ppermute | solution.py:175
  23.6 0.5 %collective-permute-done.8 = f32[2,16,96]{2,1,0:T(8,128)S(1)} collective-permute-done((f32[2,16,96]{2,1,0:T(8,128)S(1)}, f32[2,16,96]{2,1,0:T(8,128)S(1)}, u32[]{:S(2)}, u32[]{:S(2)}) %collective-permute-start.8) | collective-permute-done | bytes 12320 | tf_op jit(solution)/shard_map/ppermute | solution.py:175
  24.7 0.8 %collective-permute-done.10 = f32[2,16,96]{2,1,0:T(8,128)S(1)} collective-permute-done((f32[2,16,96]{2,1,0:T(8,128)S(1)}, f32[2,16,96]{2,1,0:T(8,128)S(1)}, u32[]{:S(2)}, u32[]{:S(2)}) %collective-permute-start.10) | collective-permute-done | bytes 12320 | tf_op jit(solution)/shard_map/ppermute | solution.py:175
  25.5 1.4 %collective-permute-start.12 = (f32[2,16,96]{2,1,0:T(8,128)S(1)}, f32[2,16,96]{2,1,0:T(8,128)S(1)}, u32[]{:S(2)}, u32[]{:S(2)}) collective-permute-start(f32[2,16,96]{2,1,0:T(8,128)S(1)} %maximum_add_fusion.3), channel_id=1, source_target_pairs={{16,0},{17,1},{18,2},{19,3},{20,4},{21,5},{22,6},{23,7},{10,8},{11... | collective-permute-start | bytes 36872 | tf_op jit(solution)/shard_map/ppermute | solution.py:175
  26.9 1.5 %collective-permute-start.11 = (f32[2,16,96]{2,1,0:T(8,128)S(1)}, f32[2,16,96]{2,1,0:T(8,128)S(1)}, u32[]{:S(2)}, u32[]{:S(2)}) collective-permute-start(f32[2,16,96]{2,1,0:T(8,128)S(1)} %maximum_add_fusion.3), channel_id=1, source_target_pairs={{1,0},{0,1},{3,2},{2,3},{5,4},{4,5},{7,6},{6,7},{14,8},{15,9},{12,... | collective-permute-start | bytes 36872 | tf_op jit(solution)/shard_map/ppermute | solution.py:175
  28.6 0.7 %collective-permute-done.12 = f32[2,16,96]{2,1,0:T(8,128)S(1)} collective-permute-done((f32[2,16,96]{2,1,0:T(8,128)S(1)}, f32[2,16,96]{2,1,0:T(8,128)S(1)}, u32[]{:S(2)}, u32[]{:S(2)}) %collective-permute-start.12) | collective-permute-done | bytes 12320 | tf_op jit(solution)/shard_map/ppermute | solution.py:175
  29.6 1.1 %collective-permute-done.11 = f32[2,16,96]{2,1,0:T(8,128)S(1)} collective-permute-done((f32[2,16,96]{2,1,0:T(8,128)S(1)}, f32[2,16,96]{2,1,0:T(8,128)S(1)}, u32[]{:S(2)}, u32[]{:S(2)}) %collective-permute-start.11) | collective-permute-done | bytes 12320 | tf_op jit(solution)/shard_map/ppermute | solution.py:175
  31.2 0.9 %collective-permute-done.13 = f32[16,96]{1,0:T(8,128)S(1)} collective-permute-done((f32[16,96]{1,0:T(8,128)S(1)}, f32[16,96]{1,0:T(8,128)S(1)}, u32[]{:S(2)}, u32[]{:S(2)}) %collective-permute-start.13) | collective-permute-done | bytes 6176 | tf_op jit(solution)/shard_map/ppermute | solution.py:175
  32.7 0.8 %copy.152 = bf16[16,2,2,6,256]{4,1,3,2,0:T(2,128)(2,1)} copy(bf16[16,2,2,6,256]{4,0,1,3,2:T(8,128)(2,1)S(1)} %fusion.10) | data formatting | bytes 393216 | tf_op jit(solution)/shard_map/convert_element_type | solution.py:240
  (93 shorter events, 6.3 us)
Async XLA Ops:
  0.0 1.9 %copy-start = (bf16[2,24,12,256]{3,1,2,0:T(8,128)(2,1)S(1)}, bf16[2,24,12,256]{3,1,2,0:T(8,128)(2,1)}, u32[]{:S(2)}) copy-start(bf16[2,24,12,256]{3,1,2,0:T(8,128)(2,1)} %param.6) | copy-start | bytes 884740
  2.1 0.9 %copy-start.2 = (f32[1,9,2,2304]{3,2,1,0:T(2,128)S(1)}, f32[1,9,2,2304]{3,2,1,0:T(2,128)}, u32[]{:S(2)}) copy-start(f32[1,9,2,2304]{3,2,1,0:T(2,128)} %param.8) | copy-start | bytes 497668
  2.6 1.8 %collective-permute-start = (f32[16,96]{1,0:T(8,128)S(1)}, f32[16,96]{1,0:T(8,128)S(1)}, u32[]{:S(2)}, u32[]{:S(2)}) collective-permute-start(f32[16,96]{1,0:T(8,128)S(1)} %fusion.37), channel_id=1, source_target_pairs={{8,0},{9,1},{10,2},{11,3},{12,4},{13,5},{14,6},{15,7},{0,8},{1,9},... | collective-permute-start | bytes 18440 | tf_op jit(solution)/shard_map/ppermute | solution.py:175
  3.1 5.3 %collective-permute-start.2 = (f32[2,2,2304]{2,1,0:T(2,128)S(1)}, f32[2,2,2304]{2,1,0:T(2,128)S(1)}, u32[]{:S(2)}, u32[]{:S(2)}) collective-permute-start(f32[2,2,2304]{2,1,0:T(2,128)S(1)} %maximum_select_fusion.1), channel_id=1, source_target_pairs={{8,0},{9,1},{10,2},{11,3},{12,4},{13,5},{14,6},{15,7},{0,8},{1,9},... | collective-permute-start | bytes 110600 | tf_op jit(solution)/shard_map/ppermute | solution.py:175
  4.3 4.7 %collective-permute-start.3 = (f32[2,16,96]{2,1,0:T(8,128)S(1)}, f32[2,16,96]{2,1,0:T(8,128)S(1)}, u32[]{:S(2)}, u32[]{:S(2)}) collective-permute-start(f32[2,16,96]{2,1,0:T(8,128)S(1)} %pad_maximum_fusion.2), channel_id=1, source_target_pairs={{16,0},{17,1},{18,2},{19,3},{20,4},{21,5},{22,6},{23,7},{10,8},{11... | collective-permute-start | bytes 36872 | tf_op jit(solution)/shard_map/ppermute | solution.py:175
  7.0 3.7 %collective-permute-start.1 = (f32[2,16,96]{2,1,0:T(8,128)S(1)}, f32[2,16,96]{2,1,0:T(8,128)S(1)}, u32[]{:S(2)}, u32[]{:S(2)}) collective-permute-start(f32[2,16,96]{2,1,0:T(8,128)S(1)} %pad_maximum_fusion.2), channel_id=1, source_target_pairs={{1,0},{0,1},{3,2},{2,3},{5,4},{4,5},{7,6},{6,7},{14,8},{15,9},{12,... | collective-permute-start | bytes 36872 | tf_op jit(solution)/shard_map/ppermute | solution.py:175
  9.3 6.8 %copy-start.1 = (bf16[16,2,12,256]{3,1,2,0:T(2,128)(2,1)S(1)}, bf16[16,2,12,256]{3,1,2,0:T(2,128)(2,1)}, u32[]{:S(2)}) copy-start(bf16[16,2,12,256]{3,1,2,0:T(2,128)(2,1)} %param.5) | copy-start | bytes 589828
  10.9 1.8 %collective-permute-start.4 = (f32[2,16,96]{2,1,0:T(8,128)S(1)}, f32[2,16,96]{2,1,0:T(8,128)S(1)}, u32[]{:S(2)}, u32[]{:S(2)}) collective-permute-start(f32[2,16,96]{2,1,0:T(8,128)S(1)} %fusion.3), channel_id=1, source_target_pairs={{8,0},{9,1},{10,2},{11,3},{12,4},{13,5},{14,6},{15,7},{0,8},{1,9},... | collective-permute-start | bytes 36872 | tf_op jit(solution)/shard_map/ppermute | solution.py:175
  12.7 4.4 %collective-permute-start.6 = (f32[2,16,96]{2,1,0:T(8,128)S(1)}, f32[2,16,96]{2,1,0:T(8,128)S(1)}, u32[]{:S(2)}, u32[]{:S(2)}) collective-permute-start(f32[2,16,96]{2,1,0:T(8,128)S(1)} %maximum_add_fusion.1), channel_id=1, source_target_pairs={{16,0},{17,1},{18,2},{19,3},{20,4},{21,5},{22,6},{23,7},{10,8},{11... | collective-permute-start | bytes 36872 | tf_op jit(solution)/shard_map/ppermute | solution.py:175
  14.3 3.7 %collective-permute-start.5 = (f32[2,16,96]{2,1,0:T(8,128)S(1)}, f32[2,16,96]{2,1,0:T(8,128)S(1)}, u32[]{:S(2)}, u32[]{:S(2)}) collective-permute-start(f32[2,16,96]{2,1,0:T(8,128)S(1)} %maximum_add_fusion.1), channel_id=1, source_target_pairs={{1,0},{0,1},{3,2},{2,3},{5,4},{4,5},{7,6},{6,7},{14,8},{15,9},{12,... | collective-permute-start | bytes 36872 | tf_op jit(solution)/shard_map/ppermute | solution.py:175
  16.2 0.9 %copy-start.3 = (bf16[2,2,6,6,256]{4,1,3,2,0:T(2,128)(2,1)S(1)}, bf16[2,2,6,6,256]{4,1,3,2,0:T(2,128)(2,1)}, u32[]{:S(2)}) copy-start(bf16[2,2,6,6,256]{4,1,3,2,0:T(2,128)(2,1)} %param.7) | copy-start | bytes 221188
  18.3 1.2 %collective-permute-start.7 = (f32[2,16,96]{2,1,0:T(8,128)S(1)}, f32[2,16,96]{2,1,0:T(8,128)S(1)}, u32[]{:S(2)}, u32[]{:S(2)}) collective-permute-start(f32[2,16,96]{2,1,0:T(8,128)S(1)} %fusion.2), channel_id=1, source_target_pairs={{8,0},{9,1},{10,2},{11,3},{12,4},{13,5},{14,6},{15,7},{0,8},{1,9},... | collective-permute-start | bytes 36872 | tf_op jit(solution)/shard_map/ppermute | solution.py:175
  19.5 3.8 %collective-permute-start.9 = (f32[2,16,96]{2,1,0:T(8,128)S(1)}, f32[2,16,96]{2,1,0:T(8,128)S(1)}, u32[]{:S(2)}, u32[]{:S(2)}) collective-permute-start(f32[2,16,96]{2,1,0:T(8,128)S(1)} %maximum_add_fusion.2), channel_id=1, source_target_pairs={{16,0},{17,1},{18,2},{19,3},{20,4},{21,5},{22,6},{23,7},{10,8},{11... | collective-permute-start | bytes 36872 | tf_op jit(solution)/shard_map/ppermute | solution.py:175
  20.3 3.7 %collective-permute-start.8 = (f32[2,16,96]{2,1,0:T(8,128)S(1)}, f32[2,16,96]{2,1,0:T(8,128)S(1)}, u32[]{:S(2)}, u32[]{:S(2)}) collective-permute-start(f32[2,16,96]{2,1,0:T(8,128)S(1)} %maximum_add_fusion.2), channel_id=1, source_target_pairs={{1,0},{0,1},{3,2},{2,3},{5,4},{4,5},{7,6},{6,7},{14,8},{15,9},{12,... | collective-permute-start | bytes 36872 | tf_op jit(solution)/shard_map/ppermute | solution.py:175
  24.3 1.2 %collective-permute-start.10 = (f32[2,16,96]{2,1,0:T(8,128)S(1)}, f32[2,16,96]{2,1,0:T(8,128)S(1)}, u32[]{:S(2)}, u32[]{:S(2)}) collective-permute-start(f32[2,16,96]{2,1,0:T(8,128)S(1)} %fusion.1), channel_id=1, source_target_pairs={{8,0},{9,1},{10,2},{11,3},{12,4},{13,5},{14,6},{15,7},{0,8},{1,9},... | collective-permute-start | bytes 36872 | tf_op jit(solution)/shard_map/ppermute | solution.py:175
  25.5 3.8 %collective-permute-start.12 = (f32[2,16,96]{2,1,0:T(8,128)S(1)}, f32[2,16,96]{2,1,0:T(8,128)S(1)}, u32[]{:S(2)}, u32[]{:S(2)}) collective-permute-start(f32[2,16,96]{2,1,0:T(8,128)S(1)} %maximum_add_fusion.3), channel_id=1, source_target_pairs={{16,0},{17,1},{18,2},{19,3},{20,4},{21,5},{22,6},{23,7},{10,8},{11... | collective-permute-start | bytes 36872 | tf_op jit(solution)/shard_map/ppermute | solution.py:175
  26.9 3.7 %collective-permute-start.11 = (f32[2,16,96]{2,1,0:T(8,128)S(1)}, f32[2,16,96]{2,1,0:T(8,128)S(1)}, u32[]{:S(2)}, u32[]{:S(2)}) collective-permute-start(f32[2,16,96]{2,1,0:T(8,128)S(1)} %maximum_add_fusion.3), channel_id=1, source_target_pairs={{1,0},{0,1},{3,2},{2,3},{5,4},{4,5},{7,6},{6,7},{14,8},{15,9},{12,... | collective-permute-start | bytes 36872 | tf_op jit(solution)/shard_map/ppermute | solution.py:175
  30.9 1.2 %collective-permute-start.13 = (f32[16,96]{1,0:T(8,128)S(1)}, f32[16,96]{1,0:T(8,128)S(1)}, u32[]{:S(2)}, u32[]{:S(2)}) collective-permute-start(f32[16,96]{1,0:T(8,128)S(1)} %slice_bitcast_fusion.39), channel_id=1, source_target_pairs={{8,0},{9,1},{10,2},{11,3},{12,4},{13,5},{14,6},{15,7},{0,8},{1,9},... | collective-permute-start | bytes 18440 | tf_op jit(solution)/shard_map/ppermute | solution.py:175

commit v12 on v11

--- a/solution.py
+++ b/solution.py
@@ -47,6 +47,66 @@
 def fetch(block, link):
     axis, sources = link
     return lax.ppermute(block, axis, [(source, i) for i, source in enumerate(sources)])
+
+
+def restrict_kernel(
+    count_ref, rows_hbm, vectors_hbm, out_ref, used_ref, rows_ref, vectors_ref, scratch, sems
+):
+    rhs, parts, _, sites = rows_ref.shape
+    vecs = vectors_ref.shape[2]
+    half = parts // 2
+    copies = []
+    for chi in range(2):
+        span = pl.ds(half * chi, half)
+        copies.append(
+            [
+                pltpu.make_async_copy(rows_hbm.at[:, span], rows_ref.at[:, span], sems.at[2 * chi]),
+                pltpu.make_async_copy(vectors_hbm.at[:, span], vectors_ref.at[:, span], sems.at[2 * chi + 1]),
+            ]
+        )
+    for copy in copies[0] + copies[1]:
+        copy.start()
+    for chi in range(2):
+        for copy in copies[chi]:
+            copy.wait()
+        total = jnp.zeros((2 * rhs, 2 * vecs), jnp.float32)
+        for c in range(half * chi, half * chi + half):
+            rows = rows_ref[:, c].reshape(2 * rhs, sites)
+            vectors = jnp.concatenate([vectors_ref[0, c], vectors_ref[1, c]], 0)
+            total += lax.dot_general(
+                rows, vectors, (((1,), (1,)), ((), ())), preferred_element_type=jnp.float32
+            )
+        scratch[chi, :, : 2 * vecs] = total
+    real, imag = [], []
+    for chi in range(2):
+        even = scratch[chi, pl.ds(0, rhs, stride=2), :]
+        odd = scratch[chi, pl.ds(1, rhs, stride=2), :]
+        real.append(even[:, :vecs] + odd[:, vecs : 2 * vecs])
+        imag.append(odd[:, :vecs] - even[:, vecs : 2 * vecs])
+    lane = lax.broadcasted_iota(jnp.int32, (rhs, vecs), 1)
+    used = jnp.where(lane < count_ref[0], 1.0, 0.0)
+    out_ref[...] = jnp.concatenate([omega_step * part * used for part in real + imag], 1)
+    used_ref[...] = jnp.concatenate([used] * 4, 1)
+
+
+def restrict(count, rows, vectors):
+    rhs, vecs = rows.shape[0], vectors.shape[2]
+    in_vmem = pl.BlockSpec(memory_space=pltpu.VMEM)
+    in_hbm = pl.BlockSpec(memory_space=pltpu.HBM)
+    return pl.pallas_call(
+        restrict_kernel,
+        out_shape=[jax.ShapeDtypeStruct((rhs, 4 * vecs), jnp.float32)] * 2,
+        in_specs=[pl.BlockSpec(memory_space=pltpu.SMEM), in_hbm, in_hbm],
+        out_specs=[in_vmem, in_vmem],
+        scratch_shapes=[
+            pltpu.VMEM(rows.shape, rows.dtype),
+            pltpu.VMEM(vectors.shape, vectors.dtype),
+            pltpu.VMEM((2, 2 * rhs, 128), jnp.float32),
+            pltpu.SemaphoreType.DMA((4,)),
+        ],
+        compiler_params=pltpu.CompilerParams(vmem_limit_bytes=55168 * 2**10),
+        cost_estimate=pl.CostEstimate(flops=10**7, bytes_accessed=5 * 10**5, transcendentals=0),
+    )(count, rows, vectors)
 
 
 def local_term(residual, clover_inverse):
@@ -208,19 +268,12 @@
     vec_total = null_vectors.shape[1]
     coarse_dim = 2 * vec_total
     sites = residual.shape[3]
-    in_use = (lax.iota(jnp.int32, vec_total)[None, :] < vector_count[:, None]).astype(jnp.float32)[0]
-    used = jnp.tile(in_use, 4)
-    used, fine = lax.optimization_barrier((used, residual))
-
-    parts = fine.transpose(1, 2, 0, 3).reshape(2, 2, 6, rhs_count, sites)
-    fine_rows = jnp.stack(
-        [jnp.concatenate([parts[0], parts[1]], 2), jnp.concatenate([parts[1], -parts[0]], 2)]
-    )
-    vectors = null_vectors.transpose(0, 2, 1, 3).reshape(2, 2, 6, vec_total, sites)
-    product = jnp.einsum("pxcrs,pxcks->xrk", fine_rows, vectors, preferred_element_type=jnp.float32)
-    pieces = [product[chi, part * rhs_count : (part + 1) * rhs_count] for part in range(2) for chi in range(2)]
-    half = omega_step * (jnp.concatenate(pieces, 1) * used)
-
+    rows = residual.transpose(0, 2, 1, 3)
+    stored = null_vectors.transpose(0, 2, 1, 3)
+    half, used = restrict(vector_count, rows, stored)
+    vectors = stored.reshape(2, 2, 6, vec_total, sites)
+
+    coarse_op, half = lax.optimization_barrier((coarse_op, half))
     operator = coarse_op.reshape(9, 2, coarse_dim * coarse_dim)
     held = (residual, clover_inverse)
     if shares_chip():

time: 33.7 us -> 33.3 us (0.988)
  local copies, waits for them, and re-layouts: 3.71 us -> 1.99 us
  Pallas kernels: 0.54 us -> 2.11 us
  waiting for transfers between devices: 9.25 us -> 9.82 us
    pallas_call x0 -> x1, Pallas kernels: none -> 1.58 us  [restrict(): pl.pallas_call(restrict_kernel, out_shape=[jax.ShapeDtypeStruct((rhs, 4 *...]
    optimization_barrier x1 -> x0, local copies, waits for them, and re-layouts: 0.96 us -> none  [body(): used, fine = lax.optimization_barrier((used, residual))]
    ppermute x14, waiting for transfers between devices: 9.25 us -> 9.82 us  [swap(): lax.ppermute(block, axes, [(source, i) for i, source in enumerate(sources)])]
    slice x6 -> x0, local copies, waits for them, and re-layouts: 0.37 us -> none  [the longest x5 0.36 us: body(): product[chi, part * rhs_count:(part + 1) * rhs_count]]
  transfers between devices with their start and end apart: 14 -> 14, of which waited for: 10 -> 11; matrix products, arithmetic and copies ran while one was open for 9% -> 8% of each run, Pallas kernels for 2% -> 2%
where the time goes in v12:
time: 33.3 us; the launch traced here: 33.1 us
  starting transfers between devices  14.4 us (43%)
  waiting for transfers between devices  9.82 us (29%)
  matrix products  3.03 us (9%)
  Pallas kernels  2.11 us (6%)
  local copies, waits for them, and re-layouts  1.99 us (6%)
  between operations  0.99 us (3%)
  other arithmetic  0.83 us (2%)
    ppermute x14, starting transfers between devices, swap(): lax.ppermute(block, axes, [(source, i) for i, source in enumerate(sources)])  14.4 us
    ppermute x14, waiting for transfers between devices, swap(): lax.ppermute(block, axes, [(source, i) for i, source in enumerate(sources)])  9.82 us
    dot_general x8, matrix products, sweep_in_pairs(): lax.dot_general(vectors, around[:, link], (((2,), (2,)), ((0,), (0,))), p...  1.95 us
    pallas_call x1, Pallas kernels, restrict(): pl.pallas_call(restrict_kernel, out_shape=[jax.ShapeDtypeStruct((rhs, 4 *...  1.58 us
    unnamed x8, local copies, waits for them, and re-layouts  0.87 us
    dot_general x4, matrix products, apply(): lax.dot_general(vector, matrix, (((1,), (1,)), ((), ())), precision=exact)  0.84 us
    convert_element_type x1, local copies, waits for them, and re-layouts, body(): return result.reshape(rhs_count, 2, 12, sites).astype(jnp.bfloat16)  0.83 us
  transfers between devices with their start and end apart: 14, of which 11 were waited for; matrix products, arithmetic and copies ran while one was open for 8% of the time, Pallas kernels for 2%

profile of v12, /device:TPU:0, one launch (start us, length us, event | category | flops | bytes accessed | tf_op | source)
XLA Modules:
  0.0 33.1 jit_solution(5487100034683109712)
XLA Ops:
  0.7 1.6 %shard_map.55 = (f32[16,96]{1,0:T(8,128)S(1)}, f32[16,96]{1,0:T(8,128)S(1)}) custom-call(s32[1]{0:T(128)S(6)} %copy.57.count_ref, bf16[16,12,2,256]{3,2,1,0:T(2,128)(2,1)} %bitcast.160, bf16[2,12,24,256]{3,2,1,0:T(8,128)(2,1)} %bitcast.158), custom_call_target="tpu_custom_call" | custom-call | flops 10000000 | bytes 500000 | tf_op jit(solution)/shard_map/pallas_call | solution.py:96
  2.4 0.5 %collective-permute-start.2 = (f32[2,2,2304]{2,1,0:T(2,128)S(1)}, f32[2,2,2304]{2,1,0:T(2,128)S(1)}, u32[]{:S(2)}, u32[]{:S(2)}) collective-permute-start(f32[2,2,2304]{2,1,0:T(2,128)S(1)} %maximum_select_fusion.1), channel_id=1, source_target_pairs={{8,0},{9,1},{10,2},{11,3},{12,4},{13,5},{14,6},{15,7},{0,8},{1,9},... | collective-permute-start | bytes 110600 | tf_op jit(solution)/shard_map/ppermute | solution.py:235
  3.3 0.8 %collective-permute-done = f32[16,96]{1,0:T(8,128)S(1)} collective-permute-done((f32[16,96]{1,0:T(8,128)S(1)}, f32[16,96]{1,0:T(8,128)S(1)}, u32[]{:S(2)}, u32[]{:S(2)}) %collective-permute-start) | collective-permute-done | bytes 6176 | tf_op jit(solution)/shard_map/ppermute | solution.py:235
  4.1 2.7 %collective-permute-start.3 = (f32[2,16,96]{2,1,0:T(8,128)S(1)}, f32[2,16,96]{2,1,0:T(8,128)S(1)}, u32[]{:S(2)}, u32[]{:S(2)}) collective-permute-start(f32[2,16,96]{2,1,0:T(8,128)S(1)} %pad_maximum_fusion.1), channel_id=1, source_target_pairs={{16,0},{17,1},{18,2},{19,3},{20,4},{21,5},{22,6},{23,7},{10,8},{11... | collective-permute-start | bytes 36872 | tf_op jit(solution)/shard_map/ppermute | solution.py:235
  6.7 1.5 %collective-permute-start.1 = (f32[2,16,96]{2,1,0:T(8,128)S(1)}, f32[2,16,96]{2,1,0:T(8,128)S(1)}, u32[]{:S(2)}, u32[]{:S(2)}) collective-permute-start(f32[2,16,96]{2,1,0:T(8,128)S(1)} %pad_maximum_fusion.1), channel_id=1, source_target_pairs={{1,0},{0,1},{3,2},{2,3},{5,4},{4,5},{7,6},{6,7},{14,8},{15,9},{12,... | collective-permute-start | bytes 36872 | tf_op jit(solution)/shard_map/ppermute | solution.py:235
  9.0 1.4 %collective-permute-done.1 = f32[2,16,96]{2,1,0:T(8,128)S(1)} collective-permute-done((f32[2,16,96]{2,1,0:T(8,128)S(1)}, f32[2,16,96]{2,1,0:T(8,128)S(1)}, u32[]{:S(2)}, u32[]{:S(2)}) %collective-permute-start.1) | collective-permute-done | bytes 12320 | tf_op jit(solution)/shard_map/ppermute | solution.py:235
  10.7 0.8 %collective-permute-start.4 = (f32[2,16,96]{2,1,0:T(8,128)S(1)}, f32[2,16,96]{2,1,0:T(8,128)S(1)}, u32[]{:S(2)}, u32[]{:S(2)}) collective-permute-start(f32[2,16,96]{2,1,0:T(8,128)S(1)} %fusion.3), channel_id=1, source_target_pairs={{8,0},{9,1},{10,2},{11,3},{12,4},{13,5},{14,6},{15,7},{0,8},{1,9},... | collective-permute-start | bytes 36872 | tf_op jit(solution)/shard_map/ppermute | solution.py:235
  11.5 0.8 %collective-permute-done.4 = f32[2,16,96]{2,1,0:T(8,128)S(1)} collective-permute-done((f32[2,16,96]{2,1,0:T(8,128)S(1)}, f32[2,16,96]{2,1,0:T(8,128)S(1)}, u32[]{:S(2)}, u32[]{:S(2)}) %collective-permute-start.4) | collective-permute-done | bytes 12320 | tf_op jit(solution)/shard_map/ppermute | solution.py:235
  12.4 1.6 %collective-permute-start.6 = (f32[2,16,96]{2,1,0:T(8,128)S(1)}, f32[2,16,96]{2,1,0:T(8,128)S(1)}, u32[]{:S(2)}, u32[]{:S(2)}) collective-permute-start(f32[2,16,96]{2,1,0:T(8,128)S(1)} %maximum_add_fusion.1), channel_id=1, source_target_pairs={{16,0},{17,1},{18,2},{19,3},{20,4},{21,5},{22,6},{23,7},{10,8},{11... | collective-permute-start | bytes 36872 | tf_op jit(solution)/shard_map/ppermute | solution.py:235
  14.0 1.5 %collective-permute-start.5 = (f32[2,16,96]{2,1,0:T(8,128)S(1)}, f32[2,16,96]{2,1,0:T(8,128)S(1)}, u32[]{:S(2)}, u32[]{:S(2)}) collective-permute-start(f32[2,16,96]{2,1,0:T(8,128)S(1)} %maximum_add_fusion.1), channel_id=1, source_target_pairs={{1,0},{0,1},{3,2},{2,3},{5,4},{4,5},{7,6},{6,7},{14,8},{15,9},{12,... | collective-permute-start | bytes 36872 | tf_op jit(solution)/shard_map/ppermute | solution.py:235
  15.8 0.8 %copy-done.3 = bf16[2,2,6,6,256]{4,1,3,2,0:T(2,128)(2,1)S(1)} copy-done((bf16[2,2,6,6,256]{4,1,3,2,0:T(2,128)(2,1)S(1)}, bf16[2,2,6,6,256]{4,1,3,2,0:T(2,128)(2,1)}, u32[]{:S(2)}) %copy-start.3) | copy-done | bytes 73752
  17.0 0.7 %collective-permute-done.5 = f32[2,16,96]{2,1,0:T(8,128)S(1)} collective-permute-done((f32[2,16,96]{2,1,0:T(8,128)S(1)}, f32[2,16,96]{2,1,0:T(8,128)S(1)}, u32[]{:S(2)}, u32[]{:S(2)}) %collective-permute-start.5) | collective-permute-done | bytes 12320 | tf_op jit(solution)/shard_map/ppermute | solution.py:235
  18.3 0.8 %collective-permute-done.7 = f32[2,16,96]{2,1,0:T(8,128)S(1)} collective-permute-done((f32[2,16,96]{2,1,0:T(8,128)S(1)}, f32[2,16,96]{2,1,0:T(8,128)S(1)}, u32[]{:S(2)}, u32[]{:S(2)}) %collective-permute-start.7) | collective-permute-done | bytes 12320 | tf_op jit(solution)/shard_map/ppermute | solution.py:235
  19.2 0.8 %collective-permute-start.9 = (f32[2,16,96]{2,1,0:T(8,128)S(1)}, f32[2,16,96]{2,1,0:T(8,128)S(1)}, u32[]{:S(2)}, u32[]{:S(2)}) collective-permute-start(f32[2,16,96]{2,1,0:T(8,128)S(1)} %maximum_add_fusion.2), channel_id=1, source_target_pairs={{16,0},{17,1},{18,2},{19,3},{20,4},{21,5},{22,6},{23,7},{10,8},{11... | collective-permute-start | bytes 36872 | tf_op jit(solution)/shard_map/ppermute | solution.py:235
  20.0 1.5 %collective-permute-start.8 = (f32[2,16,96]{2,1,0:T(8,128)S(1)}, f32[2,16,96]{2,1,0:T(8,128)S(1)}, u32[]{:S(2)}, u32[]{:S(2)}) collective-permute-start(f32[2,16,96]{2,1,0:T(8,128)S(1)} %maximum_add_fusion.2), channel_id=1, source_target_pairs={{1,0},{0,1},{3,2},{2,3},{5,4},{4,5},{7,6},{6,7},{14,8},{15,9},{12,... | collective-permute-start | bytes 36872 | tf_op jit(solution)/shard_map/ppermute | solution.py:235
  21.7 1.3 %collective-permute-done.9 = f32[2,16,96]{2,1,0:T(8,128)S(1)} collective-permute-done((f32[2,16,96]{2,1,0:T(8,128)S(1)}, f32[2,16,96]{2,1,0:T(8,128)S(1)}, u32[]{:S(2)}, u32[]{:S(2)}) %collective-permute-start.9) | collective-permute-done | bytes 12320 | tf_op jit(solution)/shard_map/ppermute | solution.py:235
  23.2 0.5 %collective-permute-done.8 = f32[2,16,96]{2,1,0:T(8,128)S(1)} collective-permute-done((f32[2,16,96]{2,1,0:T(8,128)S(1)}, f32[2,16,96]{2,1,0:T(8,128)S(1)}, u32[]{:S(2)}, u32[]{:S(2)}) %collective-permute-start.8) | collective-permute-done | bytes 12320 | tf_op jit(solution)/shard_map/ppermute | solution.py:235
  24.4 0.8 %collective-permute-done.10 = f32[2,16,96]{2,1,0:T(8,128)S(1)} collective-permute-done((f32[2,16,96]{2,1,0:T(8,128)S(1)}, f32[2,16,96]{2,1,0:T(8,128)S(1)}, u32[]{:S(2)}, u32[]{:S(2)}) %collective-permute-start.10) | collective-permute-done | bytes 12320 | tf_op jit(solution)/shard_map/ppermute | solution.py:235
  25.2 1.4 %collective-permute-start.12 = (f32[2,16,96]{2,1,0:T(8,128)S(1)}, f32[2,16,96]{2,1,0:T(8,128)S(1)}, u32[]{:S(2)}, u32[]{:S(2)}) collective-permute-start(f32[2,16,96]{2,1,0:T(8,128)S(1)} %maximum_add_fusion.3), channel_id=1, source_target_pairs={{16,0},{17,1},{18,2},{19,3},{20,4},{21,5},{22,6},{23,7},{10,8},{11... | collective-permute-start | bytes 36872 | tf_op jit(solution)/shard_map/ppermute | solution.py:235
  26.6 1.5 %collective-permute-start.11 = (f32[2,16,96]{2,1,0:T(8,128)S(1)}, f32[2,16,96]{2,1,0:T(8,128)S(1)}, u32[]{:S(2)}, u32[]{:S(2)}) collective-permute-start(f32[2,16,96]{2,1,0:T(8,128)S(1)} %maximum_add_fusion.3), channel_id=1, source_target_pairs={{1,0},{0,1},{3,2},{2,3},{5,4},{4,5},{7,6},{6,7},{14,8},{15,9},{12,... | collective-permute-start | bytes 36872 | tf_op jit(solution)/shard_map/ppermute | solution.py:235
  28.3 0.7 %collective-permute-done.12 = f32[2,16,96]{2,1,0:T(8,128)S(1)} collective-permute-done((f32[2,16,96]{2,1,0:T(8,128)S(1)}, f32[2,16,96]{2,1,0:T(8,128)S(1)}, u32[]{:S(2)}, u32[]{:S(2)}) %collective-permute-start.12) | collective-permute-done | bytes 12320 | tf_op jit(solution)/shard_map/ppermute | solution.py:235
  29.2 1.1 %collective-permute-done.11 = f32[2,16,96]{2,1,0:T(8,128)S(1)} collective-permute-done((f32[2,16,96]{2,1,0:T(8,128)S(1)}, f32[2,16,96]{2,1,0:T(8,128)S(1)}, u32[]{:S(2)}, u32[]{:S(2)}) %collective-permute-start.11) | collective-permute-done | bytes 12320 | tf_op jit(solution)/shard_map/ppermute | solution.py:235
  31.0 0.8 %collective-permute-done.13 = f32[16,96]{1,0:T(8,128)S(1)} collective-permute-done((f32[16,96]{1,0:T(8,128)S(1)}, f32[16,96]{1,0:T(8,128)S(1)}, u32[]{:S(2)}, u32[]{:S(2)}) %collective-permute-start.13) | collective-permute-done | bytes 6176 | tf_op jit(solution)/shard_map/ppermute | solution.py:235
  32.3 0.8 %copy.48 = bf16[16,2,2,6,256]{4,1,3,2,0:T(2,128)(2,1)} copy(bf16[16,2,2,6,256]{4,0,1,3,2:T(8,128)(2,1)S(1)} %fusion.7) | data formatting | bytes 393216 | tf_op jit(solution)/shard_map/convert_element_type | solution.py:293
  (72 shorter events, 5.4 us)
Async XLA Ops:
  0.7 1.6 %copy-start.2 = (f32[1,9,2,2304]{3,2,1,0:T(2,128)S(1)}, f32[1,9,2,2304]{3,2,1,0:T(2,128)}, u32[]{:S(2)}) copy-start(f32[1,9,2,2304]{3,2,1,0:T(2,128)} %param.8) | copy-start | bytes 497668
  2.4 5.9 %collective-permute-start.2 = (f32[2,2,2304]{2,1,0:T(2,128)S(1)}, f32[2,2,2304]{2,1,0:T(2,128)S(1)}, u32[]{:S(2)}, u32[]{:S(2)}) collective-permute-start(f32[2,2,2304]{2,1,0:T(2,128)S(1)} %maximum_select_fusion.1), channel_id=1, source_target_pairs={{8,0},{9,1},{10,2},{11,3},{12,4},{13,5},{14,6},{15,7},{0,8},{1,9},... | collective-permute-start | bytes 110600 | tf_op jit(solution)/shard_map/ppermute | solution.py:235
  2.9 1.2 %collective-permute-start = (f32[16,96]{1,0:T(8,128)S(1)}, f32[16,96]{1,0:T(8,128)S(1)}, u32[]{:S(2)}, u32[]{:S(2)}) collective-permute-start(f32[16,96]{1,0:T(8,128)S(1)} %get-tuple-element.13), channel_id=1, source_target_pairs={{8,0},{9,1},{10,2},{11,3},{12,4},{13,5},{14,6},{15,7},{0,8},{1,9},... | collective-permute-start | bytes 18440 | tf_op jit(solution)/shard_map/ppermute | solution.py:235
  4.1 4.7 %collective-permute-start.3 = (f32[2,16,96]{2,1,0:T(8,128)S(1)}, f32[2,16,96]{2,1,0:T(8,128)S(1)}, u32[]{:S(2)}, u32[]{:S(2)}) collective-permute-start(f32[2,16,96]{2,1,0:T(8,128)S(1)} %pad_maximum_fusion.1), channel_id=1, source_target_pairs={{16,0},{17,1},{18,2},{19,3},{20,4},{21,5},{22,6},{23,7},{10,8},{11... | collective-permute-start | bytes 36872 | tf_op jit(solution)/shard_map/ppermute | solution.py:235
  6.7 3.7 %collective-permute-start.1 = (f32[2,16,96]{2,1,0:T(8,128)S(1)}, f32[2,16,96]{2,1,0:T(8,128)S(1)}, u32[]{:S(2)}, u32[]{:S(2)}) collective-permute-start(f32[2,16,96]{2,1,0:T(8,128)S(1)} %pad_maximum_fusion.1), channel_id=1, source_target_pairs={{1,0},{0,1},{3,2},{2,3},{5,4},{4,5},{7,6},{6,7},{14,8},{15,9},{12,... | collective-permute-start | bytes 36872 | tf_op jit(solution)/shard_map/ppermute | solution.py:235
  9.0 6.6 %copy-start.1 = (bf16[16,2,12,256]{3,1,2,0:T(2,128)(2,1)S(1)}, bf16[16,2,12,256]{3,1,2,0:T(2,128)(2,1)}, u32[]{:S(2)}) copy-start(bf16[16,2,12,256]{3,1,2,0:T(2,128)(2,1)} %param.5) | copy-start | bytes 589828
  10.7 1.6 %collective-permute-start.4 = (f32[2,16,96]{2,1,0:T(8,128)S(1)}, f32[2,16,96]{2,1,0:T(8,128)S(1)}, u32[]{:S(2)}, u32[]{:S(2)}) collective-permute-start(f32[2,16,96]{2,1,0:T(8,128)S(1)} %fusion.3), channel_id=1, source_target_pairs={{8,0},{9,1},{10,2},{11,3},{12,4},{13,5},{14,6},{15,7},{0,8},{1,9},... | collective-permute-start | bytes 36872 | tf_op jit(solution)/shard_map/ppermute | solution.py:235
  12.4 4.4 %collective-permute-start.6 = (f32[2,16,96]{2,1,0:T(8,128)S(1)}, f32[2,16,96]{2,1,0:T(8,128)S(1)}, u32[]{:S(2)}, u32[]{:S(2)}) collective-permute-start(f32[2,16,96]{2,1,0:T(8,128)S(1)} %maximum_add_fusion.1), channel_id=1, source_target_pairs={{16,0},{17,1},{18,2},{19,3},{20,4},{21,5},{22,6},{23,7},{10,8},{11... | collective-permute-start | bytes 36872 | tf_op jit(solution)/shard_map/ppermute | solution.py:235
  14.0 3.7 %collective-permute-start.5 = (f32[2,16,96]{2,1,0:T(8,128)S(1)}, f32[2,16,96]{2,1,0:T(8,128)S(1)}, u32[]{:S(2)}, u32[]{:S(2)}) collective-permute-start(f32[2,16,96]{2,1,0:T(8,128)S(1)} %maximum_add_fusion.1), channel_id=1, source_target_pairs={{1,0},{0,1},{3,2},{2,3},{5,4},{4,5},{7,6},{6,7},{14,8},{15,9},{12,... | collective-permute-start | bytes 36872 | tf_op jit(solution)/shard_map/ppermute | solution.py:235
  15.8 0.9 %copy-start.3 = (bf16[2,2,6,6,256]{4,1,3,2,0:T(2,128)(2,1)S(1)}, bf16[2,2,6,6,256]{4,1,3,2,0:T(2,128)(2,1)}, u32[]{:S(2)}) copy-start(bf16[2,2,6,6,256]{4,1,3,2,0:T(2,128)(2,1)} %param.7) | copy-start | bytes 221188
  17.9 1.2 %collective-permute-start.7 = (f32[2,16,96]{2,1,0:T(8,128)S(1)}, f32[2,16,96]{2,1,0:T(8,128)S(1)}, u32[]{:S(2)}, u32[]{:S(2)}) collective-permute-start(f32[2,16,96]{2,1,0:T(8,128)S(1)} %fusion.2), channel_id=1, source_target_pairs={{8,0},{9,1},{10,2},{11,3},{12,4},{13,5},{14,6},{15,7},{0,8},{1,9},... | collective-permute-start | bytes 36872 | tf_op jit(solution)/shard_map/ppermute | solution.py:235
  19.2 3.8 %collective-permute-start.9 = (f32[2,16,96]{2,1,0:T(8,128)S(1)}, f32[2,16,96]{2,1,0:T(8,128)S(1)}, u32[]{:S(2)}, u32[]{:S(2)}) collective-permute-start(f32[2,16,96]{2,1,0:T(8,128)S(1)} %maximum_add_fusion.2), channel_id=1, source_target_pairs={{16,0},{17,1},{18,2},{19,3},{20,4},{21,5},{22,6},{23,7},{10,8},{11... | collective-permute-start | bytes 36872 | tf_op jit(solution)/shard_map/ppermute | solution.py:235
  20.0 3.7 %collective-permute-start.8 = (f32[2,16,96]{2,1,0:T(8,128)S(1)}, f32[2,16,96]{2,1,0:T(8,128)S(1)}, u32[]{:S(2)}, u32[]{:S(2)}) collective-permute-start(f32[2,16,96]{2,1,0:T(8,128)S(1)} %maximum_add_fusion.2), channel_id=1, source_target_pairs={{1,0},{0,1},{3,2},{2,3},{5,4},{4,5},{7,6},{6,7},{14,8},{15,9},{12,... | collective-permute-start | bytes 36872 | tf_op jit(solution)/shard_map/ppermute | solution.py:235
  24.0 1.2 %collective-permute-start.10 = (f32[2,16,96]{2,1,0:T(8,128)S(1)}, f32[2,16,96]{2,1,0:T(8,128)S(1)}, u32[]{:S(2)}, u32[]{:S(2)}) collective-permute-start(f32[2,16,96]{2,1,0:T(8,128)S(1)} %fusion.1), channel_id=1, source_target_pairs={{8,0},{9,1},{10,2},{11,3},{12,4},{13,5},{14,6},{15,7},{0,8},{1,9},... | collective-permute-start | bytes 36872 | tf_op jit(solution)/shard_map/ppermute | solution.py:235
  25.2 3.8 %collective-permute-start.12 = (f32[2,16,96]{2,1,0:T(8,128)S(1)}, f32[2,16,96]{2,1,0:T(8,128)S(1)}, u32[]{:S(2)}, u32[]{:S(2)}) collective-permute-start(f32[2,16,96]{2,1,0:T(8,128)S(1)} %maximum_add_fusion.3), channel_id=1, source_target_pairs={{16,0},{17,1},{18,2},{19,3},{20,4},{21,5},{22,6},{23,7},{10,8},{11... | collective-permute-start | bytes 36872 | tf_op jit(solution)/shard_map/ppermute | solution.py:235
  26.6 3.7 %collective-permute-start.11 = (f32[2,16,96]{2,1,0:T(8,128)S(1)}, f32[2,16,96]{2,1,0:T(8,128)S(1)}, u32[]{:S(2)}, u32[]{:S(2)}) collective-permute-start(f32[2,16,96]{2,1,0:T(8,128)S(1)} %maximum_add_fusion.3), channel_id=1, source_target_pairs={{1,0},{0,1},{3,2},{2,3},{5,4},{4,5},{7,6},{6,7},{14,8},{15,9},{12,... | collective-permute-start | bytes 36872 | tf_op jit(solution)/shard_map/ppermute | solution.py:235
  30.5 1.2 %collective-permute-start.13 = (f32[16,96]{1,0:T(8,128)S(1)}, f32[16,96]{1,0:T(8,128)S(1)}, u32[]{:S(2)}, u32[]{:S(2)}) collective-permute-start(f32[16,96]{1,0:T(8,128)S(1)} %slice_bitcast_fusion.39), channel_id=1, source_target_pairs={{8,0},{9,1},{10,2},{11,3},{12,4},{13,5},{14,6},{15,7},{0,8},{1,9},... | collective-permute-start | bytes 18440 | tf_op jit(solution)/shard_map/ppermute | solution.py:235
  30.8 1.2 %copy-start = (bf16[2,24,12,256]{3,1,2,0:T(8,128)(2,1)S(1)}, bf16[2,24,12,256]{3,1,2,0:T(8,128)(2,1)}, u32[]{:S(2)}) copy-start(bf16[2,24,12,256]{3,1,2,0:T(8,128)(2,1)} %param.6) | copy-start | bytes 884740

commit v13 on v12

--- a/solution.py
+++ b/solution.py
@@ -109,17 +109,105 @@
     )(count, rows, vectors)
 
 
-def local_term(residual, clover_inverse):
-    rhs_count, _, _, sites = residual.shape
-    rows = residual.reshape(rhs_count, 2, 2, 6, sites).astype(jnp.float32)
-    clover = clover_inverse.astype(jnp.float32)
-
-    def local_apply(left, right):
-        return sum(left[:, :, b][None] * right[:, :, b][:, :, None] for b in range(6))
-
-    local_real = local_apply(clover[0], rows[:, 0]) - local_apply(clover[1], rows[:, 1])
-    local_imag = local_apply(clover[0], rows[:, 1]) + local_apply(clover[1], rows[:, 0])
-    return local_real, local_imag
+def extend_kernel(first_ref, second_ref, used_ref, vectors_ref, local_ref, out_hbm, out_ref, scratch, sems):
+    rhs, parts, _, sites = out_ref.shape
+    vecs = vectors_ref.shape[1] // 2
+    half = parts // 2
+    coarse = (first_ref[...] + second_ref[...]) * used_ref[...]
+    for chi in range(2):
+        real = coarse[:, chi * vecs : (chi + 1) * vecs]
+        imag = coarse[:, (2 + chi) * vecs : (3 + chi) * vecs]
+        scratch[chi, pl.ds(0, rhs, stride=2), : 2 * vecs] = jnp.concatenate([real, -imag], 1)
+        scratch[chi, pl.ds(1, rhs, stride=2), : 2 * vecs] = jnp.concatenate([imag, real], 1)
+    copies = []
+    for chi in range(2):
+        weights = scratch[chi, :, : 2 * vecs].astype(jnp.bfloat16)
+        for c in range(half * chi, half * chi + half):
+            lift = jnp.dot(weights, vectors_ref[c], preferred_element_type=jnp.float32)
+            total = (local_ref[c] + lift).astype(jnp.bfloat16)
+            out_ref[:, c] = total.reshape(rhs, 2, sites)
+        span = pl.ds(half * chi, half)
+        copies.append(pltpu.make_async_copy(out_ref.at[:, span], out_hbm.at[:, span], sems.at[chi]))
+        copies[-1].start()
+    for copy in copies:
+        copy.wait()
+
+
+small = pltpu.CompilerParams(vmem_limit_bytes=8 * 2**20)
+in_vmem = pl.BlockSpec(memory_space=pltpu.VMEM)
+
+
+def extend(summands, used, vectors, local):
+    parts, _, sites = vectors.shape
+    rhs = used.shape[0]
+    shape = (rhs, parts, 2, sites)
+    return pl.pallas_call(
+        extend_kernel,
+        out_shape=jax.ShapeDtypeStruct(shape, jnp.bfloat16),
+        in_specs=[in_vmem] * 5,
+        out_specs=pl.BlockSpec(memory_space=pltpu.HBM),
+        scratch_shapes=[
+            pltpu.VMEM(shape, jnp.bfloat16),
+            pltpu.VMEM((2, 2 * rhs, 128), jnp.float32),
+            pltpu.SemaphoreType.DMA((2,)),
+        ],
+        compiler_params=small,
+        cost_estimate=pl.CostEstimate(flops=10**7, bytes_accessed=10**6, transcendentals=0),
+    )(*summands, used, vectors, local)
+
+
+def hold_kernel(vectors_ref, out_ref):
+    vecs = vectors_ref.shape[2]
+    for c in range(vectors_ref.shape[1]):
+        out_ref[c] = jnp.concatenate([vectors_ref[0, c], vectors_ref[1, c]], 0)
+
+
+def hold(vectors):
+    _, parts, vecs, sites = vectors.shape
+    return pl.pallas_call(
+        hold_kernel,
+        out_shape=jax.ShapeDtypeStruct((parts, 2 * vecs, sites), vectors.dtype),
+        in_specs=[in_vmem],
+        out_specs=in_vmem,
+        compiler_params=small,
+        cost_estimate=pl.CostEstimate(flops=10**5, bytes_accessed=10**5, transcendentals=0),
+    )(vectors)
+
+
+def local_kernel(rows_ref, clover_ref, out_ref):
+    rhs, parts, _, sites = rows_ref.shape
+    half = parts // 2
+    row = lax.broadcasted_iota(jnp.int32, (2 * rhs, 2 * rhs), 0)
+    col = lax.broadcasted_iota(jnp.int32, (2 * rhs, 2 * rhs), 1)
+    turn = jnp.where((row % 2 == 0) & (col == row + 1), -1.0, 0.0)
+    turn = jnp.where((row % 2 == 1) & (col == row - 1), 1.0, turn).astype(jnp.bfloat16)
+    for chi in range(2):
+        for start in range(0, sites, 128):
+            lanes = slice(start, start + 128)
+            plain, turned = [], []
+            for b in range(half):
+                rows = rows_ref[:, half * chi + b, :, lanes].reshape(2 * rhs, 128)
+                plain.append(rows.astype(jnp.float32))
+                turned.append(jnp.dot(turn, rows, preferred_element_type=jnp.float32))
+            for a in range(half):
+                total = jnp.zeros((2 * rhs, 128), jnp.float32)
+                for b in range(half):
+                    real = clover_ref[0, a, b, :, lanes].astype(jnp.float32)[chi : chi + 1]
+                    imag = clover_ref[1, a, b, :, lanes].astype(jnp.float32)[chi : chi + 1]
+                    total += real * plain[b] + imag * turned[b]
+                out_ref[half * chi + a, :, lanes] = total
+
+
+def local_term(rows, clover):
+    rhs, parts, _, sites = rows.shape
+    return pl.pallas_call(
+        local_kernel,
+        out_shape=jax.ShapeDtypeStruct((parts, 2 * rhs, sites), jnp.float32),
+        in_specs=[in_vmem] * 2,
+        out_specs=in_vmem,
+        compiler_params=small,
+        cost_estimate=pl.CostEstimate(flops=10**5, bytes_accessed=10**5, transcendentals=0),
+    )(rows, clover)
 
 
 def real_form(matrix, dim):
@@ -160,10 +248,14 @@
         moved = [fetch(coarse, link) for link in order]
         kept = half + apply(coarse, own)
         if sweep_id == 1:
-            rows, clover, kept = lax.optimization_barrier((*held, kept))
-            local = local_term(rows, clover)
-        coarse = kept + apply(jnp.concatenate(moved, 1), around)
-    return coarse, local
+            rows, clover, kept = lax.optimization_barrier((*held[:2], kept))
+            local, kept = lax.optimization_barrier((local_term(rows, clover), kept))
+        if sweep_id == 2:
+            stored, kept = lax.optimization_barrier((held[2], kept))
+            vectors, kept = lax.optimization_barrier((hold(stored), kept))
+        added = apply(jnp.concatenate(moved, 1), around)
+        coarse = kept + added
+    return (kept, added), vectors, local
 
 
 def shares_chip():
@@ -250,17 +342,20 @@
         moved = [swap(pair, first), swap(pair, second)]
         kept = half + apply(jnp.concatenate([pair[0], pair[1]], 1), inside)
         if sweep_id == 1:
-            rows, clover, kept = lax.optimization_barrier((*held, kept))
-            local = local_term(rows, clover)
+            rows, clover, kept = lax.optimization_barrier((*held[:2], kept))
+            local, kept = lax.optimization_barrier((local_term(rows, clover), kept))
+        if sweep_id == 2:
+            stored, kept = lax.optimization_barrier((held[2], kept))
+            vectors, kept = lax.optimization_barrier((hold(stored), kept))
         part = jnp.stack([kept, jnp.zeros_like(kept)])
-        for link, vectors in enumerate(moved):
+        for link, block in enumerate(moved):
             part = part + lax.dot_general(
-                vectors, around[:, link], (((2,), (2,)), ((0,), (0,))), precision=exact
+                block, around[:, link], (((2,), (2,)), ((0,), (0,))), precision=exact
             )
         if sweep_id < ITERS - 2:
             other = swap(part, mate)
             pair = part + jnp.stack([other[1], other[0]])
-    return part[0] + swap(part[1], mate), local
+    return (part[0], swap(part[1], mate)), vectors, local
 
 
 def body(residual, null_vectors, clover_inverse, coarse_op, vector_count):
@@ -271,26 +366,15 @@
     rows = residual.transpose(0, 2, 1, 3)
     stored = null_vectors.transpose(0, 2, 1, 3)
     half, used = restrict(vector_count, rows, stored)
-    vectors = stored.reshape(2, 2, 6, vec_total, sites)
 
     coarse_op, half = lax.optimization_barrier((coarse_op, half))
     operator = coarse_op.reshape(9, 2, coarse_dim * coarse_dim)
-    held = (residual, clover_inverse)
+    held = (rows, clover_inverse.transpose(0, 2, 3, 1, 4), stored)
     if shares_chip():
-        coarse, local = sweep_in_pairs(half, operator, coarse_dim, held)
+        summands, vectors, local = sweep_in_pairs(half, operator, coarse_dim, held)
     else:
-        coarse, local = sweep_alone(half, operator, coarse_dim, held)
-    local_real, local_imag = local
-
-    rounded = coarse * used
-    cut = [rounded[:, p * vec_total : (p + 1) * vec_total] for p in range(4)]
-    by_real = jnp.stack([jnp.concatenate([cut[chi], cut[2 + chi]], 0) for chi in range(2)])
-    by_imag = jnp.stack([jnp.concatenate([-cut[2 + chi], cut[chi]], 0) for chi in range(2)])
-    weights = jnp.stack([by_real, by_imag]).astype(jnp.bfloat16)
-    lift = jnp.einsum("pxrk,pxcks->xcrs", weights, vectors, preferred_element_type=jnp.float32)
-    lift = lift.reshape(2, 6, 2, rhs_count, sites).transpose(3, 2, 0, 1, 4)
-    result = jnp.stack([local_real, local_imag], 1) + lift
-    return result.reshape(rhs_count, 2, 12, sites).astype(jnp.bfloat16)
+        summands, vectors, local = sweep_alone(half, operator, coarse_dim, held)
+    return extend(summands, used, vectors, local).transpose(0, 2, 1, 3)
 
 
 def solution(mesh):

time: 33.3 us -> 33.5 us (level)
  local copies, waits for them, and re-layouts: 1.99 us -> 0.07 us
  waiting for transfers between devices: 9.82 us -> 11.4 us
  Pallas kernels: 2.11 us -> 3.66 us
  other arithmetic: 0.83 us -> 0.19 us
    ppermute x14, waiting for transfers between devices: 9.82 us -> 11.4 us  [swap(): lax.ppermute(block, axes, [(source, i) for i, source in enumerate(sources)])]
    pallas_call x0 -> x3, Pallas kernels: none -> 1.55 us  [the longest x1 0.94 us: extend(): pl.pallas_call(extend_kernel, out_shape=jax.ShapeDtypeStruct(shape, jnp.b...]
    convert_element_type x2 -> x0, local copies, waits for them, and re-layouts: 0.88 us -> none  [the longest x1 0.83 us: body(): return result.reshape(rhs_count, 2, 12, sites).astype(jnp.bfloat16)]
    unnamed x8, local copies, waits for them, and re-layouts: 0.87 us -> 0.05 us
    dot_general x9 -> x8, matrix products: 2.19 us -> 2.04 us  [sweep_in_pairs(): lax.dot_general(block, around[:, link], (((2,), (2,)), ((0,), (0,))), pre...]
  transfers between devices with their start and end apart: 14 -> 14, of which waited for: 11 -> 9; matrix products, arithmetic and copies ran while one was open for 8% -> 6% of each run, Pallas kernels for 2% -> 3%
where the time goes in v13:
time: 33.5 us; the launch traced here: 33.3 us
  starting transfers between devices  14.4 us (43%)
  waiting for transfers between devices  11.4 us (34%)
  Pallas kernels  3.66 us (11%)
  matrix products  2.88 us (9%)
  between operations  0.81 us (2%)
    ppermute x14, starting transfers between devices, swap(): lax.ppermute(block, axes, [(source, i) for i, source in enumerate(sources)])  14.4 us
    ppermute x14, waiting for transfers between devices, swap(): lax.ppermute(block, axes, [(source, i) for i, source in enumerate(sources)])  11.4 us
    dot_general x8, matrix products, sweep_in_pairs(): lax.dot_general(block, around[:, link], (((2,), (2,)), ((0,), (0,))), pre...  2.04 us
    pallas_call x1, Pallas kernels, restrict(): pl.pallas_call(restrict_kernel, out_shape=[jax.ShapeDtypeStruct((rhs, 4 *...  1.58 us
    pallas_call x1, Pallas kernels, extend(): pl.pallas_call(extend_kernel, out_shape=jax.ShapeDtypeStruct(shape, jnp.b...  0.94 us
    dot_general x4, matrix products, apply(): lax.dot_general(vector, matrix, (((1,), (1,)), ((), ())), precision=exact)  0.84 us
  transfers between devices with their start and end apart: 14, of which 9 were waited for; matrix products, arithmetic and copies ran while one was open for 6% of the time, Pallas kernels for 3%

profile of v13, /device:TPU:0, one launch (start us, length us, event | category | flops | bytes accessed | tf_op | source)
XLA Modules:
  0.0 33.3 jit_solution(16254927577360107959)
XLA Ops:
  0.7 1.6 %shard_map.55 = (f32[16,96]{1,0:T(8,128)S(1)}, f32[16,96]{1,0:T(8,128)S(1)}) custom-call(s32[1]{0:T(128)S(6)} %copy.6.count_ref, bf16[16,12,2,256]{3,2,1,0:T(2,128)(2,1)} %bitcast.70, bf16[2,12,24,256]{3,2,1,0:T(8,128)(2,1)} %bitcast.68), custom_call_target="tpu_custom_call" | custom-call | flops 10000000 | bytes 500000 | tf_op jit(solution)/shard_map/pallas_call | solution.py:96
  2.2 0.5 %collective-permute-start = (f32[16,96]{1,0:T(8,128)S(1)}, f32[16,96]{1,0:T(8,128)S(1)}, u32[]{:S(2)}, u32[]{:S(2)}) collective-permute-start(f32[16,96]{1,0:T(8,128)S(1)} %get-tuple-element.19), channel_id=1, source_target_pairs={{8,0},{9,1},{10,2},{11,3},{12,4},{13,5},{14,6},{15,7},{0,8},{1,9},... | collective-permute-start | bytes 18440 | tf_op jit(solution)/shard_map/ppermute | solution.py:327
  3.6 2.9 %collective-permute-start.3 = (f32[2,16,96]{2,1,0:T(8,128)S(1)}, f32[2,16,96]{2,1,0:T(8,128)S(1)}, u32[]{:S(2)}, u32[]{:S(2)}) collective-permute-start(f32[2,16,96]{2,1,0:T(8,128)S(1)} %pad_maximum_fusion.1), channel_id=1, source_target_pairs={{16,0},{17,1},{18,2},{19,3},{20,4},{21,5},{22,6},{23,7},{10,8},{11... | collective-permute-start | bytes 36872 | tf_op jit(solution)/shard_map/ppermute | solution.py:327
  6.5 1.5 %collective-permute-start.1 = (f32[2,16,96]{2,1,0:T(8,128)S(1)}, f32[2,16,96]{2,1,0:T(8,128)S(1)}, u32[]{:S(2)}, u32[]{:S(2)}) collective-permute-start(f32[2,16,96]{2,1,0:T(8,128)S(1)} %pad_maximum_fusion.1), channel_id=1, source_target_pairs={{1,0},{0,1},{3,2},{2,3},{5,4},{4,5},{7,6},{6,7},{14,8},{15,9},{12,... | collective-permute-start | bytes 36872 | tf_op jit(solution)/shard_map/ppermute | solution.py:327
  8.8 1.4 %collective-permute-done.1 = f32[2,16,96]{2,1,0:T(8,128)S(1)} collective-permute-done((f32[2,16,96]{2,1,0:T(8,128)S(1)}, f32[2,16,96]{2,1,0:T(8,128)S(1)}, u32[]{:S(2)}, u32[]{:S(2)}) %collective-permute-start.1) | collective-permute-done | bytes 12320 | tf_op jit(solution)/shard_map/ppermute | solution.py:327
  10.4 0.6 %collective-permute-start.4 = (f32[2,16,96]{2,1,0:T(8,128)S(1)}, f32[2,16,96]{2,1,0:T(8,128)S(1)}, u32[]{:S(2)}, u32[]{:S(2)}) collective-permute-start(f32[2,16,96]{2,1,0:T(8,128)S(1)} %fusion.3), channel_id=1, source_target_pairs={{8,0},{9,1},{10,2},{11,3},{12,4},{13,5},{14,6},{15,7},{0,8},{1,9},... | collective-permute-start | bytes 36872 | tf_op jit(solution)/shard_map/ppermute | solution.py:327
  11.1 0.8 %collective-permute-done.4 = f32[2,16,96]{2,1,0:T(8,128)S(1)} collective-permute-done((f32[2,16,96]{2,1,0:T(8,128)S(1)}, f32[2,16,96]{2,1,0:T(8,128)S(1)}, u32[]{:S(2)}, u32[]{:S(2)}) %collective-permute-start.4) | collective-permute-done | bytes 12320 | tf_op jit(solution)/shard_map/ppermute | solution.py:327
  11.9 1.6 %collective-permute-start.5 = (f32[2,16,96]{2,1,0:T(8,128)S(1)}, f32[2,16,96]{2,1,0:T(8,128)S(1)}, u32[]{:S(2)}, u32[]{:S(2)}) collective-permute-start(f32[2,16,96]{2,1,0:T(8,128)S(1)} %maximum_add_fusion), channel_id=1, source_target_pairs={{1,0},{0,1},{3,2},{2,3},{5,4},{4,5},{7,6},{6,7},{14,8},{15,9},{12,... | collective-permute-start | bytes 36872 | tf_op jit(solution)/shard_map/ppermute | solution.py:327
  13.5 1.5 %collective-permute-start.6 = (f32[2,16,96]{2,1,0:T(8,128)S(1)}, f32[2,16,96]{2,1,0:T(8,128)S(1)}, u32[]{:S(2)}, u32[]{:S(2)}) collective-permute-start(f32[2,16,96]{2,1,0:T(8,128)S(1)} %maximum_add_fusion), channel_id=1, source_target_pairs={{16,0},{17,1},{18,2},{19,3},{20,4},{21,5},{22,6},{23,7},{10,8},{11... | collective-permute-start | bytes 36872 | tf_op jit(solution)/shard_map/ppermute | solution.py:327
  15.3 0.6 %shard_map.58.local_ref = f32[12,32,256]{2,1,0:T(8,128)S(1)} custom-call(bf16[16,12,2,256]{3,2,1,0:T(2,128)(2,1)S(1)} %bitcast.71, bf16[2,6,6,2,256]{4,3,2,1,0:T(2,128)(2,1)S(1)} %bitcast.73), custom_call_target="tpu_custom_call" | custom-call | flops 100000 | bytes 100000 | tf_op jit(solution)/shard_map/pallas_call | solution.py:203
  15.9 1.4 %collective-permute-done.6 = f32[2,16,96]{2,1,0:T(8,128)S(1)} collective-permute-done((f32[2,16,96]{2,1,0:T(8,128)S(1)}, f32[2,16,96]{2,1,0:T(8,128)S(1)}, u32[]{:S(2)}, u32[]{:S(2)}) %collective-permute-start.6) | collective-permute-done | bytes 12320 | tf_op jit(solution)/shard_map/ppermute | solution.py:327
  17.7 0.6 %collective-permute-start.7 = (f32[2,16,96]{2,1,0:T(8,128)S(1)}, f32[2,16,96]{2,1,0:T(8,128)S(1)}, u32[]{:S(2)}, u32[]{:S(2)}) collective-permute-start(f32[2,16,96]{2,1,0:T(8,128)S(1)} %fusion.2), channel_id=1, source_target_pairs={{8,0},{9,1},{10,2},{11,3},{12,4},{13,5},{14,6},{15,7},{0,8},{1,9},... | collective-permute-start | bytes 36872 | tf_op jit(solution)/shard_map/ppermute | solution.py:327
  18.4 0.8 %collective-permute-done.7 = f32[2,16,96]{2,1,0:T(8,128)S(1)} collective-permute-done((f32[2,16,96]{2,1,0:T(8,128)S(1)}, f32[2,16,96]{2,1,0:T(8,128)S(1)}, u32[]{:S(2)}, u32[]{:S(2)}) %collective-permute-start.7) | collective-permute-done | bytes 12320 | tf_op jit(solution)/shard_map/ppermute | solution.py:327
  19.2 1.6 %collective-permute-start.8 = (f32[2,16,96]{2,1,0:T(8,128)S(1)}, f32[2,16,96]{2,1,0:T(8,128)S(1)}, u32[]{:S(2)}, u32[]{:S(2)}) collective-permute-start(f32[2,16,96]{2,1,0:T(8,128)S(1)} %maximum_add_fusion.1), channel_id=1, source_target_pairs={{1,0},{0,1},{3,2},{2,3},{5,4},{4,5},{7,6},{6,7},{14,8},{15,9},{12,... | collective-permute-start | bytes 36872 | tf_op jit(solution)/shard_map/ppermute | solution.py:327
  20.8 0.8 %collective-permute-start.9 = (f32[2,16,96]{2,1,0:T(8,128)S(1)}, f32[2,16,96]{2,1,0:T(8,128)S(1)}, u32[]{:S(2)}, u32[]{:S(2)}) collective-permute-start(f32[2,16,96]{2,1,0:T(8,128)S(1)} %maximum_add_fusion.1), channel_id=1, source_target_pairs={{16,0},{17,1},{18,2},{19,3},{20,4},{21,5},{22,6},{23,7},{10,8},{11... | collective-permute-start | bytes 36872 | tf_op jit(solution)/shard_map/ppermute | solution.py:327
  21.9 2.6 %collective-permute-done.9 = f32[2,16,96]{2,1,0:T(8,128)S(1)} collective-permute-done((f32[2,16,96]{2,1,0:T(8,128)S(1)}, f32[2,16,96]{2,1,0:T(8,128)S(1)}, u32[]{:S(2)}, u32[]{:S(2)}) %collective-permute-start.9) | collective-permute-done | bytes 12320 | tf_op jit(solution)/shard_map/ppermute | solution.py:327
  25.0 0.4 %collective-permute-start.10 = (f32[2,16,96]{2,1,0:T(8,128)S(1)}, f32[2,16,96]{2,1,0:T(8,128)S(1)}, u32[]{:S(2)}, u32[]{:S(2)}) collective-permute-start(f32[2,16,96]{2,1,0:T(8,128)S(1)} %fusion.1), channel_id=1, source_target_pairs={{8,0},{9,1},{10,2},{11,3},{12,4},{13,5},{14,6},{15,7},{0,8},{1,9},... | collective-permute-start | bytes 36872 | tf_op jit(solution)/shard_map/ppermute | solution.py:327
  25.4 0.8 %collective-permute-done.10 = f32[2,16,96]{2,1,0:T(8,128)S(1)} collective-permute-done((f32[2,16,96]{2,1,0:T(8,128)S(1)}, f32[2,16,96]{2,1,0:T(8,128)S(1)}, u32[]{:S(2)}, u32[]{:S(2)}) %collective-permute-start.10) | collective-permute-done | bytes 12320 | tf_op jit(solution)/shard_map/ppermute | solution.py:327
  26.3 0.6 %collective-permute-start.11 = (f32[2,16,96]{2,1,0:T(8,128)S(1)}, f32[2,16,96]{2,1,0:T(8,128)S(1)}, u32[]{:S(2)}, u32[]{:S(2)}) collective-permute-start(f32[2,16,96]{2,1,0:T(8,128)S(1)} %maximum_add_fusion.2), channel_id=1, source_target_pairs={{1,0},{0,1},{3,2},{2,3},{5,4},{4,5},{7,6},{6,7},{14,8},{15,9},{12,... | collective-permute-start | bytes 36872 | tf_op jit(solution)/shard_map/ppermute | solution.py:327
  26.9 1.3 %collective-permute-start.12 = (f32[2,16,96]{2,1,0:T(8,128)S(1)}, f32[2,16,96]{2,1,0:T(8,128)S(1)}, u32[]{:S(2)}, u32[]{:S(2)}) collective-permute-start(f32[2,16,96]{2,1,0:T(8,128)S(1)} %maximum_add_fusion.2), channel_id=1, source_target_pairs={{16,0},{17,1},{18,2},{19,3},{20,4},{21,5},{22,6},{23,7},{10,8},{11... | collective-permute-start | bytes 36872 | tf_op jit(solution)/shard_map/ppermute | solution.py:327
  28.4 2.3 %collective-permute-done.12 = f32[2,16,96]{2,1,0:T(8,128)S(1)} collective-permute-done((f32[2,16,96]{2,1,0:T(8,128)S(1)}, f32[2,16,96]{2,1,0:T(8,128)S(1)}, u32[]{:S(2)}, u32[]{:S(2)}) %collective-permute-start.12) | collective-permute-done | bytes 12320 | tf_op jit(solution)/shard_map/ppermute | solution.py:327
  31.2 0.4 %collective-permute-start.13 = (f32[16,96]{1,0:T(8,128)S(1)}, f32[16,96]{1,0:T(8,128)S(1)}, u32[]{:S(2)}, u32[]{:S(2)}) collective-permute-start(f32[16,96]{1,0:T(8,128)S(1)} %get-tuple-element.37), channel_id=1, source_target_pairs={{8,0},{9,1},{10,2},{11,3},{12,4},{13,5},{14,6},{15,7},{0,8},{1,9},... | collective-permute-start | bytes 18440 | tf_op jit(solution)/shard_map/ppermute | solution.py:327
  31.6 0.8 %collective-permute-done.13.second_ref = f32[16,96]{1,0:T(8,128)S(1)} collective-permute-done((f32[16,96]{1,0:T(8,128)S(1)}, f32[16,96]{1,0:T(8,128)S(1)}, u32[]{:S(2)}, u32[]{:S(2)}) %collective-permute-start.13) | collective-permute-done | bytes 6176 | tf_op jit(solution)/shard_map/ppermute | solution.py:327
  32.4 0.9 %shard_map.60 = bf16[16,12,2,256]{3,2,1,0:T(2,128)(2,1)} custom-call(f32[16,96]{1,0:T(8,128)S(1)} %get-tuple-element.38.first_ref, f32[16,96]{1,0:T(8,128)S(1)} %collective-permute-done.13.second_ref, f32[16,96]{1,0:T(8,128)S(1)} %get-tuple-element.28.used_ref, bf16[12,48,256]{2,1,0:T(8,128)(2,1)S(1)} %shard_map.59.vectors_ref, ...), custom_call_target="tpu_custom_call" | custom-call | flops 10000000 | bytes 1000000 | tf_op jit(solution)/shard_map/pallas_call | solution.py:144
  (46 shorter events, 4.2 us)
Async XLA Ops:
  0.7 2.1 %copy-start.3 = (f32[1,9,2,2304]{3,2,1,0:T(2,128)S(1)}, f32[1,9,2,2304]{3,2,1,0:T(2,128)}, u32[]{:S(2)}) copy-start(f32[1,9,2,2304]{3,2,1,0:T(2,128)} %param.8) | copy-start | bytes 497668
  2.2 1.3 %collective-permute-start = (f32[16,96]{1,0:T(8,128)S(1)}, f32[16,96]{1,0:T(8,128)S(1)}, u32[]{:S(2)}, u32[]{:S(2)}) collective-permute-start(f32[16,96]{1,0:T(8,128)S(1)} %get-tuple-element.19), channel_id=1, source_target_pairs={{8,0},{9,1},{10,2},{11,3},{12,4},{13,5},{14,6},{15,7},{0,8},{1,9},... | collective-permute-start | bytes 18440 | tf_op jit(solution)/shard_map/ppermute | solution.py:327
  2.9 5.1 %collective-permute-start.2 = (f32[2,2,2304]{2,1,0:T(2,128)S(1)}, f32[2,2,2304]{2,1,0:T(2,128)S(1)}, u32[]{:S(2)}, u32[]{:S(2)}) collective-permute-start(f32[2,2,2304]{2,1,0:T(2,128)S(1)} %maximum_select_fusion.1), channel_id=1, source_target_pairs={{8,0},{9,1},{10,2},{11,3},{12,4},{13,5},{14,6},{15,7},{0,8},{1,9},... | collective-permute-start | bytes 110600 | tf_op jit(solution)/shard_map/ppermute | solution.py:327
  3.6 4.9 %collective-permute-start.3 = (f32[2,16,96]{2,1,0:T(8,128)S(1)}, f32[2,16,96]{2,1,0:T(8,128)S(1)}, u32[]{:S(2)}, u32[]{:S(2)}) collective-permute-start(f32[2,16,96]{2,1,0:T(8,128)S(1)} %pad_maximum_fusion.1), channel_id=1, source_target_pairs={{16,0},{17,1},{18,2},{19,3},{20,4},{21,5},{22,6},{23,7},{10,8},{11... | collective-permute-start | bytes 36872 | tf_op jit(solution)/shard_map/ppermute | solution.py:327
  6.5 3.7 %collective-permute-start.1 = (f32[2,16,96]{2,1,0:T(8,128)S(1)}, f32[2,16,96]{2,1,0:T(8,128)S(1)}, u32[]{:S(2)}, u32[]{:S(2)}) collective-permute-start(f32[2,16,96]{2,1,0:T(8,128)S(1)} %pad_maximum_fusion.1), channel_id=1, source_target_pairs={{1,0},{0,1},{3,2},{2,3},{5,4},{4,5},{7,6},{6,7},{14,8},{15,9},{12,... | collective-permute-start | bytes 36872 | tf_op jit(solution)/shard_map/ppermute | solution.py:327
  8.8 6.5 %copy-start.1 = (bf16[16,2,12,256]{3,1,2,0:T(2,128)(2,1)S(1)}, bf16[16,2,12,256]{3,1,2,0:T(2,128)(2,1)}, u32[]{:S(2)}) copy-start(bf16[16,2,12,256]{3,1,2,0:T(2,128)(2,1)} %param.5) | copy-start | bytes 589828
  10.4 1.5 %collective-permute-start.4 = (f32[2,16,96]{2,1,0:T(8,128)S(1)}, f32[2,16,96]{2,1,0:T(8,128)S(1)}, u32[]{:S(2)}, u32[]{:S(2)}) collective-permute-start(f32[2,16,96]{2,1,0:T(8,128)S(1)} %fusion.3), channel_id=1, source_target_pairs={{8,0},{9,1},{10,2},{11,3},{12,4},{13,5},{14,6},{15,7},{0,8},{1,9},... | collective-permute-start | bytes 36872 | tf_op jit(solution)/shard_map/ppermute | solution.py:327
  11.9 3.3 %copy-start.2 = (bf16[2,2,6,6,256]{4,1,3,2,0:T(2,128)(2,1)S(1)}, bf16[2,2,6,6,256]{4,1,3,2,0:T(2,128)(2,1)}, u32[]{:S(2)}) copy-start(bf16[2,2,6,6,256]{4,1,3,2,0:T(2,128)(2,1)} %param.7) | copy-start | bytes 221188
  11.9 5.5 %collective-permute-start.5 = (f32[2,16,96]{2,1,0:T(8,128)S(1)}, f32[2,16,96]{2,1,0:T(8,128)S(1)}, u32[]{:S(2)}, u32[]{:S(2)}) collective-permute-start(f32[2,16,96]{2,1,0:T(8,128)S(1)} %maximum_add_fusion), channel_id=1, source_target_pairs={{1,0},{0,1},{3,2},{2,3},{5,4},{4,5},{7,6},{6,7},{14,8},{15,9},{12,... | collective-permute-start | bytes 36872 | tf_op jit(solution)/shard_map/ppermute | solution.py:327
  13.5 3.7 %collective-permute-start.6 = (f32[2,16,96]{2,1,0:T(8,128)S(1)}, f32[2,16,96]{2,1,0:T(8,128)S(1)}, u32[]{:S(2)}, u32[]{:S(2)}) collective-permute-start(f32[2,16,96]{2,1,0:T(8,128)S(1)} %maximum_add_fusion), channel_id=1, source_target_pairs={{16,0},{17,1},{18,2},{19,3},{20,4},{21,5},{22,6},{23,7},{10,8},{11... | collective-permute-start | bytes 36872 | tf_op jit(solution)/shard_map/ppermute | solution.py:327
  15.8 6.0 %copy-start = (bf16[2,24,12,256]{3,1,2,0:T(8,128)(2,1)S(1)}, bf16[2,24,12,256]{3,1,2,0:T(8,128)(2,1)}, u32[]{:S(2)}) copy-start(bf16[2,24,12,256]{3,1,2,0:T(8,128)(2,1)} %param.6) | copy-start | bytes 884740
  17.7 1.5 %collective-permute-start.7 = (f32[2,16,96]{2,1,0:T(8,128)S(1)}, f32[2,16,96]{2,1,0:T(8,128)S(1)}, u32[]{:S(2)}, u32[]{:S(2)}) collective-permute-start(f32[2,16,96]{2,1,0:T(8,128)S(1)} %fusion.2), channel_id=1, source_target_pairs={{8,0},{9,1},{10,2},{11,3},{12,4},{13,5},{14,6},{15,7},{0,8},{1,9},... | collective-permute-start | bytes 36872 | tf_op jit(solution)/shard_map/ppermute | solution.py:327
  19.2 5.5 %collective-permute-start.8 = (f32[2,16,96]{2,1,0:T(8,128)S(1)}, f32[2,16,96]{2,1,0:T(8,128)S(1)}, u32[]{:S(2)}, u32[]{:S(2)}) collective-permute-start(f32[2,16,96]{2,1,0:T(8,128)S(1)} %maximum_add_fusion.1), channel_id=1, source_target_pairs={{1,0},{0,1},{3,2},{2,3},{5,4},{4,5},{7,6},{6,7},{14,8},{15,9},{12,... | collective-permute-start | bytes 36872 | tf_op jit(solution)/shard_map/ppermute | solution.py:327
  20.8 3.7 %collective-permute-start.9 = (f32[2,16,96]{2,1,0:T(8,128)S(1)}, f32[2,16,96]{2,1,0:T(8,128)S(1)}, u32[]{:S(2)}, u32[]{:S(2)}) collective-permute-start(f32[2,16,96]{2,1,0:T(8,128)S(1)} %maximum_add_fusion.1), channel_id=1, source_target_pairs={{16,0},{17,1},{18,2},{19,3},{20,4},{21,5},{22,6},{23,7},{10,8},{11... | collective-permute-start | bytes 36872 | tf_op jit(solution)/shard_map/ppermute | solution.py:327
  25.0 1.2 %collective-permute-start.10 = (f32[2,16,96]{2,1,0:T(8,128)S(1)}, f32[2,16,96]{2,1,0:T(8,128)S(1)}, u32[]{:S(2)}, u32[]{:S(2)}) collective-permute-start(f32[2,16,96]{2,1,0:T(8,128)S(1)} %fusion.1), channel_id=1, source_target_pairs={{8,0},{9,1},{10,2},{11,3},{12,4},{13,5},{14,6},{15,7},{0,8},{1,9},... | collective-permute-start | bytes 36872 | tf_op jit(solution)/shard_map/ppermute | solution.py:327
  26.3 4.6 %collective-permute-start.11 = (f32[2,16,96]{2,1,0:T(8,128)S(1)}, f32[2,16,96]{2,1,0:T(8,128)S(1)}, u32[]{:S(2)}, u32[]{:S(2)}) collective-permute-start(f32[2,16,96]{2,1,0:T(8,128)S(1)} %maximum_add_fusion.2), channel_id=1, source_target_pairs={{1,0},{0,1},{3,2},{2,3},{5,4},{4,5},{7,6},{6,7},{14,8},{15,9},{12,... | collective-permute-start | bytes 36872 | tf_op jit(solution)/shard_map/ppermute | solution.py:327
  26.9 3.7 %collective-permute-start.12 = (f32[2,16,96]{2,1,0:T(8,128)S(1)}, f32[2,16,96]{2,1,0:T(8,128)S(1)}, u32[]{:S(2)}, u32[]{:S(2)}) collective-permute-start(f32[2,16,96]{2,1,0:T(8,128)S(1)} %maximum_add_fusion.2), channel_id=1, source_target_pairs={{16,0},{17,1},{18,2},{19,3},{20,4},{21,5},{22,6},{23,7},{10,8},{11... | collective-permute-start | bytes 36872 | tf_op jit(solution)/shard_map/ppermute | solution.py:327
  31.2 1.2 %collective-permute-start.13 = (f32[16,96]{1,0:T(8,128)S(1)}, f32[16,96]{1,0:T(8,128)S(1)}, u32[]{:S(2)}, u32[]{:S(2)}) collective-permute-start(f32[16,96]{1,0:T(8,128)S(1)} %get-tuple-element.37), channel_id=1, source_target_pairs={{8,0},{9,1},{10,2},{11,3},{12,4},{13,5},{14,6},{15,7},{0,8},{1,9},... | collective-permute-start | bytes 18440 | tf_op jit(solution)/shard_map/ppermute | solution.py:327

commit v14 on v13

--- a/solution.py
+++ b/solution.py
@@ -347,11 +347,12 @@
         if sweep_id == 2:
             stored, kept = lax.optimization_barrier((held[2], kept))
             vectors, kept = lax.optimization_barrier((hold(stored), kept))
-        part = jnp.stack([kept, jnp.zeros_like(kept)])
-        for link, block in enumerate(moved):
-            part = part + lax.dot_general(
-                block, around[:, link], (((2,), (2,)), ((0,), (0,))), precision=exact
+        def along(link):
+            return lax.dot_general(
+                moved[link], around[:, link], (((2,), (2,)), ((0,), (0,))), precision=exact
             )
+
+        part = along(1) + (jnp.stack([kept, jnp.zeros_like(kept)]) + along(0))
         if sweep_id < ITERS - 2:
             other = swap(part, mate)
             pair = part + jnp.stack([other[1], other[0]])

time: 33.5 us -> 32.6 us (0.973)
  waiting for transfers between devices: 11.4 us -> 9.64 us
  starting transfers between devices: 14.4 us -> 15.3 us
    ppermute x14, waiting for transfers between devices: 11.4 us -> 9.64 us  [swap(): lax.ppermute(block, axes, [(source, i) for i, source in enumerate(sources)])]
    ppermute x14, starting transfers between devices: 14.4 us -> 15.3 us  [swap(): lax.ppermute(block, axes, [(source, i) for i, source in enumerate(sources)])]
  transfers between devices with their start and end apart: 14 -> 14, of which waited for: 9 -> 11; matrix products, arithmetic and copies ran while one was open for 6% -> 6% of each run, Pallas kernels for 3% -> 4%
where the time goes in v14:
time: 32.6 us; the launch traced here: 32.4 us
  starting transfers between devices  15.3 us (47%)
  waiting for transfers between devices  9.64 us (30%)
  Pallas kernels  3.66 us (11%)
  matrix products  2.79 us (9%)
  between operations  0.83 us (3%)
    ppermute x14, starting transfers between devices, swap(): lax.ppermute(block, axes, [(source, i) for i, source in enumerate(sources)])  15.3 us
    ppermute x14, waiting for transfers between devices, swap(): lax.ppermute(block, axes, [(source, i) for i, source in enumerate(sources)])  9.64 us
    dot_general x8, matrix products, along(): lax.dot_general(moved[link], around[:, link], (((2,), (2,)), ((0,), (0,))...  1.95 us
    pallas_call x1, Pallas kernels, restrict(): pl.pallas_call(restrict_kernel, out_shape=[jax.ShapeDtypeStruct((rhs, 4 *...  1.58 us
    pallas_call x1, Pallas kernels, extend(): pl.pallas_call(extend_kernel, out_shape=jax.ShapeDtypeStruct(shape, jnp.b...  0.94 us
    dot_general x4, matrix products, apply(): lax.dot_general(vector, matrix, (((1,), (1,)), ((), ())), precision=exact)  0.84 us
  transfers between devices with their start and end apart: 14, of which 11 were waited for; matrix products, arithmetic and copies ran while one was open for 6% of the time, Pallas kernels for 4%

profile of v14, /device:TPU:0, one launch (start us, length us, event | category | flops | bytes accessed | tf_op | source)
XLA Modules:
  0.0 32.4 jit_solution(3545425108535066135)
XLA Ops:
  0.7 1.6 %shard_map.55 = (f32[16,96]{1,0:T(8,128)S(1)}, f32[16,96]{1,0:T(8,128)S(1)}) custom-call(s32[1]{0:T(128)S(6)} %copy.6.count_ref, bf16[16,12,2,256]{3,2,1,0:T(2,128)(2,1)} %bitcast.70, bf16[2,12,24,256]{3,2,1,0:T(8,128)(2,1)} %bitcast.68), custom_call_target="tpu_custom_call" | custom-call | flops 10000000 | bytes 500000 | tf_op jit(solution)/shard_map/pallas_call | solution.py:96
  2.2 0.5 %collective-permute-start = (f32[16,96]{1,0:T(8,128)S(1)}, f32[16,96]{1,0:T(8,128)S(1)}, u32[]{:S(2)}, u32[]{:S(2)}) collective-permute-start(f32[16,96]{1,0:T(8,128)S(1)} %get-tuple-element.19), channel_id=1, source_target_pairs={{8,0},{9,1},{10,2},{11,3},{12,4},{13,5},{14,6},{15,7},{0,8},{1,9},... | collective-permute-start | bytes 18440 | tf_op jit(solution)/shard_map/ppermute | solution.py:327
  3.6 2.8 %collective-permute-start.3 = (f32[2,16,96]{2,1,0:T(8,128)S(1)}, f32[2,16,96]{2,1,0:T(8,128)S(1)}, u32[]{:S(2)}, u32[]{:S(2)}) collective-permute-start(f32[2,16,96]{2,1,0:T(8,128)S(1)} %pad_maximum_fusion.1), channel_id=1, source_target_pairs={{1,0},{0,1},{3,2},{2,3},{5,4},{4,5},{7,6},{6,7},{14,8},{15,9},{12,... | collective-permute-start | bytes 36872 | tf_op jit(solution)/shard_map/ppermute | solution.py:327
  6.4 1.5 %collective-permute-start.1 = (f32[2,16,96]{2,1,0:T(8,128)S(1)}, f32[2,16,96]{2,1,0:T(8,128)S(1)}, u32[]{:S(2)}, u32[]{:S(2)}) collective-permute-start(f32[2,16,96]{2,1,0:T(8,128)S(1)} %pad_maximum_fusion.1), channel_id=1, source_target_pairs={{16,0},{17,1},{18,2},{19,3},{20,4},{21,5},{22,6},{23,7},{10,8},{11... | collective-permute-start | bytes 36872 | tf_op jit(solution)/shard_map/ppermute | solution.py:327
  8.8 1.4 %collective-permute-done.1 = f32[2,16,96]{2,1,0:T(8,128)S(1)} collective-permute-done((f32[2,16,96]{2,1,0:T(8,128)S(1)}, f32[2,16,96]{2,1,0:T(8,128)S(1)}, u32[]{:S(2)}, u32[]{:S(2)}) %collective-permute-start.1) | collective-permute-done | bytes 12320 | tf_op jit(solution)/shard_map/ppermute | solution.py:327
  10.4 0.9 %collective-permute-start.4 = (f32[2,16,96]{2,1,0:T(8,128)S(1)}, f32[2,16,96]{2,1,0:T(8,128)S(1)}, u32[]{:S(2)}, u32[]{:S(2)}) collective-permute-start(f32[2,16,96]{2,1,0:T(8,128)S(1)} %convolution_add_fusion.7), channel_id=1, source_target_pairs={{8,0},{9,1},{10,2},{11,3},{12,4},{13,5},{14,6},{15,7},{0,8},{1,9},... | collective-permute-start | bytes 36872 | tf_op jit(solution)/shard_map/ppermute | solution.py:327
  11.3 0.8 %collective-permute-done.4 = f32[2,16,96]{2,1,0:T(8,128)S(1)} collective-permute-done((f32[2,16,96]{2,1,0:T(8,128)S(1)}, f32[2,16,96]{2,1,0:T(8,128)S(1)}, u32[]{:S(2)}, u32[]{:S(2)}) %collective-permute-start.4) | collective-permute-done | bytes 12320 | tf_op jit(solution)/shard_map/ppermute | solution.py:327
  12.2 1.6 %collective-permute-start.6 = (f32[2,16,96]{2,1,0:T(8,128)S(1)}, f32[2,16,96]{2,1,0:T(8,128)S(1)}, u32[]{:S(2)}, u32[]{:S(2)}) collective-permute-start(f32[2,16,96]{2,1,0:T(8,128)S(1)} %maximum_add_fusion), channel_id=1, source_target_pairs={{1,0},{0,1},{3,2},{2,3},{5,4},{4,5},{7,6},{6,7},{14,8},{15,9},{12,... | collective-permute-start | bytes 36872 | tf_op jit(solution)/shard_map/ppermute | solution.py:327
  13.7 1.5 %collective-permute-start.5 = (f32[2,16,96]{2,1,0:T(8,128)S(1)}, f32[2,16,96]{2,1,0:T(8,128)S(1)}, u32[]{:S(2)}, u32[]{:S(2)}) collective-permute-start(f32[2,16,96]{2,1,0:T(8,128)S(1)} %maximum_add_fusion), channel_id=1, source_target_pairs={{16,0},{17,1},{18,2},{19,3},{20,4},{21,5},{22,6},{23,7},{10,8},{11... | collective-permute-start | bytes 36872 | tf_op jit(solution)/shard_map/ppermute | solution.py:327
  15.5 0.6 %shard_map.58.local_ref = f32[12,32,256]{2,1,0:T(8,128)S(1)} custom-call(bf16[16,12,2,256]{3,2,1,0:T(2,128)(2,1)S(1)} %bitcast.71, bf16[2,6,6,2,256]{4,3,2,1,0:T(2,128)(2,1)S(1)} %bitcast.73), custom_call_target="tpu_custom_call" | custom-call | flops 100000 | bytes 100000 | tf_op jit(solution)/shard_map/pallas_call | solution.py:203
  16.3 1.1 %collective-permute-done.5 = f32[2,16,96]{2,1,0:T(8,128)S(1)} collective-permute-done((f32[2,16,96]{2,1,0:T(8,128)S(1)}, f32[2,16,96]{2,1,0:T(8,128)S(1)}, u32[]{:S(2)}, u32[]{:S(2)}) %collective-permute-start.5) | collective-permute-done | bytes 12320 | tf_op jit(solution)/shard_map/ppermute | solution.py:327
  17.7 0.4 %collective-permute-start.7 = (f32[2,16,96]{2,1,0:T(8,128)S(1)}, f32[2,16,96]{2,1,0:T(8,128)S(1)}, u32[]{:S(2)}, u32[]{:S(2)}) collective-permute-start(f32[2,16,96]{2,1,0:T(8,128)S(1)} %convolution_add_fusion.5), channel_id=1, source_target_pairs={{8,0},{9,1},{10,2},{11,3},{12,4},{13,5},{14,6},{15,7},{0,8},{1,9},... | collective-permute-start | bytes 36872 | tf_op jit(solution)/shard_map/ppermute | solution.py:327
  18.1 0.8 %collective-permute-done.7 = f32[2,16,96]{2,1,0:T(8,128)S(1)} collective-permute-done((f32[2,16,96]{2,1,0:T(8,128)S(1)}, f32[2,16,96]{2,1,0:T(8,128)S(1)}, u32[]{:S(2)}, u32[]{:S(2)}) %collective-permute-start.7) | collective-permute-done | bytes 12320 | tf_op jit(solution)/shard_map/ppermute | solution.py:327
  18.9 1.0 %collective-permute-start.9 = (f32[2,16,96]{2,1,0:T(8,128)S(1)}, f32[2,16,96]{2,1,0:T(8,128)S(1)}, u32[]{:S(2)}, u32[]{:S(2)}) collective-permute-start(f32[2,16,96]{2,1,0:T(8,128)S(1)} %maximum_add_fusion.1), channel_id=1, source_target_pairs={{1,0},{0,1},{3,2},{2,3},{5,4},{4,5},{7,6},{6,7},{14,8},{15,9},{12,... | collective-permute-start | bytes 36872 | tf_op jit(solution)/shard_map/ppermute | solution.py:327
  19.9 1.5 %collective-permute-start.8 = (f32[2,16,96]{2,1,0:T(8,128)S(1)}, f32[2,16,96]{2,1,0:T(8,128)S(1)}, u32[]{:S(2)}, u32[]{:S(2)}) collective-permute-start(f32[2,16,96]{2,1,0:T(8,128)S(1)} %maximum_add_fusion.1), channel_id=1, source_target_pairs={{16,0},{17,1},{18,2},{19,3},{20,4},{21,5},{22,6},{23,7},{10,8},{11... | collective-permute-start | bytes 36872 | tf_op jit(solution)/shard_map/ppermute | solution.py:327
  21.7 1.0 %collective-permute-done.9 = f32[2,16,96]{2,1,0:T(8,128)S(1)} collective-permute-done((f32[2,16,96]{2,1,0:T(8,128)S(1)}, f32[2,16,96]{2,1,0:T(8,128)S(1)}, u32[]{:S(2)}, u32[]{:S(2)}) %collective-permute-start.9) | collective-permute-done | bytes 12320 | tf_op jit(solution)/shard_map/ppermute | solution.py:327
  23.0 0.7 %collective-permute-done.8 = f32[2,16,96]{2,1,0:T(8,128)S(1)} collective-permute-done((f32[2,16,96]{2,1,0:T(8,128)S(1)}, f32[2,16,96]{2,1,0:T(8,128)S(1)}, u32[]{:S(2)}, u32[]{:S(2)}) %collective-permute-start.8) | collective-permute-done | bytes 12320 | tf_op jit(solution)/shard_map/ppermute | solution.py:327
  24.3 0.8 %collective-permute-done.10 = f32[2,16,96]{2,1,0:T(8,128)S(1)} collective-permute-done((f32[2,16,96]{2,1,0:T(8,128)S(1)}, f32[2,16,96]{2,1,0:T(8,128)S(1)}, u32[]{:S(2)}, u32[]{:S(2)}) %collective-permute-start.10) | collective-permute-done | bytes 12320 | tf_op jit(solution)/shard_map/ppermute | solution.py:327
  25.1 1.2 %collective-permute-start.12 = (f32[2,16,96]{2,1,0:T(8,128)S(1)}, f32[2,16,96]{2,1,0:T(8,128)S(1)}, u32[]{:S(2)}, u32[]{:S(2)}) collective-permute-start(f32[2,16,96]{2,1,0:T(8,128)S(1)} %maximum_add_fusion.2), channel_id=1, source_target_pairs={{1,0},{0,1},{3,2},{2,3},{5,4},{4,5},{7,6},{6,7},{14,8},{15,9},{12,... | collective-permute-start | bytes 36872 | tf_op jit(solution)/shard_map/ppermute | solution.py:327
  26.3 1.5 %collective-permute-start.11 = (f32[2,16,96]{2,1,0:T(8,128)S(1)}, f32[2,16,96]{2,1,0:T(8,128)S(1)}, u32[]{:S(2)}, u32[]{:S(2)}) collective-permute-start(f32[2,16,96]{2,1,0:T(8,128)S(1)} %maximum_add_fusion.2), channel_id=1, source_target_pairs={{16,0},{17,1},{18,2},{19,3},{20,4},{21,5},{22,6},{23,7},{10,8},{11... | collective-permute-start | bytes 36872 | tf_op jit(solution)/shard_map/ppermute | solution.py:327
  28.0 0.9 %collective-permute-done.12 = f32[2,16,96]{2,1,0:T(8,128)S(1)} collective-permute-done((f32[2,16,96]{2,1,0:T(8,128)S(1)}, f32[2,16,96]{2,1,0:T(8,128)S(1)}, u32[]{:S(2)}, u32[]{:S(2)}) %collective-permute-start.12) | collective-permute-done | bytes 12320 | tf_op jit(solution)/shard_map/ppermute | solution.py:327
  29.2 0.9 %collective-permute-done.11 = f32[2,16,96]{2,1,0:T(8,128)S(1)} collective-permute-done((f32[2,16,96]{2,1,0:T(8,128)S(1)}, f32[2,16,96]{2,1,0:T(8,128)S(1)}, u32[]{:S(2)}, u32[]{:S(2)}) %collective-permute-start.11) | collective-permute-done | bytes 12320 | tf_op jit(solution)/shard_map/ppermute | solution.py:327
  30.7 0.8 %collective-permute-done.13.second_ref = f32[16,96]{1,0:T(8,128)S(1)} collective-permute-done((f32[16,96]{1,0:T(8,128)S(1)}, f32[16,96]{1,0:T(8,128)S(1)}, u32[]{:S(2)}, u32[]{:S(2)}) %collective-permute-start.13) | collective-permute-done | bytes 6176 | tf_op jit(solution)/shard_map/ppermute | solution.py:327
  31.5 0.9 %shard_map.60 = bf16[16,12,2,256]{3,2,1,0:T(2,128)(2,1)} custom-call(f32[16,96]{1,0:T(8,128)S(1)} %get-tuple-element.38.first_ref, f32[16,96]{1,0:T(8,128)S(1)} %collective-permute-done.13.second_ref, f32[16,96]{1,0:T(8,128)S(1)} %get-tuple-element.28.used_ref, bf16[12,48,256]{2,1,0:T(8,128)(2,1)S(1)} %shard_map.59.vectors_ref, ...), custom_call_target="tpu_custom_call" | custom-call | flops 10000000 | bytes 1000000 | tf_op jit(solution)/shard_map/pallas_call | solution.py:144
  (46 shorter events, 4.8 us)
Async XLA Ops:
  0.7 2.1 %copy-start.3 = (f32[1,9,2,2304]{3,2,1,0:T(2,128)S(1)}, f32[1,9,2,2304]{3,2,1,0:T(2,128)}, u32[]{:S(2)}) copy-start(f32[1,9,2,2304]{3,2,1,0:T(2,128)} %param.8) | copy-start | bytes 497668
  2.2 1.3 %collective-permute-start = (f32[16,96]{1,0:T(8,128)S(1)}, f32[16,96]{1,0:T(8,128)S(1)}, u32[]{:S(2)}, u32[]{:S(2)}) collective-permute-start(f32[16,96]{1,0:T(8,128)S(1)} %get-tuple-element.19), channel_id=1, source_target_pairs={{8,0},{9,1},{10,2},{11,3},{12,4},{13,5},{14,6},{15,7},{0,8},{1,9},... | collective-permute-start | bytes 18440 | tf_op jit(solution)/shard_map/ppermute | solution.py:327
  2.9 5.1 %collective-permute-start.2 = (f32[2,2,2304]{2,1,0:T(2,128)S(1)}, f32[2,2,2304]{2,1,0:T(2,128)S(1)}, u32[]{:S(2)}, u32[]{:S(2)}) collective-permute-start(f32[2,2,2304]{2,1,0:T(2,128)S(1)} %maximum_select_fusion.1), channel_id=1, source_target_pairs={{8,0},{9,1},{10,2},{11,3},{12,4},{13,5},{14,6},{15,7},{0,8},{1,9},... | collective-permute-start | bytes 110600 | tf_op jit(solution)/shard_map/ppermute | solution.py:327
  3.6 4.9 %collective-permute-start.3 = (f32[2,16,96]{2,1,0:T(8,128)S(1)}, f32[2,16,96]{2,1,0:T(8,128)S(1)}, u32[]{:S(2)}, u32[]{:S(2)}) collective-permute-start(f32[2,16,96]{2,1,0:T(8,128)S(1)} %pad_maximum_fusion.1), channel_id=1, source_target_pairs={{1,0},{0,1},{3,2},{2,3},{5,4},{4,5},{7,6},{6,7},{14,8},{15,9},{12,... | collective-permute-start | bytes 36872 | tf_op jit(solution)/shard_map/ppermute | solution.py:327
  6.4 3.7 %collective-permute-start.1 = (f32[2,16,96]{2,1,0:T(8,128)S(1)}, f32[2,16,96]{2,1,0:T(8,128)S(1)}, u32[]{:S(2)}, u32[]{:S(2)}) collective-permute-start(f32[2,16,96]{2,1,0:T(8,128)S(1)} %pad_maximum_fusion.1), channel_id=1, source_target_pairs={{16,0},{17,1},{18,2},{19,3},{20,4},{21,5},{22,6},{23,7},{10,8},{11... | collective-permute-start | bytes 36872 | tf_op jit(solution)/shard_map/ppermute | solution.py:327
  8.8 6.7 %copy-start.1 = (bf16[16,2,12,256]{3,1,2,0:T(2,128)(2,1)S(1)}, bf16[16,2,12,256]{3,1,2,0:T(2,128)(2,1)}, u32[]{:S(2)}) copy-start(bf16[16,2,12,256]{3,1,2,0:T(2,128)(2,1)} %param.5) | copy-start | bytes 589828
  10.4 1.7 %collective-permute-start.4 = (f32[2,16,96]{2,1,0:T(8,128)S(1)}, f32[2,16,96]{2,1,0:T(8,128)S(1)}, u32[]{:S(2)}, u32[]{:S(2)}) collective-permute-start(f32[2,16,96]{2,1,0:T(8,128)S(1)} %convolution_add_fusion.7), channel_id=1, source_target_pairs={{8,0},{9,1},{10,2},{11,3},{12,4},{13,5},{14,6},{15,7},{0,8},{1,9},... | collective-permute-start | bytes 36872 | tf_op jit(solution)/shard_map/ppermute | solution.py:327
  12.1 3.3 %copy-start.2 = (bf16[2,2,6,6,256]{4,1,3,2,0:T(2,128)(2,1)S(1)}, bf16[2,2,6,6,256]{4,1,3,2,0:T(2,128)(2,1)}, u32[]{:S(2)}) copy-start(bf16[2,2,6,6,256]{4,1,3,2,0:T(2,128)(2,1)} %param.7) | copy-start | bytes 221188
  12.2 3.9 %collective-permute-start.6 = (f32[2,16,96]{2,1,0:T(8,128)S(1)}, f32[2,16,96]{2,1,0:T(8,128)S(1)}, u32[]{:S(2)}, u32[]{:S(2)}) collective-permute-start(f32[2,16,96]{2,1,0:T(8,128)S(1)} %maximum_add_fusion), channel_id=1, source_target_pairs={{1,0},{0,1},{3,2},{2,3},{5,4},{4,5},{7,6},{6,7},{14,8},{15,9},{12,... | collective-permute-start | bytes 36872 | tf_op jit(solution)/shard_map/ppermute | solution.py:327
  13.7 3.7 %collective-permute-start.5 = (f32[2,16,96]{2,1,0:T(8,128)S(1)}, f32[2,16,96]{2,1,0:T(8,128)S(1)}, u32[]{:S(2)}, u32[]{:S(2)}) collective-permute-start(f32[2,16,96]{2,1,0:T(8,128)S(1)} %maximum_add_fusion), channel_id=1, source_target_pairs={{16,0},{17,1},{18,2},{19,3},{20,4},{21,5},{22,6},{23,7},{10,8},{11... | collective-permute-start | bytes 36872 | tf_op jit(solution)/shard_map/ppermute | solution.py:327
  16.1 5.6 %copy-start = (bf16[2,24,12,256]{3,1,2,0:T(8,128)(2,1)S(1)}, bf16[2,24,12,256]{3,1,2,0:T(8,128)(2,1)}, u32[]{:S(2)}) copy-start(bf16[2,24,12,256]{3,1,2,0:T(8,128)(2,1)} %param.6) | copy-start | bytes 884740
  17.7 1.2 %collective-permute-start.7 = (f32[2,16,96]{2,1,0:T(8,128)S(1)}, f32[2,16,96]{2,1,0:T(8,128)S(1)}, u32[]{:S(2)}, u32[]{:S(2)}) collective-permute-start(f32[2,16,96]{2,1,0:T(8,128)S(1)} %convolution_add_fusion.5), channel_id=1, source_target_pairs={{8,0},{9,1},{10,2},{11,3},{12,4},{13,5},{14,6},{15,7},{0,8},{1,9},... | collective-permute-start | bytes 36872 | tf_op jit(solution)/shard_map/ppermute | solution.py:327
  18.9 3.8 %collective-permute-start.9 = (f32[2,16,96]{2,1,0:T(8,128)S(1)}, f32[2,16,96]{2,1,0:T(8,128)S(1)}, u32[]{:S(2)}, u32[]{:S(2)}) collective-permute-start(f32[2,16,96]{2,1,0:T(8,128)S(1)} %maximum_add_fusion.1), channel_id=1, source_target_pairs={{1,0},{0,1},{3,2},{2,3},{5,4},{4,5},{7,6},{6,7},{14,8},{15,9},{12,... | collective-permute-start | bytes 36872 | tf_op jit(solution)/shard_map/ppermute | solution.py:327
  19.9 3.7 %collective-permute-start.8 = (f32[2,16,96]{2,1,0:T(8,128)S(1)}, f32[2,16,96]{2,1,0:T(8,128)S(1)}, u32[]{:S(2)}, u32[]{:S(2)}) collective-permute-start(f32[2,16,96]{2,1,0:T(8,128)S(1)} %maximum_add_fusion.1), channel_id=1, source_target_pairs={{16,0},{17,1},{18,2},{19,3},{20,4},{21,5},{22,6},{23,7},{10,8},{11... | collective-permute-start | bytes 36872 | tf_op jit(solution)/shard_map/ppermute | solution.py:327
  23.9 1.2 %collective-permute-start.10 = (f32[2,16,96]{2,1,0:T(8,128)S(1)}, f32[2,16,96]{2,1,0:T(8,128)S(1)}, u32[]{:S(2)}, u32[]{:S(2)}) collective-permute-start(f32[2,16,96]{2,1,0:T(8,128)S(1)} %convolution_add_fusion.3), channel_id=1, source_target_pairs={{8,0},{9,1},{10,2},{11,3},{12,4},{13,5},{14,6},{15,7},{0,8},{1,9},... | collective-permute-start | bytes 36872 | tf_op jit(solution)/shard_map/ppermute | solution.py:327
  25.1 3.8 %collective-permute-start.12 = (f32[2,16,96]{2,1,0:T(8,128)S(1)}, f32[2,16,96]{2,1,0:T(8,128)S(1)}, u32[]{:S(2)}, u32[]{:S(2)}) collective-permute-start(f32[2,16,96]{2,1,0:T(8,128)S(1)} %maximum_add_fusion.2), channel_id=1, source_target_pairs={{1,0},{0,1},{3,2},{2,3},{5,4},{4,5},{7,6},{6,7},{14,8},{15,9},{12,... | collective-permute-start | bytes 36872 | tf_op jit(solution)/shard_map/ppermute | solution.py:327
  26.3 3.7 %collective-permute-start.11 = (f32[2,16,96]{2,1,0:T(8,128)S(1)}, f32[2,16,96]{2,1,0:T(8,128)S(1)}, u32[]{:S(2)}, u32[]{:S(2)}) collective-permute-start(f32[2,16,96]{2,1,0:T(8,128)S(1)} %maximum_add_fusion.2), channel_id=1, source_target_pairs={{16,0},{17,1},{18,2},{19,3},{20,4},{21,5},{22,6},{23,7},{10,8},{11... | collective-permute-start | bytes 36872 | tf_op jit(solution)/shard_map/ppermute | solution.py:327
  30.3 1.2 %collective-permute-start.13 = (f32[16,96]{1,0:T(8,128)S(1)}, f32[16,96]{1,0:T(8,128)S(1)}, u32[]{:S(2)}, u32[]{:S(2)}) collective-permute-start(f32[16,96]{1,0:T(8,128)S(1)} %get-tuple-element.37), channel_id=1, source_target_pairs={{8,0},{9,1},{10,2},{11,3},{12,4},{13,5},{14,6},{15,7},{0,8},{1,9},... | collective-permute-start | bytes 18440 | tf_op jit(solution)/shard_map/ppermute | solution.py:327

commit v15 on v14

--- a/solution.py
+++ b/solution.py
@@ -300,15 +300,15 @@
                 imag = omega_step * rows_ref[base + dim : base + 2 * dim]
                 if has_own and link == 0:
                     real = real + jnp.where(row == col, 1.0, 0.0)
-                place, left = ((block,), 2 * dim * link) if has_own else ((block, link), 0)
+                left = 2 * dim * link
                 low, high = pl.ds(0, dim), pl.ds(dim, dim)
                 near, beyond = pl.ds(left, dim), pl.ds(left + dim, dim)
-                out_ref[(*place, low, near)] = real
-                out_ref[(*place, low, beyond)] = imag
-                out_ref[(*place, high, near)] = -imag
-                out_ref[(*place, high, beyond)] = real
-
-    shape = (blocks, 2 * dim, 4 * dim) if has_own else (blocks, 2, 2 * dim, 2 * dim)
+                out_ref[block, low, near] = real
+                out_ref[block, low, beyond] = imag
+                out_ref[block, high, near] = -imag
+                out_ref[block, high, beyond] = real
+
+    shape = (blocks, 2 * dim, 4 * dim)
     return pl.pallas_call(
         kernel,
         out_shape=jax.ShapeDtypeStruct(shape, jnp.float32),
@@ -326,20 +326,20 @@
     def swap(block, sources):
         return lax.ppermute(block, axes, [(source, i) for i, source in enumerate(sources)])
 
-    along_t_x = jnp.stack([operator[7] + operator[8], operator[1] + operator[2]])
+    along_x_t = jnp.stack([operator[1] + operator[2], operator[7] + operator[8]])
     odd_level = lax.axis_index("gz") % 2 == 1
     along_z = jnp.stack(
-        [jnp.where(odd_level, operator[5], operator[6]), jnp.where(odd_level, operator[6], operator[5])]
+        [jnp.where(odd_level, operator[6], operator[5]), jnp.where(odd_level, operator[5], operator[6])]
     )
     upper = lax.axis_index("gx") % 2 == 1
-    mine = jnp.where(upper, along_z, along_t_x)
-    theirs = swap(jnp.where(upper, along_t_x, along_z), mate)
+    mine = jnp.where(upper, along_z, along_x_t)
+    theirs = swap(jnp.where(upper, along_x_t, along_z), mate)
     inside = real_blocks(jnp.stack([operator[0], operator[3] + operator[4]])[None], dim, True)[0]
     around = real_blocks(jnp.stack([mine, theirs]), dim, False)
 
     pair = jnp.stack([half, swap(half, mate)])
     for sweep_id in range(ITERS - 1):
-        moved = [swap(pair, first), swap(pair, second)]
+        moved = [swap(pair, second), swap(pair, first)]
         kept = half + apply(jnp.concatenate([pair[0], pair[1]], 1), inside)
         if sweep_id == 1:
             rows, clover, kept = lax.optimization_barrier((*held[:2], kept))
@@ -347,12 +347,10 @@
         if sweep_id == 2:
             stored, kept = lax.optimization_barrier((held[2], kept))
             vectors, kept = lax.optimization_barrier((hold(stored), kept))
-        def along(link):
-            return lax.dot_general(
-                moved[link], around[:, link], (((2,), (2,)), ((0,), (0,))), precision=exact
-            )
-
-        part = along(1) + (jnp.stack([kept, jnp.zeros_like(kept)]) + along(0))
+        part = lax.dot_general(
+            jnp.concatenate(moved, 2), around, (((2,), (2,)), ((0,), (0,))), precision=exact
+        )
+        part = part + jnp.stack([kept, jnp.zeros_like(kept)])
         if sweep_id < ITERS - 2:
             other = swap(part, mate)
             pair = part + jnp.stack([other[1], other[0]])

time: 32.6 us -> 33 us (1.012)
  waiting for transfers between devices: 9.64 us -> 10.6 us
  matrix products: 2.79 us -> 2.08 us
    ppermute x14, waiting for transfers between devices: 9.64 us -> 10.6 us  [swap(): lax.ppermute(block, axes, [(source, i) for i, source in enumerate(sources)])]
    dot_general x8 -> x4, matrix products: 1.95 us -> 1.24 us  [sweep_in_pairs(): lax.dot_general(jnp.concatenate(moved, 2), around, (((2,), (2,)), ((0,),...]
  transfers between devices with their start and end apart: 14 -> 14, of which waited for: 11 -> 11; matrix products, arithmetic and copies ran while one was open for 6% -> 3% of each run, Pallas kernels for 4% -> 4%
where the time goes in v15:
time: 33 us; the launch traced here: 32.8 us
  starting transfers between devices  15.4 us (47%)
  waiting for transfers between devices  10.6 us (32%)
  Pallas kernels  3.68 us (11%)
  matrix products  2.08 us (6%)
  between operations  0.83 us (3%)
    ppermute x14, starting transfers between devices, swap(): lax.ppermute(block, axes, [(source, i) for i, source in enumerate(sources)])  15.4 us
    ppermute x14, waiting for transfers between devices, swap(): lax.ppermute(block, axes, [(source, i) for i, source in enumerate(sources)])  10.6 us
    pallas_call x1, Pallas kernels, restrict(): pl.pallas_call(restrict_kernel, out_shape=[jax.ShapeDtypeStruct((rhs, 4 *...  1.58 us
    dot_general x4, matrix products, sweep_in_pairs(): lax.dot_general(jnp.concatenate(moved, 2), around, (((2,), (2,)), ((0,),...  1.24 us
    pallas_call x1, Pallas kernels, extend(): pl.pallas_call(extend_kernel, out_shape=jax.ShapeDtypeStruct(shape, jnp.b...  0.94 us
    dot_general x4, matrix products, apply(): lax.dot_general(vector, matrix, (((1,), (1,)), ((), ())), precision=exact)  0.84 us
  transfers between devices with their start and end apart: 14, of which 11 were waited for; matrix products, arithmetic and copies ran while one was open for 3% of the time, Pallas kernels for 4%

profile of v15, /device:TPU:0, one launch (start us, length us, event | category | flops | bytes accessed | tf_op | source)
XLA Modules:
  0.0 32.8 jit_solution(748597265336014333)
XLA Ops:
  0.7 1.6 %shard_map.55 = (f32[16,96]{1,0:T(8,128)S(1)}, f32[16,96]{1,0:T(8,128)S(1)}) custom-call(s32[1]{0:T(128)S(6)} %copy.6.count_ref, bf16[16,12,2,256]{3,2,1,0:T(2,128)(2,1)} %bitcast.54, bf16[2,12,24,256]{3,2,1,0:T(8,128)(2,1)} %bitcast.52), custom_call_target="tpu_custom_call" | custom-call | flops 10000000 | bytes 500000 | tf_op jit(solution)/shard_map/pallas_call | solution.py:96
  2.2 0.5 %collective-permute-start = (f32[16,96]{1,0:T(8,128)S(1)}, f32[16,96]{1,0:T(8,128)S(1)}, u32[]{:S(2)}, u32[]{:S(2)}) collective-permute-start(f32[16,96]{1,0:T(8,128)S(1)} %get-tuple-element.19), channel_id=1, source_target_pairs={{8,0},{9,1},{10,2},{11,3},{12,4},{13,5},{14,6},{15,7},{0,8},{1,9},... | collective-permute-start | bytes 18440 | tf_op jit(solution)/shard_map/ppermute | solution.py:327
  3.6 2.8 %collective-permute-start.2 = (f32[2,16,96]{2,1,0:T(8,128)S(1)}, f32[2,16,96]{2,1,0:T(8,128)S(1)}, u32[]{:S(2)}, u32[]{:S(2)}) collective-permute-start(f32[2,16,96]{2,1,0:T(8,128)S(1)} %pad_maximum_fusion.1), channel_id=1, source_target_pairs={{1,0},{0,1},{3,2},{2,3},{5,4},{4,5},{7,6},{6,7},{14,8},{15,9},{12,... | collective-permute-start | bytes 36872 | tf_op jit(solution)/shard_map/ppermute | solution.py:327
  6.4 1.5 %collective-permute-start.1 = (f32[2,16,96]{2,1,0:T(8,128)S(1)}, f32[2,16,96]{2,1,0:T(8,128)S(1)}, u32[]{:S(2)}, u32[]{:S(2)}) collective-permute-start(f32[2,16,96]{2,1,0:T(8,128)S(1)} %pad_maximum_fusion.1), channel_id=1, source_target_pairs={{16,0},{17,1},{18,2},{19,3},{20,4},{21,5},{22,6},{23,7},{10,8},{11... | collective-permute-start | bytes 36872 | tf_op jit(solution)/shard_map/ppermute | solution.py:327
  8.5 1.6 %collective-permute-done.1 = f32[2,16,96]{2,1,0:T(8,128)S(1)} collective-permute-done((f32[2,16,96]{2,1,0:T(8,128)S(1)}, f32[2,16,96]{2,1,0:T(8,128)S(1)}, u32[]{:S(2)}, u32[]{:S(2)}) %collective-permute-start.1) | collective-permute-done | bytes 12320 | tf_op jit(solution)/shard_map/ppermute | solution.py:327
  10.5 0.9 %collective-permute-start.4 = (f32[2,16,96]{2,1,0:T(8,128)S(1)}, f32[2,16,96]{2,1,0:T(8,128)S(1)}, u32[]{:S(2)}, u32[]{:S(2)}) collective-permute-start(f32[2,16,96]{2,1,0:T(8,128)S(1)} %convolution_add_fusion.3), channel_id=1, source_target_pairs={{8,0},{9,1},{10,2},{11,3},{12,4},{13,5},{14,6},{15,7},{0,8},{1,9},... | collective-permute-start | bytes 36872 | tf_op jit(solution)/shard_map/ppermute | solution.py:327
  11.4 0.8 %collective-permute-done.4 = f32[2,16,96]{2,1,0:T(8,128)S(1)} collective-permute-done((f32[2,16,96]{2,1,0:T(8,128)S(1)}, f32[2,16,96]{2,1,0:T(8,128)S(1)}, u32[]{:S(2)}, u32[]{:S(2)}) %collective-permute-start.4) | collective-permute-done | bytes 12320 | tf_op jit(solution)/shard_map/ppermute | solution.py:327
  12.2 1.6 %collective-permute-start.6 = (f32[2,16,96]{2,1,0:T(8,128)S(1)}, f32[2,16,96]{2,1,0:T(8,128)S(1)}, u32[]{:S(2)}, u32[]{:S(2)}) collective-permute-start(f32[2,16,96]{2,1,0:T(8,128)S(1)} %maximum_add_fusion), channel_id=1, source_target_pairs={{1,0},{0,1},{3,2},{2,3},{5,4},{4,5},{7,6},{6,7},{14,8},{15,9},{12,... | collective-permute-start | bytes 36872 | tf_op jit(solution)/shard_map/ppermute | solution.py:327
  13.8 1.5 %collective-permute-start.5 = (f32[2,16,96]{2,1,0:T(8,128)S(1)}, f32[2,16,96]{2,1,0:T(8,128)S(1)}, u32[]{:S(2)}, u32[]{:S(2)}) collective-permute-start(f32[2,16,96]{2,1,0:T(8,128)S(1)} %maximum_add_fusion), channel_id=1, source_target_pairs={{16,0},{17,1},{18,2},{19,3},{20,4},{21,5},{22,6},{23,7},{10,8},{11... | collective-permute-start | bytes 36872 | tf_op jit(solution)/shard_map/ppermute | solution.py:327
  15.6 0.6 %shard_map.58.local_ref = f32[12,32,256]{2,1,0:T(8,128)S(1)} custom-call(bf16[16,12,2,256]{3,2,1,0:T(2,128)(2,1)S(1)} %bitcast.55, bf16[2,6,6,2,256]{4,3,2,1,0:T(2,128)(2,1)S(1)} %bitcast.57), custom_call_target="tpu_custom_call" | custom-call | flops 100000 | bytes 100000 | tf_op jit(solution)/shard_map/pallas_call | solution.py:203
  16.2 1.4 %collective-permute-done.5 = f32[2,16,96]{2,1,0:T(8,128)S(1)} collective-permute-done((f32[2,16,96]{2,1,0:T(8,128)S(1)}, f32[2,16,96]{2,1,0:T(8,128)S(1)}, u32[]{:S(2)}, u32[]{:S(2)}) %collective-permute-start.5) | collective-permute-done | bytes 12320 | tf_op jit(solution)/shard_map/ppermute | solution.py:327
  18.3 0.8 %collective-permute-done.7 = f32[2,16,96]{2,1,0:T(8,128)S(1)} collective-permute-done((f32[2,16,96]{2,1,0:T(8,128)S(1)}, f32[2,16,96]{2,1,0:T(8,128)S(1)}, u32[]{:S(2)}, u32[]{:S(2)}) %collective-permute-start.7) | collective-permute-done | bytes 12320 | tf_op jit(solution)/shard_map/ppermute | solution.py:327
  19.1 0.9 %collective-permute-start.9 = (f32[2,16,96]{2,1,0:T(8,128)S(1)}, f32[2,16,96]{2,1,0:T(8,128)S(1)}, u32[]{:S(2)}, u32[]{:S(2)}) collective-permute-start(f32[2,16,96]{2,1,0:T(8,128)S(1)} %maximum_add_fusion.1), channel_id=1, source_target_pairs={{1,0},{0,1},{3,2},{2,3},{5,4},{4,5},{7,6},{6,7},{14,8},{15,9},{12,... | collective-permute-start | bytes 36872 | tf_op jit(solution)/shard_map/ppermute | solution.py:327
  20.0 1.5 %collective-permute-start.8 = (f32[2,16,96]{2,1,0:T(8,128)S(1)}, f32[2,16,96]{2,1,0:T(8,128)S(1)}, u32[]{:S(2)}, u32[]{:S(2)}) collective-permute-start(f32[2,16,96]{2,1,0:T(8,128)S(1)} %maximum_add_fusion.1), channel_id=1, source_target_pairs={{16,0},{17,1},{18,2},{19,3},{20,4},{21,5},{22,6},{23,7},{10,8},{11... | collective-permute-start | bytes 36872 | tf_op jit(solution)/shard_map/ppermute | solution.py:327
  21.8 1.1 %collective-permute-done.9 = f32[2,16,96]{2,1,0:T(8,128)S(1)} collective-permute-done((f32[2,16,96]{2,1,0:T(8,128)S(1)}, f32[2,16,96]{2,1,0:T(8,128)S(1)}, u32[]{:S(2)}, u32[]{:S(2)}) %collective-permute-start.9) | collective-permute-done | bytes 12320 | tf_op jit(solution)/shard_map/ppermute | solution.py:327
  22.9 0.8 %collective-permute-done.8 = f32[2,16,96]{2,1,0:T(8,128)S(1)} collective-permute-done((f32[2,16,96]{2,1,0:T(8,128)S(1)}, f32[2,16,96]{2,1,0:T(8,128)S(1)}, u32[]{:S(2)}, u32[]{:S(2)}) %collective-permute-start.8) | collective-permute-done | bytes 12320 | tf_op jit(solution)/shard_map/ppermute | solution.py:327
  24.5 0.8 %collective-permute-done.10 = f32[2,16,96]{2,1,0:T(8,128)S(1)} collective-permute-done((f32[2,16,96]{2,1,0:T(8,128)S(1)}, f32[2,16,96]{2,1,0:T(8,128)S(1)}, u32[]{:S(2)}, u32[]{:S(2)}) %collective-permute-start.10) | collective-permute-done | bytes 12320 | tf_op jit(solution)/shard_map/ppermute | solution.py:327
  25.3 1.3 %collective-permute-start.12 = (f32[2,16,96]{2,1,0:T(8,128)S(1)}, f32[2,16,96]{2,1,0:T(8,128)S(1)}, u32[]{:S(2)}, u32[]{:S(2)}) collective-permute-start(f32[2,16,96]{2,1,0:T(8,128)S(1)} %maximum_add_fusion.2), channel_id=1, source_target_pairs={{1,0},{0,1},{3,2},{2,3},{5,4},{4,5},{7,6},{6,7},{14,8},{15,9},{12,... | collective-permute-start | bytes 36872 | tf_op jit(solution)/shard_map/ppermute | solution.py:327
  26.6 1.5 %collective-permute-start.11 = (f32[2,16,96]{2,1,0:T(8,128)S(1)}, f32[2,16,96]{2,1,0:T(8,128)S(1)}, u32[]{:S(2)}, u32[]{:S(2)}) collective-permute-start(f32[2,16,96]{2,1,0:T(8,128)S(1)} %maximum_add_fusion.2), channel_id=1, source_target_pairs={{16,0},{17,1},{18,2},{19,3},{20,4},{21,5},{22,6},{23,7},{10,8},{11... | collective-permute-start | bytes 36872 | tf_op jit(solution)/shard_map/ppermute | solution.py:327
  28.3 0.8 %collective-permute-done.12 = f32[2,16,96]{2,1,0:T(8,128)S(1)} collective-permute-done((f32[2,16,96]{2,1,0:T(8,128)S(1)}, f32[2,16,96]{2,1,0:T(8,128)S(1)}, u32[]{:S(2)}, u32[]{:S(2)}) %collective-permute-start.12) | collective-permute-done | bytes 12320 | tf_op jit(solution)/shard_map/ppermute | solution.py:327
  29.1 1.2 %collective-permute-done.11 = f32[2,16,96]{2,1,0:T(8,128)S(1)} collective-permute-done((f32[2,16,96]{2,1,0:T(8,128)S(1)}, f32[2,16,96]{2,1,0:T(8,128)S(1)}, u32[]{:S(2)}, u32[]{:S(2)}) %collective-permute-start.11) | collective-permute-done | bytes 12320 | tf_op jit(solution)/shard_map/ppermute | solution.py:327
  30.6 0.4 %collective-permute-start.13 = (f32[16,96]{1,0:T(8,128)S(1)}, f32[16,96]{1,0:T(8,128)S(1)}, u32[]{:S(2)}, u32[]{:S(2)}) collective-permute-start(f32[16,96]{1,0:T(8,128)S(1)} %get-tuple-element.37), channel_id=1, source_target_pairs={{8,0},{9,1},{10,2},{11,3},{12,4},{13,5},{14,6},{15,7},{0,8},{1,9},... | collective-permute-start | bytes 18440 | tf_op jit(solution)/shard_map/ppermute | solution.py:327
  31.1 0.8 %collective-permute-done.13.second_ref = f32[16,96]{1,0:T(8,128)S(1)} collective-permute-done((f32[16,96]{1,0:T(8,128)S(1)}, f32[16,96]{1,0:T(8,128)S(1)}, u32[]{:S(2)}, u32[]{:S(2)}) %collective-permute-start.13) | collective-permute-done | bytes 6176 | tf_op jit(solution)/shard_map/ppermute | solution.py:327
  31.9 0.9 %shard_map.60 = bf16[16,12,2,256]{3,2,1,0:T(2,128)(2,1)} custom-call(f32[16,96]{1,0:T(8,128)S(1)} %get-tuple-element.38.first_ref, f32[16,96]{1,0:T(8,128)S(1)} %collective-permute-done.13.second_ref, f32[16,96]{1,0:T(8,128)S(1)} %get-tuple-element.28.used_ref, bf16[12,48,256]{2,1,0:T(8,128)(2,1)S(1)} %shard_map.59.vectors_ref, ...), custom_call_target="tpu_custom_call" | custom-call | flops 10000000 | bytes 1000000 | tf_op jit(solution)/shard_map/pallas_call | solution.py:144
  (42 shorter events, 4.2 us)
Async XLA Ops:
  0.7 2.1 %copy-start.3 = (f32[1,9,2,2304]{3,2,1,0:T(2,128)S(1)}, f32[1,9,2,2304]{3,2,1,0:T(2,128)}, u32[]{:S(2)}) copy-start(f32[1,9,2,2304]{3,2,1,0:T(2,128)} %param.8) | copy-start | bytes 497668
  2.2 1.3 %collective-permute-start = (f32[16,96]{1,0:T(8,128)S(1)}, f32[16,96]{1,0:T(8,128)S(1)}, u32[]{:S(2)}, u32[]{:S(2)}) collective-permute-start(f32[16,96]{1,0:T(8,128)S(1)} %get-tuple-element.19), channel_id=1, source_target_pairs={{8,0},{9,1},{10,2},{11,3},{12,4},{13,5},{14,6},{15,7},{0,8},{1,9},... | collective-permute-start | bytes 18440 | tf_op jit(solution)/shard_map/ppermute | solution.py:327
  2.9 5.1 %collective-permute-start.3 = (f32[2,2,2304]{2,1,0:T(2,128)S(1)}, f32[2,2,2304]{2,1,0:T(2,128)S(1)}, u32[]{:S(2)}, u32[]{:S(2)}) collective-permute-start(f32[2,2,2304]{2,1,0:T(2,128)S(1)} %maximum_select_fusion.1), channel_id=1, source_target_pairs={{8,0},{9,1},{10,2},{11,3},{12,4},{13,5},{14,6},{15,7},{0,8},{1,9},... | collective-permute-start | bytes 110600 | tf_op jit(solution)/shard_map/ppermute | solution.py:327
  3.6 4.9 %collective-permute-start.2 = (f32[2,16,96]{2,1,0:T(8,128)S(1)}, f32[2,16,96]{2,1,0:T(8,128)S(1)}, u32[]{:S(2)}, u32[]{:S(2)}) collective-permute-start(f32[2,16,96]{2,1,0:T(8,128)S(1)} %pad_maximum_fusion.1), channel_id=1, source_target_pairs={{1,0},{0,1},{3,2},{2,3},{5,4},{4,5},{7,6},{6,7},{14,8},{15,9},{12,... | collective-permute-start | bytes 36872 | tf_op jit(solution)/shard_map/ppermute | solution.py:327
  6.4 3.7 %collective-permute-start.1 = (f32[2,16,96]{2,1,0:T(8,128)S(1)}, f32[2,16,96]{2,1,0:T(8,128)S(1)}, u32[]{:S(2)}, u32[]{:S(2)}) collective-permute-start(f32[2,16,96]{2,1,0:T(8,128)S(1)} %pad_maximum_fusion.1), channel_id=1, source_target_pairs={{16,0},{17,1},{18,2},{19,3},{20,4},{21,5},{22,6},{23,7},{10,8},{11... | collective-permute-start | bytes 36872 | tf_op jit(solution)/shard_map/ppermute | solution.py:327
  8.5 7.0 %copy-start.1 = (bf16[16,2,12,256]{3,1,2,0:T(2,128)(2,1)S(1)}, bf16[16,2,12,256]{3,1,2,0:T(2,128)(2,1)}, u32[]{:S(2)}) copy-start(bf16[16,2,12,256]{3,1,2,0:T(2,128)(2,1)} %param.5) | copy-start | bytes 589828
  10.5 1.7 %collective-permute-start.4 = (f32[2,16,96]{2,1,0:T(8,128)S(1)}, f32[2,16,96]{2,1,0:T(8,128)S(1)}, u32[]{:S(2)}, u32[]{:S(2)}) collective-permute-start(f32[2,16,96]{2,1,0:T(8,128)S(1)} %convolution_add_fusion.3), channel_id=1, source_target_pairs={{8,0},{9,1},{10,2},{11,3},{12,4},{13,5},{14,6},{15,7},{0,8},{1,9},... | collective-permute-start | bytes 36872 | tf_op jit(solution)/shard_map/ppermute | solution.py:327
  12.2 3.3 %copy-start.2 = (bf16[2,2,6,6,256]{4,1,3,2,0:T(2,128)(2,1)S(1)}, bf16[2,2,6,6,256]{4,1,3,2,0:T(2,128)(2,1)}, u32[]{:S(2)}) copy-start(bf16[2,2,6,6,256]{4,1,3,2,0:T(2,128)(2,1)} %param.7) | copy-start | bytes 221188
  12.2 3.9 %collective-permute-start.6 = (f32[2,16,96]{2,1,0:T(8,128)S(1)}, f32[2,16,96]{2,1,0:T(8,128)S(1)}, u32[]{:S(2)}, u32[]{:S(2)}) collective-permute-start(f32[2,16,96]{2,1,0:T(8,128)S(1)} %maximum_add_fusion), channel_id=1, source_target_pairs={{1,0},{0,1},{3,2},{2,3},{5,4},{4,5},{7,6},{6,7},{14,8},{15,9},{12,... | collective-permute-start | bytes 36872 | tf_op jit(solution)/shard_map/ppermute | solution.py:327
  13.8 3.7 %collective-permute-start.5 = (f32[2,16,96]{2,1,0:T(8,128)S(1)}, f32[2,16,96]{2,1,0:T(8,128)S(1)}, u32[]{:S(2)}, u32[]{:S(2)}) collective-permute-start(f32[2,16,96]{2,1,0:T(8,128)S(1)} %maximum_add_fusion), channel_id=1, source_target_pairs={{16,0},{17,1},{18,2},{19,3},{20,4},{21,5},{22,6},{23,7},{10,8},{11... | collective-permute-start | bytes 36872 | tf_op jit(solution)/shard_map/ppermute | solution.py:327
  16.2 5.6 %copy-start = (bf16[2,24,12,256]{3,1,2,0:T(8,128)(2,1)S(1)}, bf16[2,24,12,256]{3,1,2,0:T(8,128)(2,1)}, u32[]{:S(2)}) copy-start(bf16[2,24,12,256]{3,1,2,0:T(8,128)(2,1)} %param.6) | copy-start | bytes 884740
  17.9 1.2 %collective-permute-start.7 = (f32[2,16,96]{2,1,0:T(8,128)S(1)}, f32[2,16,96]{2,1,0:T(8,128)S(1)}, u32[]{:S(2)}, u32[]{:S(2)}) collective-permute-start(f32[2,16,96]{2,1,0:T(8,128)S(1)} %convolution_add_fusion.2), channel_id=1, source_target_pairs={{8,0},{9,1},{10,2},{11,3},{12,4},{13,5},{14,6},{15,7},{0,8},{1,9},... | collective-permute-start | bytes 36872 | tf_op jit(solution)/shard_map/ppermute | solution.py:327
  19.1 3.8 %collective-permute-start.9 = (f32[2,16,96]{2,1,0:T(8,128)S(1)}, f32[2,16,96]{2,1,0:T(8,128)S(1)}, u32[]{:S(2)}, u32[]{:S(2)}) collective-permute-start(f32[2,16,96]{2,1,0:T(8,128)S(1)} %maximum_add_fusion.1), channel_id=1, source_target_pairs={{1,0},{0,1},{3,2},{2,3},{5,4},{4,5},{7,6},{6,7},{14,8},{15,9},{12,... | collective-permute-start | bytes 36872 | tf_op jit(solution)/shard_map/ppermute | solution.py:327
  20.0 3.7 %collective-permute-start.8 = (f32[2,16,96]{2,1,0:T(8,128)S(1)}, f32[2,16,96]{2,1,0:T(8,128)S(1)}, u32[]{:S(2)}, u32[]{:S(2)}) collective-permute-start(f32[2,16,96]{2,1,0:T(8,128)S(1)} %maximum_add_fusion.1), channel_id=1, source_target_pairs={{16,0},{17,1},{18,2},{19,3},{20,4},{21,5},{22,6},{23,7},{10,8},{11... | collective-permute-start | bytes 36872 | tf_op jit(solution)/shard_map/ppermute | solution.py:327
  24.1 1.2 %collective-permute-start.10 = (f32[2,16,96]{2,1,0:T(8,128)S(1)}, f32[2,16,96]{2,1,0:T(8,128)S(1)}, u32[]{:S(2)}, u32[]{:S(2)}) collective-permute-start(f32[2,16,96]{2,1,0:T(8,128)S(1)} %convolution_add_fusion.1), channel_id=1, source_target_pairs={{8,0},{9,1},{10,2},{11,3},{12,4},{13,5},{14,6},{15,7},{0,8},{1,9},... | collective-permute-start | bytes 36872 | tf_op jit(solution)/shard_map/ppermute | solution.py:327
  25.3 3.8 %collective-permute-start.12 = (f32[2,16,96]{2,1,0:T(8,128)S(1)}, f32[2,16,96]{2,1,0:T(8,128)S(1)}, u32[]{:S(2)}, u32[]{:S(2)}) collective-permute-start(f32[2,16,96]{2,1,0:T(8,128)S(1)} %maximum_add_fusion.2), channel_id=1, source_target_pairs={{1,0},{0,1},{3,2},{2,3},{5,4},{4,5},{7,6},{6,7},{14,8},{15,9},{12,... | collective-permute-start | bytes 36872 | tf_op jit(solution)/shard_map/ppermute | solution.py:327
  26.6 3.7 %collective-permute-start.11 = (f32[2,16,96]{2,1,0:T(8,128)S(1)}, f32[2,16,96]{2,1,0:T(8,128)S(1)}, u32[]{:S(2)}, u32[]{:S(2)}) collective-permute-start(f32[2,16,96]{2,1,0:T(8,128)S(1)} %maximum_add_fusion.2), channel_id=1, source_target_pairs={{16,0},{17,1},{18,2},{19,3},{20,4},{21,5},{22,6},{23,7},{10,8},{11... | collective-permute-start | bytes 36872 | tf_op jit(solution)/shard_map/ppermute | solution.py:327
  30.6 1.2 %collective-permute-start.13 = (f32[16,96]{1,0:T(8,128)S(1)}, f32[16,96]{1,0:T(8,128)S(1)}, u32[]{:S(2)}, u32[]{:S(2)}) collective-permute-start(f32[16,96]{1,0:T(8,128)S(1)} %get-tuple-element.37), channel_id=1, source_target_pairs={{8,0},{9,1},{10,2},{11,3},{12,4},{13,5},{14,6},{15,7},{0,8},{1,9},... | collective-permute-start | bytes 18440 | tf_op jit(solution)/shard_map/ppermute | solution.py:327

commit v16 on v14

--- a/solution.py
+++ b/solution.py
@@ -55,27 +55,29 @@
     rhs, parts, _, sites = rows_ref.shape
     vecs = vectors_ref.shape[2]
     half = parts // 2
+    step = half // 2
     copies = []
-    for chi in range(2):
-        span = pl.ds(half * chi, half)
+    for piece in range(4):
+        span = pl.ds(step * piece, step)
         copies.append(
             [
-                pltpu.make_async_copy(rows_hbm.at[:, span], rows_ref.at[:, span], sems.at[2 * chi]),
-                pltpu.make_async_copy(vectors_hbm.at[:, span], vectors_ref.at[:, span], sems.at[2 * chi + 1]),
+                pltpu.make_async_copy(rows_hbm.at[:, span], rows_ref.at[:, span], sems.at[2 * piece]),
+                pltpu.make_async_copy(vectors_hbm.at[:, span], vectors_ref.at[:, span], sems.at[2 * piece + 1]),
             ]
         )
-    for copy in copies[0] + copies[1]:
-        copy.start()
+        for copy in copies[-1]:
+            copy.start()
     for chi in range(2):
-        for copy in copies[chi]:
-            copy.wait()
         total = jnp.zeros((2 * rhs, 2 * vecs), jnp.float32)
-        for c in range(half * chi, half * chi + half):
-            rows = rows_ref[:, c].reshape(2 * rhs, sites)
-            vectors = jnp.concatenate([vectors_ref[0, c], vectors_ref[1, c]], 0)
-            total += lax.dot_general(
-                rows, vectors, (((1,), (1,)), ((), ())), preferred_element_type=jnp.float32
-            )
+        for piece in (2 * chi, 2 * chi + 1):
+            for copy in copies[piece]:
+                copy.wait()
+            for c in range(step * piece, step * piece + step):
+                rows = rows_ref[:, c].reshape(2 * rhs, sites)
+                vectors = jnp.concatenate([vectors_ref[0, c], vectors_ref[1, c]], 0)
+                total += lax.dot_general(
+                    rows, vectors, (((1,), (1,)), ((), ())), preferred_element_type=jnp.float32
+                )
         scratch[chi, :, : 2 * vecs] = total
     real, imag = [], []
     for chi in range(2):
@@ -102,7 +104,7 @@
             pltpu.VMEM(rows.shape, rows.dtype),
             pltpu.VMEM(vectors.shape, vectors.dtype),
             pltpu.VMEM((2, 2 * rhs, 128), jnp.float32),
-            pltpu.SemaphoreType.DMA((4,)),
+            pltpu.SemaphoreType.DMA((8,)),
         ],
         compiler_params=pltpu.CompilerParams(vmem_limit_bytes=55168 * 2**10),
         cost_estimate=pl.CostEstimate(flops=10**7, bytes_accessed=5 * 10**5, transcendentals=0),
@@ -120,14 +122,15 @@
         scratch[chi, pl.ds(0, rhs, stride=2), : 2 * vecs] = jnp.concatenate([real, -imag], 1)
         scratch[chi, pl.ds(1, rhs, stride=2), : 2 * vecs] = jnp.concatenate([imag, real], 1)
     copies = []
-    for chi in range(2):
-        weights = scratch[chi, :, : 2 * vecs].astype(jnp.bfloat16)
-        for c in range(half * chi, half * chi + half):
+    step = half // 2
+    for piece in range(4):
+        weights = scratch[piece // 2, :, : 2 * vecs].astype(jnp.bfloat16)
+        for c in range(step * piece, step * piece + step):
             lift = jnp.dot(weights, vectors_ref[c], preferred_element_type=jnp.float32)
             total = (local_ref[c] + lift).astype(jnp.bfloat16)
             out_ref[:, c] = total.reshape(rhs, 2, sites)
-        span = pl.ds(half * chi, half)
-        copies.append(pltpu.make_async_copy(out_ref.at[:, span], out_hbm.at[:, span], sems.at[chi]))
+        span = pl.ds(step * piece, step)
+        copies.append(pltpu.make_async_copy(out_ref.at[:, span], out_hbm.at[:, span], sems.at[piece]))
         copies[-1].start()
     for copy in copies:
         copy.wait()
@@ -149,7 +152,7 @@
         scratch_shapes=[
             pltpu.VMEM(shape, jnp.bfloat16),
             pltpu.VMEM((2, 2 * rhs, 128), jnp.float32),
-            pltpu.SemaphoreType.DMA((2,)),
+            pltpu.SemaphoreType.DMA((4,)),
         ],
         compiler_params=small,
         cost_estimate=pl.CostEstimate(flops=10**7, bytes_accessed=10**6, transcendentals=0),
@@ -217,8 +220,8 @@
     return omega_step * jnp.concatenate([upper, lower], 0)
 
 
-def apply(vector, matrix):
-    return lax.dot_general(vector, matrix, (((1,), (1,)), ((), ())), precision=exact)
+def apply(vector, matrix, precision=exact):
+    return lax.dot_general(vector, matrix, (((1,), (1,)), ((), ())), precision=precision)
 
 
 def own_form(operator, dim):
@@ -340,7 +343,7 @@
     pair = jnp.stack([half, swap(half, mate)])
     for sweep_id in range(ITERS - 1):
         moved = [swap(pair, first), swap(pair, second)]
-        kept = half + apply(jnp.concatenate([pair[0], pair[1]], 1), inside)
+        kept = half + apply(jnp.concatenate([pair[0], pair[1]], 1), inside, lax.Precision.HIGH)
         if sweep_id == 1:
             rows, clover, kept = lax.optimization_barrier((*held[:2], kept))
             local, kept = lax.optimization_barrier((local_term(rows, clover), kept))
@@ -349,7 +352,7 @@
             vectors, kept = lax.optimization_barrier((hold(stored), kept))
         def along(link):
             return lax.dot_general(
-                moved[link], around[:, link], (((2,), (2,)), ((0,), (0,))), precision=exact
+                moved[link], around[:, link], (((2,), (2,)), ((0,), (0,))), precision=lax.Precision.HIGH
             )
 
         part = along(1) + (jnp.stack([kept, jnp.zeros_like(kept)]) + along(0))

time: 32.6 us -> 32.3 us (level)
  matrix products: 2.79 us -> 2 us
  waiting for transfers between devices: 9.64 us -> 10.1 us
    dot_general x8, matrix products: 1.95 us -> 1.32 us  [along(): lax.dot_general(moved[link], around[:, link], (((2,), (2,)), ((0,), (0,))...]
    ppermute x14, waiting for transfers between devices: 9.64 us -> 10.1 us  [swap(): lax.ppermute(block, axes, [(source, i) for i, source in enumerate(sources)])]
  transfers between devices with their start and end apart: 14 -> 14, of which waited for: 11 -> 11; matrix products, arithmetic and copies ran while one was open for 6% -> 5% of each run, Pallas kernels for 4% -> 4%
where the time goes in v16:
time: 32.3 us; the launch traced here: 32.2 us
  starting transfers between devices  15.3 us (47%)
  waiting for transfers between devices  10.1 us (31%)
  Pallas kernels  3.71 us (11%)
  matrix products  2 us (6%)
  between operations  0.8 us (2%)
    ppermute x14, starting transfers between devices, swap(): lax.ppermute(block, axes, [(source, i) for i, source in enumerate(sources)])  15.3 us
    ppermute x14, waiting for transfers between devices, swap(): lax.ppermute(block, axes, [(source, i) for i, source in enumerate(sources)])  10.1 us
    pallas_call x1, Pallas kernels, restrict(): pl.pallas_call(restrict_kernel, out_shape=[jax.ShapeDtypeStruct((rhs, 4 *...  1.6 us
    dot_general x8, matrix products, along(): lax.dot_general(moved[link], around[:, link], (((2,), (2,)), ((0,), (0,))...  1.32 us
    pallas_call x1, Pallas kernels, extend(): pl.pallas_call(extend_kernel, out_shape=jax.ShapeDtypeStruct(shape, jnp.b...  0.94 us
    dot_general x4, matrix products, apply(): lax.dot_general(vector, matrix, (((1,), (1,)), ((), ())), precision=preci...  0.68 us
  transfers between devices with their start and end apart: 14, of which 11 were waited for; matrix products, arithmetic and copies ran while one was open for 5% of the time, Pallas kernels for 4%

profile of v16, /device:TPU:0, one launch (start us, length us, event | category | flops | bytes accessed | tf_op | source)
XLA Modules:
  0.0 32.2 jit_solution(8914236897000588245)
XLA Ops:
  0.7 1.6 %shard_map.55 = (f32[16,96]{1,0:T(8,128)S(1)}, f32[16,96]{1,0:T(8,128)S(1)}) custom-call(s32[1]{0:T(128)S(6)} %copy.6.count_ref, bf16[16,12,2,256]{3,2,1,0:T(2,128)(2,1)} %bitcast.70, bf16[2,12,24,256]{3,2,1,0:T(8,128)(2,1)} %bitcast.68), custom_call_target="tpu_custom_call" | custom-call | flops 10000000 | bytes 500000 | tf_op jit(solution)/shard_map/pallas_call | solution.py:98
  2.3 0.5 %collective-permute-start = (f32[16,96]{1,0:T(8,128)S(1)}, f32[16,96]{1,0:T(8,128)S(1)}, u32[]{:S(2)}, u32[]{:S(2)}) collective-permute-start(f32[16,96]{1,0:T(8,128)S(1)} %get-tuple-element.19), channel_id=1, source_target_pairs={{8,0},{9,1},{10,2},{11,3},{12,4},{13,5},{14,6},{15,7},{0,8},{1,9},... | collective-permute-start | bytes 18440 | tf_op jit(solution)/shard_map/ppermute | solution.py:330
  3.6 2.8 %collective-permute-start.3 = (f32[2,16,96]{2,1,0:T(8,128)S(1)}, f32[2,16,96]{2,1,0:T(8,128)S(1)}, u32[]{:S(2)}, u32[]{:S(2)}) collective-permute-start(f32[2,16,96]{2,1,0:T(8,128)S(1)} %pad_maximum_fusion.1), channel_id=1, source_target_pairs={{1,0},{0,1},{3,2},{2,3},{5,4},{4,5},{7,6},{6,7},{14,8},{15,9},{12,... | collective-permute-start | bytes 36872 | tf_op jit(solution)/shard_map/ppermute | solution.py:330
  6.5 1.5 %collective-permute-start.1 = (f32[2,16,96]{2,1,0:T(8,128)S(1)}, f32[2,16,96]{2,1,0:T(8,128)S(1)}, u32[]{:S(2)}, u32[]{:S(2)}) collective-permute-start(f32[2,16,96]{2,1,0:T(8,128)S(1)} %pad_maximum_fusion.1), channel_id=1, source_target_pairs={{16,0},{17,1},{18,2},{19,3},{20,4},{21,5},{22,6},{23,7},{10,8},{11... | collective-permute-start | bytes 36872 | tf_op jit(solution)/shard_map/ppermute | solution.py:330
  8.7 1.5 %collective-permute-done.1 = f32[2,16,96]{2,1,0:T(8,128)S(1)} collective-permute-done((f32[2,16,96]{2,1,0:T(8,128)S(1)}, f32[2,16,96]{2,1,0:T(8,128)S(1)}, u32[]{:S(2)}, u32[]{:S(2)}) %collective-permute-start.1) | collective-permute-done | bytes 12320 | tf_op jit(solution)/shard_map/ppermute | solution.py:330
  10.4 0.9 %collective-permute-start.4 = (f32[2,16,96]{2,1,0:T(8,128)S(1)}, f32[2,16,96]{2,1,0:T(8,128)S(1)}, u32[]{:S(2)}, u32[]{:S(2)}) collective-permute-start(f32[2,16,96]{2,1,0:T(8,128)S(1)} %convolution_add_fusion.7), channel_id=1, source_target_pairs={{8,0},{9,1},{10,2},{11,3},{12,4},{13,5},{14,6},{15,7},{0,8},{1,9},... | collective-permute-start | bytes 36872 | tf_op jit(solution)/shard_map/ppermute | solution.py:330
  11.2 0.8 %collective-permute-done.4 = f32[2,16,96]{2,1,0:T(8,128)S(1)} collective-permute-done((f32[2,16,96]{2,1,0:T(8,128)S(1)}, f32[2,16,96]{2,1,0:T(8,128)S(1)}, u32[]{:S(2)}, u32[]{:S(2)}) %collective-permute-start.4) | collective-permute-done | bytes 12320 | tf_op jit(solution)/shard_map/ppermute | solution.py:330
  12.1 1.6 %collective-permute-start.6 = (f32[2,16,96]{2,1,0:T(8,128)S(1)}, f32[2,16,96]{2,1,0:T(8,128)S(1)}, u32[]{:S(2)}, u32[]{:S(2)}) collective-permute-start(f32[2,16,96]{2,1,0:T(8,128)S(1)} %maximum_add_fusion), channel_id=1, source_target_pairs={{1,0},{0,1},{3,2},{2,3},{5,4},{4,5},{7,6},{6,7},{14,8},{15,9},{12,... | collective-permute-start | bytes 36872 | tf_op jit(solution)/shard_map/ppermute | solution.py:330
  13.7 1.5 %collective-permute-start.5 = (f32[2,16,96]{2,1,0:T(8,128)S(1)}, f32[2,16,96]{2,1,0:T(8,128)S(1)}, u32[]{:S(2)}, u32[]{:S(2)}) collective-permute-start(f32[2,16,96]{2,1,0:T(8,128)S(1)} %maximum_add_fusion), channel_id=1, source_target_pairs={{16,0},{17,1},{18,2},{19,3},{20,4},{21,5},{22,6},{23,7},{10,8},{11... | collective-permute-start | bytes 36872 | tf_op jit(solution)/shard_map/ppermute | solution.py:330
  15.4 0.6 %shard_map.58.local_ref = f32[12,32,256]{2,1,0:T(8,128)S(1)} custom-call(bf16[16,12,2,256]{3,2,1,0:T(2,128)(2,1)S(1)} %bitcast.71, bf16[2,6,6,2,256]{4,3,2,1,0:T(2,128)(2,1)S(1)} %bitcast.73), custom_call_target="tpu_custom_call" | custom-call | flops 100000 | bytes 100000 | tf_op jit(solution)/shard_map/pallas_call | solution.py:206
  16.2 1.2 %collective-permute-done.5 = f32[2,16,96]{2,1,0:T(8,128)S(1)} collective-permute-done((f32[2,16,96]{2,1,0:T(8,128)S(1)}, f32[2,16,96]{2,1,0:T(8,128)S(1)}, u32[]{:S(2)}, u32[]{:S(2)}) %collective-permute-start.5) | collective-permute-done | bytes 12320 | tf_op jit(solution)/shard_map/ppermute | solution.py:330
  17.6 0.4 %collective-permute-start.7 = (f32[2,16,96]{2,1,0:T(8,128)S(1)}, f32[2,16,96]{2,1,0:T(8,128)S(1)}, u32[]{:S(2)}, u32[]{:S(2)}) collective-permute-start(f32[2,16,96]{2,1,0:T(8,128)S(1)} %convolution_add_fusion.5), channel_id=1, source_target_pairs={{8,0},{9,1},{10,2},{11,3},{12,4},{13,5},{14,6},{15,7},{0,8},{1,9},... | collective-permute-start | bytes 36872 | tf_op jit(solution)/shard_map/ppermute | solution.py:330
  17.9 0.8 %collective-permute-done.7 = f32[2,16,96]{2,1,0:T(8,128)S(1)} collective-permute-done((f32[2,16,96]{2,1,0:T(8,128)S(1)}, f32[2,16,96]{2,1,0:T(8,128)S(1)}, u32[]{:S(2)}, u32[]{:S(2)}) %collective-permute-start.7) | collective-permute-done | bytes 12320 | tf_op jit(solution)/shard_map/ppermute | solution.py:330
  18.8 0.9 %collective-permute-start.9 = (f32[2,16,96]{2,1,0:T(8,128)S(1)}, f32[2,16,96]{2,1,0:T(8,128)S(1)}, u32[]{:S(2)}, u32[]{:S(2)}) collective-permute-start(f32[2,16,96]{2,1,0:T(8,128)S(1)} %maximum_add_fusion.1), channel_id=1, source_target_pairs={{1,0},{0,1},{3,2},{2,3},{5,4},{4,5},{7,6},{6,7},{14,8},{15,9},{12,... | collective-permute-start | bytes 36872 | tf_op jit(solution)/shard_map/ppermute | solution.py:330
  19.7 1.5 %collective-permute-start.8 = (f32[2,16,96]{2,1,0:T(8,128)S(1)}, f32[2,16,96]{2,1,0:T(8,128)S(1)}, u32[]{:S(2)}, u32[]{:S(2)}) collective-permute-start(f32[2,16,96]{2,1,0:T(8,128)S(1)} %maximum_add_fusion.1), channel_id=1, source_target_pairs={{16,0},{17,1},{18,2},{19,3},{20,4},{21,5},{22,6},{23,7},{10,8},{11... | collective-permute-start | bytes 36872 | tf_op jit(solution)/shard_map/ppermute | solution.py:330
  21.5 1.1 %collective-permute-done.9 = f32[2,16,96]{2,1,0:T(8,128)S(1)} collective-permute-done((f32[2,16,96]{2,1,0:T(8,128)S(1)}, f32[2,16,96]{2,1,0:T(8,128)S(1)}, u32[]{:S(2)}, u32[]{:S(2)}) %collective-permute-start.9) | collective-permute-done | bytes 12320 | tf_op jit(solution)/shard_map/ppermute | solution.py:330
  22.8 0.7 %collective-permute-done.8 = f32[2,16,96]{2,1,0:T(8,128)S(1)} collective-permute-done((f32[2,16,96]{2,1,0:T(8,128)S(1)}, f32[2,16,96]{2,1,0:T(8,128)S(1)}, u32[]{:S(2)}, u32[]{:S(2)}) %collective-permute-start.8) | collective-permute-done | bytes 12320 | tf_op jit(solution)/shard_map/ppermute | solution.py:330
  24.0 0.8 %collective-permute-done.10 = f32[2,16,96]{2,1,0:T(8,128)S(1)} collective-permute-done((f32[2,16,96]{2,1,0:T(8,128)S(1)}, f32[2,16,96]{2,1,0:T(8,128)S(1)}, u32[]{:S(2)}, u32[]{:S(2)}) %collective-permute-start.10) | collective-permute-done | bytes 12320 | tf_op jit(solution)/shard_map/ppermute | solution.py:330
  24.9 1.2 %collective-permute-start.12 = (f32[2,16,96]{2,1,0:T(8,128)S(1)}, f32[2,16,96]{2,1,0:T(8,128)S(1)}, u32[]{:S(2)}, u32[]{:S(2)}) collective-permute-start(f32[2,16,96]{2,1,0:T(8,128)S(1)} %maximum_add_fusion.2), channel_id=1, source_target_pairs={{1,0},{0,1},{3,2},{2,3},{5,4},{4,5},{7,6},{6,7},{14,8},{15,9},{12,... | collective-permute-start | bytes 36872 | tf_op jit(solution)/shard_map/ppermute | solution.py:330
  26.1 1.5 %collective-permute-start.11 = (f32[2,16,96]{2,1,0:T(8,128)S(1)}, f32[2,16,96]{2,1,0:T(8,128)S(1)}, u32[]{:S(2)}, u32[]{:S(2)}) collective-permute-start(f32[2,16,96]{2,1,0:T(8,128)S(1)} %maximum_add_fusion.2), channel_id=1, source_target_pairs={{16,0},{17,1},{18,2},{19,3},{20,4},{21,5},{22,6},{23,7},{10,8},{11... | collective-permute-start | bytes 36872 | tf_op jit(solution)/shard_map/ppermute | solution.py:330
  27.8 0.9 %collective-permute-done.12 = f32[2,16,96]{2,1,0:T(8,128)S(1)} collective-permute-done((f32[2,16,96]{2,1,0:T(8,128)S(1)}, f32[2,16,96]{2,1,0:T(8,128)S(1)}, u32[]{:S(2)}, u32[]{:S(2)}) %collective-permute-start.12) | collective-permute-done | bytes 12320 | tf_op jit(solution)/shard_map/ppermute | solution.py:330
  28.8 1.0 %collective-permute-done.11 = f32[2,16,96]{2,1,0:T(8,128)S(1)} collective-permute-done((f32[2,16,96]{2,1,0:T(8,128)S(1)}, f32[2,16,96]{2,1,0:T(8,128)S(1)}, u32[]{:S(2)}, u32[]{:S(2)}) %collective-permute-start.11) | collective-permute-done | bytes 12320 | tf_op jit(solution)/shard_map/ppermute | solution.py:330
  30.4 0.8 %collective-permute-done.13.second_ref = f32[16,96]{1,0:T(8,128)S(1)} collective-permute-done((f32[16,96]{1,0:T(8,128)S(1)}, f32[16,96]{1,0:T(8,128)S(1)}, u32[]{:S(2)}, u32[]{:S(2)}) %collective-permute-start.13) | collective-permute-done | bytes 6176 | tf_op jit(solution)/shard_map/ppermute | solution.py:330
  31.2 0.9 %shard_map.60 = bf16[16,12,2,256]{3,2,1,0:T(2,128)(2,1)} custom-call(f32[16,96]{1,0:T(8,128)S(1)} %get-tuple-element.38.first_ref, f32[16,96]{1,0:T(8,128)S(1)} %collective-permute-done.13.second_ref, f32[16,96]{1,0:T(8,128)S(1)} %get-tuple-element.28.used_ref, bf16[12,48,256]{2,1,0:T(8,128)(2,1)S(1)} %shard_map.59.vectors_ref, ...), custom_call_target="tpu_custom_call" | custom-call | flops 10000000 | bytes 1000000 | tf_op jit(solution)/shard_map/pallas_call | solution.py:147
  (46 shorter events, 4.1 us)
Async XLA Ops:
  0.7 2.1 %copy-start.3 = (f32[1,9,2,2304]{3,2,1,0:T(2,128)S(1)}, f32[1,9,2,2304]{3,2,1,0:T(2,128)}, u32[]{:S(2)}) copy-start(f32[1,9,2,2304]{3,2,1,0:T(2,128)} %param.8) | copy-start | bytes 497668
  2.3 1.3 %collective-permute-start = (f32[16,96]{1,0:T(8,128)S(1)}, f32[16,96]{1,0:T(8,128)S(1)}, u32[]{:S(2)}, u32[]{:S(2)}) collective-permute-start(f32[16,96]{1,0:T(8,128)S(1)} %get-tuple-element.19), channel_id=1, source_target_pairs={{8,0},{9,1},{10,2},{11,3},{12,4},{13,5},{14,6},{15,7},{0,8},{1,9},... | collective-permute-start | bytes 18440 | tf_op jit(solution)/shard_map/ppermute | solution.py:330
  2.9 5.1 %collective-permute-start.2 = (f32[2,2,2304]{2,1,0:T(2,128)S(1)}, f32[2,2,2304]{2,1,0:T(2,128)S(1)}, u32[]{:S(2)}, u32[]{:S(2)}) collective-permute-start(f32[2,2,2304]{2,1,0:T(2,128)S(1)} %maximum_select_fusion.1), channel_id=1, source_target_pairs={{8,0},{9,1},{10,2},{11,3},{12,4},{13,5},{14,6},{15,7},{0,8},{1,9},... | collective-permute-start | bytes 110600 | tf_op jit(solution)/shard_map/ppermute | solution.py:330
  3.6 4.9 %collective-permute-start.3 = (f32[2,16,96]{2,1,0:T(8,128)S(1)}, f32[2,16,96]{2,1,0:T(8,128)S(1)}, u32[]{:S(2)}, u32[]{:S(2)}) collective-permute-start(f32[2,16,96]{2,1,0:T(8,128)S(1)} %pad_maximum_fusion.1), channel_id=1, source_target_pairs={{1,0},{0,1},{3,2},{2,3},{5,4},{4,5},{7,6},{6,7},{14,8},{15,9},{12,... | collective-permute-start | bytes 36872 | tf_op jit(solution)/shard_map/ppermute | solution.py:330
  6.5 3.7 %collective-permute-start.1 = (f32[2,16,96]{2,1,0:T(8,128)S(1)}, f32[2,16,96]{2,1,0:T(8,128)S(1)}, u32[]{:S(2)}, u32[]{:S(2)}) collective-permute-start(f32[2,16,96]{2,1,0:T(8,128)S(1)} %pad_maximum_fusion.1), channel_id=1, source_target_pairs={{16,0},{17,1},{18,2},{19,3},{20,4},{21,5},{22,6},{23,7},{10,8},{11... | collective-permute-start | bytes 36872 | tf_op jit(solution)/shard_map/ppermute | solution.py:330
  8.7 6.7 %copy-start.1 = (bf16[16,2,12,256]{3,1,2,0:T(2,128)(2,1)S(1)}, bf16[16,2,12,256]{3,1,2,0:T(2,128)(2,1)}, u32[]{:S(2)}) copy-start(bf16[16,2,12,256]{3,1,2,0:T(2,128)(2,1)} %param.5) | copy-start | bytes 589828
  10.4 1.7 %collective-permute-start.4 = (f32[2,16,96]{2,1,0:T(8,128)S(1)}, f32[2,16,96]{2,1,0:T(8,128)S(1)}, u32[]{:S(2)}, u32[]{:S(2)}) collective-permute-start(f32[2,16,96]{2,1,0:T(8,128)S(1)} %convolution_add_fusion.7), channel_id=1, source_target_pairs={{8,0},{9,1},{10,2},{11,3},{12,4},{13,5},{14,6},{15,7},{0,8},{1,9},... | collective-permute-start | bytes 36872 | tf_op jit(solution)/shard_map/ppermute | solution.py:330
  12.1 3.3 %copy-start.2 = (bf16[2,2,6,6,256]{4,1,3,2,0:T(2,128)(2,1)S(1)}, bf16[2,2,6,6,256]{4,1,3,2,0:T(2,128)(2,1)}, u32[]{:S(2)}) copy-start(bf16[2,2,6,6,256]{4,1,3,2,0:T(2,128)(2,1)} %param.7) | copy-start | bytes 221188
  12.1 3.9 %collective-permute-start.6 = (f32[2,16,96]{2,1,0:T(8,128)S(1)}, f32[2,16,96]{2,1,0:T(8,128)S(1)}, u32[]{:S(2)}, u32[]{:S(2)}) collective-permute-start(f32[2,16,96]{2,1,0:T(8,128)S(1)} %maximum_add_fusion), channel_id=1, source_target_pairs={{1,0},{0,1},{3,2},{2,3},{5,4},{4,5},{7,6},{6,7},{14,8},{15,9},{12,... | collective-permute-start | bytes 36872 | tf_op jit(solution)/shard_map/ppermute | solution.py:330
  13.7 3.7 %collective-permute-start.5 = (f32[2,16,96]{2,1,0:T(8,128)S(1)}, f32[2,16,96]{2,1,0:T(8,128)S(1)}, u32[]{:S(2)}, u32[]{:S(2)}) collective-permute-start(f32[2,16,96]{2,1,0:T(8,128)S(1)} %maximum_add_fusion), channel_id=1, source_target_pairs={{16,0},{17,1},{18,2},{19,3},{20,4},{21,5},{22,6},{23,7},{10,8},{11... | collective-permute-start | bytes 36872 | tf_op jit(solution)/shard_map/ppermute | solution.py:330
  16.0 5.4 %copy-start = (bf16[2,24,12,256]{3,1,2,0:T(8,128)(2,1)S(1)}, bf16[2,24,12,256]{3,1,2,0:T(8,128)(2,1)}, u32[]{:S(2)}) copy-start(bf16[2,24,12,256]{3,1,2,0:T(8,128)(2,1)} %param.6) | copy-start | bytes 884740
  17.6 1.2 %collective-permute-start.7 = (f32[2,16,96]{2,1,0:T(8,128)S(1)}, f32[2,16,96]{2,1,0:T(8,128)S(1)}, u32[]{:S(2)}, u32[]{:S(2)}) collective-permute-start(f32[2,16,96]{2,1,0:T(8,128)S(1)} %convolution_add_fusion.5), channel_id=1, source_target_pairs={{8,0},{9,1},{10,2},{11,3},{12,4},{13,5},{14,6},{15,7},{0,8},{1,9},... | collective-permute-start | bytes 36872 | tf_op jit(solution)/shard_map/ppermute | solution.py:330
  18.8 3.8 %collective-permute-start.9 = (f32[2,16,96]{2,1,0:T(8,128)S(1)}, f32[2,16,96]{2,1,0:T(8,128)S(1)}, u32[]{:S(2)}, u32[]{:S(2)}) collective-permute-start(f32[2,16,96]{2,1,0:T(8,128)S(1)} %maximum_add_fusion.1), channel_id=1, source_target_pairs={{1,0},{0,1},{3,2},{2,3},{5,4},{4,5},{7,6},{6,7},{14,8},{15,9},{12,... | collective-permute-start | bytes 36872 | tf_op jit(solution)/shard_map/ppermute | solution.py:330
  19.7 3.7 %collective-permute-start.8 = (f32[2,16,96]{2,1,0:T(8,128)S(1)}, f32[2,16,96]{2,1,0:T(8,128)S(1)}, u32[]{:S(2)}, u32[]{:S(2)}) collective-permute-start(f32[2,16,96]{2,1,0:T(8,128)S(1)} %maximum_add_fusion.1), channel_id=1, source_target_pairs={{16,0},{17,1},{18,2},{19,3},{20,4},{21,5},{22,6},{23,7},{10,8},{11... | collective-permute-start | bytes 36872 | tf_op jit(solution)/shard_map/ppermute | solution.py:330
  23.6 1.2 %collective-permute-start.10 = (f32[2,16,96]{2,1,0:T(8,128)S(1)}, f32[2,16,96]{2,1,0:T(8,128)S(1)}, u32[]{:S(2)}, u32[]{:S(2)}) collective-permute-start(f32[2,16,96]{2,1,0:T(8,128)S(1)} %convolution_add_fusion.3), channel_id=1, source_target_pairs={{8,0},{9,1},{10,2},{11,3},{12,4},{13,5},{14,6},{15,7},{0,8},{1,9},... | collective-permute-start | bytes 36872 | tf_op jit(solution)/shard_map/ppermute | solution.py:330
  24.9 3.8 %collective-permute-start.12 = (f32[2,16,96]{2,1,0:T(8,128)S(1)}, f32[2,16,96]{2,1,0:T(8,128)S(1)}, u32[]{:S(2)}, u32[]{:S(2)}) collective-permute-start(f32[2,16,96]{2,1,0:T(8,128)S(1)} %maximum_add_fusion.2), channel_id=1, source_target_pairs={{1,0},{0,1},{3,2},{2,3},{5,4},{4,5},{7,6},{6,7},{14,8},{15,9},{12,... | collective-permute-start | bytes 36872 | tf_op jit(solution)/shard_map/ppermute | solution.py:330
  26.1 3.7 %collective-permute-start.11 = (f32[2,16,96]{2,1,0:T(8,128)S(1)}, f32[2,16,96]{2,1,0:T(8,128)S(1)}, u32[]{:S(2)}, u32[]{:S(2)}) collective-permute-start(f32[2,16,96]{2,1,0:T(8,128)S(1)} %maximum_add_fusion.2), channel_id=1, source_target_pairs={{16,0},{17,1},{18,2},{19,3},{20,4},{21,5},{22,6},{23,7},{10,8},{11... | collective-permute-start | bytes 36872 | tf_op jit(solution)/shard_map/ppermute | solution.py:330
  30.0 1.2 %collective-permute-start.13 = (f32[16,96]{1,0:T(8,128)S(1)}, f32[16,96]{1,0:T(8,128)S(1)}, u32[]{:S(2)}, u32[]{:S(2)}) collective-permute-start(f32[16,96]{1,0:T(8,128)S(1)} %get-tuple-element.37), channel_id=1, source_target_pairs={{8,0},{9,1},{10,2},{11,3},{12,4},{13,5},{14,6},{15,7},{0,8},{1,9},... | collective-permute-start | bytes 18440 | tf_op jit(solution)/shard_map/ppermute | solution.py:330

commit v17 on v14

--- a/solution.py
+++ b/solution.py
@@ -69,14 +69,13 @@
     for chi in range(2):
         for copy in copies[chi]:
             copy.wait()
-        total = jnp.zeros((2 * rhs, 2 * vecs), jnp.float32)
-        for c in range(half * chi, half * chi + half):
-            rows = rows_ref[:, c].reshape(2 * rhs, sites)
-            vectors = jnp.concatenate([vectors_ref[0, c], vectors_ref[1, c]], 0)
-            total += lax.dot_general(
+        span = range(half * chi, half * chi + half)
+        rows = jnp.concatenate([rows_ref[:, c].reshape(2 * rhs, sites) for c in span], 1)
+        for part in range(2):
+            vectors = jnp.concatenate([vectors_ref[part, c] for c in span], 1)
+            scratch[chi, :, part * vecs : (part + 1) * vecs] = lax.dot_general(
                 rows, vectors, (((1,), (1,)), ((), ())), preferred_element_type=jnp.float32
             )
-        scratch[chi, :, : 2 * vecs] = total
     real, imag = [], []
     for chi in range(2):
         even = scratch[chi, pl.ds(0, rhs, stride=2), :]
@@ -120,14 +119,15 @@
         scratch[chi, pl.ds(0, rhs, stride=2), : 2 * vecs] = jnp.concatenate([real, -imag], 1)
         scratch[chi, pl.ds(1, rhs, stride=2), : 2 * vecs] = jnp.concatenate([imag, real], 1)
     copies = []
-    for chi in range(2):
-        weights = scratch[chi, :, : 2 * vecs].astype(jnp.bfloat16)
-        for c in range(half * chi, half * chi + half):
+    step = half // 2
+    for piece in range(4):
+        weights = scratch[piece // 2, :, : 2 * vecs].astype(jnp.bfloat16)
+        for c in range(step * piece, step * piece + step):
             lift = jnp.dot(weights, vectors_ref[c], preferred_element_type=jnp.float32)
             total = (local_ref[c] + lift).astype(jnp.bfloat16)
             out_ref[:, c] = total.reshape(rhs, 2, sites)
-        span = pl.ds(half * chi, half)
-        copies.append(pltpu.make_async_copy(out_ref.at[:, span], out_hbm.at[:, span], sems.at[chi]))
+        span = pl.ds(step * piece, step)
+        copies.append(pltpu.make_async_copy(out_ref.at[:, span], out_hbm.at[:, span], sems.at[piece]))
         copies[-1].start()
     for copy in copies:
         copy.wait()
@@ -149,7 +149,7 @@
         scratch_shapes=[
             pltpu.VMEM(shape, jnp.bfloat16),
             pltpu.VMEM((2, 2 * rhs, 128), jnp.float32),
-            pltpu.SemaphoreType.DMA((2,)),
+            pltpu.SemaphoreType.DMA((4,)),
         ],
         compiler_params=small,
         cost_estimate=pl.CostEstimate(flops=10**7, bytes_accessed=10**6, transcendentals=0),
@@ -217,8 +217,8 @@
     return omega_step * jnp.concatenate([upper, lower], 0)
 
 
-def apply(vector, matrix):
-    return lax.dot_general(vector, matrix, (((1,), (1,)), ((), ())), precision=exact)
+def apply(vector, matrix, precision=exact):
+    return lax.dot_general(vector, matrix, (((1,), (1,)), ((), ())), precision=precision)
 
 
 def own_form(operator, dim):
@@ -340,7 +340,7 @@
     pair = jnp.stack([half, swap(half, mate)])
     for sweep_id in range(ITERS - 1):
         moved = [swap(pair, first), swap(pair, second)]
-        kept = half + apply(jnp.concatenate([pair[0], pair[1]], 1), inside)
+        kept = half + apply(jnp.concatenate([pair[0], pair[1]], 1), inside, lax.Precision.HIGH)
         if sweep_id == 1:
             rows, clover, kept = lax.optimization_barrier((*held[:2], kept))
             local, kept = lax.optimization_barrier((local_term(rows, clover), kept))
@@ -349,7 +349,7 @@
             vectors, kept = lax.optimization_barrier((hold(stored), kept))
         def along(link):
             return lax.dot_general(
-                moved[link], around[:, link], (((2,), (2,)), ((0,), (0,))), precision=exact
+                moved[link], around[:, link], (((2,), (2,)), ((0,), (0,))), precision=lax.Precision.HIGH
             )
 
         part = along(1) + (jnp.stack([kept, jnp.zeros_like(kept)]) + along(0))

time: 32.6 us -> 32.4 us (level)
  matrix products: 2.79 us -> 2 us
  waiting for transfers between devices: 9.64 us -> 10.1 us
    dot_general x8, matrix products: 1.95 us -> 1.32 us  [along(): lax.dot_general(moved[link], around[:, link], (((2,), (2,)), ((0,), (0,))...]
    ppermute x14, waiting for transfers between devices: 9.64 us -> 10.1 us  [swap(): lax.ppermute(block, axes, [(source, i) for i, source in enumerate(sources)])]
  transfers between devices with their start and end apart: 14 -> 14, of which waited for: 11 -> 11; matrix products, arithmetic and copies ran while one was open for 6% -> 5% of each run, Pallas kernels for 4% -> 4%
where the time goes in v17:
time: 32.4 us; the launch traced here: 32.3 us
  starting transfers between devices  15.3 us (47%)
  waiting for transfers between devices  10.1 us (31%)
  Pallas kernels  3.8 us (12%)
  matrix products  2 us (6%)
  between operations  0.8 us (2%)
    ppermute x14, starting transfers between devices, swap(): lax.ppermute(block, axes, [(source, i) for i, source in enumerate(sources)])  15.3 us
    ppermute x14, waiting for transfers between devices, swap(): lax.ppermute(block, axes, [(source, i) for i, source in enumerate(sources)])  10.1 us
    pallas_call x1, Pallas kernels, restrict(): pl.pallas_call(restrict_kernel, out_shape=[jax.ShapeDtypeStruct((rhs, 4 *...  1.7 us
    dot_general x8, matrix products, along(): lax.dot_general(moved[link], around[:, link], (((2,), (2,)), ((0,), (0,))...  1.32 us
    pallas_call x1, Pallas kernels, extend(): pl.pallas_call(extend_kernel, out_shape=jax.ShapeDtypeStruct(shape, jnp.b...  0.94 us
    dot_general x4, matrix products, apply(): lax.dot_general(vector, matrix, (((1,), (1,)), ((), ())), precision=preci...  0.68 us
  transfers between devices with their start and end apart: 14, of which 11 were waited for; matrix products, arithmetic and copies ran while one was open for 5% of the time, Pallas kernels for 4%

profile of v17, /device:TPU:0, one launch (start us, length us, event | category | flops | bytes accessed | tf_op | source)
XLA Modules:
  0.0 32.3 jit_solution(15833885889384070735)
XLA Ops:
  0.7 1.7 %shard_map.55 = (f32[16,96]{1,0:T(8,128)S(1)}, f32[16,96]{1,0:T(8,128)S(1)}) custom-call(s32[1]{0:T(128)S(6)} %copy.6.count_ref, bf16[16,12,2,256]{3,2,1,0:T(2,128)(2,1)} %bitcast.70, bf16[2,12,24,256]{3,2,1,0:T(8,128)(2,1)} %bitcast.68), custom_call_target="tpu_custom_call" | custom-call | flops 10000000 | bytes 500000 | tf_op jit(solution)/shard_map/pallas_call | solution.py:95
  2.4 0.5 %collective-permute-start = (f32[16,96]{1,0:T(8,128)S(1)}, f32[16,96]{1,0:T(8,128)S(1)}, u32[]{:S(2)}, u32[]{:S(2)}) collective-permute-start(f32[16,96]{1,0:T(8,128)S(1)} %get-tuple-element.19), channel_id=1, source_target_pairs={{8,0},{9,1},{10,2},{11,3},{12,4},{13,5},{14,6},{15,7},{0,8},{1,9},... | collective-permute-start | bytes 18440 | tf_op jit(solution)/shard_map/ppermute | solution.py:327
  3.7 2.8 %collective-permute-start.3 = (f32[2,16,96]{2,1,0:T(8,128)S(1)}, f32[2,16,96]{2,1,0:T(8,128)S(1)}, u32[]{:S(2)}, u32[]{:S(2)}) collective-permute-start(f32[2,16,96]{2,1,0:T(8,128)S(1)} %pad_maximum_fusion.1), channel_id=1, source_target_pairs={{1,0},{0,1},{3,2},{2,3},{5,4},{4,5},{7,6},{6,7},{14,8},{15,9},{12,... | collective-permute-start | bytes 36872 | tf_op jit(solution)/shard_map/ppermute | solution.py:327
  6.5 1.5 %collective-permute-start.1 = (f32[2,16,96]{2,1,0:T(8,128)S(1)}, f32[2,16,96]{2,1,0:T(8,128)S(1)}, u32[]{:S(2)}, u32[]{:S(2)}) collective-permute-start(f32[2,16,96]{2,1,0:T(8,128)S(1)} %pad_maximum_fusion.1), channel_id=1, source_target_pairs={{16,0},{17,1},{18,2},{19,3},{20,4},{21,5},{22,6},{23,7},{10,8},{11... | collective-permute-start | bytes 36872 | tf_op jit(solution)/shard_map/ppermute | solution.py:327
  8.8 1.5 %collective-permute-done.1 = f32[2,16,96]{2,1,0:T(8,128)S(1)} collective-permute-done((f32[2,16,96]{2,1,0:T(8,128)S(1)}, f32[2,16,96]{2,1,0:T(8,128)S(1)}, u32[]{:S(2)}, u32[]{:S(2)}) %collective-permute-start.1) | collective-permute-done | bytes 12320 | tf_op jit(solution)/shard_map/ppermute | solution.py:327
  10.5 0.9 %collective-permute-start.4 = (f32[2,16,96]{2,1,0:T(8,128)S(1)}, f32[2,16,96]{2,1,0:T(8,128)S(1)}, u32[]{:S(2)}, u32[]{:S(2)}) collective-permute-start(f32[2,16,96]{2,1,0:T(8,128)S(1)} %convolution_add_fusion.7), channel_id=1, source_target_pairs={{8,0},{9,1},{10,2},{11,3},{12,4},{13,5},{14,6},{15,7},{0,8},{1,9},... | collective-permute-start | bytes 36872 | tf_op jit(solution)/shard_map/ppermute | solution.py:327
  11.3 0.8 %collective-permute-done.4 = f32[2,16,96]{2,1,0:T(8,128)S(1)} collective-permute-done((f32[2,16,96]{2,1,0:T(8,128)S(1)}, f32[2,16,96]{2,1,0:T(8,128)S(1)}, u32[]{:S(2)}, u32[]{:S(2)}) %collective-permute-start.4) | collective-permute-done | bytes 12320 | tf_op jit(solution)/shard_map/ppermute | solution.py:327
  12.2 1.6 %collective-permute-start.6 = (f32[2,16,96]{2,1,0:T(8,128)S(1)}, f32[2,16,96]{2,1,0:T(8,128)S(1)}, u32[]{:S(2)}, u32[]{:S(2)}) collective-permute-start(f32[2,16,96]{2,1,0:T(8,128)S(1)} %maximum_add_fusion), channel_id=1, source_target_pairs={{1,0},{0,1},{3,2},{2,3},{5,4},{4,5},{7,6},{6,7},{14,8},{15,9},{12,... | collective-permute-start | bytes 36872 | tf_op jit(solution)/shard_map/ppermute | solution.py:327
  13.8 1.5 %collective-permute-start.5 = (f32[2,16,96]{2,1,0:T(8,128)S(1)}, f32[2,16,96]{2,1,0:T(8,128)S(1)}, u32[]{:S(2)}, u32[]{:S(2)}) collective-permute-start(f32[2,16,96]{2,1,0:T(8,128)S(1)} %maximum_add_fusion), channel_id=1, source_target_pairs={{16,0},{17,1},{18,2},{19,3},{20,4},{21,5},{22,6},{23,7},{10,8},{11... | collective-permute-start | bytes 36872 | tf_op jit(solution)/shard_map/ppermute | solution.py:327
  15.5 0.6 %shard_map.58.local_ref = f32[12,32,256]{2,1,0:T(8,128)S(1)} custom-call(bf16[16,12,2,256]{3,2,1,0:T(2,128)(2,1)S(1)} %bitcast.71, bf16[2,6,6,2,256]{4,3,2,1,0:T(2,128)(2,1)S(1)} %bitcast.73), custom_call_target="tpu_custom_call" | custom-call | flops 100000 | bytes 100000 | tf_op jit(solution)/shard_map/pallas_call | solution.py:203
  16.3 1.2 %collective-permute-done.5 = f32[2,16,96]{2,1,0:T(8,128)S(1)} collective-permute-done((f32[2,16,96]{2,1,0:T(8,128)S(1)}, f32[2,16,96]{2,1,0:T(8,128)S(1)}, u32[]{:S(2)}, u32[]{:S(2)}) %collective-permute-start.5) | collective-permute-done | bytes 12320 | tf_op jit(solution)/shard_map/ppermute | solution.py:327
  17.7 0.4 %collective-permute-start.7 = (f32[2,16,96]{2,1,0:T(8,128)S(1)}, f32[2,16,96]{2,1,0:T(8,128)S(1)}, u32[]{:S(2)}, u32[]{:S(2)}) collective-permute-start(f32[2,16,96]{2,1,0:T(8,128)S(1)} %convolution_add_fusion.5), channel_id=1, source_target_pairs={{8,0},{9,1},{10,2},{11,3},{12,4},{13,5},{14,6},{15,7},{0,8},{1,9},... | collective-permute-start | bytes 36872 | tf_op jit(solution)/shard_map/ppermute | solution.py:327
  18.0 0.8 %collective-permute-done.7 = f32[2,16,96]{2,1,0:T(8,128)S(1)} collective-permute-done((f32[2,16,96]{2,1,0:T(8,128)S(1)}, f32[2,16,96]{2,1,0:T(8,128)S(1)}, u32[]{:S(2)}, u32[]{:S(2)}) %collective-permute-start.7) | collective-permute-done | bytes 12320 | tf_op jit(solution)/shard_map/ppermute | solution.py:327
  18.9 0.9 %collective-permute-start.9 = (f32[2,16,96]{2,1,0:T(8,128)S(1)}, f32[2,16,96]{2,1,0:T(8,128)S(1)}, u32[]{:S(2)}, u32[]{:S(2)}) collective-permute-start(f32[2,16,96]{2,1,0:T(8,128)S(1)} %maximum_add_fusion.1), channel_id=1, source_target_pairs={{1,0},{0,1},{3,2},{2,3},{5,4},{4,5},{7,6},{6,7},{14,8},{15,9},{12,... | collective-permute-start | bytes 36872 | tf_op jit(solution)/shard_map/ppermute | solution.py:327
  19.8 1.5 %collective-permute-start.8 = (f32[2,16,96]{2,1,0:T(8,128)S(1)}, f32[2,16,96]{2,1,0:T(8,128)S(1)}, u32[]{:S(2)}, u32[]{:S(2)}) collective-permute-start(f32[2,16,96]{2,1,0:T(8,128)S(1)} %maximum_add_fusion.1), channel_id=1, source_target_pairs={{16,0},{17,1},{18,2},{19,3},{20,4},{21,5},{22,6},{23,7},{10,8},{11... | collective-permute-start | bytes 36872 | tf_op jit(solution)/shard_map/ppermute | solution.py:327
  21.6 1.1 %collective-permute-done.9 = f32[2,16,96]{2,1,0:T(8,128)S(1)} collective-permute-done((f32[2,16,96]{2,1,0:T(8,128)S(1)}, f32[2,16,96]{2,1,0:T(8,128)S(1)}, u32[]{:S(2)}, u32[]{:S(2)}) %collective-permute-start.9) | collective-permute-done | bytes 12320 | tf_op jit(solution)/shard_map/ppermute | solution.py:327
  22.9 0.7 %collective-permute-done.8 = f32[2,16,96]{2,1,0:T(8,128)S(1)} collective-permute-done((f32[2,16,96]{2,1,0:T(8,128)S(1)}, f32[2,16,96]{2,1,0:T(8,128)S(1)}, u32[]{:S(2)}, u32[]{:S(2)}) %collective-permute-start.8) | collective-permute-done | bytes 12320 | tf_op jit(solution)/shard_map/ppermute | solution.py:327
  24.1 0.8 %collective-permute-done.10 = f32[2,16,96]{2,1,0:T(8,128)S(1)} collective-permute-done((f32[2,16,96]{2,1,0:T(8,128)S(1)}, f32[2,16,96]{2,1,0:T(8,128)S(1)}, u32[]{:S(2)}, u32[]{:S(2)}) %collective-permute-start.10) | collective-permute-done | bytes 12320 | tf_op jit(solution)/shard_map/ppermute | solution.py:327
  25.0 1.2 %collective-permute-start.12 = (f32[2,16,96]{2,1,0:T(8,128)S(1)}, f32[2,16,96]{2,1,0:T(8,128)S(1)}, u32[]{:S(2)}, u32[]{:S(2)}) collective-permute-start(f32[2,16,96]{2,1,0:T(8,128)S(1)} %maximum_add_fusion.2), channel_id=1, source_target_pairs={{1,0},{0,1},{3,2},{2,3},{5,4},{4,5},{7,6},{6,7},{14,8},{15,9},{12,... | collective-permute-start | bytes 36872 | tf_op jit(solution)/shard_map/ppermute | solution.py:327
  26.2 1.5 %collective-permute-start.11 = (f32[2,16,96]{2,1,0:T(8,128)S(1)}, f32[2,16,96]{2,1,0:T(8,128)S(1)}, u32[]{:S(2)}, u32[]{:S(2)}) collective-permute-start(f32[2,16,96]{2,1,0:T(8,128)S(1)} %maximum_add_fusion.2), channel_id=1, source_target_pairs={{16,0},{17,1},{18,2},{19,3},{20,4},{21,5},{22,6},{23,7},{10,8},{11... | collective-permute-start | bytes 36872 | tf_op jit(solution)/shard_map/ppermute | solution.py:327
  27.9 0.9 %collective-permute-done.12 = f32[2,16,96]{2,1,0:T(8,128)S(1)} collective-permute-done((f32[2,16,96]{2,1,0:T(8,128)S(1)}, f32[2,16,96]{2,1,0:T(8,128)S(1)}, u32[]{:S(2)}, u32[]{:S(2)}) %collective-permute-start.12) | collective-permute-done | bytes 12320 | tf_op jit(solution)/shard_map/ppermute | solution.py:327
  28.9 1.0 %collective-permute-done.11 = f32[2,16,96]{2,1,0:T(8,128)S(1)} collective-permute-done((f32[2,16,96]{2,1,0:T(8,128)S(1)}, f32[2,16,96]{2,1,0:T(8,128)S(1)}, u32[]{:S(2)}, u32[]{:S(2)}) %collective-permute-start.11) | collective-permute-done | bytes 12320 | tf_op jit(solution)/shard_map/ppermute | solution.py:327
  30.5 0.8 %collective-permute-done.13.second_ref = f32[16,96]{1,0:T(8,128)S(1)} collective-permute-done((f32[16,96]{1,0:T(8,128)S(1)}, f32[16,96]{1,0:T(8,128)S(1)}, u32[]{:S(2)}, u32[]{:S(2)}) %collective-permute-start.13) | collective-permute-done | bytes 6176 | tf_op jit(solution)/shard_map/ppermute | solution.py:327
  31.3 0.9 %shard_map.60 = bf16[16,12,2,256]{3,2,1,0:T(2,128)(2,1)} custom-call(f32[16,96]{1,0:T(8,128)S(1)} %get-tuple-element.38.first_ref, f32[16,96]{1,0:T(8,128)S(1)} %collective-permute-done.13.second_ref, f32[16,96]{1,0:T(8,128)S(1)} %get-tuple-element.28.used_ref, bf16[12,48,256]{2,1,0:T(8,128)(2,1)S(1)} %shard_map.59.vectors_ref, ...), custom_call_target="tpu_custom_call" | custom-call | flops 10000000 | bytes 1000000 | tf_op jit(solution)/shard_map/pallas_call | solution.py:144
  (46 shorter events, 4.1 us)
Async XLA Ops:
  0.7 2.2 %copy-start.3 = (f32[1,9,2,2304]{3,2,1,0:T(2,128)S(1)}, f32[1,9,2,2304]{3,2,1,0:T(2,128)}, u32[]{:S(2)}) copy-start(f32[1,9,2,2304]{3,2,1,0:T(2,128)} %param.8) | copy-start | bytes 497668
  2.4 1.3 %collective-permute-start = (f32[16,96]{1,0:T(8,128)S(1)}, f32[16,96]{1,0:T(8,128)S(1)}, u32[]{:S(2)}, u32[]{:S(2)}) collective-permute-start(f32[16,96]{1,0:T(8,128)S(1)} %get-tuple-element.19), channel_id=1, source_target_pairs={{8,0},{9,1},{10,2},{11,3},{12,4},{13,5},{14,6},{15,7},{0,8},{1,9},... | collective-permute-start | bytes 18440 | tf_op jit(solution)/shard_map/ppermute | solution.py:327
  3.0 5.1 %collective-permute-start.2 = (f32[2,2,2304]{2,1,0:T(2,128)S(1)}, f32[2,2,2304]{2,1,0:T(2,128)S(1)}, u32[]{:S(2)}, u32[]{:S(2)}) collective-permute-start(f32[2,2,2304]{2,1,0:T(2,128)S(1)} %maximum_select_fusion.1), channel_id=1, source_target_pairs={{8,0},{9,1},{10,2},{11,3},{12,4},{13,5},{14,6},{15,7},{0,8},{1,9},... | collective-permute-start | bytes 110600 | tf_op jit(solution)/shard_map/ppermute | solution.py:327
  3.7 4.9 %collective-permute-start.3 = (f32[2,16,96]{2,1,0:T(8,128)S(1)}, f32[2,16,96]{2,1,0:T(8,128)S(1)}, u32[]{:S(2)}, u32[]{:S(2)}) collective-permute-start(f32[2,16,96]{2,1,0:T(8,128)S(1)} %pad_maximum_fusion.1), channel_id=1, source_target_pairs={{1,0},{0,1},{3,2},{2,3},{5,4},{4,5},{7,6},{6,7},{14,8},{15,9},{12,... | collective-permute-start | bytes 36872 | tf_op jit(solution)/shard_map/ppermute | solution.py:327
  6.5 3.7 %collective-permute-start.1 = (f32[2,16,96]{2,1,0:T(8,128)S(1)}, f32[2,16,96]{2,1,0:T(8,128)S(1)}, u32[]{:S(2)}, u32[]{:S(2)}) collective-permute-start(f32[2,16,96]{2,1,0:T(8,128)S(1)} %pad_maximum_fusion.1), channel_id=1, source_target_pairs={{16,0},{17,1},{18,2},{19,3},{20,4},{21,5},{22,6},{23,7},{10,8},{11... | collective-permute-start | bytes 36872 | tf_op jit(solution)/shard_map/ppermute | solution.py:327
  8.8 6.7 %copy-start.1 = (bf16[16,2,12,256]{3,1,2,0:T(2,128)(2,1)S(1)}, bf16[16,2,12,256]{3,1,2,0:T(2,128)(2,1)}, u32[]{:S(2)}) copy-start(bf16[16,2,12,256]{3,1,2,0:T(2,128)(2,1)} %param.5) | copy-start | bytes 589828
  10.5 1.7 %collective-permute-start.4 = (f32[2,16,96]{2,1,0:T(8,128)S(1)}, f32[2,16,96]{2,1,0:T(8,128)S(1)}, u32[]{:S(2)}, u32[]{:S(2)}) collective-permute-start(f32[2,16,96]{2,1,0:T(8,128)S(1)} %convolution_add_fusion.7), channel_id=1, source_target_pairs={{8,0},{9,1},{10,2},{11,3},{12,4},{13,5},{14,6},{15,7},{0,8},{1,9},... | collective-permute-start | bytes 36872 | tf_op jit(solution)/shard_map/ppermute | solution.py:327
  12.2 3.3 %copy-start.2 = (bf16[2,2,6,6,256]{4,1,3,2,0:T(2,128)(2,1)S(1)}, bf16[2,2,6,6,256]{4,1,3,2,0:T(2,128)(2,1)}, u32[]{:S(2)}) copy-start(bf16[2,2,6,6,256]{4,1,3,2,0:T(2,128)(2,1)} %param.7) | copy-start | bytes 221188
  12.2 3.9 %collective-permute-start.6 = (f32[2,16,96]{2,1,0:T(8,128)S(1)}, f32[2,16,96]{2,1,0:T(8,128)S(1)}, u32[]{:S(2)}, u32[]{:S(2)}) collective-permute-start(f32[2,16,96]{2,1,0:T(8,128)S(1)} %maximum_add_fusion), channel_id=1, source_target_pairs={{1,0},{0,1},{3,2},{2,3},{5,4},{4,5},{7,6},{6,7},{14,8},{15,9},{12,... | collective-permute-start | bytes 36872 | tf_op jit(solution)/shard_map/ppermute | solution.py:327
  13.8 3.7 %collective-permute-start.5 = (f32[2,16,96]{2,1,0:T(8,128)S(1)}, f32[2,16,96]{2,1,0:T(8,128)S(1)}, u32[]{:S(2)}, u32[]{:S(2)}) collective-permute-start(f32[2,16,96]{2,1,0:T(8,128)S(1)} %maximum_add_fusion), channel_id=1, source_target_pairs={{16,0},{17,1},{18,2},{19,3},{20,4},{21,5},{22,6},{23,7},{10,8},{11... | collective-permute-start | bytes 36872 | tf_op jit(solution)/shard_map/ppermute | solution.py:327
  16.1 5.4 %copy-start = (bf16[2,24,12,256]{3,1,2,0:T(8,128)(2,1)S(1)}, bf16[2,24,12,256]{3,1,2,0:T(8,128)(2,1)}, u32[]{:S(2)}) copy-start(bf16[2,24,12,256]{3,1,2,0:T(8,128)(2,1)} %param.6) | copy-start | bytes 884740
  17.7 1.2 %collective-permute-start.7 = (f32[2,16,96]{2,1,0:T(8,128)S(1)}, f32[2,16,96]{2,1,0:T(8,128)S(1)}, u32[]{:S(2)}, u32[]{:S(2)}) collective-permute-start(f32[2,16,96]{2,1,0:T(8,128)S(1)} %convolution_add_fusion.5), channel_id=1, source_target_pairs={{8,0},{9,1},{10,2},{11,3},{12,4},{13,5},{14,6},{15,7},{0,8},{1,9},... | collective-permute-start | bytes 36872 | tf_op jit(solution)/shard_map/ppermute | solution.py:327
  18.9 3.8 %collective-permute-start.9 = (f32[2,16,96]{2,1,0:T(8,128)S(1)}, f32[2,16,96]{2,1,0:T(8,128)S(1)}, u32[]{:S(2)}, u32[]{:S(2)}) collective-permute-start(f32[2,16,96]{2,1,0:T(8,128)S(1)} %maximum_add_fusion.1), channel_id=1, source_target_pairs={{1,0},{0,1},{3,2},{2,3},{5,4},{4,5},{7,6},{6,7},{14,8},{15,9},{12,... | collective-permute-start | bytes 36872 | tf_op jit(solution)/shard_map/ppermute | solution.py:327
  19.8 3.7 %collective-permute-start.8 = (f32[2,16,96]{2,1,0:T(8,128)S(1)}, f32[2,16,96]{2,1,0:T(8,128)S(1)}, u32[]{:S(2)}, u32[]{:S(2)}) collective-permute-start(f32[2,16,96]{2,1,0:T(8,128)S(1)} %maximum_add_fusion.1), channel_id=1, source_target_pairs={{16,0},{17,1},{18,2},{19,3},{20,4},{21,5},{22,6},{23,7},{10,8},{11... | collective-permute-start | bytes 36872 | tf_op jit(solution)/shard_map/ppermute | solution.py:327
  23.7 1.2 %collective-permute-start.10 = (f32[2,16,96]{2,1,0:T(8,128)S(1)}, f32[2,16,96]{2,1,0:T(8,128)S(1)}, u32[]{:S(2)}, u32[]{:S(2)}) collective-permute-start(f32[2,16,96]{2,1,0:T(8,128)S(1)} %convolution_add_fusion.3), channel_id=1, source_target_pairs={{8,0},{9,1},{10,2},{11,3},{12,4},{13,5},{14,6},{15,7},{0,8},{1,9},... | collective-permute-start | bytes 36872 | tf_op jit(solution)/shard_map/ppermute | solution.py:327
  25.0 3.8 %collective-permute-start.12 = (f32[2,16,96]{2,1,0:T(8,128)S(1)}, f32[2,16,96]{2,1,0:T(8,128)S(1)}, u32[]{:S(2)}, u32[]{:S(2)}) collective-permute-start(f32[2,16,96]{2,1,0:T(8,128)S(1)} %maximum_add_fusion.2), channel_id=1, source_target_pairs={{1,0},{0,1},{3,2},{2,3},{5,4},{4,5},{7,6},{6,7},{14,8},{15,9},{12,... | collective-permute-start | bytes 36872 | tf_op jit(solution)/shard_map/ppermute | solution.py:327
  26.2 3.7 %collective-permute-start.11 = (f32[2,16,96]{2,1,0:T(8,128)S(1)}, f32[2,16,96]{2,1,0:T(8,128)S(1)}, u32[]{:S(2)}, u32[]{:S(2)}) collective-permute-start(f32[2,16,96]{2,1,0:T(8,128)S(1)} %maximum_add_fusion.2), channel_id=1, source_target_pairs={{16,0},{17,1},{18,2},{19,3},{20,4},{21,5},{22,6},{23,7},{10,8},{11... | collective-permute-start | bytes 36872 | tf_op jit(solution)/shard_map/ppermute | solution.py:327
  30.1 1.2 %collective-permute-start.13 = (f32[16,96]{1,0:T(8,128)S(1)}, f32[16,96]{1,0:T(8,128)S(1)}, u32[]{:S(2)}, u32[]{:S(2)}) collective-permute-start(f32[16,96]{1,0:T(8,128)S(1)} %get-tuple-element.37), channel_id=1, source_target_pairs={{8,0},{9,1},{10,2},{11,3},{12,4},{13,5},{14,6},{15,7},{0,8},{1,9},... | collective-permute-start | bytes 18440 | tf_op jit(solution)/shard_map/ppermute | solution.py:327

commit v18 on v16

--- a/solution.py
+++ b/solution.py
@@ -55,30 +55,22 @@
     rhs, parts, _, sites = rows_ref.shape
     vecs = vectors_ref.shape[2]
     half = parts // 2
-    step = half // 2
-    copies = []
-    for piece in range(4):
-        span = pl.ds(step * piece, step)
-        copies.append(
-            [
-                pltpu.make_async_copy(rows_hbm.at[:, span], rows_ref.at[:, span], sems.at[2 * piece]),
-                pltpu.make_async_copy(vectors_hbm.at[:, span], vectors_ref.at[:, span], sems.at[2 * piece + 1]),
-            ]
-        )
-        for copy in copies[-1]:
-            copy.start()
-    for chi in range(2):
-        total = jnp.zeros((2 * rhs, 2 * vecs), jnp.float32)
-        for piece in (2 * chi, 2 * chi + 1):
-            for copy in copies[piece]:
-                copy.wait()
-            for c in range(step * piece, step * piece + step):
+    copies = [pltpu.make_async_copy(rows_hbm, rows_ref, sems.at[2])]
+    for part in range(2):
+        copies.append(pltpu.make_async_copy(vectors_hbm.at[part], vectors_ref.at[part], sems.at[part]))
+    for copy in copies:
+        copy.start()
+    copies[0].wait()
+    for part in range(2):
+        copies[1 + part].wait()
+        for chi in range(2):
+            total = jnp.zeros((2 * rhs, vecs), jnp.float32)
+            for c in range(half * chi, half * chi + half):
                 rows = rows_ref[:, c].reshape(2 * rhs, sites)
-                vectors = jnp.concatenate([vectors_ref[0, c], vectors_ref[1, c]], 0)
                 total += lax.dot_general(
-                    rows, vectors, (((1,), (1,)), ((), ())), preferred_element_type=jnp.float32
+                    rows, vectors_ref[part, c], (((1,), (1,)), ((), ())), preferred_element_type=jnp.float32
                 )
-        scratch[chi, :, : 2 * vecs] = total
+            scratch[chi, :, part * vecs : (part + 1) * vecs] = total
     real, imag = [], []
     for chi in range(2):
         even = scratch[chi, pl.ds(0, rhs, stride=2), :]
@@ -104,7 +96,7 @@
             pltpu.VMEM(rows.shape, rows.dtype),
             pltpu.VMEM(vectors.shape, vectors.dtype),
             pltpu.VMEM((2, 2 * rhs, 128), jnp.float32),
-            pltpu.SemaphoreType.DMA((8,)),
+            pltpu.SemaphoreType.DMA((3,)),
         ],
         compiler_params=pltpu.CompilerParams(vmem_limit_bytes=55168 * 2**10),
         cost_estimate=pl.CostEstimate(flops=10**7, bytes_accessed=5 * 10**5, transcendentals=0),

time: 32.3 us -> 32.4 us (level)
  no operation moved by 1% of the time
where the time goes in v18:
time: 32.4 us; the launch traced here: 32.2 us
  starting transfers between devices  15.3 us (47%)
  waiting for transfers between devices  10.1 us (31%)
  Pallas kernels  3.78 us (12%)
  matrix products  2 us (6%)
  between operations  0.8 us (2%)
    ppermute x14, starting transfers between devices, swap(): lax.ppermute(block, axes, [(source, i) for i, source in enumerate(sources)])  15.3 us
    ppermute x14, waiting for transfers between devices, swap(): lax.ppermute(block, axes, [(source, i) for i, source in enumerate(sources)])  10.1 us
    pallas_call x1, Pallas kernels, restrict(): pl.pallas_call(restrict_kernel, out_shape=[jax.ShapeDtypeStruct((rhs, 4 *...  1.67 us
    dot_general x8, matrix products, along(): lax.dot_general(moved[link], around[:, link], (((2,), (2,)), ((0,), (0,))...  1.32 us
    pallas_call x1, Pallas kernels, extend(): pl.pallas_call(extend_kernel, out_shape=jax.ShapeDtypeStruct(shape, jnp.b...  0.94 us
    dot_general x4, matrix products, apply(): lax.dot_general(vector, matrix, (((1,), (1,)), ((), ())), precision=preci...  0.68 us
  transfers between devices with their start and end apart: 14, of which 11 were waited for; matrix products, arithmetic and copies ran while one was open for 5% of the time, Pallas kernels for 4%

profile of v18, /device:TPU:0, one launch (start us, length us, event | category | flops | bytes accessed | tf_op | source)
XLA Modules:
  0.0 32.2 jit_solution(4098733975238872616)
XLA Ops:
  0.7 1.7 %shard_map.55 = (f32[16,96]{1,0:T(8,128)S(1)}, f32[16,96]{1,0:T(8,128)S(1)}) custom-call(s32[1]{0:T(128)S(6)} %copy.6.count_ref, bf16[16,12,2,256]{3,2,1,0:T(2,128)(2,1)} %bitcast.70, bf16[2,12,24,256]{3,2,1,0:T(8,128)(2,1)} %bitcast.68), custom_call_target="tpu_custom_call" | custom-call | flops 10000000 | bytes 500000 | tf_op jit(solution)/shard_map/pallas_call | solution.py:90
  2.3 0.5 %collective-permute-start = (f32[16,96]{1,0:T(8,128)S(1)}, f32[16,96]{1,0:T(8,128)S(1)}, u32[]{:S(2)}, u32[]{:S(2)}) collective-permute-start(f32[16,96]{1,0:T(8,128)S(1)} %get-tuple-element.19), channel_id=1, source_target_pairs={{8,0},{9,1},{10,2},{11,3},{12,4},{13,5},{14,6},{15,7},{0,8},{1,9},... | collective-permute-start | bytes 18440 | tf_op jit(solution)/shard_map/ppermute | solution.py:322
  3.7 2.8 %collective-permute-start.3 = (f32[2,16,96]{2,1,0:T(8,128)S(1)}, f32[2,16,96]{2,1,0:T(8,128)S(1)}, u32[]{:S(2)}, u32[]{:S(2)}) collective-permute-start(f32[2,16,96]{2,1,0:T(8,128)S(1)} %pad_maximum_fusion.1), channel_id=1, source_target_pairs={{1,0},{0,1},{3,2},{2,3},{5,4},{4,5},{7,6},{6,7},{14,8},{15,9},{12,... | collective-permute-start | bytes 36872 | tf_op jit(solution)/shard_map/ppermute | solution.py:322
  6.5 1.5 %collective-permute-start.1 = (f32[2,16,96]{2,1,0:T(8,128)S(1)}, f32[2,16,96]{2,1,0:T(8,128)S(1)}, u32[]{:S(2)}, u32[]{:S(2)}) collective-permute-start(f32[2,16,96]{2,1,0:T(8,128)S(1)} %pad_maximum_fusion.1), channel_id=1, source_target_pairs={{16,0},{17,1},{18,2},{19,3},{20,4},{21,5},{22,6},{23,7},{10,8},{11... | collective-permute-start | bytes 36872 | tf_op jit(solution)/shard_map/ppermute | solution.py:322
  8.8 1.5 %collective-permute-done.1 = f32[2,16,96]{2,1,0:T(8,128)S(1)} collective-permute-done((f32[2,16,96]{2,1,0:T(8,128)S(1)}, f32[2,16,96]{2,1,0:T(8,128)S(1)}, u32[]{:S(2)}, u32[]{:S(2)}) %collective-permute-start.1) | collective-permute-done | bytes 12320 | tf_op jit(solution)/shard_map/ppermute | solution.py:322
  10.4 0.9 %collective-permute-start.4 = (f32[2,16,96]{2,1,0:T(8,128)S(1)}, f32[2,16,96]{2,1,0:T(8,128)S(1)}, u32[]{:S(2)}, u32[]{:S(2)}) collective-permute-start(f32[2,16,96]{2,1,0:T(8,128)S(1)} %convolution_add_fusion.7), channel_id=1, source_target_pairs={{8,0},{9,1},{10,2},{11,3},{12,4},{13,5},{14,6},{15,7},{0,8},{1,9},... | collective-permute-start | bytes 36872 | tf_op jit(solution)/shard_map/ppermute | solution.py:322
  11.3 0.8 %collective-permute-done.4 = f32[2,16,96]{2,1,0:T(8,128)S(1)} collective-permute-done((f32[2,16,96]{2,1,0:T(8,128)S(1)}, f32[2,16,96]{2,1,0:T(8,128)S(1)}, u32[]{:S(2)}, u32[]{:S(2)}) %collective-permute-start.4) | collective-permute-done | bytes 12320 | tf_op jit(solution)/shard_map/ppermute | solution.py:322
  12.2 1.6 %collective-permute-start.6 = (f32[2,16,96]{2,1,0:T(8,128)S(1)}, f32[2,16,96]{2,1,0:T(8,128)S(1)}, u32[]{:S(2)}, u32[]{:S(2)}) collective-permute-start(f32[2,16,96]{2,1,0:T(8,128)S(1)} %maximum_add_fusion), channel_id=1, source_target_pairs={{1,0},{0,1},{3,2},{2,3},{5,4},{4,5},{7,6},{6,7},{14,8},{15,9},{12,... | collective-permute-start | bytes 36872 | tf_op jit(solution)/shard_map/ppermute | solution.py:322
  13.7 1.5 %collective-permute-start.5 = (f32[2,16,96]{2,1,0:T(8,128)S(1)}, f32[2,16,96]{2,1,0:T(8,128)S(1)}, u32[]{:S(2)}, u32[]{:S(2)}) collective-permute-start(f32[2,16,96]{2,1,0:T(8,128)S(1)} %maximum_add_fusion), channel_id=1, source_target_pairs={{16,0},{17,1},{18,2},{19,3},{20,4},{21,5},{22,6},{23,7},{10,8},{11... | collective-permute-start | bytes 36872 | tf_op jit(solution)/shard_map/ppermute | solution.py:322
  15.5 0.6 %shard_map.58.local_ref = f32[12,32,256]{2,1,0:T(8,128)S(1)} custom-call(bf16[16,12,2,256]{3,2,1,0:T(2,128)(2,1)S(1)} %bitcast.71, bf16[2,6,6,2,256]{4,3,2,1,0:T(2,128)(2,1)S(1)} %bitcast.73), custom_call_target="tpu_custom_call" | custom-call | flops 100000 | bytes 100000 | tf_op jit(solution)/shard_map/pallas_call | solution.py:198
  16.3 1.2 %collective-permute-done.5 = f32[2,16,96]{2,1,0:T(8,128)S(1)} collective-permute-done((f32[2,16,96]{2,1,0:T(8,128)S(1)}, f32[2,16,96]{2,1,0:T(8,128)S(1)}, u32[]{:S(2)}, u32[]{:S(2)}) %collective-permute-start.5) | collective-permute-done | bytes 12320 | tf_op jit(solution)/shard_map/ppermute | solution.py:322
  17.6 0.4 %collective-permute-start.7 = (f32[2,16,96]{2,1,0:T(8,128)S(1)}, f32[2,16,96]{2,1,0:T(8,128)S(1)}, u32[]{:S(2)}, u32[]{:S(2)}) collective-permute-start(f32[2,16,96]{2,1,0:T(8,128)S(1)} %convolution_add_fusion.5), channel_id=1, source_target_pairs={{8,0},{9,1},{10,2},{11,3},{12,4},{13,5},{14,6},{15,7},{0,8},{1,9},... | collective-permute-start | bytes 36872 | tf_op jit(solution)/shard_map/ppermute | solution.py:322
  18.0 0.8 %collective-permute-done.7 = f32[2,16,96]{2,1,0:T(8,128)S(1)} collective-permute-done((f32[2,16,96]{2,1,0:T(8,128)S(1)}, f32[2,16,96]{2,1,0:T(8,128)S(1)}, u32[]{:S(2)}, u32[]{:S(2)}) %collective-permute-start.7) | collective-permute-done | bytes 12320 | tf_op jit(solution)/shard_map/ppermute | solution.py:322
  18.9 0.9 %collective-permute-start.9 = (f32[2,16,96]{2,1,0:T(8,128)S(1)}, f32[2,16,96]{2,1,0:T(8,128)S(1)}, u32[]{:S(2)}, u32[]{:S(2)}) collective-permute-start(f32[2,16,96]{2,1,0:T(8,128)S(1)} %maximum_add_fusion.1), channel_id=1, source_target_pairs={{1,0},{0,1},{3,2},{2,3},{5,4},{4,5},{7,6},{6,7},{14,8},{15,9},{12,... | collective-permute-start | bytes 36872 | tf_op jit(solution)/shard_map/ppermute | solution.py:322
  19.8 1.5 %collective-permute-start.8 = (f32[2,16,96]{2,1,0:T(8,128)S(1)}, f32[2,16,96]{2,1,0:T(8,128)S(1)}, u32[]{:S(2)}, u32[]{:S(2)}) collective-permute-start(f32[2,16,96]{2,1,0:T(8,128)S(1)} %maximum_add_fusion.1), channel_id=1, source_target_pairs={{16,0},{17,1},{18,2},{19,3},{20,4},{21,5},{22,6},{23,7},{10,8},{11... | collective-permute-start | bytes 36872 | tf_op jit(solution)/shard_map/ppermute | solution.py:322
  21.6 1.1 %collective-permute-done.9 = f32[2,16,96]{2,1,0:T(8,128)S(1)} collective-permute-done((f32[2,16,96]{2,1,0:T(8,128)S(1)}, f32[2,16,96]{2,1,0:T(8,128)S(1)}, u32[]{:S(2)}, u32[]{:S(2)}) %collective-permute-start.9) | collective-permute-done | bytes 12320 | tf_op jit(solution)/shard_map/ppermute | solution.py:322
  22.8 0.7 %collective-permute-done.8 = f32[2,16,96]{2,1,0:T(8,128)S(1)} collective-permute-done((f32[2,16,96]{2,1,0:T(8,128)S(1)}, f32[2,16,96]{2,1,0:T(8,128)S(1)}, u32[]{:S(2)}, u32[]{:S(2)}) %collective-permute-start.8) | collective-permute-done | bytes 12320 | tf_op jit(solution)/shard_map/ppermute | solution.py:322
  24.1 0.8 %collective-permute-done.10 = f32[2,16,96]{2,1,0:T(8,128)S(1)} collective-permute-done((f32[2,16,96]{2,1,0:T(8,128)S(1)}, f32[2,16,96]{2,1,0:T(8,128)S(1)}, u32[]{:S(2)}, u32[]{:S(2)}) %collective-permute-start.10) | collective-permute-done | bytes 12320 | tf_op jit(solution)/shard_map/ppermute | solution.py:322
  24.9 1.2 %collective-permute-start.12 = (f32[2,16,96]{2,1,0:T(8,128)S(1)}, f32[2,16,96]{2,1,0:T(8,128)S(1)}, u32[]{:S(2)}, u32[]{:S(2)}) collective-permute-start(f32[2,16,96]{2,1,0:T(8,128)S(1)} %maximum_add_fusion.2), channel_id=1, source_target_pairs={{1,0},{0,1},{3,2},{2,3},{5,4},{4,5},{7,6},{6,7},{14,8},{15,9},{12,... | collective-permute-start | bytes 36872 | tf_op jit(solution)/shard_map/ppermute | solution.py:322
  26.2 1.5 %collective-permute-start.11 = (f32[2,16,96]{2,1,0:T(8,128)S(1)}, f32[2,16,96]{2,1,0:T(8,128)S(1)}, u32[]{:S(2)}, u32[]{:S(2)}) collective-permute-start(f32[2,16,96]{2,1,0:T(8,128)S(1)} %maximum_add_fusion.2), channel_id=1, source_target_pairs={{16,0},{17,1},{18,2},{19,3},{20,4},{21,5},{22,6},{23,7},{10,8},{11... | collective-permute-start | bytes 36872 | tf_op jit(solution)/shard_map/ppermute | solution.py:322
  27.9 0.9 %collective-permute-done.12 = f32[2,16,96]{2,1,0:T(8,128)S(1)} collective-permute-done((f32[2,16,96]{2,1,0:T(8,128)S(1)}, f32[2,16,96]{2,1,0:T(8,128)S(1)}, u32[]{:S(2)}, u32[]{:S(2)}) %collective-permute-start.12) | collective-permute-done | bytes 12320 | tf_op jit(solution)/shard_map/ppermute | solution.py:322
  28.9 1.0 %collective-permute-done.11 = f32[2,16,96]{2,1,0:T(8,128)S(1)} collective-permute-done((f32[2,16,96]{2,1,0:T(8,128)S(1)}, f32[2,16,96]{2,1,0:T(8,128)S(1)}, u32[]{:S(2)}, u32[]{:S(2)}) %collective-permute-start.11) | collective-permute-done | bytes 12320 | tf_op jit(solution)/shard_map/ppermute | solution.py:322
  30.5 0.8 %collective-permute-done.13.second_ref = f32[16,96]{1,0:T(8,128)S(1)} collective-permute-done((f32[16,96]{1,0:T(8,128)S(1)}, f32[16,96]{1,0:T(8,128)S(1)}, u32[]{:S(2)}, u32[]{:S(2)}) %collective-permute-start.13) | collective-permute-done | bytes 6176 | tf_op jit(solution)/shard_map/ppermute | solution.py:322
  31.3 0.9 %shard_map.60 = bf16[16,12,2,256]{3,2,1,0:T(2,128)(2,1)} custom-call(f32[16,96]{1,0:T(8,128)S(1)} %get-tuple-element.38.first_ref, f32[16,96]{1,0:T(8,128)S(1)} %collective-permute-done.13.second_ref, f32[16,96]{1,0:T(8,128)S(1)} %get-tuple-element.28.used_ref, bf16[12,48,256]{2,1,0:T(8,128)(2,1)S(1)} %shard_map.59.vectors_ref, ...), custom_call_target="tpu_custom_call" | custom-call | flops 10000000 | bytes 1000000 | tf_op jit(solution)/shard_map/pallas_call | solution.py:139
  (46 shorter events, 4.1 us)
Async XLA Ops:
  0.7 2.2 %copy-start.3 = (f32[1,9,2,2304]{3,2,1,0:T(2,128)S(1)}, f32[1,9,2,2304]{3,2,1,0:T(2,128)}, u32[]{:S(2)}) copy-start(f32[1,9,2,2304]{3,2,1,0:T(2,128)} %param.8) | copy-start | bytes 497668
  2.3 1.3 %collective-permute-start = (f32[16,96]{1,0:T(8,128)S(1)}, f32[16,96]{1,0:T(8,128)S(1)}, u32[]{:S(2)}, u32[]{:S(2)}) collective-permute-start(f32[16,96]{1,0:T(8,128)S(1)} %get-tuple-element.19), channel_id=1, source_target_pairs={{8,0},{9,1},{10,2},{11,3},{12,4},{13,5},{14,6},{15,7},{0,8},{1,9},... | collective-permute-start | bytes 18440 | tf_op jit(solution)/shard_map/ppermute | solution.py:322
  3.0 5.1 %collective-permute-start.2 = (f32[2,2,2304]{2,1,0:T(2,128)S(1)}, f32[2,2,2304]{2,1,0:T(2,128)S(1)}, u32[]{:S(2)}, u32[]{:S(2)}) collective-permute-start(f32[2,2,2304]{2,1,0:T(2,128)S(1)} %maximum_select_fusion.1), channel_id=1, source_target_pairs={{8,0},{9,1},{10,2},{11,3},{12,4},{13,5},{14,6},{15,7},{0,8},{1,9},... | collective-permute-start | bytes 110600 | tf_op jit(solution)/shard_map/ppermute | solution.py:322
  3.7 4.9 %collective-permute-start.3 = (f32[2,16,96]{2,1,0:T(8,128)S(1)}, f32[2,16,96]{2,1,0:T(8,128)S(1)}, u32[]{:S(2)}, u32[]{:S(2)}) collective-permute-start(f32[2,16,96]{2,1,0:T(8,128)S(1)} %pad_maximum_fusion.1), channel_id=1, source_target_pairs={{1,0},{0,1},{3,2},{2,3},{5,4},{4,5},{7,6},{6,7},{14,8},{15,9},{12,... | collective-permute-start | bytes 36872 | tf_op jit(solution)/shard_map/ppermute | solution.py:322
  6.5 3.7 %collective-permute-start.1 = (f32[2,16,96]{2,1,0:T(8,128)S(1)}, f32[2,16,96]{2,1,0:T(8,128)S(1)}, u32[]{:S(2)}, u32[]{:S(2)}) collective-permute-start(f32[2,16,96]{2,1,0:T(8,128)S(1)} %pad_maximum_fusion.1), channel_id=1, source_target_pairs={{16,0},{17,1},{18,2},{19,3},{20,4},{21,5},{22,6},{23,7},{10,8},{11... | collective-permute-start | bytes 36872 | tf_op jit(solution)/shard_map/ppermute | solution.py:322
  8.7 6.7 %copy-start.1 = (bf16[16,2,12,256]{3,1,2,0:T(2,128)(2,1)S(1)}, bf16[16,2,12,256]{3,1,2,0:T(2,128)(2,1)}, u32[]{:S(2)}) copy-start(bf16[16,2,12,256]{3,1,2,0:T(2,128)(2,1)} %param.5) | copy-start | bytes 589828
  10.4 1.7 %collective-permute-start.4 = (f32[2,16,96]{2,1,0:T(8,128)S(1)}, f32[2,16,96]{2,1,0:T(8,128)S(1)}, u32[]{:S(2)}, u32[]{:S(2)}) collective-permute-start(f32[2,16,96]{2,1,0:T(8,128)S(1)} %convolution_add_fusion.7), channel_id=1, source_target_pairs={{8,0},{9,1},{10,2},{11,3},{12,4},{13,5},{14,6},{15,7},{0,8},{1,9},... | collective-permute-start | bytes 36872 | tf_op jit(solution)/shard_map/ppermute | solution.py:322
  12.2 3.3 %copy-start.2 = (bf16[2,2,6,6,256]{4,1,3,2,0:T(2,128)(2,1)S(1)}, bf16[2,2,6,6,256]{4,1,3,2,0:T(2,128)(2,1)}, u32[]{:S(2)}) copy-start(bf16[2,2,6,6,256]{4,1,3,2,0:T(2,128)(2,1)} %param.7) | copy-start | bytes 221188
  12.2 3.9 %collective-permute-start.6 = (f32[2,16,96]{2,1,0:T(8,128)S(1)}, f32[2,16,96]{2,1,0:T(8,128)S(1)}, u32[]{:S(2)}, u32[]{:S(2)}) collective-permute-start(f32[2,16,96]{2,1,0:T(8,128)S(1)} %maximum_add_fusion), channel_id=1, source_target_pairs={{1,0},{0,1},{3,2},{2,3},{5,4},{4,5},{7,6},{6,7},{14,8},{15,9},{12,... | collective-permute-start | bytes 36872 | tf_op jit(solution)/shard_map/ppermute | solution.py:322
  13.7 3.7 %collective-permute-start.5 = (f32[2,16,96]{2,1,0:T(8,128)S(1)}, f32[2,16,96]{2,1,0:T(8,128)S(1)}, u32[]{:S(2)}, u32[]{:S(2)}) collective-permute-start(f32[2,16,96]{2,1,0:T(8,128)S(1)} %maximum_add_fusion), channel_id=1, source_target_pairs={{16,0},{17,1},{18,2},{19,3},{20,4},{21,5},{22,6},{23,7},{10,8},{11... | collective-permute-start | bytes 36872 | tf_op jit(solution)/shard_map/ppermute | solution.py:322
  16.1 5.4 %copy-start = (bf16[2,24,12,256]{3,1,2,0:T(8,128)(2,1)S(1)}, bf16[2,24,12,256]{3,1,2,0:T(8,128)(2,1)}, u32[]{:S(2)}) copy-start(bf16[2,24,12,256]{3,1,2,0:T(8,128)(2,1)} %param.6) | copy-start | bytes 884740
  17.6 1.2 %collective-permute-start.7 = (f32[2,16,96]{2,1,0:T(8,128)S(1)}, f32[2,16,96]{2,1,0:T(8,128)S(1)}, u32[]{:S(2)}, u32[]{:S(2)}) collective-permute-start(f32[2,16,96]{2,1,0:T(8,128)S(1)} %convolution_add_fusion.5), channel_id=1, source_target_pairs={{8,0},{9,1},{10,2},{11,3},{12,4},{13,5},{14,6},{15,7},{0,8},{1,9},... | collective-permute-start | bytes 36872 | tf_op jit(solution)/shard_map/ppermute | solution.py:322
  18.9 3.8 %collective-permute-start.9 = (f32[2,16,96]{2,1,0:T(8,128)S(1)}, f32[2,16,96]{2,1,0:T(8,128)S(1)}, u32[]{:S(2)}, u32[]{:S(2)}) collective-permute-start(f32[2,16,96]{2,1,0:T(8,128)S(1)} %maximum_add_fusion.1), channel_id=1, source_target_pairs={{1,0},{0,1},{3,2},{2,3},{5,4},{4,5},{7,6},{6,7},{14,8},{15,9},{12,... | collective-permute-start | bytes 36872 | tf_op jit(solution)/shard_map/ppermute | solution.py:322
  19.8 3.7 %collective-permute-start.8 = (f32[2,16,96]{2,1,0:T(8,128)S(1)}, f32[2,16,96]{2,1,0:T(8,128)S(1)}, u32[]{:S(2)}, u32[]{:S(2)}) collective-permute-start(f32[2,16,96]{2,1,0:T(8,128)S(1)} %maximum_add_fusion.1), channel_id=1, source_target_pairs={{16,0},{17,1},{18,2},{19,3},{20,4},{21,5},{22,6},{23,7},{10,8},{11... | collective-permute-start | bytes 36872 | tf_op jit(solution)/shard_map/ppermute | solution.py:322
  23.7 1.2 %collective-permute-start.10 = (f32[2,16,96]{2,1,0:T(8,128)S(1)}, f32[2,16,96]{2,1,0:T(8,128)S(1)}, u32[]{:S(2)}, u32[]{:S(2)}) collective-permute-start(f32[2,16,96]{2,1,0:T(8,128)S(1)} %convolution_add_fusion.3), channel_id=1, source_target_pairs={{8,0},{9,1},{10,2},{11,3},{12,4},{13,5},{14,6},{15,7},{0,8},{1,9},... | collective-permute-start | bytes 36872 | tf_op jit(solution)/shard_map/ppermute | solution.py:322
  24.9 3.8 %collective-permute-start.12 = (f32[2,16,96]{2,1,0:T(8,128)S(1)}, f32[2,16,96]{2,1,0:T(8,128)S(1)}, u32[]{:S(2)}, u32[]{:S(2)}) collective-permute-start(f32[2,16,96]{2,1,0:T(8,128)S(1)} %maximum_add_fusion.2), channel_id=1, source_target_pairs={{1,0},{0,1},{3,2},{2,3},{5,4},{4,5},{7,6},{6,7},{14,8},{15,9},{12,... | collective-permute-start | bytes 36872 | tf_op jit(solution)/shard_map/ppermute | solution.py:322
  26.2 3.7 %collective-permute-start.11 = (f32[2,16,96]{2,1,0:T(8,128)S(1)}, f32[2,16,96]{2,1,0:T(8,128)S(1)}, u32[]{:S(2)}, u32[]{:S(2)}) collective-permute-start(f32[2,16,96]{2,1,0:T(8,128)S(1)} %maximum_add_fusion.2), channel_id=1, source_target_pairs={{16,0},{17,1},{18,2},{19,3},{20,4},{21,5},{22,6},{23,7},{10,8},{11... | collective-permute-start | bytes 36872 | tf_op jit(solution)/shard_map/ppermute | solution.py:322
  30.1 1.2 %collective-permute-start.13 = (f32[16,96]{1,0:T(8,128)S(1)}, f32[16,96]{1,0:T(8,128)S(1)}, u32[]{:S(2)}, u32[]{:S(2)}) collective-permute-start(f32[16,96]{1,0:T(8,128)S(1)} %get-tuple-element.37), channel_id=1, source_target_pairs={{8,0},{9,1},{10,2},{11,3},{12,4},{13,5},{14,6},{15,7},{0,8},{1,9},... | collective-permute-start | bytes 18440 | tf_op jit(solution)/shard_map/ppermute | solution.py:322

commit v19 on v17

--- a/solution.py
+++ b/solution.py
@@ -69,13 +69,14 @@
     for chi in range(2):
         for copy in copies[chi]:
             copy.wait()
-        span = range(half * chi, half * chi + half)
-        rows = jnp.concatenate([rows_ref[:, c].reshape(2 * rhs, sites) for c in span], 1)
-        for part in range(2):
-            vectors = jnp.concatenate([vectors_ref[part, c] for c in span], 1)
-            scratch[chi, :, part * vecs : (part + 1) * vecs] = lax.dot_general(
+        total = jnp.zeros((2 * rhs, 2 * vecs), jnp.float32)
+        for c in range(half * chi, half * chi + half):
+            rows = rows_ref[:, c].reshape(2 * rhs, sites)
+            vectors = jnp.concatenate([vectors_ref[0, c], vectors_ref[1, c]], 0)
+            total += lax.dot_general(
                 rows, vectors, (((1,), (1,)), ((), ())), preferred_element_type=jnp.float32
             )
+        scratch[chi, :, : 2 * vecs] = total
     real, imag = [], []
     for chi in range(2):
         even = scratch[chi, pl.ds(0, rhs, stride=2), :]

time: 32.4 us -> 32.3 us (level)
  no operation moved by 1% of the time
where the time goes in v19:
time: 32.3 us; the launch traced here: 32.1 us
  starting transfers between devices  15.3 us (47%)
  waiting for transfers between devices  10.1 us (31%)
  Pallas kernels  3.69 us (11%)
  matrix products  2 us (6%)
  between operations  0.8 us (2%)
    ppermute x14, starting transfers between devices, swap(): lax.ppermute(block, axes, [(source, i) for i, source in enumerate(sources)])  15.3 us
    ppermute x14, waiting for transfers between devices, swap(): lax.ppermute(block, axes, [(source, i) for i, source in enumerate(sources)])  10.1 us
    pallas_call x1, Pallas kernels, restrict(): pl.pallas_call(restrict_kernel, out_shape=[jax.ShapeDtypeStruct((rhs, 4 *...  1.58 us
    dot_general x8, matrix products, along(): lax.dot_general(moved[link], around[:, link], (((2,), (2,)), ((0,), (0,))...  1.32 us
    pallas_call x1, Pallas kernels, extend(): pl.pallas_call(extend_kernel, out_shape=jax.ShapeDtypeStruct(shape, jnp.b...  0.94 us
    dot_general x4, matrix products, apply(): lax.dot_general(vector, matrix, (((1,), (1,)), ((), ())), precision=preci...  0.68 us
  transfers between devices with their start and end apart: 14, of which 11 were waited for; matrix products, arithmetic and copies ran while one was open for 5% of the time, Pallas kernels for 4%

profile of v19, /device:TPU:0, one launch (start us, length us, event | category | flops | bytes accessed | tf_op | source)
XLA Modules:
  0.0 32.1 jit_solution(13130814297617850786)
XLA Ops:
  0.7 1.6 %shard_map.55 = (f32[16,96]{1,0:T(8,128)S(1)}, f32[16,96]{1,0:T(8,128)S(1)}) custom-call(s32[1]{0:T(128)S(6)} %copy.6.count_ref, bf16[16,12,2,256]{3,2,1,0:T(2,128)(2,1)} %bitcast.70, bf16[2,12,24,256]{3,2,1,0:T(8,128)(2,1)} %bitcast.68), custom_call_target="tpu_custom_call" | custom-call | flops 10000000 | bytes 500000 | tf_op jit(solution)/shard_map/pallas_call | solution.py:96
  2.2 0.5 %collective-permute-start = (f32[16,96]{1,0:T(8,128)S(1)}, f32[16,96]{1,0:T(8,128)S(1)}, u32[]{:S(2)}, u32[]{:S(2)}) collective-permute-start(f32[16,96]{1,0:T(8,128)S(1)} %get-tuple-element.19), channel_id=1, source_target_pairs={{8,0},{9,1},{10,2},{11,3},{12,4},{13,5},{14,6},{15,7},{0,8},{1,9},... | collective-permute-start | bytes 18440 | tf_op jit(solution)/shard_map/ppermute | solution.py:328
  3.6 2.8 %collective-permute-start.3 = (f32[2,16,96]{2,1,0:T(8,128)S(1)}, f32[2,16,96]{2,1,0:T(8,128)S(1)}, u32[]{:S(2)}, u32[]{:S(2)}) collective-permute-start(f32[2,16,96]{2,1,0:T(8,128)S(1)} %pad_maximum_fusion.1), channel_id=1, source_target_pairs={{1,0},{0,1},{3,2},{2,3},{5,4},{4,5},{7,6},{6,7},{14,8},{15,9},{12,... | collective-permute-start | bytes 36872 | tf_op jit(solution)/shard_map/ppermute | solution.py:328
  6.4 1.5 %collective-permute-start.1 = (f32[2,16,96]{2,1,0:T(8,128)S(1)}, f32[2,16,96]{2,1,0:T(8,128)S(1)}, u32[]{:S(2)}, u32[]{:S(2)}) collective-permute-start(f32[2,16,96]{2,1,0:T(8,128)S(1)} %pad_maximum_fusion.1), channel_id=1, source_target_pairs={{16,0},{17,1},{18,2},{19,3},{20,4},{21,5},{22,6},{23,7},{10,8},{11... | collective-permute-start | bytes 36872 | tf_op jit(solution)/shard_map/ppermute | solution.py:328
  8.7 1.5 %collective-permute-done.1 = f32[2,16,96]{2,1,0:T(8,128)S(1)} collective-permute-done((f32[2,16,96]{2,1,0:T(8,128)S(1)}, f32[2,16,96]{2,1,0:T(8,128)S(1)}, u32[]{:S(2)}, u32[]{:S(2)}) %collective-permute-start.1) | collective-permute-done | bytes 12320 | tf_op jit(solution)/shard_map/ppermute | solution.py:328
  10.3 0.9 %collective-permute-start.4 = (f32[2,16,96]{2,1,0:T(8,128)S(1)}, f32[2,16,96]{2,1,0:T(8,128)S(1)}, u32[]{:S(2)}, u32[]{:S(2)}) collective-permute-start(f32[2,16,96]{2,1,0:T(8,128)S(1)} %convolution_add_fusion.7), channel_id=1, source_target_pairs={{8,0},{9,1},{10,2},{11,3},{12,4},{13,5},{14,6},{15,7},{0,8},{1,9},... | collective-permute-start | bytes 36872 | tf_op jit(solution)/shard_map/ppermute | solution.py:328
  11.2 0.8 %collective-permute-done.4 = f32[2,16,96]{2,1,0:T(8,128)S(1)} collective-permute-done((f32[2,16,96]{2,1,0:T(8,128)S(1)}, f32[2,16,96]{2,1,0:T(8,128)S(1)}, u32[]{:S(2)}, u32[]{:S(2)}) %collective-permute-start.4) | collective-permute-done | bytes 12320 | tf_op jit(solution)/shard_map/ppermute | solution.py:328
  12.1 1.6 %collective-permute-start.6 = (f32[2,16,96]{2,1,0:T(8,128)S(1)}, f32[2,16,96]{2,1,0:T(8,128)S(1)}, u32[]{:S(2)}, u32[]{:S(2)}) collective-permute-start(f32[2,16,96]{2,1,0:T(8,128)S(1)} %maximum_add_fusion), channel_id=1, source_target_pairs={{1,0},{0,1},{3,2},{2,3},{5,4},{4,5},{7,6},{6,7},{14,8},{15,9},{12,... | collective-permute-start | bytes 36872 | tf_op jit(solution)/shard_map/ppermute | solution.py:328
  13.6 1.5 %collective-permute-start.5 = (f32[2,16,96]{2,1,0:T(8,128)S(1)}, f32[2,16,96]{2,1,0:T(8,128)S(1)}, u32[]{:S(2)}, u32[]{:S(2)}) collective-permute-start(f32[2,16,96]{2,1,0:T(8,128)S(1)} %maximum_add_fusion), channel_id=1, source_target_pairs={{16,0},{17,1},{18,2},{19,3},{20,4},{21,5},{22,6},{23,7},{10,8},{11... | collective-permute-start | bytes 36872 | tf_op jit(solution)/shard_map/ppermute | solution.py:328
  15.4 0.6 %shard_map.58.local_ref = f32[12,32,256]{2,1,0:T(8,128)S(1)} custom-call(bf16[16,12,2,256]{3,2,1,0:T(2,128)(2,1)S(1)} %bitcast.71, bf16[2,6,6,2,256]{4,3,2,1,0:T(2,128)(2,1)S(1)} %bitcast.73), custom_call_target="tpu_custom_call" | custom-call | flops 100000 | bytes 100000 | tf_op jit(solution)/shard_map/pallas_call | solution.py:204
  16.2 1.2 %collective-permute-done.5 = f32[2,16,96]{2,1,0:T(8,128)S(1)} collective-permute-done((f32[2,16,96]{2,1,0:T(8,128)S(1)}, f32[2,16,96]{2,1,0:T(8,128)S(1)}, u32[]{:S(2)}, u32[]{:S(2)}) %collective-permute-start.5) | collective-permute-done | bytes 12320 | tf_op jit(solution)/shard_map/ppermute | solution.py:328
  17.5 0.4 %collective-permute-start.7 = (f32[2,16,96]{2,1,0:T(8,128)S(1)}, f32[2,16,96]{2,1,0:T(8,128)S(1)}, u32[]{:S(2)}, u32[]{:S(2)}) collective-permute-start(f32[2,16,96]{2,1,0:T(8,128)S(1)} %convolution_add_fusion.5), channel_id=1, source_target_pairs={{8,0},{9,1},{10,2},{11,3},{12,4},{13,5},{14,6},{15,7},{0,8},{1,9},... | collective-permute-start | bytes 36872 | tf_op jit(solution)/shard_map/ppermute | solution.py:328
  17.9 0.8 %collective-permute-done.7 = f32[2,16,96]{2,1,0:T(8,128)S(1)} collective-permute-done((f32[2,16,96]{2,1,0:T(8,128)S(1)}, f32[2,16,96]{2,1,0:T(8,128)S(1)}, u32[]{:S(2)}, u32[]{:S(2)}) %collective-permute-start.7) | collective-permute-done | bytes 12320 | tf_op jit(solution)/shard_map/ppermute | solution.py:328
  18.8 0.9 %collective-permute-start.9 = (f32[2,16,96]{2,1,0:T(8,128)S(1)}, f32[2,16,96]{2,1,0:T(8,128)S(1)}, u32[]{:S(2)}, u32[]{:S(2)}) collective-permute-start(f32[2,16,96]{2,1,0:T(8,128)S(1)} %maximum_add_fusion.1), channel_id=1, source_target_pairs={{1,0},{0,1},{3,2},{2,3},{5,4},{4,5},{7,6},{6,7},{14,8},{15,9},{12,... | collective-permute-start | bytes 36872 | tf_op jit(solution)/shard_map/ppermute | solution.py:328
  19.7 1.5 %collective-permute-start.8 = (f32[2,16,96]{2,1,0:T(8,128)S(1)}, f32[2,16,96]{2,1,0:T(8,128)S(1)}, u32[]{:S(2)}, u32[]{:S(2)}) collective-permute-start(f32[2,16,96]{2,1,0:T(8,128)S(1)} %maximum_add_fusion.1), channel_id=1, source_target_pairs={{16,0},{17,1},{18,2},{19,3},{20,4},{21,5},{22,6},{23,7},{10,8},{11... | collective-permute-start | bytes 36872 | tf_op jit(solution)/shard_map/ppermute | solution.py:328
  21.5 1.1 %collective-permute-done.9 = f32[2,16,96]{2,1,0:T(8,128)S(1)} collective-permute-done((f32[2,16,96]{2,1,0:T(8,128)S(1)}, f32[2,16,96]{2,1,0:T(8,128)S(1)}, u32[]{:S(2)}, u32[]{:S(2)}) %collective-permute-start.9) | collective-permute-done | bytes 12320 | tf_op jit(solution)/shard_map/ppermute | solution.py:328
  22.8 0.7 %collective-permute-done.8 = f32[2,16,96]{2,1,0:T(8,128)S(1)} collective-permute-done((f32[2,16,96]{2,1,0:T(8,128)S(1)}, f32[2,16,96]{2,1,0:T(8,128)S(1)}, u32[]{:S(2)}, u32[]{:S(2)}) %collective-permute-start.8) | collective-permute-done | bytes 12320 | tf_op jit(solution)/shard_map/ppermute | solution.py:328
  24.0 0.8 %collective-permute-done.10 = f32[2,16,96]{2,1,0:T(8,128)S(1)} collective-permute-done((f32[2,16,96]{2,1,0:T(8,128)S(1)}, f32[2,16,96]{2,1,0:T(8,128)S(1)}, u32[]{:S(2)}, u32[]{:S(2)}) %collective-permute-start.10) | collective-permute-done | bytes 12320 | tf_op jit(solution)/shard_map/ppermute | solution.py:328
  24.8 1.2 %collective-permute-start.12 = (f32[2,16,96]{2,1,0:T(8,128)S(1)}, f32[2,16,96]{2,1,0:T(8,128)S(1)}, u32[]{:S(2)}, u32[]{:S(2)}) collective-permute-start(f32[2,16,96]{2,1,0:T(8,128)S(1)} %maximum_add_fusion.2), channel_id=1, source_target_pairs={{1,0},{0,1},{3,2},{2,3},{5,4},{4,5},{7,6},{6,7},{14,8},{15,9},{12,... | collective-permute-start | bytes 36872 | tf_op jit(solution)/shard_map/ppermute | solution.py:328
  26.1 1.5 %collective-permute-start.11 = (f32[2,16,96]{2,1,0:T(8,128)S(1)}, f32[2,16,96]{2,1,0:T(8,128)S(1)}, u32[]{:S(2)}, u32[]{:S(2)}) collective-permute-start(f32[2,16,96]{2,1,0:T(8,128)S(1)} %maximum_add_fusion.2), channel_id=1, source_target_pairs={{16,0},{17,1},{18,2},{19,3},{20,4},{21,5},{22,6},{23,7},{10,8},{11... | collective-permute-start | bytes 36872 | tf_op jit(solution)/shard_map/ppermute | solution.py:328
  27.8 0.9 %collective-permute-done.12 = f32[2,16,96]{2,1,0:T(8,128)S(1)} collective-permute-done((f32[2,16,96]{2,1,0:T(8,128)S(1)}, f32[2,16,96]{2,1,0:T(8,128)S(1)}, u32[]{:S(2)}, u32[]{:S(2)}) %collective-permute-start.12) | collective-permute-done | bytes 12320 | tf_op jit(solution)/shard_map/ppermute | solution.py:328
  28.8 1.0 %collective-permute-done.11 = f32[2,16,96]{2,1,0:T(8,128)S(1)} collective-permute-done((f32[2,16,96]{2,1,0:T(8,128)S(1)}, f32[2,16,96]{2,1,0:T(8,128)S(1)}, u32[]{:S(2)}, u32[]{:S(2)}) %collective-permute-start.11) | collective-permute-done | bytes 12320 | tf_op jit(solution)/shard_map/ppermute | solution.py:328
  30.4 0.8 %collective-permute-done.13.second_ref = f32[16,96]{1,0:T(8,128)S(1)} collective-permute-done((f32[16,96]{1,0:T(8,128)S(1)}, f32[16,96]{1,0:T(8,128)S(1)}, u32[]{:S(2)}, u32[]{:S(2)}) %collective-permute-start.13) | collective-permute-done | bytes 6176 | tf_op jit(solution)/shard_map/ppermute | solution.py:328
  31.2 0.9 %shard_map.60 = bf16[16,12,2,256]{3,2,1,0:T(2,128)(2,1)} custom-call(f32[16,96]{1,0:T(8,128)S(1)} %get-tuple-element.38.first_ref, f32[16,96]{1,0:T(8,128)S(1)} %collective-permute-done.13.second_ref, f32[16,96]{1,0:T(8,128)S(1)} %get-tuple-element.28.used_ref, bf16[12,48,256]{2,1,0:T(8,128)(2,1)S(1)} %shard_map.59.vectors_ref, ...), custom_call_target="tpu_custom_call" | custom-call | flops 10000000 | bytes 1000000 | tf_op jit(solution)/shard_map/pallas_call | solution.py:145
  (46 shorter events, 4.1 us)
Async XLA Ops:
  0.7 2.1 %copy-start.3 = (f32[1,9,2,2304]{3,2,1,0:T(2,128)S(1)}, f32[1,9,2,2304]{3,2,1,0:T(2,128)}, u32[]{:S(2)}) copy-start(f32[1,9,2,2304]{3,2,1,0:T(2,128)} %param.8) | copy-start | bytes 497668
  2.2 1.3 %collective-permute-start = (f32[16,96]{1,0:T(8,128)S(1)}, f32[16,96]{1,0:T(8,128)S(1)}, u32[]{:S(2)}, u32[]{:S(2)}) collective-permute-start(f32[16,96]{1,0:T(8,128)S(1)} %get-tuple-element.19), channel_id=1, source_target_pairs={{8,0},{9,1},{10,2},{11,3},{12,4},{13,5},{14,6},{15,7},{0,8},{1,9},... | collective-permute-start | bytes 18440 | tf_op jit(solution)/shard_map/ppermute | solution.py:328
  2.9 5.1 %collective-permute-start.2 = (f32[2,2,2304]{2,1,0:T(2,128)S(1)}, f32[2,2,2304]{2,1,0:T(2,128)S(1)}, u32[]{:S(2)}, u32[]{:S(2)}) collective-permute-start(f32[2,2,2304]{2,1,0:T(2,128)S(1)} %maximum_select_fusion.1), channel_id=1, source_target_pairs={{8,0},{9,1},{10,2},{11,3},{12,4},{13,5},{14,6},{15,7},{0,8},{1,9},... | collective-permute-start | bytes 110600 | tf_op jit(solution)/shard_map/ppermute | solution.py:328
  3.6 4.9 %collective-permute-start.3 = (f32[2,16,96]{2,1,0:T(8,128)S(1)}, f32[2,16,96]{2,1,0:T(8,128)S(1)}, u32[]{:S(2)}, u32[]{:S(2)}) collective-permute-start(f32[2,16,96]{2,1,0:T(8,128)S(1)} %pad_maximum_fusion.1), channel_id=1, source_target_pairs={{1,0},{0,1},{3,2},{2,3},{5,4},{4,5},{7,6},{6,7},{14,8},{15,9},{12,... | collective-permute-start | bytes 36872 | tf_op jit(solution)/shard_map/ppermute | solution.py:328
  6.4 3.7 %collective-permute-start.1 = (f32[2,16,96]{2,1,0:T(8,128)S(1)}, f32[2,16,96]{2,1,0:T(8,128)S(1)}, u32[]{:S(2)}, u32[]{:S(2)}) collective-permute-start(f32[2,16,96]{2,1,0:T(8,128)S(1)} %pad_maximum_fusion.1), channel_id=1, source_target_pairs={{16,0},{17,1},{18,2},{19,3},{20,4},{21,5},{22,6},{23,7},{10,8},{11... | collective-permute-start | bytes 36872 | tf_op jit(solution)/shard_map/ppermute | solution.py:328
  8.7 6.7 %copy-start.1 = (bf16[16,2,12,256]{3,1,2,0:T(2,128)(2,1)S(1)}, bf16[16,2,12,256]{3,1,2,0:T(2,128)(2,1)}, u32[]{:S(2)}) copy-start(bf16[16,2,12,256]{3,1,2,0:T(2,128)(2,1)} %param.5) | copy-start | bytes 589828
  10.3 1.7 %collective-permute-start.4 = (f32[2,16,96]{2,1,0:T(8,128)S(1)}, f32[2,16,96]{2,1,0:T(8,128)S(1)}, u32[]{:S(2)}, u32[]{:S(2)}) collective-permute-start(f32[2,16,96]{2,1,0:T(8,128)S(1)} %convolution_add_fusion.7), channel_id=1, source_target_pairs={{8,0},{9,1},{10,2},{11,3},{12,4},{13,5},{14,6},{15,7},{0,8},{1,9},... | collective-permute-start | bytes 36872 | tf_op jit(solution)/shard_map/ppermute | solution.py:328
  12.1 3.3 %copy-start.2 = (bf16[2,2,6,6,256]{4,1,3,2,0:T(2,128)(2,1)S(1)}, bf16[2,2,6,6,256]{4,1,3,2,0:T(2,128)(2,1)}, u32[]{:S(2)}) copy-start(bf16[2,2,6,6,256]{4,1,3,2,0:T(2,128)(2,1)} %param.7) | copy-start | bytes 221188
  12.1 3.9 %collective-permute-start.6 = (f32[2,16,96]{2,1,0:T(8,128)S(1)}, f32[2,16,96]{2,1,0:T(8,128)S(1)}, u32[]{:S(2)}, u32[]{:S(2)}) collective-permute-start(f32[2,16,96]{2,1,0:T(8,128)S(1)} %maximum_add_fusion), channel_id=1, source_target_pairs={{1,0},{0,1},{3,2},{2,3},{5,4},{4,5},{7,6},{6,7},{14,8},{15,9},{12,... | collective-permute-start | bytes 36872 | tf_op jit(solution)/shard_map/ppermute | solution.py:328
  13.6 3.7 %collective-permute-start.5 = (f32[2,16,96]{2,1,0:T(8,128)S(1)}, f32[2,16,96]{2,1,0:T(8,128)S(1)}, u32[]{:S(2)}, u32[]{:S(2)}) collective-permute-start(f32[2,16,96]{2,1,0:T(8,128)S(1)} %maximum_add_fusion), channel_id=1, source_target_pairs={{16,0},{17,1},{18,2},{19,3},{20,4},{21,5},{22,6},{23,7},{10,8},{11... | collective-permute-start | bytes 36872 | tf_op jit(solution)/shard_map/ppermute | solution.py:328
  16.0 5.4 %copy-start = (bf16[2,24,12,256]{3,1,2,0:T(8,128)(2,1)S(1)}, bf16[2,24,12,256]{3,1,2,0:T(8,128)(2,1)}, u32[]{:S(2)}) copy-start(bf16[2,24,12,256]{3,1,2,0:T(8,128)(2,1)} %param.6) | copy-start | bytes 884740
  17.5 1.2 %collective-permute-start.7 = (f32[2,16,96]{2,1,0:T(8,128)S(1)}, f32[2,16,96]{2,1,0:T(8,128)S(1)}, u32[]{:S(2)}, u32[]{:S(2)}) collective-permute-start(f32[2,16,96]{2,1,0:T(8,128)S(1)} %convolution_add_fusion.5), channel_id=1, source_target_pairs={{8,0},{9,1},{10,2},{11,3},{12,4},{13,5},{14,6},{15,7},{0,8},{1,9},... | collective-permute-start | bytes 36872 | tf_op jit(solution)/shard_map/ppermute | solution.py:328
  18.8 3.8 %collective-permute-start.9 = (f32[2,16,96]{2,1,0:T(8,128)S(1)}, f32[2,16,96]{2,1,0:T(8,128)S(1)}, u32[]{:S(2)}, u32[]{:S(2)}) collective-permute-start(f32[2,16,96]{2,1,0:T(8,128)S(1)} %maximum_add_fusion.1), channel_id=1, source_target_pairs={{1,0},{0,1},{3,2},{2,3},{5,4},{4,5},{7,6},{6,7},{14,8},{15,9},{12,... | collective-permute-start | bytes 36872 | tf_op jit(solution)/shard_map/ppermute | solution.py:328
  19.7 3.7 %collective-permute-start.8 = (f32[2,16,96]{2,1,0:T(8,128)S(1)}, f32[2,16,96]{2,1,0:T(8,128)S(1)}, u32[]{:S(2)}, u32[]{:S(2)}) collective-permute-start(f32[2,16,96]{2,1,0:T(8,128)S(1)} %maximum_add_fusion.1), channel_id=1, source_target_pairs={{16,0},{17,1},{18,2},{19,3},{20,4},{21,5},{22,6},{23,7},{10,8},{11... | collective-permute-start | bytes 36872 | tf_op jit(solution)/shard_map/ppermute | solution.py:328
  23.6 1.2 %collective-permute-start.10 = (f32[2,16,96]{2,1,0:T(8,128)S(1)}, f32[2,16,96]{2,1,0:T(8,128)S(1)}, u32[]{:S(2)}, u32[]{:S(2)}) collective-permute-start(f32[2,16,96]{2,1,0:T(8,128)S(1)} %convolution_add_fusion.3), channel_id=1, source_target_pairs={{8,0},{9,1},{10,2},{11,3},{12,4},{13,5},{14,6},{15,7},{0,8},{1,9},... | collective-permute-start | bytes 36872 | tf_op jit(solution)/shard_map/ppermute | solution.py:328
  24.8 3.8 %collective-permute-start.12 = (f32[2,16,96]{2,1,0:T(8,128)S(1)}, f32[2,16,96]{2,1,0:T(8,128)S(1)}, u32[]{:S(2)}, u32[]{:S(2)}) collective-permute-start(f32[2,16,96]{2,1,0:T(8,128)S(1)} %maximum_add_fusion.2), channel_id=1, source_target_pairs={{1,0},{0,1},{3,2},{2,3},{5,4},{4,5},{7,6},{6,7},{14,8},{15,9},{12,... | collective-permute-start | bytes 36872 | tf_op jit(solution)/shard_map/ppermute | solution.py:328
  26.1 3.7 %collective-permute-start.11 = (f32[2,16,96]{2,1,0:T(8,128)S(1)}, f32[2,16,96]{2,1,0:T(8,128)S(1)}, u32[]{:S(2)}, u32[]{:S(2)}) collective-permute-start(f32[2,16,96]{2,1,0:T(8,128)S(1)} %maximum_add_fusion.2), channel_id=1, source_target_pairs={{16,0},{17,1},{18,2},{19,3},{20,4},{21,5},{22,6},{23,7},{10,8},{11... | collective-permute-start | bytes 36872 | tf_op jit(solution)/shard_map/ppermute | solution.py:328
  30.0 1.2 %collective-permute-start.13 = (f32[16,96]{1,0:T(8,128)S(1)}, f32[16,96]{1,0:T(8,128)S(1)}, u32[]{:S(2)}, u32[]{:S(2)}) collective-permute-start(f32[16,96]{1,0:T(8,128)S(1)} %get-tuple-element.37), channel_id=1, source_target_pairs={{8,0},{9,1},{10,2},{11,3},{12,4},{13,5},{14,6},{15,7},{0,8},{1,9},... | collective-permute-start | bytes 18440 | tf_op jit(solution)/shard_map/ppermute | solution.py:328

commit v20 on v19

--- a/solution.py
+++ b/solution.py
@@ -64,7 +64,7 @@
                 pltpu.make_async_copy(vectors_hbm.at[:, span], vectors_ref.at[:, span], sems.at[2 * chi + 1]),
             ]
         )
-    for copy in copies[0] + copies[1]:
+    for copy in copies[0][::-1] + copies[1][::-1]:
         copy.start()
     for chi in range(2):
         for copy in copies[chi]:

time: 32.3 us -> 32.3 us (level)
  no operation moved by 1% of the time
where the time goes in v20:
time: 32.3 us; the launch traced here: 32.1 us
  starting transfers between devices  15.3 us (47%)
  waiting for transfers between devices  10.1 us (31%)
  Pallas kernels  3.69 us (11%)
  matrix products  2 us (6%)
  between operations  0.8 us (2%)
    ppermute x14, starting transfers between devices, swap(): lax.ppermute(block, axes, [(source, i) for i, source in enumerate(sources)])  15.3 us
    ppermute x14, waiting for transfers between devices, swap(): lax.ppermute(block, axes, [(source, i) for i, source in enumerate(sources)])  10.1 us
    pallas_call x1, Pallas kernels, restrict(): pl.pallas_call(restrict_kernel, out_shape=[jax.ShapeDtypeStruct((rhs, 4 *...  1.58 us
    dot_general x8, matrix products, along(): lax.dot_general(moved[link], around[:, link], (((2,), (2,)), ((0,), (0,))...  1.32 us
    pallas_call x1, Pallas kernels, extend(): pl.pallas_call(extend_kernel, out_shape=jax.ShapeDtypeStruct(shape, jnp.b...  0.94 us
    dot_general x4, matrix products, apply(): lax.dot_general(vector, matrix, (((1,), (1,)), ((), ())), precision=preci...  0.68 us
  transfers between devices with their start and end apart: 14, of which 11 were waited for; matrix products, arithmetic and copies ran while one was open for 5% of the time, Pallas kernels for 4%

profile of v20, /device:TPU:0, one launch (start us, length us, event | category | flops | bytes accessed | tf_op | source)
XLA Modules:
  0.0 32.1 jit_solution(484711913066907485)
XLA Ops:
  0.7 1.6 %shard_map.55 = (f32[16,96]{1,0:T(8,128)S(1)}, f32[16,96]{1,0:T(8,128)S(1)}) custom-call(s32[1]{0:T(128)S(6)} %copy.6.count_ref, bf16[16,12,2,256]{3,2,1,0:T(2,128)(2,1)} %bitcast.70, bf16[2,12,24,256]{3,2,1,0:T(8,128)(2,1)} %bitcast.68), custom_call_target="tpu_custom_call" | custom-call | flops 10000000 | bytes 500000 | tf_op jit(solution)/shard_map/pallas_call | solution.py:96
  2.3 0.5 %collective-permute-start = (f32[16,96]{1,0:T(8,128)S(1)}, f32[16,96]{1,0:T(8,128)S(1)}, u32[]{:S(2)}, u32[]{:S(2)}) collective-permute-start(f32[16,96]{1,0:T(8,128)S(1)} %get-tuple-element.19), channel_id=1, source_target_pairs={{8,0},{9,1},{10,2},{11,3},{12,4},{13,5},{14,6},{15,7},{0,8},{1,9},... | collective-permute-start | bytes 18440 | tf_op jit(solution)/shard_map/ppermute | solution.py:328
  3.6 2.8 %collective-permute-start.3 = (f32[2,16,96]{2,1,0:T(8,128)S(1)}, f32[2,16,96]{2,1,0:T(8,128)S(1)}, u32[]{:S(2)}, u32[]{:S(2)}) collective-permute-start(f32[2,16,96]{2,1,0:T(8,128)S(1)} %pad_maximum_fusion.1), channel_id=1, source_target_pairs={{1,0},{0,1},{3,2},{2,3},{5,4},{4,5},{7,6},{6,7},{14,8},{15,9},{12,... | collective-permute-start | bytes 36872 | tf_op jit(solution)/shard_map/ppermute | solution.py:328
  6.4 1.5 %collective-permute-start.1 = (f32[2,16,96]{2,1,0:T(8,128)S(1)}, f32[2,16,96]{2,1,0:T(8,128)S(1)}, u32[]{:S(2)}, u32[]{:S(2)}) collective-permute-start(f32[2,16,96]{2,1,0:T(8,128)S(1)} %pad_maximum_fusion.1), channel_id=1, source_target_pairs={{16,0},{17,1},{18,2},{19,3},{20,4},{21,5},{22,6},{23,7},{10,8},{11... | collective-permute-start | bytes 36872 | tf_op jit(solution)/shard_map/ppermute | solution.py:328
  8.7 1.5 %collective-permute-done.1 = f32[2,16,96]{2,1,0:T(8,128)S(1)} collective-permute-done((f32[2,16,96]{2,1,0:T(8,128)S(1)}, f32[2,16,96]{2,1,0:T(8,128)S(1)}, u32[]{:S(2)}, u32[]{:S(2)}) %collective-permute-start.1) | collective-permute-done | bytes 12320 | tf_op jit(solution)/shard_map/ppermute | solution.py:328
  10.3 0.9 %collective-permute-start.4 = (f32[2,16,96]{2,1,0:T(8,128)S(1)}, f32[2,16,96]{2,1,0:T(8,128)S(1)}, u32[]{:S(2)}, u32[]{:S(2)}) collective-permute-start(f32[2,16,96]{2,1,0:T(8,128)S(1)} %convolution_add_fusion.7), channel_id=1, source_target_pairs={{8,0},{9,1},{10,2},{11,3},{12,4},{13,5},{14,6},{15,7},{0,8},{1,9},... | collective-permute-start | bytes 36872 | tf_op jit(solution)/shard_map/ppermute | solution.py:328
  11.2 0.8 %collective-permute-done.4 = f32[2,16,96]{2,1,0:T(8,128)S(1)} collective-permute-done((f32[2,16,96]{2,1,0:T(8,128)S(1)}, f32[2,16,96]{2,1,0:T(8,128)S(1)}, u32[]{:S(2)}, u32[]{:S(2)}) %collective-permute-start.4) | collective-permute-done | bytes 12320 | tf_op jit(solution)/shard_map/ppermute | solution.py:328
  12.1 1.6 %collective-permute-start.6 = (f32[2,16,96]{2,1,0:T(8,128)S(1)}, f32[2,16,96]{2,1,0:T(8,128)S(1)}, u32[]{:S(2)}, u32[]{:S(2)}) collective-permute-start(f32[2,16,96]{2,1,0:T(8,128)S(1)} %maximum_add_fusion), channel_id=1, source_target_pairs={{1,0},{0,1},{3,2},{2,3},{5,4},{4,5},{7,6},{6,7},{14,8},{15,9},{12,... | collective-permute-start | bytes 36872 | tf_op jit(solution)/shard_map/ppermute | solution.py:328
  13.6 1.5 %collective-permute-start.5 = (f32[2,16,96]{2,1,0:T(8,128)S(1)}, f32[2,16,96]{2,1,0:T(8,128)S(1)}, u32[]{:S(2)}, u32[]{:S(2)}) collective-permute-start(f32[2,16,96]{2,1,0:T(8,128)S(1)} %maximum_add_fusion), channel_id=1, source_target_pairs={{16,0},{17,1},{18,2},{19,3},{20,4},{21,5},{22,6},{23,7},{10,8},{11... | collective-permute-start | bytes 36872 | tf_op jit(solution)/shard_map/ppermute | solution.py:328
  15.4 0.6 %shard_map.58.local_ref = f32[12,32,256]{2,1,0:T(8,128)S(1)} custom-call(bf16[16,12,2,256]{3,2,1,0:T(2,128)(2,1)S(1)} %bitcast.71, bf16[2,6,6,2,256]{4,3,2,1,0:T(2,128)(2,1)S(1)} %bitcast.73), custom_call_target="tpu_custom_call" | custom-call | flops 100000 | bytes 100000 | tf_op jit(solution)/shard_map/pallas_call | solution.py:204
  16.2 1.2 %collective-permute-done.5 = f32[2,16,96]{2,1,0:T(8,128)S(1)} collective-permute-done((f32[2,16,96]{2,1,0:T(8,128)S(1)}, f32[2,16,96]{2,1,0:T(8,128)S(1)}, u32[]{:S(2)}, u32[]{:S(2)}) %collective-permute-start.5) | collective-permute-done | bytes 12320 | tf_op jit(solution)/shard_map/ppermute | solution.py:328
  17.5 0.4 %collective-permute-start.7 = (f32[2,16,96]{2,1,0:T(8,128)S(1)}, f32[2,16,96]{2,1,0:T(8,128)S(1)}, u32[]{:S(2)}, u32[]{:S(2)}) collective-permute-start(f32[2,16,96]{2,1,0:T(8,128)S(1)} %convolution_add_fusion.5), channel_id=1, source_target_pairs={{8,0},{9,1},{10,2},{11,3},{12,4},{13,5},{14,6},{15,7},{0,8},{1,9},... | collective-permute-start | bytes 36872 | tf_op jit(solution)/shard_map/ppermute | solution.py:328
  17.9 0.8 %collective-permute-done.7 = f32[2,16,96]{2,1,0:T(8,128)S(1)} collective-permute-done((f32[2,16,96]{2,1,0:T(8,128)S(1)}, f32[2,16,96]{2,1,0:T(8,128)S(1)}, u32[]{:S(2)}, u32[]{:S(2)}) %collective-permute-start.7) | collective-permute-done | bytes 12320 | tf_op jit(solution)/shard_map/ppermute | solution.py:328
  18.8 0.9 %collective-permute-start.9 = (f32[2,16,96]{2,1,0:T(8,128)S(1)}, f32[2,16,96]{2,1,0:T(8,128)S(1)}, u32[]{:S(2)}, u32[]{:S(2)}) collective-permute-start(f32[2,16,96]{2,1,0:T(8,128)S(1)} %maximum_add_fusion.1), channel_id=1, source_target_pairs={{1,0},{0,1},{3,2},{2,3},{5,4},{4,5},{7,6},{6,7},{14,8},{15,9},{12,... | collective-permute-start | bytes 36872 | tf_op jit(solution)/shard_map/ppermute | solution.py:328
  19.7 1.5 %collective-permute-start.8 = (f32[2,16,96]{2,1,0:T(8,128)S(1)}, f32[2,16,96]{2,1,0:T(8,128)S(1)}, u32[]{:S(2)}, u32[]{:S(2)}) collective-permute-start(f32[2,16,96]{2,1,0:T(8,128)S(1)} %maximum_add_fusion.1), channel_id=1, source_target_pairs={{16,0},{17,1},{18,2},{19,3},{20,4},{21,5},{22,6},{23,7},{10,8},{11... | collective-permute-start | bytes 36872 | tf_op jit(solution)/shard_map/ppermute | solution.py:328
  21.5 1.1 %collective-permute-done.9 = f32[2,16,96]{2,1,0:T(8,128)S(1)} collective-permute-done((f32[2,16,96]{2,1,0:T(8,128)S(1)}, f32[2,16,96]{2,1,0:T(8,128)S(1)}, u32[]{:S(2)}, u32[]{:S(2)}) %collective-permute-start.9) | collective-permute-done | bytes 12320 | tf_op jit(solution)/shard_map/ppermute | solution.py:328
  22.8 0.7 %collective-permute-done.8 = f32[2,16,96]{2,1,0:T(8,128)S(1)} collective-permute-done((f32[2,16,96]{2,1,0:T(8,128)S(1)}, f32[2,16,96]{2,1,0:T(8,128)S(1)}, u32[]{:S(2)}, u32[]{:S(2)}) %collective-permute-start.8) | collective-permute-done | bytes 12320 | tf_op jit(solution)/shard_map/ppermute | solution.py:328
  24.0 0.8 %collective-permute-done.10 = f32[2,16,96]{2,1,0:T(8,128)S(1)} collective-permute-done((f32[2,16,96]{2,1,0:T(8,128)S(1)}, f32[2,16,96]{2,1,0:T(8,128)S(1)}, u32[]{:S(2)}, u32[]{:S(2)}) %collective-permute-start.10) | collective-permute-done | bytes 12320 | tf_op jit(solution)/shard_map/ppermute | solution.py:328
  24.9 1.2 %collective-permute-start.12 = (f32[2,16,96]{2,1,0:T(8,128)S(1)}, f32[2,16,96]{2,1,0:T(8,128)S(1)}, u32[]{:S(2)}, u32[]{:S(2)}) collective-permute-start(f32[2,16,96]{2,1,0:T(8,128)S(1)} %maximum_add_fusion.2), channel_id=1, source_target_pairs={{1,0},{0,1},{3,2},{2,3},{5,4},{4,5},{7,6},{6,7},{14,8},{15,9},{12,... | collective-permute-start | bytes 36872 | tf_op jit(solution)/shard_map/ppermute | solution.py:328
  26.1 1.5 %collective-permute-start.11 = (f32[2,16,96]{2,1,0:T(8,128)S(1)}, f32[2,16,96]{2,1,0:T(8,128)S(1)}, u32[]{:S(2)}, u32[]{:S(2)}) collective-permute-start(f32[2,16,96]{2,1,0:T(8,128)S(1)} %maximum_add_fusion.2), channel_id=1, source_target_pairs={{16,0},{17,1},{18,2},{19,3},{20,4},{21,5},{22,6},{23,7},{10,8},{11... | collective-permute-start | bytes 36872 | tf_op jit(solution)/shard_map/ppermute | solution.py:328
  27.8 0.9 %collective-permute-done.12 = f32[2,16,96]{2,1,0:T(8,128)S(1)} collective-permute-done((f32[2,16,96]{2,1,0:T(8,128)S(1)}, f32[2,16,96]{2,1,0:T(8,128)S(1)}, u32[]{:S(2)}, u32[]{:S(2)}) %collective-permute-start.12) | collective-permute-done | bytes 12320 | tf_op jit(solution)/shard_map/ppermute | solution.py:328
  28.8 1.0 %collective-permute-done.11 = f32[2,16,96]{2,1,0:T(8,128)S(1)} collective-permute-done((f32[2,16,96]{2,1,0:T(8,128)S(1)}, f32[2,16,96]{2,1,0:T(8,128)S(1)}, u32[]{:S(2)}, u32[]{:S(2)}) %collective-permute-start.11) | collective-permute-done | bytes 12320 | tf_op jit(solution)/shard_map/ppermute | solution.py:328
  30.4 0.8 %collective-permute-done.13.second_ref = f32[16,96]{1,0:T(8,128)S(1)} collective-permute-done((f32[16,96]{1,0:T(8,128)S(1)}, f32[16,96]{1,0:T(8,128)S(1)}, u32[]{:S(2)}, u32[]{:S(2)}) %collective-permute-start.13) | collective-permute-done | bytes 6176 | tf_op jit(solution)/shard_map/ppermute | solution.py:328
  31.2 0.9 %shard_map.60 = bf16[16,12,2,256]{3,2,1,0:T(2,128)(2,1)} custom-call(f32[16,96]{1,0:T(8,128)S(1)} %get-tuple-element.38.first_ref, f32[16,96]{1,0:T(8,128)S(1)} %collective-permute-done.13.second_ref, f32[16,96]{1,0:T(8,128)S(1)} %get-tuple-element.28.used_ref, bf16[12,48,256]{2,1,0:T(8,128)(2,1)S(1)} %shard_map.59.vectors_ref, ...), custom_call_target="tpu_custom_call" | custom-call | flops 10000000 | bytes 1000000 | tf_op jit(solution)/shard_map/pallas_call | solution.py:145
  (46 shorter events, 4.1 us)
Async XLA Ops:
  0.7 2.1 %copy-start.3 = (f32[1,9,2,2304]{3,2,1,0:T(2,128)S(1)}, f32[1,9,2,2304]{3,2,1,0:T(2,128)}, u32[]{:S(2)}) copy-start(f32[1,9,2,2304]{3,2,1,0:T(2,128)} %param.8) | copy-start | bytes 497668
  2.3 1.3 %collective-permute-start = (f32[16,96]{1,0:T(8,128)S(1)}, f32[16,96]{1,0:T(8,128)S(1)}, u32[]{:S(2)}, u32[]{:S(2)}) collective-permute-start(f32[16,96]{1,0:T(8,128)S(1)} %get-tuple-element.19), channel_id=1, source_target_pairs={{8,0},{9,1},{10,2},{11,3},{12,4},{13,5},{14,6},{15,7},{0,8},{1,9},... | collective-permute-start | bytes 18440 | tf_op jit(solution)/shard_map/ppermute | solution.py:328
  2.9 5.1 %collective-permute-start.2 = (f32[2,2,2304]{2,1,0:T(2,128)S(1)}, f32[2,2,2304]{2,1,0:T(2,128)S(1)}, u32[]{:S(2)}, u32[]{:S(2)}) collective-permute-start(f32[2,2,2304]{2,1,0:T(2,128)S(1)} %maximum_select_fusion.1), channel_id=1, source_target_pairs={{8,0},{9,1},{10,2},{11,3},{12,4},{13,5},{14,6},{15,7},{0,8},{1,9},... | collective-permute-start | bytes 110600 | tf_op jit(solution)/shard_map/ppermute | solution.py:328
  3.6 4.9 %collective-permute-start.3 = (f32[2,16,96]{2,1,0:T(8,128)S(1)}, f32[2,16,96]{2,1,0:T(8,128)S(1)}, u32[]{:S(2)}, u32[]{:S(2)}) collective-permute-start(f32[2,16,96]{2,1,0:T(8,128)S(1)} %pad_maximum_fusion.1), channel_id=1, source_target_pairs={{1,0},{0,1},{3,2},{2,3},{5,4},{4,5},{7,6},{6,7},{14,8},{15,9},{12,... | collective-permute-start | bytes 36872 | tf_op jit(solution)/shard_map/ppermute | solution.py:328
  6.4 3.7 %collective-permute-start.1 = (f32[2,16,96]{2,1,0:T(8,128)S(1)}, f32[2,16,96]{2,1,0:T(8,128)S(1)}, u32[]{:S(2)}, u32[]{:S(2)}) collective-permute-start(f32[2,16,96]{2,1,0:T(8,128)S(1)} %pad_maximum_fusion.1), channel_id=1, source_target_pairs={{16,0},{17,1},{18,2},{19,3},{20,4},{21,5},{22,6},{23,7},{10,8},{11... | collective-permute-start | bytes 36872 | tf_op jit(solution)/shard_map/ppermute | solution.py:328
  8.7 6.7 %copy-start.1 = (bf16[16,2,12,256]{3,1,2,0:T(2,128)(2,1)S(1)}, bf16[16,2,12,256]{3,1,2,0:T(2,128)(2,1)}, u32[]{:S(2)}) copy-start(bf16[16,2,12,256]{3,1,2,0:T(2,128)(2,1)} %param.5) | copy-start | bytes 589828
  10.3 1.7 %collective-permute-start.4 = (f32[2,16,96]{2,1,0:T(8,128)S(1)}, f32[2,16,96]{2,1,0:T(8,128)S(1)}, u32[]{:S(2)}, u32[]{:S(2)}) collective-permute-start(f32[2,16,96]{2,1,0:T(8,128)S(1)} %convolution_add_fusion.7), channel_id=1, source_target_pairs={{8,0},{9,1},{10,2},{11,3},{12,4},{13,5},{14,6},{15,7},{0,8},{1,9},... | collective-permute-start | bytes 36872 | tf_op jit(solution)/shard_map/ppermute | solution.py:328
  12.1 3.3 %copy-start.2 = (bf16[2,2,6,6,256]{4,1,3,2,0:T(2,128)(2,1)S(1)}, bf16[2,2,6,6,256]{4,1,3,2,0:T(2,128)(2,1)}, u32[]{:S(2)}) copy-start(bf16[2,2,6,6,256]{4,1,3,2,0:T(2,128)(2,1)} %param.7) | copy-start | bytes 221188
  12.1 3.9 %collective-permute-start.6 = (f32[2,16,96]{2,1,0:T(8,128)S(1)}, f32[2,16,96]{2,1,0:T(8,128)S(1)}, u32[]{:S(2)}, u32[]{:S(2)}) collective-permute-start(f32[2,16,96]{2,1,0:T(8,128)S(1)} %maximum_add_fusion), channel_id=1, source_target_pairs={{1,0},{0,1},{3,2},{2,3},{5,4},{4,5},{7,6},{6,7},{14,8},{15,9},{12,... | collective-permute-start | bytes 36872 | tf_op jit(solution)/shard_map/ppermute | solution.py:328
  13.6 3.7 %collective-permute-start.5 = (f32[2,16,96]{2,1,0:T(8,128)S(1)}, f32[2,16,96]{2,1,0:T(8,128)S(1)}, u32[]{:S(2)}, u32[]{:S(2)}) collective-permute-start(f32[2,16,96]{2,1,0:T(8,128)S(1)} %maximum_add_fusion), channel_id=1, source_target_pairs={{16,0},{17,1},{18,2},{19,3},{20,4},{21,5},{22,6},{23,7},{10,8},{11... | collective-permute-start | bytes 36872 | tf_op jit(solution)/shard_map/ppermute | solution.py:328
  16.0 5.4 %copy-start = (bf16[2,24,12,256]{3,1,2,0:T(8,128)(2,1)S(1)}, bf16[2,24,12,256]{3,1,2,0:T(8,128)(2,1)}, u32[]{:S(2)}) copy-start(bf16[2,24,12,256]{3,1,2,0:T(8,128)(2,1)} %param.6) | copy-start | bytes 884740
  17.5 1.2 %collective-permute-start.7 = (f32[2,16,96]{2,1,0:T(8,128)S(1)}, f32[2,16,96]{2,1,0:T(8,128)S(1)}, u32[]{:S(2)}, u32[]{:S(2)}) collective-permute-start(f32[2,16,96]{2,1,0:T(8,128)S(1)} %convolution_add_fusion.5), channel_id=1, source_target_pairs={{8,0},{9,1},{10,2},{11,3},{12,4},{13,5},{14,6},{15,7},{0,8},{1,9},... | collective-permute-start | bytes 36872 | tf_op jit(solution)/shard_map/ppermute | solution.py:328
  18.8 3.8 %collective-permute-start.9 = (f32[2,16,96]{2,1,0:T(8,128)S(1)}, f32[2,16,96]{2,1,0:T(8,128)S(1)}, u32[]{:S(2)}, u32[]{:S(2)}) collective-permute-start(f32[2,16,96]{2,1,0:T(8,128)S(1)} %maximum_add_fusion.1), channel_id=1, source_target_pairs={{1,0},{0,1},{3,2},{2,3},{5,4},{4,5},{7,6},{6,7},{14,8},{15,9},{12,... | collective-permute-start | bytes 36872 | tf_op jit(solution)/shard_map/ppermute | solution.py:328
  19.7 3.7 %collective-permute-start.8 = (f32[2,16,96]{2,1,0:T(8,128)S(1)}, f32[2,16,96]{2,1,0:T(8,128)S(1)}, u32[]{:S(2)}, u32[]{:S(2)}) collective-permute-start(f32[2,16,96]{2,1,0:T(8,128)S(1)} %maximum_add_fusion.1), channel_id=1, source_target_pairs={{16,0},{17,1},{18,2},{19,3},{20,4},{21,5},{22,6},{23,7},{10,8},{11... | collective-permute-start | bytes 36872 | tf_op jit(solution)/shard_map/ppermute | solution.py:328
  23.6 1.2 %collective-permute-start.10 = (f32[2,16,96]{2,1,0:T(8,128)S(1)}, f32[2,16,96]{2,1,0:T(8,128)S(1)}, u32[]{:S(2)}, u32[]{:S(2)}) collective-permute-start(f32[2,16,96]{2,1,0:T(8,128)S(1)} %convolution_add_fusion.3), channel_id=1, source_target_pairs={{8,0},{9,1},{10,2},{11,3},{12,4},{13,5},{14,6},{15,7},{0,8},{1,9},... | collective-permute-start | bytes 36872 | tf_op jit(solution)/shard_map/ppermute | solution.py:328
  24.9 3.8 %collective-permute-start.12 = (f32[2,16,96]{2,1,0:T(8,128)S(1)}, f32[2,16,96]{2,1,0:T(8,128)S(1)}, u32[]{:S(2)}, u32[]{:S(2)}) collective-permute-start(f32[2,16,96]{2,1,0:T(8,128)S(1)} %maximum_add_fusion.2), channel_id=1, source_target_pairs={{1,0},{0,1},{3,2},{2,3},{5,4},{4,5},{7,6},{6,7},{14,8},{15,9},{12,... | collective-permute-start | bytes 36872 | tf_op jit(solution)/shard_map/ppermute | solution.py:328
  26.1 3.7 %collective-permute-start.11 = (f32[2,16,96]{2,1,0:T(8,128)S(1)}, f32[2,16,96]{2,1,0:T(8,128)S(1)}, u32[]{:S(2)}, u32[]{:S(2)}) collective-permute-start(f32[2,16,96]{2,1,0:T(8,128)S(1)} %maximum_add_fusion.2), channel_id=1, source_target_pairs={{16,0},{17,1},{18,2},{19,3},{20,4},{21,5},{22,6},{23,7},{10,8},{11... | collective-permute-start | bytes 36872 | tf_op jit(solution)/shard_map/ppermute | solution.py:328
  30.0 1.2 %collective-permute-start.13 = (f32[16,96]{1,0:T(8,128)S(1)}, f32[16,96]{1,0:T(8,128)S(1)}, u32[]{:S(2)}, u32[]{:S(2)}) collective-permute-start(f32[16,96]{1,0:T(8,128)S(1)} %get-tuple-element.37), channel_id=1, source_target_pairs={{8,0},{9,1},{10,2},{11,3},{12,4},{13,5},{14,6},{15,7},{0,8},{1,9},... | collective-permute-start | bytes 18440 | tf_op jit(solution)/shard_map/ppermute | solution.py:328

commit v21 on v19

--- a/solution.py
+++ b/solution.py
@@ -120,9 +120,9 @@
         scratch[chi, pl.ds(0, rhs, stride=2), : 2 * vecs] = jnp.concatenate([real, -imag], 1)
         scratch[chi, pl.ds(1, rhs, stride=2), : 2 * vecs] = jnp.concatenate([imag, real], 1)
     copies = []
-    step = half // 2
-    for piece in range(4):
-        weights = scratch[piece // 2, :, : 2 * vecs].astype(jnp.bfloat16)
+    step = half // 3
+    for piece in range(6):
+        weights = scratch[piece // 3, :, : 2 * vecs].astype(jnp.bfloat16)
         for c in range(step * piece, step * piece + step):
             lift = jnp.dot(weights, vectors_ref[c], preferred_element_type=jnp.float32)
             total = (local_ref[c] + lift).astype(jnp.bfloat16)
@@ -150,7 +150,7 @@
         scratch_shapes=[
             pltpu.VMEM(shape, jnp.bfloat16),
             pltpu.VMEM((2, 2 * rhs, 128), jnp.float32),
-            pltpu.SemaphoreType.DMA((4,)),
+            pltpu.SemaphoreType.DMA((6,)),
         ],
         compiler_params=small,
         cost_estimate=pl.CostEstimate(flops=10**7, bytes_accessed=10**6, transcendentals=0),

time: 32.3 us -> 32.3 us (level)
  no operation moved by 1% of the time
where the time goes in v21:
time: 32.3 us; the launch traced here: 32.1 us
  starting transfers between devices  15.3 us (47%)
  waiting for transfers between devices  10.1 us (31%)
  Pallas kernels  3.7 us (11%)
  matrix products  2 us (6%)
  between operations  0.8 us (2%)
    ppermute x14, starting transfers between devices, swap(): lax.ppermute(block, axes, [(source, i) for i, source in enumerate(sources)])  15.3 us
    ppermute x14, waiting for transfers between devices, swap(): lax.ppermute(block, axes, [(source, i) for i, source in enumerate(sources)])  10.1 us
    pallas_call x1, Pallas kernels, restrict(): pl.pallas_call(restrict_kernel, out_shape=[jax.ShapeDtypeStruct((rhs, 4 *...  1.58 us
    dot_general x8, matrix products, along(): lax.dot_general(moved[link], around[:, link], (((2,), (2,)), ((0,), (0,))...  1.32 us
    pallas_call x1, Pallas kernels, extend(): pl.pallas_call(extend_kernel, out_shape=jax.ShapeDtypeStruct(shape, jnp.b...  0.95 us
    dot_general x4, matrix products, apply(): lax.dot_general(vector, matrix, (((1,), (1,)), ((), ())), precision=preci...  0.68 us
  transfers between devices with their start and end apart: 14, of which 11 were waited for; matrix products, arithmetic and copies ran while one was open for 5% of the time, Pallas kernels for 4%

profile of v21, /device:TPU:0, one launch (start us, length us, event | category | flops | bytes accessed | tf_op | source)
XLA Modules:
  0.0 32.1 jit_solution(11624579944422144780)
XLA Ops:
  0.7 1.6 %shard_map.55 = (f32[16,96]{1,0:T(8,128)S(1)}, f32[16,96]{1,0:T(8,128)S(1)}) custom-call(s32[1]{0:T(128)S(6)} %copy.6.count_ref, bf16[16,12,2,256]{3,2,1,0:T(2,128)(2,1)} %bitcast.70, bf16[2,12,24,256]{3,2,1,0:T(8,128)(2,1)} %bitcast.68), custom_call_target="tpu_custom_call" | custom-call | flops 10000000 | bytes 500000 | tf_op jit(solution)/shard_map/pallas_call | solution.py:96
  2.2 0.5 %collective-permute-start = (f32[16,96]{1,0:T(8,128)S(1)}, f32[16,96]{1,0:T(8,128)S(1)}, u32[]{:S(2)}, u32[]{:S(2)}) collective-permute-start(f32[16,96]{1,0:T(8,128)S(1)} %get-tuple-element.19), channel_id=1, source_target_pairs={{8,0},{9,1},{10,2},{11,3},{12,4},{13,5},{14,6},{15,7},{0,8},{1,9},... | collective-permute-start | bytes 18440 | tf_op jit(solution)/shard_map/ppermute | solution.py:328
  3.6 2.8 %collective-permute-start.3 = (f32[2,16,96]{2,1,0:T(8,128)S(1)}, f32[2,16,96]{2,1,0:T(8,128)S(1)}, u32[]{:S(2)}, u32[]{:S(2)}) collective-permute-start(f32[2,16,96]{2,1,0:T(8,128)S(1)} %pad_maximum_fusion.1), channel_id=1, source_target_pairs={{1,0},{0,1},{3,2},{2,3},{5,4},{4,5},{7,6},{6,7},{14,8},{15,9},{12,... | collective-permute-start | bytes 36872 | tf_op jit(solution)/shard_map/ppermute | solution.py:328
  6.4 1.5 %collective-permute-start.1 = (f32[2,16,96]{2,1,0:T(8,128)S(1)}, f32[2,16,96]{2,1,0:T(8,128)S(1)}, u32[]{:S(2)}, u32[]{:S(2)}) collective-permute-start(f32[2,16,96]{2,1,0:T(8,128)S(1)} %pad_maximum_fusion.1), channel_id=1, source_target_pairs={{16,0},{17,1},{18,2},{19,3},{20,4},{21,5},{22,6},{23,7},{10,8},{11... | collective-permute-start | bytes 36872 | tf_op jit(solution)/shard_map/ppermute | solution.py:328
  8.7 1.5 %collective-permute-done.1 = f32[2,16,96]{2,1,0:T(8,128)S(1)} collective-permute-done((f32[2,16,96]{2,1,0:T(8,128)S(1)}, f32[2,16,96]{2,1,0:T(8,128)S(1)}, u32[]{:S(2)}, u32[]{:S(2)}) %collective-permute-start.1) | collective-permute-done | bytes 12320 | tf_op jit(solution)/shard_map/ppermute | solution.py:328
  10.3 0.9 %collective-permute-start.4 = (f32[2,16,96]{2,1,0:T(8,128)S(1)}, f32[2,16,96]{2,1,0:T(8,128)S(1)}, u32[]{:S(2)}, u32[]{:S(2)}) collective-permute-start(f32[2,16,96]{2,1,0:T(8,128)S(1)} %convolution_add_fusion.7), channel_id=1, source_target_pairs={{8,0},{9,1},{10,2},{11,3},{12,4},{13,5},{14,6},{15,7},{0,8},{1,9},... | collective-permute-start | bytes 36872 | tf_op jit(solution)/shard_map/ppermute | solution.py:328
  11.2 0.8 %collective-permute-done.4 = f32[2,16,96]{2,1,0:T(8,128)S(1)} collective-permute-done((f32[2,16,96]{2,1,0:T(8,128)S(1)}, f32[2,16,96]{2,1,0:T(8,128)S(1)}, u32[]{:S(2)}, u32[]{:S(2)}) %collective-permute-start.4) | collective-permute-done | bytes 12320 | tf_op jit(solution)/shard_map/ppermute | solution.py:328
  12.1 1.6 %collective-permute-start.6 = (f32[2,16,96]{2,1,0:T(8,128)S(1)}, f32[2,16,96]{2,1,0:T(8,128)S(1)}, u32[]{:S(2)}, u32[]{:S(2)}) collective-permute-start(f32[2,16,96]{2,1,0:T(8,128)S(1)} %maximum_add_fusion), channel_id=1, source_target_pairs={{1,0},{0,1},{3,2},{2,3},{5,4},{4,5},{7,6},{6,7},{14,8},{15,9},{12,... | collective-permute-start | bytes 36872 | tf_op jit(solution)/shard_map/ppermute | solution.py:328
  13.6 1.5 %collective-permute-start.5 = (f32[2,16,96]{2,1,0:T(8,128)S(1)}, f32[2,16,96]{2,1,0:T(8,128)S(1)}, u32[]{:S(2)}, u32[]{:S(2)}) collective-permute-start(f32[2,16,96]{2,1,0:T(8,128)S(1)} %maximum_add_fusion), channel_id=1, source_target_pairs={{16,0},{17,1},{18,2},{19,3},{20,4},{21,5},{22,6},{23,7},{10,8},{11... | collective-permute-start | bytes 36872 | tf_op jit(solution)/shard_map/ppermute | solution.py:328
  15.4 0.6 %shard_map.58.local_ref = f32[12,32,256]{2,1,0:T(8,128)S(1)} custom-call(bf16[16,12,2,256]{3,2,1,0:T(2,128)(2,1)S(1)} %bitcast.71, bf16[2,6,6,2,256]{4,3,2,1,0:T(2,128)(2,1)S(1)} %bitcast.73), custom_call_target="tpu_custom_call" | custom-call | flops 100000 | bytes 100000 | tf_op jit(solution)/shard_map/pallas_call | solution.py:204
  16.2 1.2 %collective-permute-done.5 = f32[2,16,96]{2,1,0:T(8,128)S(1)} collective-permute-done((f32[2,16,96]{2,1,0:T(8,128)S(1)}, f32[2,16,96]{2,1,0:T(8,128)S(1)}, u32[]{:S(2)}, u32[]{:S(2)}) %collective-permute-start.5) | collective-permute-done | bytes 12320 | tf_op jit(solution)/shard_map/ppermute | solution.py:328
  17.9 0.8 %collective-permute-done.7 = f32[2,16,96]{2,1,0:T(8,128)S(1)} collective-permute-done((f32[2,16,96]{2,1,0:T(8,128)S(1)}, f32[2,16,96]{2,1,0:T(8,128)S(1)}, u32[]{:S(2)}, u32[]{:S(2)}) %collective-permute-start.7) | collective-permute-done | bytes 12320 | tf_op jit(solution)/shard_map/ppermute | solution.py:328
  18.8 0.9 %collective-permute-start.9 = (f32[2,16,96]{2,1,0:T(8,128)S(1)}, f32[2,16,96]{2,1,0:T(8,128)S(1)}, u32[]{:S(2)}, u32[]{:S(2)}) collective-permute-start(f32[2,16,96]{2,1,0:T(8,128)S(1)} %maximum_add_fusion.1), channel_id=1, source_target_pairs={{1,0},{0,1},{3,2},{2,3},{5,4},{4,5},{7,6},{6,7},{14,8},{15,9},{12,... | collective-permute-start | bytes 36872 | tf_op jit(solution)/shard_map/ppermute | solution.py:328
  19.7 1.5 %collective-permute-start.8 = (f32[2,16,96]{2,1,0:T(8,128)S(1)}, f32[2,16,96]{2,1,0:T(8,128)S(1)}, u32[]{:S(2)}, u32[]{:S(2)}) collective-permute-start(f32[2,16,96]{2,1,0:T(8,128)S(1)} %maximum_add_fusion.1), channel_id=1, source_target_pairs={{16,0},{17,1},{18,2},{19,3},{20,4},{21,5},{22,6},{23,7},{10,8},{11... | collective-permute-start | bytes 36872 | tf_op jit(solution)/shard_map/ppermute | solution.py:328
  21.5 1.1 %collective-permute-done.9 = f32[2,16,96]{2,1,0:T(8,128)S(1)} collective-permute-done((f32[2,16,96]{2,1,0:T(8,128)S(1)}, f32[2,16,96]{2,1,0:T(8,128)S(1)}, u32[]{:S(2)}, u32[]{:S(2)}) %collective-permute-start.9) | collective-permute-done | bytes 12320 | tf_op jit(solution)/shard_map/ppermute | solution.py:328
  22.8 0.7 %collective-permute-done.8 = f32[2,16,96]{2,1,0:T(8,128)S(1)} collective-permute-done((f32[2,16,96]{2,1,0:T(8,128)S(1)}, f32[2,16,96]{2,1,0:T(8,128)S(1)}, u32[]{:S(2)}, u32[]{:S(2)}) %collective-permute-start.8) | collective-permute-done | bytes 12320 | tf_op jit(solution)/shard_map/ppermute | solution.py:328
  24.0 0.8 %collective-permute-done.10 = f32[2,16,96]{2,1,0:T(8,128)S(1)} collective-permute-done((f32[2,16,96]{2,1,0:T(8,128)S(1)}, f32[2,16,96]{2,1,0:T(8,128)S(1)}, u32[]{:S(2)}, u32[]{:S(2)}) %collective-permute-start.10) | collective-permute-done | bytes 12320 | tf_op jit(solution)/shard_map/ppermute | solution.py:328
  24.8 1.2 %collective-permute-start.12 = (f32[2,16,96]{2,1,0:T(8,128)S(1)}, f32[2,16,96]{2,1,0:T(8,128)S(1)}, u32[]{:S(2)}, u32[]{:S(2)}) collective-permute-start(f32[2,16,96]{2,1,0:T(8,128)S(1)} %maximum_add_fusion.2), channel_id=1, source_target_pairs={{1,0},{0,1},{3,2},{2,3},{5,4},{4,5},{7,6},{6,7},{14,8},{15,9},{12,... | collective-permute-start | bytes 36872 | tf_op jit(solution)/shard_map/ppermute | solution.py:328
  26.1 1.5 %collective-permute-start.11 = (f32[2,16,96]{2,1,0:T(8,128)S(1)}, f32[2,16,96]{2,1,0:T(8,128)S(1)}, u32[]{:S(2)}, u32[]{:S(2)}) collective-permute-start(f32[2,16,96]{2,1,0:T(8,128)S(1)} %maximum_add_fusion.2), channel_id=1, source_target_pairs={{16,0},{17,1},{18,2},{19,3},{20,4},{21,5},{22,6},{23,7},{10,8},{11... | collective-permute-start | bytes 36872 | tf_op jit(solution)/shard_map/ppermute | solution.py:328
  27.8 0.9 %collective-permute-done.12 = f32[2,16,96]{2,1,0:T(8,128)S(1)} collective-permute-done((f32[2,16,96]{2,1,0:T(8,128)S(1)}, f32[2,16,96]{2,1,0:T(8,128)S(1)}, u32[]{:S(2)}, u32[]{:S(2)}) %collective-permute-start.12) | collective-permute-done | bytes 12320 | tf_op jit(solution)/shard_map/ppermute | solution.py:328
  28.8 1.0 %collective-permute-done.11 = f32[2,16,96]{2,1,0:T(8,128)S(1)} collective-permute-done((f32[2,16,96]{2,1,0:T(8,128)S(1)}, f32[2,16,96]{2,1,0:T(8,128)S(1)}, u32[]{:S(2)}, u32[]{:S(2)}) %collective-permute-start.11) | collective-permute-done | bytes 12320 | tf_op jit(solution)/shard_map/ppermute | solution.py:328
  30.0 0.4 %collective-permute-start.13 = (f32[16,96]{1,0:T(8,128)S(1)}, f32[16,96]{1,0:T(8,128)S(1)}, u32[]{:S(2)}, u32[]{:S(2)}) collective-permute-start(f32[16,96]{1,0:T(8,128)S(1)} %get-tuple-element.37), channel_id=1, source_target_pairs={{8,0},{9,1},{10,2},{11,3},{12,4},{13,5},{14,6},{15,7},{0,8},{1,9},... | collective-permute-start | bytes 18440 | tf_op jit(solution)/shard_map/ppermute | solution.py:328
  30.4 0.8 %collective-permute-done.13.second_ref = f32[16,96]{1,0:T(8,128)S(1)} collective-permute-done((f32[16,96]{1,0:T(8,128)S(1)}, f32[16,96]{1,0:T(8,128)S(1)}, u32[]{:S(2)}, u32[]{:S(2)}) %collective-permute-start.13) | collective-permute-done | bytes 6176 | tf_op jit(solution)/shard_map/ppermute | solution.py:328
  31.2 0.9 %shard_map.60 = bf16[16,12,2,256]{3,2,1,0:T(2,128)(2,1)} custom-call(f32[16,96]{1,0:T(8,128)S(1)} %get-tuple-element.38.first_ref, f32[16,96]{1,0:T(8,128)S(1)} %collective-permute-done.13.second_ref, f32[16,96]{1,0:T(8,128)S(1)} %get-tuple-element.28.used_ref, bf16[12,48,256]{2,1,0:T(8,128)(2,1)S(1)} %shard_map.59.vectors_ref, ...), custom_call_target="tpu_custom_call" | custom-call | flops 10000000 | bytes 1000000 | tf_op jit(solution)/shard_map/pallas_call | solution.py:145
  (46 shorter events, 4.1 us)
Async XLA Ops:
  0.7 2.1 %copy-start.3 = (f32[1,9,2,2304]{3,2,1,0:T(2,128)S(1)}, f32[1,9,2,2304]{3,2,1,0:T(2,128)}, u32[]{:S(2)}) copy-start(f32[1,9,2,2304]{3,2,1,0:T(2,128)} %param.8) | copy-start | bytes 497668
  2.2 1.3 %collective-permute-start = (f32[16,96]{1,0:T(8,128)S(1)}, f32[16,96]{1,0:T(8,128)S(1)}, u32[]{:S(2)}, u32[]{:S(2)}) collective-permute-start(f32[16,96]{1,0:T(8,128)S(1)} %get-tuple-element.19), channel_id=1, source_target_pairs={{8,0},{9,1},{10,2},{11,3},{12,4},{13,5},{14,6},{15,7},{0,8},{1,9},... | collective-permute-start | bytes 18440 | tf_op jit(solution)/shard_map/ppermute | solution.py:328
  2.9 5.1 %collective-permute-start.2 = (f32[2,2,2304]{2,1,0:T(2,128)S(1)}, f32[2,2,2304]{2,1,0:T(2,128)S(1)}, u32[]{:S(2)}, u32[]{:S(2)}) collective-permute-start(f32[2,2,2304]{2,1,0:T(2,128)S(1)} %maximum_select_fusion.1), channel_id=1, source_target_pairs={{8,0},{9,1},{10,2},{11,3},{12,4},{13,5},{14,6},{15,7},{0,8},{1,9},... | collective-permute-start | bytes 110600 | tf_op jit(solution)/shard_map/ppermute | solution.py:328
  3.6 4.9 %collective-permute-start.3 = (f32[2,16,96]{2,1,0:T(8,128)S(1)}, f32[2,16,96]{2,1,0:T(8,128)S(1)}, u32[]{:S(2)}, u32[]{:S(2)}) collective-permute-start(f32[2,16,96]{2,1,0:T(8,128)S(1)} %pad_maximum_fusion.1), channel_id=1, source_target_pairs={{1,0},{0,1},{3,2},{2,3},{5,4},{4,5},{7,6},{6,7},{14,8},{15,9},{12,... | collective-permute-start | bytes 36872 | tf_op jit(solution)/shard_map/ppermute | solution.py:328
  6.4 3.7 %collective-permute-start.1 = (f32[2,16,96]{2,1,0:T(8,128)S(1)}, f32[2,16,96]{2,1,0:T(8,128)S(1)}, u32[]{:S(2)}, u32[]{:S(2)}) collective-permute-start(f32[2,16,96]{2,1,0:T(8,128)S(1)} %pad_maximum_fusion.1), channel_id=1, source_target_pairs={{16,0},{17,1},{18,2},{19,3},{20,4},{21,5},{22,6},{23,7},{10,8},{11... | collective-permute-start | bytes 36872 | tf_op jit(solution)/shard_map/ppermute | solution.py:328
  8.7 6.7 %copy-start.1 = (bf16[16,2,12,256]{3,1,2,0:T(2,128)(2,1)S(1)}, bf16[16,2,12,256]{3,1,2,0:T(2,128)(2,1)}, u32[]{:S(2)}) copy-start(bf16[16,2,12,256]{3,1,2,0:T(2,128)(2,1)} %param.5) | copy-start | bytes 589828
  10.3 1.7 %collective-permute-start.4 = (f32[2,16,96]{2,1,0:T(8,128)S(1)}, f32[2,16,96]{2,1,0:T(8,128)S(1)}, u32[]{:S(2)}, u32[]{:S(2)}) collective-permute-start(f32[2,16,96]{2,1,0:T(8,128)S(1)} %convolution_add_fusion.7), channel_id=1, source_target_pairs={{8,0},{9,1},{10,2},{11,3},{12,4},{13,5},{14,6},{15,7},{0,8},{1,9},... | collective-permute-start | bytes 36872 | tf_op jit(solution)/shard_map/ppermute | solution.py:328
  12.1 3.3 %copy-start.2 = (bf16[2,2,6,6,256]{4,1,3,2,0:T(2,128)(2,1)S(1)}, bf16[2,2,6,6,256]{4,1,3,2,0:T(2,128)(2,1)}, u32[]{:S(2)}) copy-start(bf16[2,2,6,6,256]{4,1,3,2,0:T(2,128)(2,1)} %param.7) | copy-start | bytes 221188
  12.1 3.9 %collective-permute-start.6 = (f32[2,16,96]{2,1,0:T(8,128)S(1)}, f32[2,16,96]{2,1,0:T(8,128)S(1)}, u32[]{:S(2)}, u32[]{:S(2)}) collective-permute-start(f32[2,16,96]{2,1,0:T(8,128)S(1)} %maximum_add_fusion), channel_id=1, source_target_pairs={{1,0},{0,1},{3,2},{2,3},{5,4},{4,5},{7,6},{6,7},{14,8},{15,9},{12,... | collective-permute-start | bytes 36872 | tf_op jit(solution)/shard_map/ppermute | solution.py:328
  13.6 3.7 %collective-permute-start.5 = (f32[2,16,96]{2,1,0:T(8,128)S(1)}, f32[2,16,96]{2,1,0:T(8,128)S(1)}, u32[]{:S(2)}, u32[]{:S(2)}) collective-permute-start(f32[2,16,96]{2,1,0:T(8,128)S(1)} %maximum_add_fusion), channel_id=1, source_target_pairs={{16,0},{17,1},{18,2},{19,3},{20,4},{21,5},{22,6},{23,7},{10,8},{11... | collective-permute-start | bytes 36872 | tf_op jit(solution)/shard_map/ppermute | solution.py:328
  16.0 5.4 %copy-start = (bf16[2,24,12,256]{3,1,2,0:T(8,128)(2,1)S(1)}, bf16[2,24,12,256]{3,1,2,0:T(8,128)(2,1)}, u32[]{:S(2)}) copy-start(bf16[2,24,12,256]{3,1,2,0:T(8,128)(2,1)} %param.6) | copy-start | bytes 884740
  17.5 1.2 %collective-permute-start.7 = (f32[2,16,96]{2,1,0:T(8,128)S(1)}, f32[2,16,96]{2,1,0:T(8,128)S(1)}, u32[]{:S(2)}, u32[]{:S(2)}) collective-permute-start(f32[2,16,96]{2,1,0:T(8,128)S(1)} %convolution_add_fusion.5), channel_id=1, source_target_pairs={{8,0},{9,1},{10,2},{11,3},{12,4},{13,5},{14,6},{15,7},{0,8},{1,9},... | collective-permute-start | bytes 36872 | tf_op jit(solution)/shard_map/ppermute | solution.py:328
  18.8 3.8 %collective-permute-start.9 = (f32[2,16,96]{2,1,0:T(8,128)S(1)}, f32[2,16,96]{2,1,0:T(8,128)S(1)}, u32[]{:S(2)}, u32[]{:S(2)}) collective-permute-start(f32[2,16,96]{2,1,0:T(8,128)S(1)} %maximum_add_fusion.1), channel_id=1, source_target_pairs={{1,0},{0,1},{3,2},{2,3},{5,4},{4,5},{7,6},{6,7},{14,8},{15,9},{12,... | collective-permute-start | bytes 36872 | tf_op jit(solution)/shard_map/ppermute | solution.py:328
  19.7 3.7 %collective-permute-start.8 = (f32[2,16,96]{2,1,0:T(8,128)S(1)}, f32[2,16,96]{2,1,0:T(8,128)S(1)}, u32[]{:S(2)}, u32[]{:S(2)}) collective-permute-start(f32[2,16,96]{2,1,0:T(8,128)S(1)} %maximum_add_fusion.1), channel_id=1, source_target_pairs={{16,0},{17,1},{18,2},{19,3},{20,4},{21,5},{22,6},{23,7},{10,8},{11... | collective-permute-start | bytes 36872 | tf_op jit(solution)/shard_map/ppermute | solution.py:328
  23.6 1.2 %collective-permute-start.10 = (f32[2,16,96]{2,1,0:T(8,128)S(1)}, f32[2,16,96]{2,1,0:T(8,128)S(1)}, u32[]{:S(2)}, u32[]{:S(2)}) collective-permute-start(f32[2,16,96]{2,1,0:T(8,128)S(1)} %convolution_add_fusion.3), channel_id=1, source_target_pairs={{8,0},{9,1},{10,2},{11,3},{12,4},{13,5},{14,6},{15,7},{0,8},{1,9},... | collective-permute-start | bytes 36872 | tf_op jit(solution)/shard_map/ppermute | solution.py:328
  24.8 3.8 %collective-permute-start.12 = (f32[2,16,96]{2,1,0:T(8,128)S(1)}, f32[2,16,96]{2,1,0:T(8,128)S(1)}, u32[]{:S(2)}, u32[]{:S(2)}) collective-permute-start(f32[2,16,96]{2,1,0:T(8,128)S(1)} %maximum_add_fusion.2), channel_id=1, source_target_pairs={{1,0},{0,1},{3,2},{2,3},{5,4},{4,5},{7,6},{6,7},{14,8},{15,9},{12,... | collective-permute-start | bytes 36872 | tf_op jit(solution)/shard_map/ppermute | solution.py:328
  26.1 3.7 %collective-permute-start.11 = (f32[2,16,96]{2,1,0:T(8,128)S(1)}, f32[2,16,96]{2,1,0:T(8,128)S(1)}, u32[]{:S(2)}, u32[]{:S(2)}) collective-permute-start(f32[2,16,96]{2,1,0:T(8,128)S(1)} %maximum_add_fusion.2), channel_id=1, source_target_pairs={{16,0},{17,1},{18,2},{19,3},{20,4},{21,5},{22,6},{23,7},{10,8},{11... | collective-permute-start | bytes 36872 | tf_op jit(solution)/shard_map/ppermute | solution.py:328
  30.0 1.2 %collective-permute-start.13 = (f32[16,96]{1,0:T(8,128)S(1)}, f32[16,96]{1,0:T(8,128)S(1)}, u32[]{:S(2)}, u32[]{:S(2)}) collective-permute-start(f32[16,96]{1,0:T(8,128)S(1)} %get-tuple-element.37), channel_id=1, source_target_pairs={{8,0},{9,1},{10,2},{11,3},{12,4},{13,5},{14,6},{15,7},{0,8},{1,9},... | collective-permute-start | bytes 18440 | tf_op jit(solution)/shard_map/ppermute | solution.py:328
